TPU v7x, 32 devices: a whole 2x2x4 slice. The times are simulated.
32 devices in a mesh: ulysses: 4 (over z), blk: 8 (over y, x, core).
Axes of the slice: x: 2, y: 2, z: 4, core: 2. Of those that a mesh axis runs over, the one named last changes fastest.
Arguments:
- tokens: bfloat16 [4096, 1536], P(('ulysses', 'blk')), may hold values from -6 to 6
- lengths: int32 [3], replicated, may hold values from 1 to 2048, 4096 in all
- routes: int32 [4096, 8], P(('ulysses', 'blk')), may hold values from 0 to 15, all different within a row; in each aligned block of 128 rows (0 to 127, 128 to 255, ...) at most 96 rows name the same one
- gain_attn: bfloat16 [1536], P(('ulysses', 'blk')), may hold values from 0.5 to 1.5
- w_query: bfloat16 [1536, 1536], P(('ulysses', 'blk')), may hold values from -0.21875 to 0.21875
- key_projection: bfloat16 [1536, 512], P(('ulysses', 'blk')), may hold values from -0.15625 to 0.15625
- value_projection: bfloat16 [1536, 512], P(('ulysses', 'blk')), may hold values from -0.15625 to 0.15625
- w_output: bfloat16 [1536, 1536], P(('ulysses', 'blk')), may hold values from -2.5 to 2.5
- gain_moe: bfloat16 [1536], P(('ulysses', 'blk')), may hold values from 0.5 to 1.5
- w_router: bfloat16 [1536, 16], P(('ulysses', 'blk')), may hold values from -0.078125 to 0.078125
- w_inner: bfloat16 [16, 1536, 1024], P('blk', 'ulysses'), may hold values from -0.15625 to 0.15625
- w_outer: bfloat16 [16, 512, 1536], P('blk', None, 'ulysses'), may hold values from -1 to 1
- cotangent: bfloat16 [4096, 1536], P(('ulysses', 'blk')), may hold values from -6 to 6
Outputs:
- out: float32 [4096, 1536], P(('ulysses', 'blk'))
- d_tokens: float32 [4096, 1536], P(('ulysses', 'blk'))
- d_gain_attn: float32 [1536], P(('ulysses', 'blk'))
- d_w_query: float32 [1536, 1536], P(('ulysses', 'blk'))
- d_w_key: float32 [1536, 512], P(('ulysses', 'blk'))
- d_w_value: float32 [1536, 512], P(('ulysses', 'blk'))
- d_w_output: float32 [1536, 1536], P(('ulysses', 'blk'))
- d_gain_moe: float32 [1536], P(('ulysses', 'blk'))
- d_w_router: float32 [1536, 16], P(('ulysses', 'blk'))
- d_w_inner: float32 [16, 1536, 1024], P('blk', 'ulysses')
- d_w_outer: float32 [16, 512, 1536], P('blk', None, 'ulysses')
Inputs may be any that keep to these rules, and one draw needn't show every extreme that they name: `lengths`: the 3 sequences fill the 4096 rows in order; the longest has exactly 2048 rows. `routes`: A row names 8 different experts; among the rows of one device no expert is named by more than 96 rows, and some expert reaches 96.
All inputs are finite; a program needn't handle non-finite values.
Results may differ from a plain program's by a relative error of at most 0.04.
Values may be sent and summed in bfloat16 or wider, within the bound.
A program may use at most 192 MiB of HBM per device.

v0:
```python
import math

import jax
import jax.numpy as jnp
from jax import lax
from jax.sharding import PartitionSpec as P

MODEL_WIDTH = 1536
QUERY_HEADS = 24
KEY_VALUE_HEADS = 8
HEAD_WIDTH = 64
FF = 512
TOPK = 8
EXP_DEV = 2
LENMAX = 4096


EPSILON = 1e-05
THETA = 10000.0
NEGATIVE = -1e30
faraway = 1 << 30


def locate(global_rows, lengths):
    ends = jnp.cumsum(lengths)
    passed = global_rows[..., None] >= ends
    segment = jnp.sum(passed.astype(jnp.int32), axis=-1)
    opening = jnp.sum(jnp.where(passed, lengths, 0), axis=-1)
    return (segment, global_rows - opening)


def rope_tables(positions, head_size):
    halves = head_size // 2
    frequency = THETA ** (-(jnp.arange(halves, dtype=jnp.float32) * 2.0 / head_size))
    angles = positions.astype(jnp.float32)[:, None] * frequency[None, :]
    return (jnp.cos(angles), jnp.sin(angles))


def rotate(value_tensor, cosine, sine_table):
    halves = value_tensor.shape[-1] // 2
    leading = value_tensor[..., :halves]
    trailing = value_tensor[..., halves:]
    cosine_rows = cosine[:, None, :]
    sine_rows = sine_table[:, None, :]
    return jnp.concatenate(
        [
            leading * cosine_rows - trailing * sine_rows,
            trailing * cosine_rows + leading * sine_rows,
        ],
        axis=-1,
    )


def rotate_back(gradient, cosine, sine_table):
    halves = gradient.shape[-1] // 2
    leading = gradient[..., :halves]
    trailing = gradient[..., halves:]
    cosine_rows = cosine[:, None, :]
    sine_rows = sine_table[:, None, :]
    return jnp.concatenate(
        [
            leading * cosine_rows + trailing * sine_rows,
            trailing * cosine_rows - leading * sine_rows,
        ],
        axis=-1,
    )


def norm_rows(value_tensor, gain):
    inverse = lax.rsqrt(jnp.mean(value_tensor * value_tensor, axis=-1, keepdims=True) + EPSILON)
    normed = value_tensor * inverse
    return (normed, inverse, normed * gain)


def norm_back(upstream, normed, inverse, gain):
    d_normed = upstream * gain
    d_gain = jnp.sum(upstream * normed, axis=0)
    d_values = inverse * (d_normed - normed * jnp.mean(d_normed * normed, axis=-1, keepdims=True))
    return (d_values, d_gain)


def window(stripes, reach, fill_value):
    count_rows = stripes.shape[0]
    layers = []
    for offset in range(reach):
        padding = jnp.full((offset,) + stripes.shape[1:], fill_value, stripes.dtype)
        layers.append(jnp.concatenate([padding, stripes[: count_rows - offset]], axis=0))
    return jnp.stack(layers, axis=0)


def unwindow(layered):
    reach = layered.shape[0]
    summed = layered[0]
    for offset in range(1, reach):
        padding = jnp.zeros((offset,) + layered.shape[2:], layered.dtype)
        summed = summed + jnp.concatenate([layered[offset, offset:], padding], axis=0)
    return summed


def dispatch(route_rows, experts, capacity):
    flat_routes = route_rows.reshape(-1)
    onehot = (flat_routes[:, None] == jnp.arange(experts, dtype=jnp.int32)[None, :]).astype(
        jnp.int32
    )
    ranking = jnp.sum(jnp.cumsum(onehot, axis=0) * onehot, axis=1) - 1
    slot_place = flat_routes * capacity + ranking
    slot_count = flat_routes.shape[0]
    slot_of_row = (
        jnp.full((experts * capacity,), slot_count, jnp.int32)
        .at[slot_place]
        .set(jnp.arange(slot_count, dtype=jnp.int32))
    )
    return (slot_place, slot_of_row)


def to_experts(buffer):
    return lax.all_to_all(buffer, "blk", split_axis=0, concat_axis=1, tiled=True)


def to_tokens(buffer):
    return lax.all_to_all(buffer, "blk", split_axis=1, concat_axis=0, tiled=True)


def on_device(
    tokens,
    lengths,
    routes,
    gain_attn,
    w_query,
    key_projection,
    value_projection,
    w_output,
    gain_moe,
    w_router,
    w_inner,
    w_outer,
    cotangent,
):
    sequence_parallel_count = lax.axis_size("ulysses")
    blk_count = lax.axis_size("blk")
    uly_index = lax.axis_index("ulysses")
    blk_index = lax.axis_index("blk")
    count_of_rows = tokens.shape[0]
    heads_per_group = QUERY_HEADS // KEY_VALUE_HEADS
    query_local = QUERY_HEADS // sequence_parallel_count
    shared_locally = KEY_VALUE_HEADS // sequence_parallel_count
    expert_count = EXP_DEV * blk_count
    capacity = 3 * count_of_rows * TOPK // (2 * expert_count)
    longest = min(LENMAX, sequence_parallel_count * blk_count * count_of_rows // 2)
    reach = min(
        sequence_parallel_count,
        (longest + blk_count * count_of_rows - 2) // (blk_count * count_of_rows) + 1,
    )
    scale = 1.0 / math.sqrt(HEAD_WIDTH)
    f32 = jnp.float32
    bf16 = jnp.bfloat16
    attn_gain, query_weight, key_matrix, value_matrix, output_weight, moe_gain, router_weight = (
        lax.all_gather(gain_attn, ("ulysses", "blk"), axis=0, tiled=True),
        lax.all_gather(w_query, ("ulysses", "blk"), axis=0, tiled=True),
        lax.all_gather(key_projection, ("ulysses", "blk"), axis=0, tiled=True),
        lax.all_gather(value_projection, ("ulysses", "blk"), axis=0, tiled=True),
        lax.all_gather(w_output, ("ulysses", "blk"), axis=0, tiled=True),
        lax.all_gather(gain_moe, ("ulysses", "blk"), axis=0, tiled=True),
        lax.all_gather(w_router, ("ulysses", "blk"), axis=0, tiled=True),
    )
    inner_full, outer_full = (
        lax.all_gather(w_inner, "ulysses", axis=1, tiled=True),
        lax.all_gather(w_outer, "ulysses", axis=2, tiled=True),
    )
    attn_gain = attn_gain.astype(f32)
    moe_gain = moe_gain.astype(f32)
    own_rows = (uly_index * blk_count + blk_index) * count_of_rows + jnp.arange(
        count_of_rows, dtype=jnp.int32
    )
    _, positions = locate(own_rows, lengths)
    cosine, sine_table = rope_tables(positions, HEAD_WIDTH)
    inputs = tokens.astype(f32)
    normed_one, inverse_one, scaled_one = norm_rows(inputs, attn_gain)
    first_hidden = scaled_one.astype(bf16)
    query_lin = jnp.dot(first_hidden, query_weight, preferred_element_type=f32).reshape(
        count_of_rows, QUERY_HEADS, HEAD_WIDTH
    )
    key_linear = jnp.dot(first_hidden, key_matrix, preferred_element_type=f32).reshape(
        count_of_rows, KEY_VALUE_HEADS, HEAD_WIDTH
    )
    rows_of_value = (
        jnp.dot(first_hidden, value_matrix, preferred_element_type=f32)
        .astype(bf16)
        .reshape(count_of_rows, KEY_VALUE_HEADS, HEAD_WIDTH)
    )
    query_rows_tok = rotate(query_lin, cosine, sine_table).astype(bf16)
    key_rows_tok = rotate(key_linear, cosine, sine_table).astype(bf16)
    query_split, key_split, value_split = (
        lax.all_to_all(query_rows_tok, "ulysses", split_axis=1, concat_axis=0, tiled=True),
        lax.all_to_all(key_rows_tok, "ulysses", split_axis=1, concat_axis=0, tiled=True),
        lax.all_to_all(rows_of_value, "ulysses", split_axis=1, concat_axis=0, tiled=True),
    )
    query_tensor = query_split.reshape(
        sequence_parallel_count, count_of_rows, shared_locally, heads_per_group, HEAD_WIDTH
    )
    key_heads = key_split.reshape(
        sequence_parallel_count, count_of_rows, shared_locally, HEAD_WIDTH
    )
    value_heads = value_split.reshape(
        sequence_parallel_count, count_of_rows, shared_locally, HEAD_WIDTH
    )
    key_all, value_all = (
        lax.all_gather(key_heads[None], "blk", axis=0, tiled=True),
        lax.all_gather(value_heads[None], "blk", axis=0, tiled=True),
    )
    stripe_index = jnp.arange(sequence_parallel_count, dtype=jnp.int32)
    row_offsets = jnp.arange(count_of_rows, dtype=jnp.int32)

    def stripe_rows(device):
        return (stripe_index[:, None] * blk_count + device) * count_of_rows + row_offsets[None, :]

    query_rows = stripe_rows(blk_index)
    query_segs, _ = locate(query_rows, lengths)

    def scores_for(query_tile, rows_query, segs_query, key_stripes, key_device):
        key_layers = window(key_stripes, reach, 0)
        rows_key = stripe_rows(key_device)
        segs_key, _ = locate(rows_key, lengths)
        rows_window = jnp.transpose(window(rows_key, reach, faraway), (1, 0, 2))
        segs_window = jnp.transpose(window(segs_key, reach, -1), (1, 0, 2))
        scores = (
            jnp.einsum("uqhgd,juthd->uqhgjt", query_tile, key_layers, preferred_element_type=f32)
            * scale
        )
        visible = (rows_window[:, None] <= rows_query[:, :, None, None]) & (
            segs_window[:, None] == segs_query[:, :, None, None]
        )
        return (scores, visible[:, :, None, None], key_layers)

    def forward_step(device, carried):
        run_max, run_sum, accumulated = carried
        scores, visible, _ = scores_for(
            query_tensor, query_rows, query_segs, key_all[device], device
        )
        value_layers = window(value_all[device], reach, 0)
        scores = jnp.where(visible, scores, NEGATIVE)
        new_max = jnp.maximum(run_max, jnp.max(scores, axis=(4, 5)))
        factor = jnp.exp(run_max - new_max)
        weights = jnp.where(visible, jnp.exp(scores - new_max[..., None, None]), 0.0)
        run_sum = run_sum * factor + jnp.sum(weights, axis=(4, 5))
        accumulated = accumulated * factor[..., None] + jnp.einsum(
            "uqhgjt,juthd->uqhgd", weights.astype(bf16), value_layers, preferred_element_type=f32
        )
        return (new_max, run_sum, accumulated)

    stat_shape = (sequence_parallel_count, count_of_rows, shared_locally, heads_per_group)
    starting = (
        jnp.full(stat_shape, NEGATIVE, f32),
        jnp.zeros(stat_shape, f32),
        jnp.zeros(stat_shape + (HEAD_WIDTH,), f32),
    )
    run_max, run_sum, accumulated = lax.fori_loop(0, blk_count, forward_step, starting)
    attn_full = accumulated / run_sum[..., None]
    log_total = run_max + jnp.log(run_sum)
    mixed_heads = attn_full.astype(bf16).reshape(
        sequence_parallel_count * count_of_rows, query_local, HEAD_WIDTH
    )
    mixed_tok = lax.all_to_all(
        mixed_heads, "ulysses", split_axis=0, concat_axis=1, tiled=True
    ).reshape(count_of_rows, QUERY_HEADS * HEAD_WIDTH)
    attn_out = jnp.dot(mixed_tok, output_weight, preferred_element_type=f32)
    residual = inputs + attn_out
    normed_two, inverse_two, scaled_two = norm_rows(residual, moe_gain)
    hidden_two = scaled_two.astype(bf16)
    logits = jnp.dot(hidden_two, router_weight, preferred_element_type=f32)
    chosen_hot = routes[:, :, None] == jnp.arange(expert_count, dtype=jnp.int32)[None, None, :]
    chosen = jnp.sum(jnp.where(chosen_hot, logits[:, None, :], 0.0), axis=2)
    gates = jax.nn.softmax(chosen, axis=1)
    slot_place, slot_of_row = dispatch(routes, expert_count, capacity)
    token_of_row = slot_of_row // TOPK
    padded_hidden = jnp.concatenate([hidden_two, jnp.zeros((1, MODEL_WIDTH), bf16)], axis=0)
    send_rows = jnp.take(padded_hidden, token_of_row, axis=0).reshape(
        expert_count, capacity, MODEL_WIDTH
    )
    expert_rows = to_experts(send_rows)
    gate_up = jnp.einsum("erd,edf->erf", expert_rows, inner_full, preferred_element_type=f32)
    gate_part = gate_up[..., :FF]
    up_part = gate_up[..., FF:]
    sigmoid_gate = jax.nn.sigmoid(gate_part)
    silu_gate = gate_part * sigmoid_gate
    activation = (silu_gate * up_part).astype(bf16)
    expert_out = jnp.einsum(
        "erf,efd->erd", activation, outer_full, preferred_element_type=f32
    ).astype(bf16)
    returned = to_tokens(expert_out).reshape(expert_count * capacity, MODEL_WIDTH)
    picked = (
        jnp.take(returned, slot_place, axis=0).reshape(count_of_rows, TOPK, MODEL_WIDTH).astype(f32)
    )
    result = residual + jnp.sum(gates[:, :, None] * picked, axis=1)
    upstream = cotangent.astype(f32)
    d_gates = jnp.sum(upstream[:, None, :] * picked, axis=2)
    slot_grads = (
        (gates[:, :, None] * upstream[:, None, :])
        .astype(bf16)
        .reshape(count_of_rows * TOPK, MODEL_WIDTH)
    )
    padded_grads = jnp.concatenate([slot_grads, jnp.zeros((1, MODEL_WIDTH), bf16)], axis=0)
    grad_rows = to_experts(
        jnp.take(padded_grads, slot_of_row, axis=0).reshape(expert_count, capacity, MODEL_WIDTH)
    )
    d_activation = jnp.einsum("erd,efd->erf", grad_rows, outer_full, preferred_element_type=f32)
    d_outer = jnp.einsum("erf,erd->efd", activation, grad_rows, preferred_element_type=f32)
    d_gate_part = d_activation * up_part * (sigmoid_gate * (1.0 + gate_part * (1.0 - sigmoid_gate)))
    d_up_part = d_activation * silu_gate
    d_gate_up = jnp.concatenate([d_gate_part, d_up_part], axis=-1).astype(bf16)
    d_inner = jnp.einsum("erd,erf->edf", expert_rows, d_gate_up, preferred_element_type=f32)
    d_rows = jnp.einsum("erf,edf->erd", d_gate_up, inner_full, preferred_element_type=f32).astype(
        bf16
    )
    back_rows = to_tokens(d_rows).reshape(expert_count * capacity, MODEL_WIDTH)
    d_hidden_two = jnp.sum(
        jnp.take(back_rows, slot_place, axis=0)
        .reshape(count_of_rows, TOPK, MODEL_WIDTH)
        .astype(f32),
        axis=1,
    )
    d_chosen = gates * (d_gates - jnp.sum(gates * d_gates, axis=1, keepdims=True))
    d_logits = jnp.sum(jnp.where(chosen_hot, d_chosen[:, :, None], 0.0), axis=1).astype(bf16)
    d_router = jnp.dot(hidden_two.T, d_logits, preferred_element_type=f32)
    d_hidden_two = d_hidden_two + jnp.dot(d_logits, router_weight.T, preferred_element_type=f32)
    d_norm_two, d_gain_two = norm_back(d_hidden_two, normed_two, inverse_two, moe_gain)
    d_residual = upstream + d_norm_two
    d_attn = d_residual.astype(bf16)
    d_output_weight = jnp.dot(mixed_tok.T, d_attn, preferred_element_type=f32)
    d_mixed = (
        jnp.dot(d_attn, output_weight.T, preferred_element_type=f32)
        .astype(bf16)
        .reshape(count_of_rows, QUERY_HEADS, HEAD_WIDTH)
    )
    d_mixed_heads = lax.all_to_all(
        d_mixed, "ulysses", split_axis=1, concat_axis=0, tiled=True
    ).reshape(sequence_parallel_count, count_of_rows, shared_locally, heads_per_group, HEAD_WIDTH)
    delta = jnp.sum(d_mixed_heads.astype(f32) * attn_full, axis=-1)

    def block_grads(
        query_tile,
        grad_block,
        total_block,
        delta_block,
        rows_query,
        segs_query,
        key_stripes,
        value_stripes,
        key_device,
    ):
        scores, visible, key_layers = scores_for(
            query_tile, rows_query, segs_query, key_stripes, key_device
        )
        value_layers = window(value_stripes, reach, 0)
        probs = jnp.where(visible, jnp.exp(scores - total_block[..., None, None]), 0.0)
        d_probs = jnp.einsum(
            "uqhgd,juthd->uqhgjt", grad_block, value_layers, preferred_element_type=f32
        )
        d_scores = (probs * (d_probs - delta_block[..., None, None])).astype(bf16)
        d_query = (
            jnp.einsum("uqhgjt,juthd->uqhgd", d_scores, key_layers, preferred_element_type=f32)
            * scale
        )
        d_key = unwindow(
            jnp.einsum("uqhgjt,uqhgd->juthd", d_scores, query_tile, preferred_element_type=f32)
            * scale
        )
        d_value = unwindow(
            jnp.einsum(
                "uqhgjt,uqhgd->juthd", probs.astype(bf16), grad_block, preferred_element_type=f32
            )
        )
        return (d_query, d_key, d_value)

    def query_step(device, d_query_sum):
        d_query, _, _ = block_grads(
            query_tensor,
            d_mixed_heads,
            log_total,
            delta,
            query_rows,
            query_segs,
            key_all[device],
            value_all[device],
            device,
        )
        return d_query_sum + d_query

    d_query_sum = lax.fori_loop(
        0, blk_count, query_step, jnp.zeros(stat_shape + (HEAD_WIDTH,), f32)
    )
    far_query, far_grad, far_total, far_delta = (
        lax.all_gather(query_tensor[None], "blk", axis=0, tiled=True),
        lax.all_gather(d_mixed_heads[None], "blk", axis=0, tiled=True),
        lax.all_gather(log_total[None].astype(jnp.bfloat16), "blk", axis=0, tiled=True).astype(
            jnp.float32
        ),
        lax.all_gather(delta[None].astype(jnp.bfloat16), "blk", axis=0, tiled=True).astype(
            jnp.float32
        ),
    )

    def key_step(device, carried):
        d_key_sum, d_value_sum = carried
        rows_query = stripe_rows(device)
        segs_query, _ = locate(rows_query, lengths)
        _, d_key, d_value = block_grads(
            far_query[device],
            far_grad[device],
            far_total[device],
            far_delta[device],
            rows_query,
            segs_query,
            key_heads,
            value_heads,
            blk_index,
        )
        return (d_key_sum + d_key, d_value_sum + d_value)

    d_key_own, d_value_own = lax.fori_loop(
        0, blk_count, key_step, (jnp.zeros(key_heads.shape, f32), jnp.zeros(value_heads.shape, f32))
    )
    d_query_tok, d_key_tok, value_token_gradient = (
        lax.all_to_all(
            d_query_sum.astype(bf16).reshape(
                sequence_parallel_count * count_of_rows, query_local, HEAD_WIDTH
            ),
            "ulysses",
            split_axis=0,
            concat_axis=1,
            tiled=True,
        ),
        lax.all_to_all(
            d_key_own.astype(bf16).reshape(
                sequence_parallel_count * count_of_rows, shared_locally, HEAD_WIDTH
            ),
            "ulysses",
            split_axis=0,
            concat_axis=1,
            tiled=True,
        ),
        lax.all_to_all(
            d_value_own.astype(bf16).reshape(
                sequence_parallel_count * count_of_rows, shared_locally, HEAD_WIDTH
            ),
            "ulysses",
            split_axis=0,
            concat_axis=1,
            tiled=True,
        ),
    )
    d_query_lin = (
        rotate_back(d_query_tok.astype(f32), cosine, sine_table)
        .astype(bf16)
        .reshape(count_of_rows, QUERY_HEADS * HEAD_WIDTH)
    )
    d_key_lin = (
        rotate_back(d_key_tok.astype(f32), cosine, sine_table)
        .astype(bf16)
        .reshape(count_of_rows, KEY_VALUE_HEADS * HEAD_WIDTH)
    )
    value_linear_gradient = value_token_gradient.reshape(
        count_of_rows, KEY_VALUE_HEADS * HEAD_WIDTH
    )
    d_query_weight = jnp.dot(first_hidden.T, d_query_lin, preferred_element_type=f32)
    d_key_weight = jnp.dot(first_hidden.T, d_key_lin, preferred_element_type=f32)
    d_value_weight = jnp.dot(first_hidden.T, value_linear_gradient, preferred_element_type=f32)
    d_hidden_one = (
        jnp.dot(d_query_lin, query_weight.T, preferred_element_type=f32)
        + jnp.dot(d_key_lin, key_matrix.T, preferred_element_type=f32)
        + jnp.dot(value_linear_gradient, value_matrix.T, preferred_element_type=f32)
    )
    d_norm_one, d_gain_one = norm_back(d_hidden_one, normed_one, inverse_one, attn_gain)
    d_tokens = d_residual + d_norm_one
    (
        shard_gain_one,
        shard_query,
        shard_key,
        shard_value,
        shard_output,
        shard_gain_two,
        shard_router,
    ) = (
        lax.psum_scatter(d_gain_one, ("ulysses", "blk"), scatter_dimension=0, tiled=True),
        lax.psum_scatter(d_query_weight, ("ulysses", "blk"), scatter_dimension=0, tiled=True),
        lax.psum_scatter(d_key_weight, ("ulysses", "blk"), scatter_dimension=0, tiled=True),
        lax.psum_scatter(d_value_weight, ("ulysses", "blk"), scatter_dimension=0, tiled=True),
        lax.psum_scatter(d_output_weight, ("ulysses", "blk"), scatter_dimension=0, tiled=True),
        lax.psum_scatter(d_gain_two, ("ulysses", "blk"), scatter_dimension=0, tiled=True),
        lax.psum_scatter(d_router, ("ulysses", "blk"), scatter_dimension=0, tiled=True),
    )
    shard_inner, shard_outer = (
        lax.psum_scatter(d_inner, "ulysses", scatter_dimension=1, tiled=True),
        lax.psum_scatter(d_outer, "ulysses", scatter_dimension=2, tiled=True),
    )
    return (
        result,
        d_tokens,
        shard_gain_one,
        shard_query,
        shard_key,
        shard_value,
        shard_output,
        shard_gain_two,
        shard_router,
        shard_inner,
        shard_outer,
    )


def solution(mesh):
    return jax.shard_map(
        on_device,
        mesh=mesh,
        in_specs=(
            P(("ulysses", "blk"), None),
            P(),
            P(("ulysses", "blk"), None),
            P(("ulysses", "blk")),
            P(("ulysses", "blk"), None),
            P(("ulysses", "blk"), None),
            P(("ulysses", "blk"), None),
            P(("ulysses", "blk"), None),
            P(("ulysses", "blk")),
            P(("ulysses", "blk"), None),
            P("blk", "ulysses", None),
            P("blk", None, "ulysses"),
            P(("ulysses", "blk"), None),
        ),
        out_specs=(
            P(("ulysses", "blk"), None),
            P(("ulysses", "blk"), None),
            P(("ulysses", "blk")),
            P(("ulysses", "blk"), None),
            P(("ulysses", "blk"), None),
            P(("ulysses", "blk"), None),
            P(("ulysses", "blk"), None),
            P(("ulysses", "blk")),
            P(("ulysses", "blk"), None),
            P("blk", "ulysses", None),
            P("blk", None, "ulysses"),
        ),
        check_vma=False,
    )
```

profile of v0, /device:TPU:1, one launch (start us, length us, event | category | flops | bytes accessed | tf_op | source)
XLA Modules:
  0.0 1794.5 jit_solution(12645115443911294243)
XLA Ops:
  11.2 40.7 %all-reduce.35 = (bf16[1536]{0:T(1024)(128)(2,1)S(1)}, bf16[1536]{0:T(1024)(128)(2,1)S(1)}) all-reduce(bf16[1536]{0:T(1024)(128)(2,1)S(1)} %dynamic-update-slice, bf16[1536]{0:T(1024)(128)(2,1)S(1)} %dynamic-update-slice.1), channel_id=1, replica_groups=mesh['ulysses'=4,'blk'=8] {'ulysses','blk'}, use_global_device_ids=true, to_apply=%add.30 | all-reduce | flops 3072 | bytes 12288
  55.0 13.5 all-gather.16.cloned.1.call-done
  70.9 7.9 all_to_all.180
  78.8 46.3 %all-gather.20.cloned.1.call-done = bf16[1536,512]{1,0:T(8,128)(2,1)} async-done(((bf16[48,512]{1,0:T(8,128)(2,1)}), bf16[1536,512]{1,0:T(8,128)(2,1)}) %all-gather.20.cloned.1.call-update) | async-done | bytes 1572880 | tf_op jit(solution)/shard_map/all_gather | solution.py:161
  127.3 7.9 all_to_all.181
  136.8 53.8 %all-gather.18.cloned.1.call-done = bf16[1536,1536]{1,0:T(8,128)(2,1)} async-done(((bf16[48,1536]{1,0:T(8,128)(2,1)}), bf16[1536,1536]{1,0:T(8,128)(2,1)}) %all-gather.18.cloned.1.call-update) | async-done | bytes 4718608 | tf_op jit(solution)/shard_map/all_gather | solution.py:159
  204.7 10.0 all-gather.32.cloned.1.call-done
  214.7 25.3 %all-gather.34.cloned.1.call-done = bf16[32,128,2,64]{1,3,2,0:T(8,128)(2,1)} async-done(((bf16[4,128,2,64]{1,3,2,0:T(8,128)(2,1)}), bf16[32,128,2,64]{1,3,2,0:T(8,128)(2,1)}) %all-gather.34.cloned.1.call-update) | async-done | bytes 1048592 | tf_op jit(solution)/shard_map/all_gather | solution.py:209
  240.0 97.4 %while.58 = (s32[]{:T(128)}, f32[4,128,2,3]{1,3,2,0:T(4,128)S(1)}, f32[4,128,2,3]{1,3,2,0:T(4,128)S(1)}, f32[4,128,2,3,64]{1,4,3,2,0:T(8,128)S(1)}, s32[1,1,3]{2...) while((s32[]{:T(128)}, f32[4,128,2,3]{1,3,2,0:T(4,128)S(1)}, ...), condition=%wide.region_9.10_spmd.clone.clone, body=%wide.region_5.9_spmd.clone.clone.sunk | while | flops 320891392 | bytes 38890752 | solution.py:257
  350.0 16.7 all-to-all-done.3
  372.6 6.3 gather_fusion
  389.7 50.5 %all-to-all-done.4 = bf16[16,96,1536]{2,1,0:T(8,128)(2,1)} async-done(((bf16[16,96,1536]{2,1,0:T(8,128)(2,1)}), bf16[16,96,1536]{2,1,0:T(8,128)(2,1)}, u32[]{:S(2)}, u32[]{:S(2)}) %all-to-all-start.4) | async-done | bytes 4718624 | tf_op jit(solution)/shard_map/all_to_all | solution.py:117
  445.2 8.6 fusion.206
  457.5 35.7 %all-gather.26.cloned.1.call-done = bf16[2,512,1536]{2,1,0:T(8,128)(2,1)} async-done(((bf16[2,512,384]{2,1,0:T(8,128)(2,1)}), bf16[2,512,1536]{2,1,0:T(8,128)(2,1)}) %all-gather.26.cloned.1.call-update) | async-done | bytes 3145744 | tf_op jit(solution)/shard_map/all_gather | solution.py:168
  493.2 6.2 convolution_convert_fusion.1
  499.3 9.4 copy.561
  508.7 5.3 all-to-all-start.5
  515.0 83.5 %all-gather.4 = bf16[32,48,16]{1,2,0:T(8,128)(2,1)S(1)} all-gather(bf16[1,48,16]{1,2,0:T(8,128)(2,1)S(1)} %bitcast.744), channel_id=1, replica_groups=mesh['ulysses'=4,'blk'=8] {'ulysses','blk'}, dimensions={0}, use_global_device_ids=true | all-gather | bytes 50688 | tf_op jit(solution)/shard_map/all_gather | solution.py:164
  599.2 5.5 copy.562
  604.6 9.6 gather_fusion.2
  619.2 6.3 gather_fusion.1
  628.3 56.4 %all_to_all.182 = bf16[16,96,1536]{2,1,0:T(8,128)(2,1)S(1)} all-to-all(bf16[16,96,1536]{2,1,0:T(8,128)(2,1)S(1)} %broadcast_select_fusion), channel_id=1, replica_groups=mesh['ulysses'=4,'blk'=8] {'blk'}, dimensions={0} | all-to-all | bytes 9437184 | tf_op jit(solution)/shard_map/all_to_all | solution.py:117
  686.8 6.9 multiply_convert_fusion.1
  695.4 6.8 convolution_convert_fusion
  702.2 9.4 copy.567
  711.6 5.8 all-to-all-start.7
  718.4 62.9 %all-to-all-done.7 = bf16[2,768,1536]{2,0,1:T(2,128)(2,1)} async-done(((bf16[2,768,1536]{2,0,1:T(2,128)(2,1)}), bf16[2,768,1536]{2,0,1:T(2,128)(2,1)}, u32[]{:S(2)}, u32[]{:S(2)}) %all-to-all-start.7) | async-done | bytes 4718624 | tf_op jit(solution)/shard_map/all_to_all | solution.py:121
  781.3 5.5 copy.568
  786.8 10.4 gather_fusion.3
  797.1 7.0 convert_reduce_fusion.4
  810.6 10.9 all_to_all.183
  823.7 16.0 all-gather.2
  841.6 8.2 fusion.208
  851.8 8.4 all-gather.3
  860.9 138.7 %while.60 = (s32[]{:T(128)}, f32[4,128,2,64]{1,3,2,0:T(8,128)}, f32[4,128,2,64]{1,3,2,0:T(8,128)}, bf16[8,4,128,2,3,64]{2,5,4,3,1,0:T(8,128)(2,1)}, s32[]{:T(128...) while((s32[]{:T(128)}, f32[4,128,2,64]{1,3,2,0:T(8,128)}, ...), condition=%wide.wide.region_31.33_spmd.clone.clone, body=%wide.wide.region_28.32_spmd.clone.clone.sunk | while | flops 619462144 | bytes 44200308 | solution.py:420
  1001.0 12.8 all_to_all.184
  1018.1 14.8 all_to_all.185
  1041.9 97.2 %while.59 = (s32[]{:T(128)}, f32[4,128,2,3,64]{1,4,3,2,0:T(8,128)}, bf16[8,4,128,2,64]{2,4,3,1,0:T(8,128)(2,1)}, s32[1,1,3]{2,1,0:T(1,128)S(1)}, s32[4,128]{1,0:...) while((s32[]{:T(128)}, f32[4,128,2,3,64]{1,4,3,2,0:T(8,128)}, ...), condition=%wide.region_27.29_spmd.clone.clone, body=%wide.region_25.28_spmd.clone.clone.sunk | while | flops 464793088 | bytes 15518955 | solution.py:389
  1097.2 5.3 fusion.291
  1109.5 5.3 fusion.291
  1121.7 5.3 fusion.291
  1142.3 12.6 all_to_all.186
  1163.2 10.1 fusion.162
  1181.5 42.2 %all-reduce.34 = (f32[1536]{0:T(1024)S(1)}, f32[1536]{0:T(1024)S(1)}) all-reduce(f32[1536]{0:T(1024)S(1)} %get-tuple-element.1341, f32[1536]{0:T(1024)S(1)} %copy-done.49), channel_id=6, replica_groups=mesh['ulysses'=4,'blk'=8] {'ulysses','blk'}, use_global_device_ids=true, to_apply=%region_34.36.clone | all-reduce | flops 3072 | bytes 24576
  1226.7 62.6 %reduce-scatter.14.cloned.1.call-done = f32[48,512]{1,0:T(8,128)} async-done(((f32[1536,512]{1,0:T(8,128)}), f32[48,512]{1,0:T(8,128)}) %reduce-scatter.14.cloned.1.call-update) | async-done | bytes 98320 | tf_op jit(solution)/shard_map/reduce_scatter | solution.py:487
  1289.4 140.7 %reduce-scatter.16.cloned.1.call-done = f32[48,1536]{1,0:T(8,128)} async-done(((f32[1536,1536]{1,0:T(8,128)}), f32[48,1536]{1,0:T(8,128)}) %reduce-scatter.16.cloned.1.call-update) | async-done | bytes 294928 | tf_op jit(solution)/shard_map/reduce_scatter | solution.py:488
  1430.0 142.0 %reduce-scatter.10.cloned.1.call-done = f32[48,1536]{1,0:T(8,128)} async-done(((f32[1536,1536]{1,0:T(8,128)}), f32[48,1536]{1,0:T(8,128)}) %reduce-scatter.10.cloned.1.call-update) | async-done | bytes 294928 | tf_op jit(solution)/shard_map/reduce_scatter | solution.py:485
  1572.0 215.7 %reduce-scatter.18.cloned.1.call-done = f32[2,384,1024]{2,1,0:T(8,128)} async-done(((f32[2,1536,1024]{2,1,0:T(8,128)}), f32[2,384,1024]{2,1,0:T(8,128)}) %reduce-scatter.18.cloned.1.call-update) | async-done | bytes 3145744 | tf_op jit(solution)/shard_map/reduce_scatter | solution.py:493
  (1082 shorter events, 443.5 us)
Async XLA Ops:
  7.2 183.5 %copy-start.2 = (bf16[128,1536]{1,0:T(8,128)(2,1)S(1)}, bf16[128,1536]{1,0:T(8,128)(2,1)}, u32[]{:S(2)}) copy-start(bf16[128,1536]{1,0:T(8,128)(2,1)} %param.21) | copy-start | bytes 1179652
  7.2 129.4 %copy-start.45 = (s32[128,8]{0,1:T(8,128)S(1)}, s32[128,8]{0,1:T(8,128)}, u32[]{:S(2)}) copy-start(s32[128,8]{0,1:T(8,128)} %param.23) | copy-start | bytes 12292
  7.2 61.3 %all-gather.16.cloned.1.call-start = ((), (), s32[]{:S(2)}) async-start(), calls=%async_computation.19 | async-start | bytes 1622016 | tf_op jit(solution)/shard_map/all_gather | solution.py:160
  7.9 117.2 %all-gather.20.cloned.1.call-start = ((), (), s32[]{:S(2)}) async-start(), calls=%async_computation.21 | async-start | bytes 1622016 | tf_op jit(solution)/shard_map/all_gather | solution.py:161
  8.7 182.0 %all-gather.18.cloned.1.call-start = ((), (), s32[]{:S(2)}) async-start(), calls=%async_computation.20 | async-start | bytes 4866048 | tf_op jit(solution)/shard_map/all_gather | solution.py:159
  9.4 205.3 %all-gather.32.cloned.1.call-start = ((), (), s32[]{:S(2)}) async-start(), calls=%async_computation.33 | async-start | bytes 1179648 | tf_op jit(solution)/shard_map/all_gather | solution.py:208
  51.9 143.1 %copy-start.32 = (f32[1536]{0:T(1024)}, f32[1536]{0:T(1024)S(1)}, u32[]{:S(2)}) copy-start(f32[1536]{0:T(1024)S(1)} %convert_element_type.225) | copy-start | bytes 18436
  54.8 140.2 %copy-start.50 = (f32[128]{0:T(128)}, f32[128]{0:T(128)S(1)}, u32[]{:S(2)}) copy-start(f32[128]{0:T(128)S(1)} %add_rsqrt_fusion.1) | copy-start | bytes 1540
  55.0 140.0 %copy-start.36 = (f32[128,32]{0,1:T(8,128)}, f32[128,32]{0,1:T(8,128)S(1)}, u32[]{:S(2)}) copy-start(f32[128,32]{0,1:T(8,128)S(1)} %get-tuple-element.1464) | copy-start | bytes 49156
  55.0 140.0 %copy-start.38 = (f32[128,32]{0,1:T(8,128)}, f32[128,32]{0,1:T(8,128)S(1)}, u32[]{:S(2)}) copy-start(f32[128,32]{0,1:T(8,128)S(1)} %get-tuple-element.1465) | copy-start | bytes 49156
  78.8 161.2 %all-gather.34.cloned.1.call-start = ((), (), s32[]{:S(2)}) async-start(), calls=%async_computation.34 | async-start | bytes 1179648 | tf_op jit(solution)/shard_map/all_gather | solution.py:209
  135.2 232.9 %all-gather.22.cloned.1.call-start = ((), (), s32[]{:S(2)}) async-start(), calls=%async_computation.22 | async-start | bytes 4866048 | tf_op jit(solution)/shard_map/all_gather | solution.py:162
  135.8 309.4 %all-gather.24.cloned.1.call-start = ((), (), s32[]{:S(2)}) async-start(), calls=%async_computation.23 | async-start | bytes 7864320 | tf_op jit(solution)/shard_map/all_gather | solution.py:167
  136.5 63.0 %copy-start.53 = (s32[3]{0:T(128)S(1)}, s32[3]{0:T(128)}, u32[]{:S(2)}) copy-start(s32[3]{0:T(128)} %param.22) | copy-start | bytes 40
  195.9 44.1 %all-to-all-start.1 = ((bf16[128,24,64]{0,2,1:T(8,128)(2,1)}), bf16[128,24,64]{0,2,1:T(8,128)(2,1)S(1)}, u32[]{:S(2)}, u32[]{:S(2)}) async-start(bf16[128,24,64]{0,2,1:T(8,128)(2,1)} %pad_maximum_fusion.3), calls=%async_computation.1 | async-start | bytes 786432 | tf_op jit(solution)/shard_map/all_to_all | solution.py:194
  337.4 30.6 %copy-start.6 = (bf16[4,128,2,3,64]{1,4,3,2,0:T(8,128)(2,1)}, bf16[4,128,2,3,64]{1,4,3,2,0:T(8,128)(2,1)S(1)}, u32[]{:S(2)}) copy-start(bf16[4,128,2,3,64]{1,4,3,2,0:T(8,128)(2,1)S(1)} %get-tuple-element.1948) | copy-start | bytes 1179652
  340.8 25.9 %all-to-all-start.3 = ((bf16[4,2,24576]{2,1,0:T(2,128)(2,1)}), bf16[4,2,24576]{2,1,0:T(2,128)(2,1)S(1)}, u32[]{:S(2)}, u32[]{:S(2)}) async-start(bf16[4,2,24576]{2,1,0:T(2,128)(2,1)} %reshape.954), calls=%async_computation.3 | async-start | bytes 786432 | tf_op jit(solution)/shard_map/all_to_all | solution.py:263
  372.6 226.3 %copy-start.15 = (bf16[128,1536]{1,0:T(8,128)(2,1)}, bf16[128,1536]{1,0:T(8,128)(2,1)S(1)}, u32[]{:S(2)}) copy-start(bf16[128,1536]{1,0:T(8,128)(2,1)S(1)} %multiply_convert_fusion.3) | copy-start | bytes 1179652
  383.9 56.2 %all-to-all-start.4 = ((bf16[16,96,1536]{2,1,0:T(8,128)(2,1)}), bf16[16,96,1536]{2,1,0:T(8,128)(2,1)}, u32[]{:S(2)}, u32[]{:S(2)}) async-start(bf16[16,96,1536]{2,1,0:T(8,128)(2,1)} %broadcast_select_fusion.1), calls=%async_computation.4 | async-start | bytes 9437184 | tf_op jit(solution)/shard_map/all_to_all | solution.py:117
  388.9 104.2 %all-gather.26.cloned.1.call-start = ((), (), s32[]{:S(2)}) async-start(), calls=%async_computation.24 | async-start | bytes 3932160 | tf_op jit(solution)/shard_map/all_gather | solution.py:168
  457.5 41.8 %copy-start.28 = (bf16[2,768,512]{2,1,0:T(8,128)(2,1)}, bf16[2,768,512]{2,1,0:T(8,128)(2,1)S(1)}, u32[]{:S(2)}) copy-start(bf16[2,768,512]{2,1,0:T(8,128)(2,1)S(1)} %multiply_convert_fusion.2) | copy-start | bytes 4718596
  508.7 90.5 %all-to-all-start.5 = ((bf16[2,768,1536]{2,0,1:T(2,128)(2,1)}), bf16[2,768,1536]{2,0,1:T(2,128)(2,1)}, u32[]{:S(2)}, u32[]{:S(2)}) async-start(bf16[2,768,1536]{2,0,1:T(2,128)(2,1)} %copy.561), calls=%async_computation.5 | async-start | bytes 9437184 | tf_op jit(solution)/shard_map/all_to_all | solution.py:121
  628.3 56.9 %slice-start = ((s8[6291456]{0:T(1024)(128)(4,1)}), s8[4194304]{0:T(1024)(128)(4,1)S(1)}, s32[]{:S(2)}) async-start(s8[6291456]{0:T(1024)(128)(4,1)} %bitcast.689), calls=%async_computation.36 | async-start | bytes 8388608
  684.8 10.6 slice-start.2
  711.6 69.7 %all-to-all-start.7 = ((bf16[2,768,1536]{2,0,1:T(2,128)(2,1)}), bf16[2,768,1536]{2,0,1:T(2,128)(2,1)}, u32[]{:S(2)}, u32[]{:S(2)}) async-start(bf16[2,768,1536]{2,0,1:T(2,128)(2,1)} %copy.567), calls=%async_computation.7 | async-start | bytes 9437184 | tf_op jit(solution)/shard_map/all_to_all | solution.py:121
  717.4 143.5 %all-gather.28.cloned.1.call-start = ((), (), s32[]{:S(2)}) async-start(), calls=%async_computation.25 | async-start | bytes 3538944 | tf_op jit(solution)/shard_map/all_gather | solution.py:393
  718.2 142.7 %all-gather.30.cloned.1.call-start = ((), (), s32[]{:S(2)}) async-start(), calls=%async_computation.26 | async-start | bytes 3538944 | tf_op jit(solution)/shard_map/all_gather | solution.py:394
  786.8 10.4 copy-start.5
  806.3 15.2 copy-start.10
  806.3 15.3 copy-start.11
  806.3 34.0 %copy-start.16 = (bf16[128,1536]{1,0:T(8,128)(2,1)S(1)}, bf16[128,1536]{1,0:T(8,128)(2,1)}, u32[]{:S(2)}) copy-start(bf16[128,1536]{1,0:T(8,128)(2,1)} %copy-done.15) | copy-start | bytes 1179652
  821.5 351.9 %reduce-scatter.22.cloned.1.call-start = ((), (), s32[]{:S(2)}) async-start(), calls=%async_computation.35 | async-start | bytes 811008
  821.6 28.2 %copy-start.34 = (bf16[4,2,8,8,128]{4,3,0,2,1:T(8,128)(2,1)}, bf16[4,2,8,8,128]{4,3,0,2,1:T(8,128)(2,1)S(1)}, u32[]{:S(2)}) copy-start(bf16[4,2,8,8,128]{4,3,0,2,1:T(8,128)(2,1)S(1)} %copy.653) | copy-start | bytes 393220
  821.6 28.2 %copy-start.35 = (bf16[4,2,8,8,128]{4,3,0,2,1:T(8,128)(2,1)}, bf16[4,2,8,8,128]{4,3,0,2,1:T(8,128)(2,1)S(1)}, u32[]{:S(2)}) copy-start(bf16[4,2,8,8,128]{4,3,0,2,1:T(8,128)(2,1)S(1)} %copy.652) | copy-start | bytes 393220
  841.6 385.2 %reduce-scatter.20.cloned.1.call-start = ((), (), s32[]{:S(2)}) async-start(), calls=%async_computation.32 | async-start | bytes 7864320 | tf_op jit(solution)/shard_map/reduce_scatter | solution.py:494
  849.8 376.9 %reduce-scatter.12.cloned.1.call-start = ((), (), s32[]{:S(2)}) async-start(), calls=%async_computation.28 | async-start | bytes 3244032 | tf_op jit(solution)/shard_map/reduce_scatter | solution.py:486
  860.9 154.3 %copy-start.3 = (bf16[128,1536]{1,0:T(8,128)(2,1)S(1)}, bf16[128,1536]{1,0:T(8,128)(2,1)}, u32[]{:S(2)}) copy-start(bf16[128,1536]{1,0:T(8,128)(2,1)} %param.21) | copy-start | bytes 1179652
  860.9 154.3 %copy-start.33 = (f32[1536]{0:T(1024)S(1)}, f32[1536]{0:T(1024)}, u32[]{:S(2)}) copy-start(f32[1536]{0:T(1024)} %copy-done.32) | copy-start | bytes 18436
  860.9 154.3 %copy-start.51 = (f32[128]{0:T(128)S(1)}, f32[128]{0:T(128)}, u32[]{:S(2)}) copy-start(f32[128]{0:T(128)} %copy-done.50) | copy-start | bytes 1540
  1001.0 16.6 copy-start.12
  1017.6 18.2 %copy-start.48 = (f32[4,128,2,3]{1,2,3,0:T(2,128)S(1)}, f32[4,128,2,3]{1,2,3,0:T(2,128)}, u32[]{:S(2)}) copy-start(f32[4,128,2,3]{1,2,3,0:T(2,128)} %get-tuple-element.1420) | copy-start | bytes 36868
  1017.6 18.2 %copy-start.20 = (bf16[128,4,6,64]{0,3,2,1:T(8,128)(2,1)S(1)}, bf16[128,4,6,64]{0,3,2,1:T(8,128)(2,1)}, u32[]{:S(2)}) copy-start(bf16[128,4,6,64]{0,3,2,1:T(8,128)(2,1)} %copy-done.19) | copy-start | bytes 1179652
  1017.6 271.8 %reduce-scatter.14.cloned.1.call-start = ((), (), s32[]{:S(2)}) async-start(), calls=%async_computation.29 | async-start | bytes 3244032 | tf_op jit(solution)/shard_map/reduce_scatter | solution.py:487
  1035.7 394.3 %reduce-scatter.16.cloned.1.call-start = ((), (), s32[]{:S(2)}) async-start(), calls=%async_computation.30 | async-start | bytes 9732096 | tf_op jit(solution)/shard_map/reduce_scatter | solution.py:488
  1040.8 531.2 %reduce-scatter.10.cloned.1.call-start = ((), (), s32[]{:S(2)}) async-start(), calls=%async_computation.27 | async-start | bytes 9732096 | tf_op jit(solution)/shard_map/reduce_scatter | solution.py:485
  1140.8 15.7 copy-start.37
  1140.8 15.7 copy-start.39
  1161.8 625.9 %reduce-scatter.18.cloned.1.call-start = ((), (), s32[]{:S(2)}) async-start(), calls=%async_computation.31 | async-start | bytes 15728640 | tf_op jit(solution)/shard_map/reduce_scatter | solution.py:493
  (63 other events, 212.4 us)
Sparse Core Ops, SparseCore 0:
  10.9 57.5 all-gather.15
  71.3 53.7 all-gather.19
  128.1 62.5 all-gather.17
  192.4 22.3 all-gather.31
  216.5 23.4 all-gather.33
  242.7 63.6 all-gather.21
  308.0 122.2 all-gather.23
  431.9 61.2 all-gather.25
  720.1 55.2 all-gather.27
  821.6 37.3 all-gather.29
  864.1 93.5 reduce-scatter.21
  960.4 115.7 reduce-scatter.19
  1082.2 100.7 reduce-scatter.11
  1188.8 100.4 reduce-scatter.13
  1295.7 134.2 reduce-scatter.15
  1437.3 134.6 reduce-scatter.9
  1574.8 212.8 reduce-scatter.17
where the time goes:
time: 1810 us; the launch traced here: 1790 us
  waiting for transfers between devices  881 us (49%)
  blocking collectives  314 us (17%)
  matrix products  258 us (14%)
  local copies, waits for them, and re-layouts  194 us (11%)
  other arithmetic  104 us (6%)
  starting transfers between devices  25.3 us (1%)
    reduce_scatter x1, waiting for transfers between devices, on_device(): lax.psum_scatter(d_inner, 'ulysses', scatter_dimension=1, tiled=True)  216 us
    reduce_scatter x1, waiting for transfers between devices, on_device(): lax.psum_scatter(d_query_weight, ('ulysses', 'blk'), scatter_dimension=0,...  142 us
    reduce_scatter x1, waiting for transfers between devices, on_device(): lax.psum_scatter(d_output_weight, ('ulysses', 'blk'), scatter_dimension=0...  141 us
    all_gather x1, blocking collectives, on_device(): lax.all_gather(w_router, ('ulysses', 'blk'), axis=0, tiled=True)  83.5 us
    unnamed x2, blocking collectives  82.9 us
    dot_general x24, matrix products, scores_for(): jnp.einsum('uqhgd,juthd->uqhgjt', query_tile, key_layers, preferred_eleme...  63.3 us
    all_to_all x2, waiting for transfers between devices, to_tokens(): lax.all_to_all(buffer, 'blk', split_axis=1, concat_axis=0, tiled=True)  62.9 us
    reduce_scatter x1, waiting for transfers between devices, on_device(): lax.psum_scatter(d_value_weight, ('ulysses', 'blk'), scatter_dimension=0,...  62.6 us
  transfers between devices with their start and end apart: 22, of which 13 were waited for; matrix products, arithmetic and copies ran while one was open for 26% of the time, Pallas kernels for 0%

commit v1 on v0

v1 whole, which is shorter than its diff:
```python
import functools
import math

import jax
import jax.numpy as jnp
from jax import lax
from jax.experimental import pallas as pl
from jax.experimental.pallas import tpu as pltpu
from jax.sharding import PartitionSpec as P

D = 1536
HEADS = 24
KV = 8
HW = 64
GROUP = HEADS // KV
FF = 512
TOPK = 8
EXP_DEV = 2
LENMAX = 4096
EPS = 1e-05
THETA = 10000.0
NEG = -1e30
LANES = 128
AUX = 384
ROUTER_AT = 320
QCOLS = GROUP * HW

f32 = jnp.float32
bf16 = jnp.bfloat16
MESH = pl.DeviceIdType.MESH
ANY = pl.BlockSpec(memory_space=pl.ANY)
VMEM = pl.BlockSpec(memory_space=pltpu.VMEM)
DMA = pltpu.SemaphoreType.DMA
MIB = 1 << 20


def dev(u, b):
    return {"ulysses": u, "blk": b}


def remote(src, dst, ss, rs, u, b):
    return pltpu.make_async_remote_copy(
        src_ref=src, dst_ref=dst, send_sem=ss, recv_sem=rs,
        device_id=dev(u, b), device_id_type=MESH,
    )


def signal(sem, u, b):
    pl.semaphore_signal(sem, inc=1, device_id=dev(u, b), device_id_type=MESH)


class Layer:
    def __init__(self, nb):
        self.u = lax.axis_index("ulysses")
        self.b = lax.axis_index("blk")
        self.nb = nb
        self.nc = nb // 2
        self.chip = self.b // 2
        self.core = lax.rem(self.b, 2)
        self.sib = self.chip * 2 + 1 - self.core

    def peer(self, i):
        return lax.rem(self.chip + i, self.nc) * 2 + self.core

    def behind(self, i):
        return lax.rem(self.chip + self.nc - i, self.nc) * 2 + self.core

    def enter(self):
        bar = pltpu.get_barrier_semaphore()
        for i in range(1, self.nc):
            signal(bar, self.u, self.peer(i))
        signal(bar, self.u, self.sib)
        pl.semaphore_wait(bar, self.nc)


def gather_start(me, src, dst, ss, rs, fs, frs):
    sends = []
    for i in range(1, me.nc):
        c = remote(src, dst.at[me.b], ss.at[i], rs.at[i], me.u, me.peer(i))
        c.start()
        sends.append(c)
    c = remote(src, dst.at[me.b], fs.at[0], frs.at[0], me.u, me.sib)
    c.start()
    own = pltpu.make_async_copy(src, dst.at[me.b], ss.at[0])
    own.start()
    return sends, [c], own


def gather_forward(me, dst, state, fs, frs):
    sends, passed, _ = state
    for i in range(1, me.nc):
        sends[i - 1].wait_recv()
        at = me.behind(i)
        c = remote(dst.at[at], dst.at[at], fs.at[i], frs.at[i], me.u, me.sib)
        c.start()
        passed.append(c)


def gather_finish(state):
    sends, passed, own = state
    for c in sends:
        c.wait_send()
    for c in passed:
        c.wait()
    own.wait()


def gather_layer(x, nb, cid):
    nc = nb // 2

    def kernel(x_ref, o_ref, ss, rs, fs, frs):
        me = Layer(nb)
        me.enter()
        state = gather_start(me, x_ref, o_ref, ss, rs, fs, frs)
        gather_forward(me, o_ref, state, fs, frs)
        gather_finish(state)

    return pl.pallas_call(
        kernel,
        out_shape=jax.ShapeDtypeStruct((nb,) + x.shape, x.dtype),
        in_specs=[ANY],
        out_specs=ANY,
        scratch_shapes=[DMA((nc,))] * 4,
        compiler_params=pltpu.CompilerParams(collective_id=cid, has_side_effects=True),
        name="gather_layer%d" % cid,
    )(x)


def gather_inputs(x, gm, pieces, wo, nz, nb, cid):
    n = nz * nb
    nc = nb // 2
    groups, shard, _ = pieces.shape
    rp = nb // groups
    n_o = QCOLS // shard

    def kernel(x_ref, g_ref, p_ref, w_ref, xo, go, po, wo_out, ss, rs, fs, frs, ps, pr, ws, wr, ls):
        me = Layer(nb)
        lin = me.u * nb + me.b
        bar = pltpu.get_barrier_semaphore()

        def place(i):
            t = lax.rem(lin + i, n)
            return t // nb, lax.rem(t, nb)

        @pl.loop(1, n)
        def _(i):
            tz, tb = place(i)
            signal(bar, tz, tb)

        pl.semaphore_wait(bar, n - 1)
        xs = gather_start(me, x_ref, xo, ss.at[0], rs.at[0], fs.at[0], frs.at[0])

        def piece(i):
            tz, tb = place(i)
            return remote(p_ref.at[tb // rp], po.at[lin], ps.at[i], pr.at[i], tz, tb)

        @pl.loop(1, n)
        def _(i):
            piece(i).start()

        own = pltpu.make_async_copy(p_ref.at[me.b // rp], po.at[lin], ls.at[0])
        own.start()
        hg = lin // n_o
        slot = lax.rem(lin, n_o)

        def weight(zo, p):
            tz, tb = lax.rem(me.u + zo, nz), hg * rp + p
            k = zo * rp + p
            return tb, remote(w_ref, wo_out.at[slot], ws.at[k], wr.at[slot], tz, tb)

        keep = pltpu.make_async_copy(w_ref, wo_out.at[slot], ls.at[1])
        for zo in range(nz):
            for p in range(rp):
                tb, c = weight(zo, p)
                if zo:
                    c.start()
                else:
                    pl.when(tb != me.b)(c.start)
                    pl.when(tb == me.b)(keep.start)
        gs = gather_start(me, g_ref, go, ss.at[1], rs.at[1], fs.at[1], frs.at[1])
        gather_forward(me, xo, xs, fs.at[0], frs.at[0])

        @pl.loop(1, n)
        def _(i):
            piece(i).wait()

        own.wait()
        for zo in range(nz):
            for p in range(rp):
                tb, c = weight(zo, p)
                if zo:
                    c.wait_send()
                else:
                    pl.when(tb != me.b)(c.wait_send)
                    pl.when(tb == me.b)(keep.wait)
        for j in range(n_o):
            src = (me.b // rp) * n_o + j
            c = remote(w_ref, wo_out.at[j], ws.at[0], wr.at[j], me.u, me.sib)
            pl.when(src != lin)(c.wait_recv)
        gather_forward(me, go, gs, fs.at[1], frs.at[1])
        gather_finish(xs)
        gather_finish(gs)

    sh = jax.ShapeDtypeStruct
    return pl.pallas_call(
        kernel,
        out_shape=(
            sh((nb,) + x.shape, x.dtype),
            sh((nb,) + gm.shape, gm.dtype),
            sh((n, shard, AUX), bf16),
            sh((n_o, shard, D), bf16),
        ),
        in_specs=[ANY] * 4,
        out_specs=(ANY,) * 4,
        scratch_shapes=[DMA((2, nc))] * 4
        + [DMA((n,))] * 2
        + [DMA((nz * rp,)), DMA((n_o,)), DMA((2,))],
        compiler_params=pltpu.CompilerParams(collective_id=cid, has_side_effects=True),
        name="gather_inputs",
    )(x, gm, pieces, wo)


def halo_forward(kv, nz, nb, back, cid):
    def kernel(x_ref, o_ref, ss, rs):
        u = lax.axis_index("ulysses")
        b = lax.axis_index("blk")
        bar = pltpu.get_barrier_semaphore()
        for d in range(1, nz):
            signal(bar, lax.rem(u + d, nz), b)
        pl.semaphore_wait(bar, nz - 1)

        def copy(d):
            return remote(x_ref, o_ref.at[d - 1], ss.at[d - 1], rs.at[d - 1], u + d, b)

        for d in range(1, back + 1):
            pl.when(u + d < nz)(lambda d=d: copy(d).start())
        for d in range(1, back + 1):
            pl.when(u + d < nz)(lambda d=d: copy(d).wait_send())
            pl.when(u >= d)(lambda d=d: copy(d).wait_recv())

    return pl.pallas_call(
        kernel,
        out_shape=jax.ShapeDtypeStruct((back,) + kv.shape, kv.dtype),
        in_specs=[ANY],
        out_specs=ANY,
        scratch_shapes=[DMA((back,))] * 2,
        compiler_params=pltpu.CompilerParams(collective_id=cid, has_side_effects=True),
        name="halo_forward",
    )(kv)


def reduce_blocks(me, block, sib_out, sib_in, snd, land, ss, rs, fs, frs):
    nc = me.nc
    passed = []
    for i in [*range(1, nc), 0]:
        to = lax.rem(me.chip + i, nc) * 2 + 1 - me.core
        sib_out[i] = block(to).astype(bf16)
        c = remote(sib_out.at[i], sib_in.at[i], fs.at[i], frs.at[i], me.u, me.sib)
        c.start()
        passed.append(c)
    sends = []
    for i in range(1, nc):
        mine = block(me.peer(i))
        passed[i - 1].wait_recv()
        snd[i] = (mine + sib_in[i].astype(f32)).astype(bf16)
        c = remote(snd.at[i], land.at[i], ss.at[i], rs.at[i], me.u, me.peer(i))
        c.start()
        sends.append(c)
    total = block(me.b)
    passed[nc - 1].wait_recv()
    total = total + sib_in[0].astype(f32)
    for i in range(1, nc):
        sends[i - 1].wait_recv()
        total = total + land[i].astype(f32)
    for c in passed + sends:
        c.wait_send()
    return total


def reduce_scratch(nb, rows, cols):
    nc = nb // 2
    return [pltpu.VMEM((nc, rows, cols), bf16)] * 4 + [DMA((nc,))] * 4


def reduce_product(lhs, rhs, nb, cid, transpose_rhs=False):
    rows = lhs.shape[0] // nb
    cols = rhs.shape[0] if transpose_rhs else rhs.shape[1]
    dims = (((1,), (1,)), ((), ())) if transpose_rhs else (((1,), (0,)), ((), ()))

    def kernel(l_ref, r_ref, o_ref, *scratch):
        me = Layer(nb)
        me.enter()

        def block(t):
            part = l_ref[pl.ds(pl.multiple_of(t * rows, rows), rows), :]
            return lax.dot_general(part, r_ref[...], dims, preferred_element_type=f32)

        o_ref[...] = reduce_blocks(me, block, *scratch)

    return pl.pallas_call(
        kernel,
        out_shape=jax.ShapeDtypeStruct((rows, cols), f32),
        in_specs=[VMEM, VMEM],
        out_specs=VMEM,
        scratch_shapes=reduce_scratch(nb, rows, cols),
        compiler_params=pltpu.CompilerParams(
            collective_id=cid, has_side_effects=True, vmem_limit_bytes=48 * MIB
        ),
        name="reduce_product%d" % cid,
    )(lhs, rhs)


def reduce_ready(part, nb, cid):
    _, rows, cols = part.shape

    def kernel(p_ref, o_ref, *scratch):
        me = Layer(nb)
        me.enter()

        def block(t):
            return p_ref[t].astype(f32)

        o_ref[...] = reduce_blocks(me, block, *scratch)

    return pl.pallas_call(
        kernel,
        out_shape=jax.ShapeDtypeStruct((rows, cols), f32),
        in_specs=[VMEM],
        out_specs=VMEM,
        scratch_shapes=reduce_scratch(nb, rows, cols),
        compiler_params=pltpu.CompilerParams(
            collective_id=cid, has_side_effects=True, vmem_limit_bytes=48 * MIB
        ),
        name="reduce_ready%d" % cid,
    )(part)


def halo_back(dkv, ypart, dwo, nz, nb, rp, back, cid):
    _, rows, cols = ypart.shape
    n_o, shard, _ = dwo.shape
    R = dkv.shape[1]

    def kernel(d_ref, y_ref, w_ref, kin, o_ref, win, *scratch):
        ks, kr, ws, wr, ls = scratch[:5]
        me = Layer(nb)
        lin = me.u * nb + me.b
        first = (me.b // rp) * rp
        part = lax.rem(me.b, rp)
        n = nz * nb
        bar = pltpu.get_barrier_semaphore()

        @pl.loop(1, n)
        def _(i):
            t = lax.rem(lin + i, n)
            signal(bar, t // nb, lax.rem(t, nb))

        pl.semaphore_wait(bar, n - 1)

        def copy(d, p):
            k = d * rp + p
            return remote(d_ref.at[d], kin.at[d * rp + part], ks.at[k], kr.at[d * rp + part], me.u - d, first + p)

        def arrival(d, p):
            k = d * rp + p
            return remote(d_ref.at[d], kin.at[k], ks.at[k], kr.at[k], me.u, me.sib)

        for d in range(back + 1):
            for p in range(rp):
                if d:
                    pl.when(me.u >= d)(lambda d=d, p=p: copy(d, p).start())
                elif rp > 1:
                    pl.when(part != p)(lambda d=d, p=p: copy(d, p).start())

        def weight(j):
            t = (me.b // rp) * n_o + j
            at = me.u * rp + part
            return t, remote(w_ref.at[j], win.at[at], ws.at[j], wr.at[at], t // nb, lax.rem(t, nb))

        for j in range(n_o):
            t, c = weight(j)
            keep = pltpu.make_async_copy(w_ref.at[j], win.at[me.u * rp + part], ls.at[0])
            pl.when(t != lin)(c.start)
            pl.when(t == lin)(keep.start)

        def block(t):
            return y_ref[t].astype(f32)

        o_ref[...] = reduce_blocks(me, block, *scratch[5:])

        for d in range(back + 1):
            for p in range(rp):
                if d:
                    pl.when(me.u >= d)(lambda d=d, p=p: copy(d, p).wait_send())
                    pl.when(me.u + d < nz)(lambda d=d, p=p: arrival(d, p).wait_recv())
                elif rp > 1:
                    pl.when(part != p)(lambda d=d, p=p: copy(d, p).wait_send())
                    pl.when(part != p)(lambda d=d, p=p: arrival(d, p).wait_recv())
        for j in range(n_o):
            t, c = weight(j)
            keep = pltpu.make_async_copy(w_ref.at[j], win.at[me.u * rp + part], ls.at[0])
            pl.when(t != lin)(c.wait_send)
            pl.when(t == lin)(keep.wait)
        hg = lin // n_o
        for z in range(nz):
            for p in range(rp):
                k = z * rp + p
                c = remote(w_ref.at[0], win.at[k], ws.at[0], wr.at[k], me.u, me.sib)
                pl.when(z * nb + hg * rp + p != lin)(c.wait_recv)

    sh = jax.ShapeDtypeStruct
    return pl.pallas_call(
        kernel,
        out_shape=(
            sh(((back + 1) * rp, R, LANES), bf16),
            sh((rows, cols), f32),
            sh((nz * rp, shard, D), bf16),
        ),
        in_specs=[ANY, VMEM, ANY],
        out_specs=(ANY, VMEM, ANY),
        scratch_shapes=[DMA(((back + 1) * rp,))] * 2
        + [DMA((n_o,)), DMA((nz * rp,)), DMA((1,))]
        + reduce_scratch(nb, rows, cols),
        compiler_params=pltpu.CompilerParams(
            collective_id=cid, has_side_effects=True, vmem_limit_bytes=48 * MIB
        ),
        name="halo_back",
    )(dkv, ypart, dwo)


def reduce_last(lhs, rhs, pieces, nz, nb, cid):
    rows = lhs.shape[0] // nb
    cols = rhs.shape[0]
    n, shard, width = pieces.shape

    def kernel(l_ref, r_ref, p_ref, o_ref, pin, *scratch):
        ps, pr, ls = scratch[:3]
        me = Layer(nb)
        lin = me.u * nb + me.b
        bar = pltpu.get_barrier_semaphore()

        def place(i):
            t = lax.rem(lin + i, n)
            return t, t // nb, lax.rem(t, nb)

        @pl.loop(1, n)
        def _(i):
            _, tz, tb = place(i)
            signal(bar, tz, tb)

        pl.semaphore_wait(bar, n - 1)

        def piece(i):
            t, tz, tb = place(i)
            return remote(p_ref.at[t], pin.at[lin], ps.at[i], pr.at[i], tz, tb)

        @pl.loop(1, n)
        def _(i):
            piece(i).start()

        own = pltpu.make_async_copy(p_ref.at[lin], pin.at[lin], ls.at[0])
        own.start()

        def block(t):
            part = l_ref[pl.ds(pl.multiple_of(t * rows, rows), rows), :]
            return lax.dot_general(
                part, r_ref[...], (((1,), (1,)), ((), ())), preferred_element_type=f32
            )

        o_ref[...] = reduce_blocks(me, block, *scratch[3:])

        @pl.loop(1, n)
        def _(i):
            piece(i).wait()

        own.wait()

    sh = jax.ShapeDtypeStruct
    return pl.pallas_call(
        kernel,
        out_shape=(sh((rows, cols), f32), sh((n, shard, width), bf16)),
        in_specs=[VMEM, VMEM, ANY],
        out_specs=(VMEM, ANY),
        scratch_shapes=[DMA((n,))] * 2 + [DMA((1,))] + reduce_scratch(nb, rows, cols),
        compiler_params=pltpu.CompilerParams(
            collective_id=cid, has_side_effects=True, vmem_limit_bytes=48 * MIB
        ),
        name="reduce_last",
    )(lhs, rhs, pieces)


def turn(a, c, s1, s2):
    return a * c + pltpu.roll(a, LANES - HW // 2, 1) * s1 + pltpu.roll(a, HW // 2, 1) * s2


def project(x, gain, wbig, c, s1, s2):
    R = x.shape[0]
    step = 256

    def kernel(x_ref, g_ref, w_ref, c_ref, a_ref, b_ref, q_ref, kv_ref, h_ref):
        v = x_ref[...].astype(f32)
        inv = lax.rsqrt(jnp.mean(v * v, axis=1, keepdims=True) + EPS)
        h = (v * inv * g_ref[...]).astype(bf16)
        h_ref[...] = h
        out = jnp.dot(h, w_ref[...], preferred_element_type=f32)
        tables = (c_ref[...], a_ref[...], b_ref[...])
        for k in range(GROUP):
            q = turn(out[:, k * LANES:(k + 1) * LANES], *tables)
            q_ref[k] = (q.astype(bf16).astype(f32) * (1.0 / math.sqrt(HW))).astype(bf16)
        kv_ref[...] = turn(out[:, GROUP * LANES:], *tables).astype(bf16)

    row = lambda w: pl.BlockSpec((step, w), lambda i: (i, 0))
    whole = lambda a: pl.BlockSpec(a.shape, lambda i: (0, 0))
    sh = jax.ShapeDtypeStruct
    return pl.pallas_call(
        kernel,
        grid=(R // step,),
        out_shape=(sh((GROUP, R, LANES), bf16), sh((R, LANES), bf16), sh((R, D), bf16)),
        in_specs=[row(D), whole(gain), whole(wbig), row(LANES), row(LANES), row(LANES)],
        out_specs=(pl.BlockSpec((GROUP, step, LANES), lambda i: (0, i, 0)), row(LANES), row(D)),
        compiler_params=pltpu.CompilerParams(vmem_limit_bytes=32 * MIB),
        name="project",
    )(x, gain, wbig, c, s1, s2)


BQ = 256
BK = 512


def seen(meta, st, i, kb, nq):
    qpos = meta[nq] + i * BQ + lax.broadcasted_iota(jnp.int32, (BQ, 1), 0)
    kpos = kb * BK + lax.broadcasted_iota(jnp.int32, (1, BK), 1)
    return ((kpos <= qpos) & (kpos >= st))[None]


NT = (((1,), (1,)), ((), ()))
NN = (((1,), (0,)), ((), ()))
TN = (((0,), (0,)), ((), ()))


def attend(q, kv, starts, meta):
    _, Rq, _ = q.shape
    nq = Rq // BQ
    M = GROUP * BQ

    def kernel(meta, q_ref, kv_ref, st_ref, o_ref, l_ref):
        i = pl.program_id(0)
        qv = q_ref[...].reshape(M, LANES)
        st = st_ref[...]
        last = (meta[nq] + i * BQ + BQ - 1) // BK + 1

        def step(kb, carry):
            m, l, acc = carry
            keys = kv_ref[pl.ds(pl.multiple_of(kb * BK, BK), BK), :]
            s = lax.dot_general(qv, keys, NT, preferred_element_type=f32).reshape(GROUP, BQ, BK)
            s = jnp.where(seen(meta, st, i, kb, nq), s, NEG)
            m2 = jnp.maximum(m, jnp.max(s, axis=2, keepdims=True))
            w = jnp.exp(s - m2)
            f = jnp.exp(m - m2)
            l = l * f + jnp.sum(w, axis=2, keepdims=True)
            pv = lax.dot_general(w.astype(bf16).reshape(M, BK), keys, NN, preferred_element_type=f32)
            return m2, l, acc * f + pv.reshape(GROUP, BQ, LANES)

        init = (
            jnp.full((GROUP, BQ, 1), NEG, f32),
            jnp.zeros((GROUP, BQ, 1), f32),
            jnp.zeros((GROUP, BQ, LANES), f32),
        )
        m, l, acc = lax.fori_loop(meta[i], last, step, init)
        lane = lax.broadcasted_iota(jnp.int32, (1, 1, LANES), 2)
        o_ref[...] = jnp.where(lane >= HW, acc / l, 0.0).astype(bf16)
        l_ref[...] = m + jnp.log(l)

    sh = jax.ShapeDtypeStruct
    blk = lambda w: pl.BlockSpec((GROUP, BQ, w), lambda i, m: (0, i, 0))
    return pl.pallas_call(
        kernel,
        grid_spec=pltpu.PrefetchScalarGridSpec(
            num_scalar_prefetch=1,
            grid=(nq,),
            in_specs=[
                blk(LANES),
                pl.BlockSpec(kv.shape, lambda i, m: (0, 0)),
                pl.BlockSpec((BQ, 1), lambda i, m: (i, 0)),
            ],
            out_specs=(blk(LANES), blk(1)),
        ),
        out_shape=(sh((GROUP, Rq, LANES), bf16), sh((GROUP, Rq, 1), f32)),
        compiler_params=pltpu.CompilerParams(vmem_limit_bytes=48 * MIB),
        name="attend",
    )(meta, q, kv, starts)


def attend_back(q, kv, starts, meta, lse, mixed, do):
    _, Rq, _ = q.shape
    nq = Rq // BQ
    M = GROUP * BQ
    K = kv.shape[0]

    def kernel(meta, q_ref, kv_ref, st_ref, l_ref, o_ref, g_ref, dq_ref, dkv_ref):
        i = pl.program_id(0)

        @pl.when(i == 0)
        def _():
            dkv_ref[...] = jnp.zeros_like(dkv_ref)

        qv = q_ref[...].reshape(M, LANES)
        do = g_ref[...].reshape(M, LANES)
        lse = l_ref[...]
        delta = jnp.sum(
            g_ref[...].astype(f32) * o_ref[...].astype(f32), axis=2, keepdims=True
        )
        st = st_ref[...]
        last = (meta[nq] + i * BQ + BQ - 1) // BK + 1

        def step(kb, dq):
            at = pl.ds(pl.multiple_of(kb * BK, BK), BK)
            keys = kv_ref[at, :]
            s = lax.dot_general(qv, keys, NT, preferred_element_type=f32).reshape(GROUP, BQ, BK)
            p = jnp.where(seen(meta, st, i, kb, nq), jnp.exp(s - lse), 0.0)
            dp = lax.dot_general(do, keys, NT, preferred_element_type=f32).reshape(GROUP, BQ, BK)
            ds = (p * (dp - delta)).astype(bf16).reshape(M, BK)
            pb = p.astype(bf16).reshape(M, BK)
            dkv_ref[at, :] += lax.dot_general(
                ds, qv, TN, preferred_element_type=f32
            ) + lax.dot_general(pb, do, TN, preferred_element_type=f32)
            return dq + lax.dot_general(ds, keys, NN, preferred_element_type=f32)

        dq = lax.fori_loop(meta[i], last, step, jnp.zeros((M, LANES), f32))
        lane = lax.broadcasted_iota(jnp.int32, (1, LANES), 1)
        dq = jnp.where(lane < HW, dq * (1.0 / math.sqrt(HW)), 0.0)
        dq_ref[...] = dq.astype(bf16).reshape(GROUP, BQ, LANES)

    sh = jax.ShapeDtypeStruct
    blk = lambda w: pl.BlockSpec((GROUP, BQ, w), lambda i, m: (0, i, 0))
    return pl.pallas_call(
        kernel,
        grid_spec=pltpu.PrefetchScalarGridSpec(
            num_scalar_prefetch=1,
            grid=(nq,),
            in_specs=[
                blk(LANES),
                pl.BlockSpec(kv.shape, lambda i, m: (0, 0)),
                pl.BlockSpec((BQ, 1), lambda i, m: (i, 0)),
                blk(1),
                blk(LANES),
                blk(LANES),
            ],
            out_specs=(blk(LANES), pl.BlockSpec((K, LANES), lambda i, m: (0, 0))),
        ),
        out_shape=(sh((GROUP, Rq, LANES), bf16), sh((K, LANES), f32)),
        compiler_params=pltpu.CompilerParams(vmem_limit_bytes=48 * MIB),
        name="attend_back",
    )(meta, q, kv, starts, lse, mixed, do)


def locate(rows, lengths):
    passed = rows[:, None] >= jnp.cumsum(lengths)
    return jnp.sum(jnp.where(passed, lengths, 0), axis=-1)


def norm_rows(v, gain):
    inverse = lax.rsqrt(jnp.mean(v * v, axis=-1, keepdims=True) + EPS)
    normed = v * inverse
    return normed, inverse, normed * gain


def norm_back(upstream, normed, inverse, gain):
    d_normed = upstream * gain
    d_gain = jnp.sum(upstream * normed, axis=0)
    d_values = inverse * (d_normed - normed * jnp.mean(d_normed * normed, axis=-1, keepdims=True))
    return d_values, d_gain


def dot(a, b):
    return jnp.dot(a, b, preferred_element_type=f32)


def rows_of(a, start, count):
    return a if a.shape[0] == count else lax.dynamic_slice_in_dim(a, start, count, 0)


def widen(a, start, count):
    if a.shape[0] == count:
        return a
    return lax.dynamic_update_slice_in_dim(jnp.zeros((count,) + a.shape[1:], a.dtype), a, start, 0)


def on_device(tokens, lengths, routes, gain_attn, w_query, w_key, w_value, w_output, gain_moe,
              w_router, w_inner, w_outer, cotangent):
    nz = lax.axis_size("ulysses")
    nb = lax.axis_size("blk")
    z = lax.axis_index("ulysses")
    b = lax.axis_index("blk")
    T = tokens.shape[0]
    R = nb * T
    rp = nb // KV
    Rq = R // rp
    part = b % rp
    at = part * Rq
    n = nz * nb
    S = D // n
    E = w_router.shape[1]
    longest = min(LENMAX, n * T // 2)
    back = min(nz - 1, (longest - 1 + R - 1) // R)
    n_o = QCOLS // S

    inner = [lax.all_gather(w_inner[e], "ulysses", axis=0, tiled=True) for e in range(EXP_DEV)]
    outer = [lax.all_gather(w_outer[e], "ulysses", axis=1, tiled=True) for e in range(EXP_DEV)]

    tail = jnp.concatenate(
        [w_router, gain_attn[:, None], gain_moe[:, None],
         jnp.zeros((S, AUX - ROUTER_AT - E - 2), bf16)], axis=1)
    pieces = jnp.stack([
        jnp.concatenate([
            w_query[:, h * QCOLS:(h + 1) * QCOLS], w_key[:, h * HW:(h + 1) * HW],
            w_value[:, h * HW:(h + 1) * HW], tail], axis=1)
        for h in range(KV)])
    lanes = jnp.arange(LANES, dtype=jnp.int32)
    named = jnp.any(routes[:, :, None] == lanes[None, None, :], axis=1)
    cot_mask = jnp.concatenate([cotangent, named.astype(bf16)], axis=1)
    xg, gg, packed, wo = gather_inputs(tokens, cot_mask, pieces, w_output, nz, nb, 0)
    xg = xg.reshape(R, D)
    gg = gg.reshape(R, D + LANES)
    packed = packed.reshape(D, AUX)
    wo = wo.reshape(QCOLS, D)
    router = packed[:, ROUTER_AT:ROUTER_AT + E]
    gains = packed[:, ROUTER_AT + E:ROUTER_AT + E + 2].astype(f32).T
    gain1, gain2 = gains[0:1], gains[1:2]
    gap = jnp.zeros((D, LANES - HW), bf16)
    wbig = jnp.concatenate(
        sum([[packed[:, h * HW:(h + 1) * HW], gap] for h in range(GROUP)], [])
        + [packed[:, QCOLS:ROUTER_AT]], axis=1)
    gap = jnp.zeros((HW, D), bf16)
    wo_wide = jnp.concatenate(
        sum([[gap, wo[h * HW:(h + 1) * HW]] for h in range(GROUP)], []), axis=0)

    rows = z * R + jnp.arange(R, dtype=jnp.int32)
    opening = locate(rows, lengths)
    frequency = THETA ** (-(jnp.arange(HW // 2, dtype=f32) * 2.0 / HW))
    angles = (rows - opening).astype(f32)[:, None] * frequency[None, :]
    cos, sin = jnp.cos(angles), jnp.sin(angles)
    none = jnp.zeros((R, HW // 2), f32)
    half = jnp.zeros((R, HW), f32)
    tc = jnp.concatenate([cos, cos, half + 1.0], axis=1)
    ts1 = jnp.concatenate([-sin, none, half], axis=1)
    ts2 = jnp.concatenate([none, sin, half], axis=1)

    q, kv, h1 = project(xg, gain1, wbig, tc, ts1, ts2)
    if rp > 1:
        q = lax.dynamic_slice_in_dim(q, at, Rq, 1)
    far = halo_forward(kv, nz, nb, back, 1)
    kv_all = jnp.concatenate([far[d - 1] for d in range(back, 0, -1)] + [kv], axis=0)
    base = (z - back) * R
    starts = rows_of(opening, at, Rq) - base
    meta = jnp.concatenate([starts[::BQ] // BK, (back * R + at)[None]]).astype(jnp.int32)
    starts = starts[:, None]
    mixed, lse = attend(q, kv_all, starts, meta)
    mixed_rows = jnp.concatenate([mixed[h] for h in range(GROUP)], axis=1)
    attn = reduce_product(widen(mixed_rows, at, R), wo_wide, nb, 2)

    x = tokens.astype(f32)
    resid = x + attn
    n2, inv2, scaled2 = norm_rows(resid, gain2)
    h2_own = scaled2.astype(bf16)
    h2 = gather_layer(h2_own, nb, 3).reshape(R, D)

    def gates_of(hidden, mask):
        logits = dot(hidden, router)
        mask = mask > 0
        top = jnp.max(jnp.where(mask, logits, NEG), axis=1, keepdims=True)
        w = jnp.where(mask, jnp.exp(jnp.where(mask, logits - top, 0.0)), 0.0)
        return w / jnp.sum(w, axis=1, keepdims=True)

    gates = gates_of(h2, gg[:, D:D + E])
    gates = lax.dynamic_slice_in_dim(gates, b * EXP_DEV, EXP_DEV, 1)
    g = gg[:, :D]

    y = 0.0
    dh2 = 0.0
    extra = jnp.zeros((R, LANES), f32)
    inner_grads, outer_grads = [], []
    for e in range(EXP_DEV):
        gate = gates[:, e:e + 1]
        gu = dot(h2, inner[e])
        a, up = gu[:, :FF], gu[:, FF:]
        sg = jax.nn.sigmoid(a)
        silu = a * sg
        act = (silu * up).astype(bf16)
        y = y + gate * dot(act, outer[e])
        raw = lax.dot_general(g, outer[e], NT, preferred_element_type=f32)
        dgate = jnp.sum(act.astype(f32) * raw, axis=1, keepdims=True)
        dact = gate * raw
        dgu = jnp.concatenate(
            [dact * up * (sg * (1.0 + a * (1.0 - sg))), dact * silu], axis=1).astype(bf16)
        dy = (gate * g.astype(f32)).astype(bf16)
        d_out = lax.dot_general(act, dy, TN, preferred_element_type=f32).astype(bf16)
        d_in = lax.dot_general(h2, dgu, TN, preferred_element_type=f32).astype(bf16)
        inner_grads.append(lax.psum_scatter(d_in, "ulysses", scatter_dimension=0, tiled=True))
        outer_grads.append(lax.psum_scatter(d_out, "ulysses", scatter_dimension=1, tiled=True))
        dh2 = dh2 + lax.dot_general(dgu, inner[e], NT, preferred_element_type=f32)
        hi = dgate.astype(bf16).astype(f32)
        place = b * EXP_DEV + e
        extra = extra + jnp.where(lanes[None, :] == place, hi, 0.0)
        extra = extra + jnp.where(lanes[None, :] == place + HW, dgate - hi, 0.0)
    back_rows = jnp.concatenate([dh2.astype(bf16), extra.astype(bf16)], axis=1)
    summed = reduce_ready(back_rows.reshape(nb, T, D + LANES), nb, 4)
    y = y.astype(bf16).reshape(nb, T, D)

    upstream = cotangent.astype(f32)
    dgates = summed[:, D:D + E] + summed[:, D + HW:D + HW + E]
    own_gates = gates_of(h2_own, named[:, :E].astype(bf16))
    dlogits = own_gates * (dgates - jnp.sum(own_gates * dgates, axis=1, keepdims=True))
    dlogits = dlogits.astype(bf16)
    d_router = lax.dot_general(h2_own, dlogits, TN, preferred_element_type=f32)
    dh2_own = summed[:, :D] + lax.dot_general(dlogits, router, NT, preferred_element_type=f32)
    d_norm2, d_gain2 = norm_back(dh2_own, n2, inv2, gain2)
    dresid = upstream + d_norm2
    dattn = gather_layer(dresid.astype(bf16), nb, 5).reshape(R, D)

    dattn = rows_of(dattn, at, Rq)
    dmixed = lax.dot_general(dattn, wo_wide, NT, preferred_element_type=f32).astype(bf16)
    dmixed = jnp.stack([dmixed[:, h * LANES:(h + 1) * LANES] for h in range(GROUP)])
    dwo = lax.dot_general(mixed_rows, dattn, TN, preferred_element_type=f32).astype(bf16)
    dwo = jnp.concatenate(
        [dwo[h * LANES + HW:(h + 1) * LANES] for h in range(GROUP)], axis=0)
    dq, dkv = attend_back(q, kv_all, starts, meta, lse, mixed, dmixed)
    dkv = dkv.reshape(back + 1, R, LANES)
    dkv_out = jnp.stack([dkv[back - d] for d in range(back + 1)]).astype(bf16)
    kin, ysum, win = halo_back(dkv_out, y, dwo.reshape(n_o, S, D), nz, nb, rp, back, 6)
    out = resid + ysum
    d_output = jnp.sum(win.astype(f32), axis=0)

    dkv_own = rows_of(dkv[back], at, Rq)
    for d in range(back + 1):
        for p in range(rp):
            if d:
                ok = z + d < nz
            elif rp > 1:
                ok = part != p
            else:
                continue
            dkv_own = dkv_own + jnp.where(ok, rows_of(kin[d * rp + p], at, Rq).astype(f32), 0.0)
    flat = jnp.concatenate([dq[h] for h in range(GROUP)] + [dkv_own.astype(bf16)], axis=1)
    flat = flat.astype(f32).reshape(Rq, GROUP + 1, LANES)
    mc, m1, m2 = (rows_of(t, at, Rq)[:, None, :] for t in (tc, ts1, ts2))
    turned = (flat * mc - jnp.roll(flat, -(HW // 2), 2) * m1 - jnp.roll(flat, HW // 2, 2) * m2)
    turned = turned.astype(bf16).reshape(Rq, (GROUP + 1) * LANES)
    dw = lax.dot_general(rows_of(h1, at, Rq), turned, TN, preferred_element_type=f32)
    n1, inv1, _ = norm_rows(x, gain1)
    d_gain1 = jnp.sum(dw * wbig.astype(f32), axis=1) / gain1[0]
    narrow = jnp.concatenate(
        [dw[:, h * LANES:h * LANES + HW] for h in range(GROUP)]
        + [dw[:, GROUP * LANES:], d_router, d_gain2[:, None], d_gain1[:, None],
           jnp.zeros((D, AUX - ROUTER_AT - E - 2), f32)], axis=1).astype(bf16)
    dh1, pin = reduce_last(widen(turned, at, R), wbig, narrow.reshape(n, S, AUX), nz, nb, 7)
    d_norm1, _ = norm_back(dh1, n1, inv1, gain1)
    d_tokens = dresid + d_norm1

    pin = pin.astype(f32)
    small = jnp.sum(pin[:, :, ROUTER_AT:], axis=0)
    dqkv = jnp.sum(pin.reshape(nz, KV, rp, S, AUX)[..., :ROUTER_AT], axis=(0, 2))
    lay = lambda a: jnp.transpose(a, (1, 0, 2)).reshape(S, -1)
    d_query = lay(dqkv[:, :, :QCOLS])
    d_key = lay(dqkv[:, :, QCOLS:QCOLS + HW])
    d_value = lay(dqkv[:, :, QCOLS + HW:])
    return (
        out, d_tokens, small[:, E + 1], d_query, d_key, d_value, d_output,
        small[:, E], small[:, :E],
        jnp.stack(inner_grads).astype(f32), jnp.stack(outer_grads).astype(f32),
    )


def solution(mesh):
    both = ("ulysses", "blk")
    rows = P(both, None)
    weights = (P(both), rows, rows, rows, rows, P(both), rows, P("blk", "ulysses", None), P("blk", None, "ulysses"))
    return jax.shard_map(
        on_device,
        mesh=mesh,
        in_specs=(rows, P(), rows) + weights + (rows,),
        out_specs=(rows, rows) + weights,
        check_vma=False,
    )
```

time: 1810 us -> 642 us (0.35)
  waiting for transfers between devices: 881 us -> 1.35 us
  Pallas kernels: 0 us -> 395 us
  blocking collectives: 314 us -> 0 us
  matrix products: 258 us -> 89.3 us
  local copies, waits for them, and re-layouts: 194 us -> 87.9 us
  other arithmetic: 104 us -> 44.3 us
  starting transfers between devices: 25.3 us -> 0.96 us
    reduce_scatter x6 -> x2, waiting for transfers between devices: 561 us -> 0.01 us  [on_device(): lax.psum_scatter(d_in, 'ulysses', scatter_dimension=0, tiled=True)]
    pallas_call x0 -> x11, Pallas kernels: none -> 395 us  [the longest x1 109 us: halo_back(): pl.pallas_call(kernel, out_shape=(sh(((back + 1) * rp, R, LANES), bf16),...]
    all_gather x10 -> x4, waiting for transfers between devices: 185 us -> 0.02 us  [the longest x2 0.02 us: on_device(): lax.all_gather(w_inner[e], 'ulysses', axis=0, tiled=True)]
    dot_general x76 -> x19, matrix products: 257 us -> 89.3 us  [the longest x6 28.7 us: dot(): return jnp.dot(a, b, preferred_element_type=f32)]
    all_to_all x5 -> x0, waiting for transfers between devices: 130 us -> none  [the longest x2 62.9 us: to_tokens(): lax.all_to_all(buffer, 'blk', split_axis=1, concat_axis=0, tiled=True)]
    all_to_all x7 -> x0, blocking collectives: 123 us -> none  [the longest x1 56.4 us: to_experts(): lax.all_to_all(buffer, 'blk', split_axis=0, concat_axis=1, tiled=True)]
    all_gather x3 -> x0, blocking collectives: 108 us -> none  [the longest x1 83.5 us: on_device(): lax.all_gather(w_router, ('ulysses', 'blk'), axis=0, tiled=True)]
    unnamed x2 -> x0, blocking collectives: 82.9 us -> none
  transfers between devices with their start and end apart: 22 -> 8, of which waited for: 13 -> 0; matrix products, arithmetic and copies ran while one was open for 26% -> 30% of each run, Pallas kernels for 0% -> 62%
where the time goes in v1:
time: 642 us; the launch traced here: 635 us
  Pallas kernels  395 us (62%)
  matrix products  89.3 us (14%)
  local copies, waits for them, and re-layouts  87.9 us (14%)
  other arithmetic  44.3 us (7%)
  between operations  16 us (2%)
    pallas_call x1, Pallas kernels, halo_back(): pl.pallas_call(kernel, out_shape=(sh(((back + 1) * rp, R, LANES), bf16),...  109 us
    pallas_call x1, Pallas kernels, gather_inputs(): pl.pallas_call(kernel, out_shape=(sh((nb,) + x.shape, x.dtype), sh((nb,)...  68.8 us
    pallas_call x1, Pallas kernels, reduce_last(): pl.pallas_call(kernel, out_shape=(sh((rows, cols), f32), sh((n, shard, wi...  50.8 us
    pallas_call x1, Pallas kernels, halo_forward(): pl.pallas_call(kernel, out_shape=jax.ShapeDtypeStruct((back,) + kv.shape,...  48.4 us
    pallas_call x2, Pallas kernels, gather_layer(): pl.pallas_call(kernel, out_shape=jax.ShapeDtypeStruct((nb,) + x.shape, x....  46 us
    unnamed x212, local copies, waits for them, and re-layouts  32.3 us
    dot_general x6, matrix products, dot(): return jnp.dot(a, b, preferred_element_type=f32)  28.7 us
    pallas_call x1, Pallas kernels, reduce_ready(): pl.pallas_call(kernel, out_shape=jax.ShapeDtypeStruct((rows, cols), f32),...  24.3 us
  transfers between devices with their start and end apart: 8, of which 0 were waited for; matrix products, arithmetic and copies ran while one was open for 30% of the time, Pallas kernels for 62%

profile of v1, /device:TPU:1, one launch (start us, length us, event | category | flops | bytes accessed | tf_op | source)
XLA Modules:
  0.0 635.2 jit_solution(7344705966449695229)
XLA Ops:
  7.2 2.7 fusion.70
  16.0 68.8 %gather_inputs.1 = (bf16[8,128,1536]{2,1,0:T(8,128)(2,1)}, bf16[8,128,1664]{2,1,0:T(8,128)(2,1)}, bf16[32,48,384]{2,1,0:T(8,128)(2,1)}, bf16[4,48,1536]{2,1,0:T(8,128)(2,1)}) custom-call(bf16[128,1536]{1,0:T(8,128)(2,1)} %x_ref.1, bf16[128,1664]{1,0:T(8,128)(2,1)} %pad_maximum_fusion.12.g_ref, bf16[8,48,384]{2,1,0:T(8,128)(2,1)} %copy-done.65, ...), custom_call_target="tpu_custom_call" | custom-call | tf_op jit(solution)/shard_map/gather_inputs/pallas_call | solution.py:205
  91.2 3.1 multiply_sine_fusion
  94.3 5.1 concatenate.121.w_ref.r_ref
  99.5 2.2 maximum_maximum_fusion.2
  102.0 4.1 project.1
  109.5 48.4 %halo_forward.1 = bf16[2,1024,128]{2,1,0:T(8,128)(2,1)} custom-call(bf16[1024,128]{1,0:T(8,128)(2,1)} %copy-done.17), custom_call_target="tpu_custom_call" | custom-call | tf_op jit(solution)/shard_map/halo_forward/pallas_call | solution.py:241
  157.8 1.9 slice_bitcast_fusion.13
  163.1 8.8 %attend.1 = (bf16[3,1024,128]{2,1,0:T(8,128)(2,1)S(1)}, f32[3,1024,1]{2,1,0:T(8,128)S(1)}) custom-call(s32[5]{0:T(128)S(1)} %pad_add_fusion.meta, bf16[3,1024,128]{2,1,0:T(8,128)(2,1)S(1)} %copy-done.10, bf16[3072,128]{1,0:T(8,128)(2,1)S(1)} %pad_maximum_fusion.7.kv_ref, s32[1024,1]{1,0:T(8,128)S(1)} %copy-done.3), custom_call_target="tpu_custom_call" | custom-call | tf_op jit(solution)/shard_map/attend/pallas_call | solution.py:575
  175.8 23.9 %reduce_product2.1 = f32[128,1536]{1,0:T(8,128)S(1)} custom-call(bf16[1024,384]{1,0:T(8,128)(2,1)S(1)} %pad_maximum_fusion.8.l_ref, bf16[384,1536]{1,0:T(8,128)(2,1)S(1)} %copy-done.15), custom_call_target="tpu_custom_call" | custom-call | tf_op jit(solution)/shard_map/reduce_product2/pallas_call | solution.py:300
  202.3 23.2 %gather_layer3.1 = bf16[8,128,1536]{2,1,0:T(8,128)(2,1)} custom-call(bf16[128,1536]{1,0:T(8,128)(2,1)} %multiply_convert_fusion.6.x_ref), custom_call_target="tpu_custom_call" | custom-call | tf_op jit(solution)/shard_map/gather_layer3/pallas_call | solution.py:118
  228.9 3.0 select_reduce_fusion.1
  233.9 8.5 %fusion.11 = f32[1024,1024]{0,1:T(8,128)} fusion(bf16[1024,1536]{1,0:T(8,128)(2,1)} %bitcast.154, bf16[1,1536,1024]{2,1,0:T(8,128)(2,1)} %all-gather.11.cloned.1.call-done), kind=kOutput, calls=%fused_computation.16 | convolution fusion | flops 3221225472 | bytes 10485760 | tf_op jit(solution)/shard_map/dot_general | solution.py:675
  242.4 8.4 %multiply_convert_fusion.5 = (bf16[1024,512]{0,1:T(8,128)(2,1)}, bf16[1024,512]{0,1:T(8,128)(2,1)}, f32[1024]{0:T(1024)}, bf16[1024,512]{0,1:T(8,128)(2,1)S(1)}) fusion(f32[1024,1024]{0,1:T(8,128)} %fusion.11, f32[1024]{0:T(1024)} %bitcast.193, bf16[1,512,1536]{2,1,0:T(8,128)(2,1)} %all-gather.9.cloned.1.call-done, bf16[1024,1664]{1,0:T(8,128)(2,1)} %bitcast.186), kind=kOutput, calls=%fused_computation.43 | convolution fusion | flops 1620573184 | bytes 12066816 | tf_op jit(solution)/shard_map/dot_general | solution.py:790
  251.8 3.1 fusion.15
  254.9 2.6 copy.230
  258.1 8.3 %fusion.7 = f32[1024,1024]{0,1:T(8,128)} fusion(bf16[1024,1536]{1,0:T(8,128)(2,1)} %bitcast.155, bf16[1,1536,1024]{2,1,0:T(8,128)(2,1)} %all-gather.15.cloned.1.call-done), kind=kOutput, calls=%fused_computation.12 | convolution fusion | flops 3221225472 | bytes 10485760 | tf_op jit(solution)/shard_map/dot_general | solution.py:675
  266.3 8.3 %multiply_convert_fusion.3 = (bf16[1024,512]{0,1:T(8,128)(2,1)}, bf16[1024,512]{0,1:T(8,128)(2,1)}, f32[1024]{0:T(1024)}, bf16[1024,512]{0,1:T(8,128)(2,1)S(1)}) fusion(f32[1024,1024]{0,1:T(8,128)} %fusion.7, f32[1024]{0:T(1024)S(1)} %bitcast.190, bf16[1,512,1536]{2,1,0:T(8,128)(2,1)} %all-gather.13.cloned.1.call-done, bf16[1024,1664]{1,0:T(8,128)(2,1)} %bitcast.187), kind=kOutput, calls=%fused_computation.39 | convolution fusion | flops 1620573184 | bytes 12066816 | tf_op jit(solution)/shard_map/dot_general | solution.py:790
  275.7 3.0 fusion.18
  278.7 2.6 copy.232
  290.1 7.7 %convolution_convert_fusion.1 = bf16[1536,1024]{1,0:T(8,128)(2,1)} fusion(bf16[1024,1536]{1,0:T(8,128)(2,1)} %bitcast.156, bf16[1024,512]{0,1:T(8,128)(2,1)} %get-tuple-element.93, bf16[1024,512]{0,1:T(8,128)(2,1)} %get-tuple-element.92), kind=kOutput, calls=%fused_computation.7 | convolution fusion | flops 3226992640 | bytes 8388608 | tf_op jit(solution)/shard_map/dot_general | solution.py:797
  299.5 6.2 fusion.9
  305.7 3.8 add_convert_fusion.1
  309.8 24.3 %reduce_ready4.1 = f32[128,1664]{1,0:T(8,128)S(1)} custom-call(bf16[8,128,1664]{2,1,0:T(8,128)(2,1)S(1)} %bitcast.149), custom_call_target="tpu_custom_call" | custom-call | tf_op jit(solution)/shard_map/reduce_ready4/pallas_call | solution.py:325
  334.5 2.1 multiply_reduce_fusion.3
  338.5 22.9 %gather_layer5.1 = bf16[8,128,1536]{2,1,0:T(8,128)(2,1)} custom-call(bf16[128,1536]{1,0:T(8,128)(2,1)} %fusion.65.x_ref), custom_call_target="tpu_custom_call" | custom-call | tf_op jit(solution)/shard_map/gather_layer5/pallas_call | solution.py:118
  361.4 4.1 convolution_convert_fusion.4
  367.3 11.6 %attend_back.1 = (bf16[3,1024,128]{2,1,0:T(8,128)(2,1)S(1)}, f32[3072,128]{1,0:T(8,128)S(1)}) custom-call(s32[5]{0:T(128)S(1)} %pad_add_fusion.meta, bf16[3,1024,128]{2,1,0:T(8,128)(2,1)S(1)} %copy-done.11, bf16[3072,128]{1,0:T(8,128)(2,1)S(1)} %copy-done.1, s32[1024,1]{1,0:T(8,128)S(1)} %copy-done.4, f32[3,1024,1]{2,1,0:T(8,128)} %copy-done.16, ...), custom_call_target="tpu_custom_call" | custom-call | tf_op jit(solution)/shard_map/attend_back/pallas_call | solution.py:635
  384.8 5.9 convolution_convert_fusion
  392.0 3.7 fusion.34
  395.8 3.6 add_convert_fusion
  399.5 108.7 %halo_back.1 = (bf16[3,1024,128]{2,1,0:T(8,128)(2,1)S(1)}, f32[128,1536]{1,0:T(8,128)S(1)}, bf16[4,48,1536]{2,1,0:T(8,128)(2,1)S(1)}) custom-call(bf16[3,1024,128]{2,1,0:T(8,128)(2,1)S(1)} %pad_maximum_fusion.10.d_ref, bf16[8,128,1536]{2,1,0:T(8,128)(2,1)} %bitcast.158, bf16[4,48,1536]{2,1,0:T(8,128)(2,1)S(1)} %bitcast.151), custom_call_target="tpu_custom_call" | custom-call | tf_op jit(solution)/shard_map/halo_back/pallas_call | solution.py:411
  513.0 2.1 copy-done.7
  515.1 4.8 fusion.78
  519.9 3.6 copy.222
  523.5 2.9 multiply_reduce_fusion
  526.4 2.2 reduce_sum.153
  530.4 2.0 fusion.69
  532.3 1.8 copy.217
  534.2 1.8 copy.218
  536.0 1.8 copy.219
  537.9 1.9 copy.220
  544.8 2.2 divide_convert_fusion
  547.8 5.1 concatenate.145.p_ref
  552.9 4.4 copy_bitcast_fusion.l_ref
  557.3 50.8 %reduce_last.1 = (f32[128,1536]{1,0:T(8,128)S(1)}, bf16[32,48,384]{2,1,0:T(8,128)(2,1)S(1)}) custom-call(bf16[1024,512]{1,0:T(8,128)(2,1)S(1)} %copy_bitcast_fusion.l_ref, bf16[1536,512]{1,0:T(8,128)(2,1)S(1)} %concatenate.121.w_ref.r_ref, bf16[32,48,384]{2,1,0:T(8,128)(2,1)S(1)} %copy-done.2), custom_call_target="tpu_custom_call" | custom-call | tf_op jit(solution)/shard_map/reduce_last/pallas_call | solution.py:478
  618.7 2.2 fusion.43
  624.7 3.2 maximum_convert_fusion
  (330 shorter events, 81.7 us)
Async XLA Ops:
  7.2 226.8 %all-gather.11.cloned.1.call-start = ((), (), s32[]{:S(2)}) async-start(), calls=%async_computation.7 | async-start | bytes 3932160 | tf_op jit(solution)/shard_map/all_gather | solution.py:707
  10.0 232.4 %all-gather.9.cloned.1.call-start = ((), (), s32[]{:S(2)}) async-start(), calls=%async_computation.6 | async-start | bytes 1966080 | tf_op jit(solution)/shard_map/all_gather | solution.py:708
  11.1 4.0 copy-start.43
  11.1 246.9 %all-gather.15.cloned.1.call-start = ((), (), s32[]{:S(2)}) async-start(), calls=%async_computation.9 | async-start | bytes 3932160 | tf_op jit(solution)/shard_map/all_gather | solution.py:707
  11.9 254.5 %all-gather.13.cloned.1.call-start = ((), (), s32[]{:S(2)}) async-start(), calls=%async_computation.8 | async-start | bytes 1966080 | tf_op jit(solution)/shard_map/all_gather | solution.py:708
  12.4 608.5 %reduce-scatter.13.cloned.1.call-start = ((), (), s32[]{:S(2)}) async-start(), calls=%async_computation.10 | async-start | bytes 1966080
  87.7 6.6 %copy-start.14 = (bf16[384,1536]{1,0:T(8,128)(2,1)}, bf16[384,1536]{1,0:T(8,128)(2,1)S(1)}, u32[]{:S(2)}) copy-start(bf16[384,1536]{1,0:T(8,128)(2,1)S(1)} %slice_dynamic-update-slice_fusion.r_ref) | copy-start | bytes 3538948
  88.8 5.5 copy-start.36
  102.0 57.7 %copy-start.76 = (s32[1024]{0:T(1024)S(1)}, s32[1024]{0:T(1024)}, u32[]{:S(2)}) copy-start(s32[1024]{0:T(1024)} %get-tuple-element.170) | copy-start | bytes 12292
  109.5 51.4 %copy-start.18 = (bf16[1024,128]{1,0:T(8,128)(2,1)S(1)}, bf16[1024,128]{1,0:T(8,128)(2,1)}, u32[]{:S(2)}) copy-start(bf16[1024,128]{1,0:T(8,128)(2,1)} %copy-done.17) | copy-start | bytes 786436
  174.0 25.7 %copy-start.50 = (bf16[1024,128]{1,0:T(8,128)(2,1)}, bf16[1024,128]{1,0:T(8,128)(2,1)S(1)}, u32[]{:S(2)}) copy-start(bf16[1024,128]{1,0:T(8,128)(2,1)S(1)} %get-tuple-element.126) | copy-start | bytes 786436
  174.0 25.7 %copy-start.52 = (bf16[1024,128]{1,0:T(8,128)(2,1)}, bf16[1024,128]{1,0:T(8,128)(2,1)S(1)}, u32[]{:S(2)}) copy-start(bf16[1024,128]{1,0:T(8,128)(2,1)S(1)} %get-tuple-element.127) | copy-start | bytes 786436
  174.0 25.7 %copy-start.54 = (bf16[1024,128]{1,0:T(8,128)(2,1)}, bf16[1024,128]{1,0:T(8,128)(2,1)S(1)}, u32[]{:S(2)}) copy-start(bf16[1024,128]{1,0:T(8,128)(2,1)S(1)} %get-tuple-element.128) | copy-start | bytes 786436
  174.8 24.9 %copy-start.38 = (bf16[128,1536]{1,0:T(8,128)(2,1)S(1)}, bf16[128,1536]{1,0:T(8,128)(2,1)}, u32[]{:S(2)}) copy-start(bf16[128,1536]{1,0:T(8,128)(2,1)} %x_ref.1) | copy-start | bytes 1179652
  200.5 25.0 %copy-start.77 = (f32[128]{0:T(128)}, f32[128]{0:T(128)S(1)}, u32[]{:S(2)}) copy-start(f32[128]{0:T(128)S(1)} %add_rsqrt_fusion.1) | copy-start | bytes 1540
  242.4 9.4 %copy-start.71 = (bf16[8,128,1664]{2,1,0:T(8,128)(2,1)S(1)}, bf16[8,128,1664]{2,1,0:T(8,128)(2,1)}, u32[]{:S(2)}) copy-start(bf16[8,128,1664]{2,1,0:T(8,128)(2,1)} %get-tuple-element.34) | copy-start | bytes 10223620
  242.4 9.4 %copy-start.73 = (f32[1024,1]{0,1:T(1,128)S(1)}, f32[1024,1]{0,1:T(1,128)}, u32[]{:S(2)}) copy-start(f32[1024,1]{0,1:T(1,128)} %get-tuple-element.161) | copy-start | bytes 12292
  257.5 364.7 %reduce-scatter.15.cloned.1.call-start = ((), (), s32[]{:S(2)}) async-start(), calls=%async_computation.11 | async-start | bytes 1966080
  266.3 9.3 %copy-start.72 = (bf16[8,128,1664]{2,1,0:T(8,128)(2,1)S(1)}, bf16[8,128,1664]{2,1,0:T(8,128)(2,1)}, u32[]{:S(2)}) copy-start(bf16[8,128,1664]{2,1,0:T(8,128)(2,1)} %get-tuple-element.34) | copy-start | bytes 10223620
  281.3 343.3 %reduce-scatter.9.cloned.1.call-start = ((), (), s32[]{:S(2)}) async-start(), calls=%async_computation.4 | async-start | bytes 3932160 | tf_op jit(solution)/shard_map/reduce_scatter | solution.py:798
  297.9 326.8 %reduce-scatter.11.cloned.1.call-start = ((), (), s32[]{:S(2)}) async-start(), calls=%async_computation.5 | async-start | bytes 3932160 | tf_op jit(solution)/shard_map/reduce_scatter | solution.py:798
  299.5 6.2 copy-start.90
  299.5 6.2 copy-start.92
  299.5 6.2 copy-start.94
  309.7 24.3 %copy-start.62 = (f32[128,16]{1,0:T(8,128)S(1)}, f32[128,16]{1,0:T(8,128)}, u32[]{:S(2)}) copy-start(f32[128,16]{1,0:T(8,128)} %copy-done.61) | copy-start | bytes 24580
  309.7 24.3 %copy-start.64 = (pred[128,128]{1,0:T(8,128)(4,1)S(1)}, pred[128,128]{1,0:T(8,128)(4,1)}, u32[]{:S(2)}) copy-start(pred[128,128]{1,0:T(8,128)(4,1)} %copy-done.63) | copy-start | bytes 49156
  309.8 24.3 %copy-start.81 = (f32[128]{0:T(128)S(1)}, f32[128]{0:T(128)}, u32[]{:S(2)}) copy-start(f32[128]{0:T(128)} %copy-done.80) | copy-start | bytes 1540
  309.8 24.3 %copy-start.82 = (f32[128]{0:T(128)S(1)}, f32[128]{0:T(128)}, u32[]{:S(2)}) copy-start(f32[128]{0:T(128)} %fusion.56) | copy-start | bytes 1540
  309.8 24.7 %copy-start.26 = (f32[128,1536]{1,0:T(8,128)S(1)}, f32[128,1536]{1,0:T(8,128)}, u32[]{:S(2)}) copy-start(f32[128,1536]{1,0:T(8,128)} %copy-done.25) | copy-start | bytes 2359300
  309.8 24.7 %copy-start.78 = (f32[128]{0:T(128)S(1)}, f32[128]{0:T(128)}, u32[]{:S(2)}) copy-start(f32[128]{0:T(128)} %copy-done.77) | copy-start | bytes 1540
  378.9 4.7 copy-start.5
  378.9 4.6 copy-start.21
  392.0 3.8 copy-start.47
  392.0 3.8 copy-start.49
  392.0 3.8 copy-start.74
  395.8 3.7 copy-start.56
  395.8 3.7 copy-start.57
  399.5 108.8 %copy-start.22 = (bf16[3,1024,128]{2,1,0:T(8,128)(2,1)S(1)}, bf16[3,1024,128]{2,1,0:T(8,128)(2,1)}, u32[]{:S(2)}) copy-start(bf16[3,1024,128]{2,1,0:T(8,128)(2,1)} %copy-done.21) | copy-start | bytes 2359300
  510.9 4.2 copy-start.7
  511.6 8.3 %copy-start.30 = (f32[1024,4,96]{2,0,1:T(8,128)}, f32[1024,4,96]{2,0,1:T(8,128)S(1)}, u32[]{:S(2)}) copy-start(f32[1024,4,96]{2,0,1:T(8,128)S(1)} %get-tuple-element.98) | copy-start | bytes 4718596
  511.6 8.3 %copy-start.31 = (f32[1024,4,96]{2,0,1:T(8,128)}, f32[1024,4,96]{2,0,1:T(8,128)S(1)}, u32[]{:S(2)}) copy-start(f32[1024,4,96]{2,0,1:T(8,128)S(1)} %get-tuple-element.99) | copy-start | bytes 4718596
  530.3 13.0 %copy-start.75 = (bf16[1536]{0:T(1024)(128)(2,1)S(1)}, bf16[1536]{0:T(1024)(128)(2,1)}, u32[]{:S(2)}) copy-start(bf16[1536]{0:T(1024)(128)(2,1)} %get-tuple-element.76) | copy-start | bytes 9220
  552.9 4.4 copy-start.2
  609.7 7.2 %copy-start.24 = (bf16[4,48,1536]{2,1,0:T(8,128)(2,1)S(1)}, bf16[4,48,1536]{2,1,0:T(8,128)(2,1)}, u32[]{:S(2)}) copy-start(bf16[4,48,1536]{2,1,0:T(8,128)(2,1)} %copy-done.23) | copy-start | bytes 1769476
  610.8 6.9 %copy-start.85 = (f32[128]{0:T(128)S(1)}, f32[128]{0:T(128)}, u32[]{:S(2)}) copy-start(f32[128]{0:T(128)} %add_rsqrt_fusion) | copy-start | bytes 1540
  611.6 7.1 %copy-start.20 = (f32[128,1536]{1,0:T(8,128)S(1)}, f32[128,1536]{1,0:T(8,128)}, u32[]{:S(2)}) copy-start(f32[128,1536]{1,0:T(8,128)} %copy-done.19) | copy-start | bytes 2359300
  611.6 7.1 %copy-start.27 = (f32[128,1536]{1,0:T(8,128)S(1)}, f32[128,1536]{1,0:T(8,128)}, u32[]{:S(2)}) copy-start(f32[128,1536]{1,0:T(8,128)} %copy-done.25) | copy-start | bytes 2359300
  611.6 7.1 %copy-start.79 = (f32[128]{0:T(128)S(1)}, f32[128]{0:T(128)}, u32[]{:S(2)}) copy-start(f32[128]{0:T(128)} %copy-done.77) | copy-start | bytes 1540
  (56 other events, 114.5 us)
Sparse Core Ops, SparseCore 0:
  10.2 103.1 all-gather.10
  114.9 42.4 all-gather.8
  159.0 67.5 all-gather.14
  228.0 35.2 all-gather.12
  265.4 41.7 reduce-scatter.12
  309.4 34.2 reduce-scatter.14
  346.0 59.2 reduce-scatter.8
  407.6 118.1 reduce-scatter.10

commit v2 on v1

v2 whole, which is shorter than its diff:
```python
import functools
import math

import jax
import jax.numpy as jnp
from jax import lax
from jax.experimental import pallas as pl
from jax.experimental.pallas import tpu as pltpu
from jax.sharding import PartitionSpec as P

D = 1536
HEADS = 24
KV = 8
HW = 64
GROUP = HEADS // KV
FF = 512
TOPK = 8
EXP_DEV = 2
LENMAX = 4096
EPS = 1e-05
THETA = 10000.0
NEG = -1e30
LANES = 128
AUX = 384
ROUTER_AT = 320
QCOLS = GROUP * HW

f32 = jnp.float32
bf16 = jnp.bfloat16
MESH = pl.DeviceIdType.MESH
ANY = pl.BlockSpec(memory_space=pl.ANY)
VMEM = pl.BlockSpec(memory_space=pltpu.VMEM)
DMA = pltpu.SemaphoreType.DMA
MIB = 1 << 20


def dev(u, b):
    return {"ulysses": u, "blk": b}


def remote(src, dst, ss, rs, u, b):
    return pltpu.make_async_remote_copy(
        src_ref=src, dst_ref=dst, send_sem=ss, recv_sem=rs,
        device_id=dev(u, b), device_id_type=MESH,
    )


def cost(us):
    return pl.CostEstimate(flops=us * 1_000_000_000, bytes_accessed=0, transcendentals=0)


def signal(sem, u, b):
    pl.semaphore_signal(sem, inc=1, device_id=dev(u, b), device_id_type=MESH)


class Layer:
    def __init__(self, nb):
        self.u = lax.axis_index("ulysses")
        self.b = lax.axis_index("blk")
        self.nb = nb
        self.nc = nb // 2
        self.chip = self.b // 2
        self.core = lax.rem(self.b, 2)
        self.sib = self.chip * 2 + 1 - self.core

    def peer(self, i):
        return lax.rem(self.chip + i, self.nc) * 2 + self.core

    def behind(self, i):
        return lax.rem(self.chip + self.nc - i, self.nc) * 2 + self.core

    def across(self, d):
        at = self.u
        for k in range(d.bit_length()):
            if (d >> k) & 1:
                at = at + (1 << k) - (2 << k) * lax.rem(self.u // (1 << k), 2)
        return at

    def enter(self, flips=()):
        bar = pltpu.get_barrier_semaphore()
        for i in range(1, self.nc):
            signal(bar, self.u, self.peer(i))
        signal(bar, self.u, self.sib)
        for d in flips:
            signal(bar, self.across(d), self.b)
        pl.semaphore_wait(bar, self.nc + len(flips))


class Swaps:
    def __init__(self, items):
        self.items = items
        self.flips = sorted({d for _, d in items})
        self.arrays = [a for a, _ in items]
        self.shapes = tuple(jax.ShapeDtypeStruct(a.shape[-2:], a.dtype) for a in self.arrays)
        self.n = len(items)
        self.specs = [ANY] * self.n
        self.scratch = [DMA((2, max(self.n, 1)))]

    def start(self, me, srcs, dsts, sems):
        copies = []
        for k, (src, dst, (_, d)) in enumerate(zip(srcs, dsts, self.items)):
            if len(src.shape) == 3:
                odd = lax.rem(me.u, 2)
                src = src.at[1 - odd if d % 2 else odd]
            c = remote(src, dst, sems.at[0, k], sems.at[1, k], me.across(d), me.b)
            c.start()
            copies.append(c)
        return copies


def both(flips, *more):
    return sorted(set(flips) | set(more))


def gather_start(me, src, dst, ss, rs, fs, frs):
    sends = []
    for i in range(1, me.nc):
        c = remote(src, dst.at[me.b], ss.at[i], rs.at[i], me.u, me.peer(i))
        c.start()
        sends.append(c)
    c = remote(src, dst.at[me.b], fs.at[0], frs.at[0], me.u, me.sib)
    c.start()
    return sends, [c]


def gather_keep(me, src, dst, sem):
    c = pltpu.make_async_copy(src, dst.at[me.b], sem)
    c.start()
    return c


def gather_forward(me, dst, state, fs, frs):
    sends, passed = state
    for i in range(1, me.nc):
        sends[i - 1].wait_recv()
        at = me.behind(i)
        c = remote(dst.at[at], dst.at[at], fs.at[i], frs.at[i], me.u, me.sib)
        c.start()
        passed.append(c)


def gather_finish(state):
    sends, passed = state
    for c in sends:
        c.wait_send()
    for c in passed:
        c.wait()


def gather_layer(x, nb, cid, swaps):
    nc = nb // 2
    m = swaps.n

    def kernel(x_ref, *rest):
        srcs, o_ref, dsts = rest[:m], rest[m], rest[m + 1:2 * m + 1]
        ss, rs, fs, frs, ls, ws = rest[2 * m + 1:]
        me = Layer(nb)
        me.enter(swaps.flips)
        state = gather_start(me, x_ref, o_ref, ss, rs, fs, frs)
        moved = swaps.start(me, srcs, dsts, ws)
        own = gather_keep(me, x_ref, o_ref, ls)
        gather_forward(me, o_ref, state, fs, frs)
        gather_finish(state)
        own.wait()
        for c in moved:
            c.wait()

    return pl.pallas_call(
        kernel,
        out_shape=(jax.ShapeDtypeStruct((nb,) + x.shape, x.dtype),) + swaps.shapes,
        in_specs=[ANY] + swaps.specs,
        out_specs=(ANY,) + tuple(swaps.specs),
        scratch_shapes=[DMA((nc,))] * 4 + [DMA] + swaps.scratch,
        compiler_params=pltpu.CompilerParams(collective_id=cid, has_side_effects=True),
        cost_estimate=cost(22),
        name="gather_layer%d" % cid,
    )(x, *swaps.arrays)


def gather_pair(x, nb, cid, swaps):
    nc = nb // 2
    m = swaps.n

    def kernel(x_ref, *rest):
        srcs, o_ref, dsts = rest[:m], rest[m], rest[m + 1:2 * m + 1]
        ss, rs, fs, frs, zs, ls, ws = rest[2 * m + 1:]
        me = Layer(nb)
        me.enter(both(swaps.flips, 1))
        own, oth = o_ref.at[0], o_ref.at[1]
        mate = remote(x_ref, oth.at[me.b], zs.at[0], zs.at[1], me.across(1), me.b)
        mate.start()
        s0 = gather_start(me, x_ref, own, ss.at[0], rs.at[0], fs.at[0], frs.at[0])
        moved = swaps.start(me, srcs, dsts, ws)
        keep = gather_keep(me, x_ref, own, ls)
        mate.wait_recv()
        s1 = gather_start(me, oth.at[me.b], oth, ss.at[1], rs.at[1], fs.at[1], frs.at[1])
        gather_forward(me, own, s0, fs.at[0], frs.at[0])
        gather_forward(me, oth, s1, fs.at[1], frs.at[1])
        gather_finish(s0)
        gather_finish(s1)
        mate.wait_send()
        keep.wait()
        for c in moved:
            c.wait()

    return pl.pallas_call(
        kernel,
        out_shape=(jax.ShapeDtypeStruct((2, nb) + x.shape, x.dtype),) + swaps.shapes,
        in_specs=[ANY] + swaps.specs,
        out_specs=(ANY,) + tuple(swaps.specs),
        scratch_shapes=[DMA((2, nc))] * 4 + [DMA((2,)), DMA] + swaps.scratch,
        compiler_params=pltpu.CompilerParams(collective_id=cid, has_side_effects=True),
        cost_estimate=cost(38),
        name="gather_pair%d" % cid,
    )(x, *swaps.arrays)


def gather_inputs(x, gm, pieces, wo, nz, nb, cid, swaps):
    n = nz * nb
    nc = nb // 2
    groups, shard, _ = pieces.shape
    rp = nb // groups
    n_o = QCOLS // shard
    m = swaps.n

    def kernel(x_ref, g_ref, p_ref, w_ref, *rest):
        srcs = rest[:m]
        xo, go, gx, po, wo_out = rest[m:m + 5]
        dsts = rest[m + 5:2 * m + 5]
        ss, rs, fs, frs, ps, pr, zs, ws, wr, ls, sw = rest[2 * m + 5:]
        me = Layer(nb)
        lin = me.u * nb + me.b
        bar = pltpu.get_barrier_semaphore()

        def place(i):
            t = lax.rem(lin + i, n)
            return t // nb, lax.rem(t, nb)

        @pl.loop(1, n)
        def _(i):
            tz, tb = place(i)
            signal(bar, tz, tb)

        pl.semaphore_wait(bar, n - 1)

        def piece(i):
            tb = lax.rem(me.b + i, nb)
            return remote(p_ref.at[tb // rp], po.at[me.u, me.b], ps.at[i], pr.at[i], me.u, tb)

        for i in range(1, nb):
            piece(i).start()
        own = pltpu.make_async_copy(p_ref.at[me.b // rp], po.at[me.u, me.b], ls.at[0])
        own.start()
        xs = gather_start(me, x_ref, xo, ss.at[0], rs.at[0], fs.at[0], frs.at[0])
        for i in range(1, nb):
            piece(i).wait()
        own.wait()
        slabs = []
        for zo in range(1, nz):
            c = remote(po.at[me.u], po.at[me.u], zs.at[0, zo], zs.at[1, zo], lax.rem(me.u + zo, nz), me.b)
            c.start()
            slabs.append(c)
        hg = lin // n_o
        slot = lax.rem(lin, n_o)

        def weight(zo, p):
            tz, tb = lax.rem(me.u + zo, nz), hg * rp + p
            k = zo * rp + p
            return tb, remote(w_ref, wo_out.at[slot], ws.at[k], wr.at[slot], tz, tb)

        mate = remote(g_ref, gx, ls.at[2], ls.at[3], me.across(1), me.b)
        mate.start()
        keep = pltpu.make_async_copy(w_ref, wo_out.at[slot], ls.at[1])
        for zo in range(nz):
            for p in range(rp):
                tb, c = weight(zo, p)
                if zo:
                    c.start()
                else:
                    pl.when(tb != me.b)(c.start)
                    pl.when(tb == me.b)(keep.start)
        gs = gather_start(me, g_ref, go, ss.at[1], rs.at[1], fs.at[1], frs.at[1])
        moved = swaps.start(me, srcs, dsts, sw)
        xk = gather_keep(me, x_ref, xo, ls.at[4])
        gk = gather_keep(me, g_ref, go, ls.at[5])
        gather_forward(me, xo, xs, fs.at[0], frs.at[0])
        gather_forward(me, go, gs, fs.at[1], frs.at[1])
        for zo in range(nz):
            for p in range(rp):
                tb, c = weight(zo, p)
                if zo:
                    c.wait_send()
                else:
                    pl.when(tb != me.b)(c.wait_send)
                    pl.when(tb == me.b)(keep.wait)
        for j in range(n_o):
            src = (me.b // rp) * n_o + j
            c = remote(w_ref, wo_out.at[j], ws.at[0], wr.at[j], me.u, me.sib)
            pl.when(src != lin)(c.wait_recv)
        gather_finish(xs)
        gather_finish(gs)
        for c in slabs + moved:
            c.wait()
        mate.wait()
        xk.wait()
        gk.wait()

    sh = jax.ShapeDtypeStruct
    return pl.pallas_call(
        kernel,
        out_shape=(
            sh((nb,) + x.shape, x.dtype),
            sh((nb,) + gm.shape, gm.dtype),
            sh(gm.shape, gm.dtype),
            sh((nz, nb, shard, AUX), bf16),
            sh((n_o, shard, D), bf16),
        )
        + swaps.shapes,
        in_specs=[ANY] * (4 + m),
        out_specs=(ANY,) * (5 + m),
        scratch_shapes=[DMA((2, nc))] * 4
        + [DMA((nb,))] * 2
        + [DMA((2, nz)), DMA((nz * rp,)), DMA((n_o,)), DMA((6,))]
        + swaps.scratch,
        compiler_params=pltpu.CompilerParams(collective_id=cid, has_side_effects=True),
        cost_estimate=cost(50),
        name="gather_inputs",
    )(x, gm, pieces, wo, *swaps.arrays)


def halo_forward(kv, gx, nz, nb, back, cid, swaps):
    nc = nb // 2
    m = swaps.n

    def kernel(x_ref, g_ref, *rest):
        srcs = rest[:m]
        o_ref, go = rest[m:m + 2]
        dsts = rest[m + 2:2 * m + 2]
        ks, kr, ss, rs, fs, frs, ls, ws = rest[2 * m + 2:]
        me = Layer(nb)
        u, b = me.u, me.b
        bar = pltpu.get_barrier_semaphore()
        for d in range(1, nz):
            signal(bar, lax.rem(u + d, nz), b)
        for i in range(1, nc):
            signal(bar, u, me.peer(i))
        signal(bar, u, me.sib)
        pl.semaphore_wait(bar, nz - 1 + nc)

        def copy(d):
            return remote(x_ref, o_ref.at[d - 1], ks.at[d - 1], kr.at[d - 1], u + d, b)

        for d in range(1, back + 1):
            pl.when(u + d < nz)(lambda d=d: copy(d).start())
        state = gather_start(me, g_ref, go, ss, rs, fs, frs)
        moved = swaps.start(me, srcs, dsts, ws)
        keep = gather_keep(me, g_ref, go, ls)
        gather_forward(me, go, state, fs, frs)
        gather_finish(state)
        keep.wait()
        for c in moved:
            c.wait()
        for d in range(1, back + 1):
            pl.when(u + d < nz)(lambda d=d: copy(d).wait_send())
            pl.when(u >= d)(lambda d=d: copy(d).wait_recv())

    sh = jax.ShapeDtypeStruct
    return pl.pallas_call(
        kernel,
        out_shape=(sh((back,) + kv.shape, kv.dtype), sh((nb,) + gx.shape, gx.dtype)) + swaps.shapes,
        in_specs=[ANY] * (2 + m),
        out_specs=(ANY,) * (2 + m),
        scratch_shapes=[DMA((back,))] * 2 + [DMA((nc,))] * 4 + [DMA] + swaps.scratch,
        compiler_params=pltpu.CompilerParams(collective_id=cid, has_side_effects=True),
        cost_estimate=cost(20),
        name="halo_forward",
    )(kv, gx, *swaps.arrays)


def reduce_start(me, source, sib_in, fs, frs):
    passed = []
    for i in [*range(1, me.nc), 0]:
        to = lax.rem(me.chip + i, me.nc) * 2 + 1 - me.core
        c = remote(source(i, to), sib_in.at[i], fs.at[i], frs.at[i], me.u, me.sib)
        c.start()
        passed.append(c)
    return passed


def reduce_rest(me, block, passed, sib_in, snd, land, ss, rs):
    nc = me.nc
    sends = []
    for i in range(1, nc):
        mine = block(me.peer(i))
        passed[i - 1].wait_recv()
        snd[i] = (mine + sib_in[i].astype(f32)).astype(bf16)
        c = remote(snd.at[i], land.at[i], ss.at[i], rs.at[i], me.u, me.peer(i))
        c.start()
        sends.append(c)
    total = block(me.b)
    passed[nc - 1].wait_recv()
    return total + sib_in[0].astype(f32), sends


def reduce_end(me, total, passed, sends, land):
    for i in range(1, me.nc):
        sends[i - 1].wait_recv()
        total = total + land[i].astype(f32)
    for c in passed + sends:
        c.wait_send()
    return total


def reduce_made(me, block, sib_out, sib_in, snd, land, ss, rs, fs, frs):
    def source(i, to):
        sib_out[i] = block(to).astype(bf16)
        return sib_out.at[i]

    passed = reduce_start(me, source, sib_in, fs, frs)
    total, sends = reduce_rest(me, block, passed, sib_in, snd, land, ss, rs)
    return reduce_end(me, total, passed, sends, land)


def reduce_scratch(nb, rows, cols):
    nc = nb // 2
    return [pltpu.VMEM((nc, rows, cols), bf16)] * 4 + [DMA((nc,))] * 4


def reduce_pair_body(me, p_ref, sib_in, snd, land, zbuf, ss, rs, fs, frs, zs):
    block = lambda h: (lambda t: p_ref[h, t].astype(f32))
    source = lambda h: (lambda i, to: p_ref.at[h, to])
    p1 = reduce_start(me, source(1), sib_in.at[1], fs.at[1], frs.at[1])
    p0 = reduce_start(me, source(0), sib_in.at[0], fs.at[0], frs.at[0])
    t1, s1 = reduce_rest(me, block(1), p1, sib_in.at[1], snd.at[1], land.at[1], ss.at[1], rs.at[1])
    zbuf[0] = reduce_end(me, t1, p1, s1, land.at[1]).astype(bf16)
    across = remote(zbuf.at[0], zbuf.at[1], zs.at[0], zs.at[1], me.across(1), me.b)
    across.start()
    t0, s0 = reduce_rest(me, block(0), p0, sib_in.at[0], snd.at[0], land.at[0], ss.at[0], rs.at[0])
    t0 = reduce_end(me, t0, p0, s0, land.at[0])
    across.wait()
    return t0 + zbuf[1].astype(f32)


def reduce_pair_scratch(nb, rows, cols):
    nc = nb // 2
    return (
        [pltpu.VMEM((2, nc, rows, cols), bf16)] * 3
        + [pltpu.VMEM((2, rows, cols), bf16)]
        + [DMA((2, nc))] * 4
        + [DMA((2,))]
    )


def reduce_product(lhs, rhs, nb, cid, swaps):
    rows = lhs.shape[0] // nb
    cols = rhs.shape[1]
    m = swaps.n

    def kernel(l_ref, r_ref, *rest):
        srcs, o_ref, dsts = rest[:m], rest[m], rest[m + 1:2 * m + 1]
        ws, *scratch = rest[2 * m + 1:]
        me = Layer(nb)
        me.enter(swaps.flips)
        moved = swaps.start(me, srcs, dsts, ws)

        def block(t):
            part = l_ref[pl.ds(pl.multiple_of(t * rows, rows), rows), :]
            return jnp.dot(part, r_ref[...], preferred_element_type=f32)

        o_ref[...] = reduce_made(me, block, *scratch)
        for c in moved:
            c.wait()

    return pl.pallas_call(
        kernel,
        out_shape=(jax.ShapeDtypeStruct((rows, cols), f32),) + swaps.shapes,
        in_specs=[VMEM, VMEM] + swaps.specs,
        out_specs=(VMEM,) + tuple(swaps.specs),
        scratch_shapes=swaps.scratch + reduce_scratch(nb, rows, cols),
        compiler_params=pltpu.CompilerParams(
            collective_id=cid, has_side_effects=True, vmem_limit_bytes=48 * MIB
        ),
        cost_estimate=cost(23),
        name="reduce_product%d" % cid,
    )(lhs, rhs, *swaps.arrays)


def reduce_pair(part, nb, cid, swaps):
    _, _, rows, cols = part.shape
    m = swaps.n

    def kernel(p_ref, *rest):
        srcs, o_ref, dsts = rest[:m], rest[m], rest[m + 1:2 * m + 1]
        ws, *scratch = rest[2 * m + 1:]
        me = Layer(nb)
        me.enter(both(swaps.flips, 1))
        moved = swaps.start(me, srcs, dsts, ws)
        o_ref[...] = reduce_pair_body(me, p_ref, *scratch)
        for c in moved:
            c.wait()

    return pl.pallas_call(
        kernel,
        out_shape=(jax.ShapeDtypeStruct((rows, cols), f32),) + swaps.shapes,
        in_specs=[VMEM] + swaps.specs,
        out_specs=(VMEM,) + tuple(swaps.specs),
        scratch_shapes=swaps.scratch + reduce_pair_scratch(nb, rows, cols),
        compiler_params=pltpu.CompilerParams(
            collective_id=cid, has_side_effects=True, vmem_limit_bytes=56 * MIB
        ),
        cost_estimate=cost(48),
        name="reduce_pair%d" % cid,
    )(part, *swaps.arrays)


def halo_back(dkv, ypart, dwo, nz, nb, rp, back, cid):
    _, _, rows, cols = ypart.shape
    n_o, shard, _ = dwo.shape
    R = dkv.shape[1]

    def kernel(d_ref, y_ref, w_ref, kin, o_ref, win, *scratch):
        ks, kr, ws, wr, ls = scratch[:5]
        me = Layer(nb)
        lin = me.u * nb + me.b
        first = (me.b // rp) * rp
        part = lax.rem(me.b, rp)
        n = nz * nb
        bar = pltpu.get_barrier_semaphore()

        @pl.loop(1, n)
        def _(i):
            t = lax.rem(lin + i, n)
            signal(bar, t // nb, lax.rem(t, nb))

        pl.semaphore_wait(bar, n - 1)

        def copy(d, p):
            k = d * rp + p
            return remote(d_ref.at[d], kin.at[d * rp + part], ks.at[k], kr.at[d * rp + part], me.u - d, first + p)

        def arrival(d, p):
            k = d * rp + p
            return remote(d_ref.at[d], kin.at[k], ks.at[k], kr.at[k], me.u, me.sib)

        for d in range(back + 1):
            for p in range(rp):
                if d:
                    pl.when(me.u >= d)(lambda d=d, p=p: copy(d, p).start())
                elif rp > 1:
                    pl.when(part != p)(lambda d=d, p=p: copy(d, p).start())

        def weight(j):
            t = (me.b // rp) * n_o + j
            at = me.u * rp + part
            return t, remote(w_ref.at[j], win.at[at], ws.at[j], wr.at[at], t // nb, lax.rem(t, nb))

        for j in range(n_o):
            t, c = weight(j)
            keep = pltpu.make_async_copy(w_ref.at[j], win.at[me.u * rp + part], ls.at[0])
            pl.when(t != lin)(c.start)
            pl.when(t == lin)(keep.start)

        o_ref[...] = reduce_pair_body(me, y_ref, *scratch[5:])

        for d in range(back + 1):
            for p in range(rp):
                if d:
                    pl.when(me.u >= d)(lambda d=d, p=p: copy(d, p).wait_send())
                    pl.when(me.u + d < nz)(lambda d=d, p=p: arrival(d, p).wait_recv())
                elif rp > 1:
                    pl.when(part != p)(lambda d=d, p=p: copy(d, p).wait_send())
                    pl.when(part != p)(lambda d=d, p=p: arrival(d, p).wait_recv())
        for j in range(n_o):
            t, c = weight(j)
            keep = pltpu.make_async_copy(w_ref.at[j], win.at[me.u * rp + part], ls.at[0])
            pl.when(t != lin)(c.wait_send)
            pl.when(t == lin)(keep.wait)
        hg = lin // n_o
        for z in range(nz):
            for p in range(rp):
                k = z * rp + p
                c = remote(w_ref.at[0], win.at[k], ws.at[0], wr.at[k], me.u, me.sib)
                pl.when(z * nb + hg * rp + p != lin)(c.wait_recv)

    sh = jax.ShapeDtypeStruct
    return pl.pallas_call(
        kernel,
        out_shape=(
            sh(((back + 1) * rp, R, LANES), bf16),
            sh((rows, cols), f32),
            sh((nz * rp, shard, D), bf16),
        ),
        in_specs=[ANY, VMEM, ANY],
        out_specs=(ANY, VMEM, ANY),
        scratch_shapes=[DMA(((back + 1) * rp,))] * 2
        + [DMA((n_o,)), DMA((nz * rp,)), DMA((1,))]
        + reduce_pair_scratch(nb, rows, cols),
        compiler_params=pltpu.CompilerParams(
            collective_id=cid, has_side_effects=True, vmem_limit_bytes=56 * MIB
        ),
        cost_estimate=cost(45),
        name="halo_back",
    )(dkv, ypart, dwo)


def reduce_last(lhs, rhs, pieces, nz, nb, cid):
    rows = lhs.shape[0] // nb
    cols = rhs.shape[0]
    _, _, shard, width = pieces.shape

    def kernel(l_ref, r_ref, p_ref, o_ref, pin, slab, total, zs, zr, ps, pr, ls, *scratch):
        me = Layer(nb)
        bar = pltpu.get_barrier_semaphore()
        for i in range(1, nb):
            signal(bar, me.u, lax.rem(me.b + i, nb))
        for i in range(1, nz):
            signal(bar, lax.rem(me.u + i, nz), me.b)
        pl.semaphore_wait(bar, nb + nz - 2)
        across = []
        for i in range(1, nz):
            to = lax.rem(me.u + i, nz)
            c = remote(p_ref.at[to], slab.at[i], zs.at[i], zr.at[i], to, me.b)
            c.start()
            across.append(c)

        def block(t):
            part = l_ref[pl.ds(pl.multiple_of(t * rows, rows), rows), :]
            return lax.dot_general(part, r_ref[...], NT, preferred_element_type=f32)

        sib_out, sib_in, snd, land, ss, rs, fs, frs = scratch

        def source(i, to):
            sib_out[i] = block(to).astype(bf16)
            return sib_out.at[i]

        passed = reduce_start(me, source, sib_in, fs, frs)
        mine, sends = reduce_rest(me, block, passed, sib_in, snd, land, ss, rs)
        for c in across:
            c.wait_recv()
        out = []
        for t in range(nb):
            tile = p_ref[me.u, t].astype(f32)
            for i in range(1, nz):
                tile = tile + slab[i, t].astype(f32)
            total[t] = tile.astype(bf16)
        for i in range(1, nb):
            t = lax.rem(me.b + i, nb)
            c = remote(total.at[t], pin.at[me.b], ps.at[i], pr.at[i], me.u, t)
            c.start()
            out.append(c)
        own = pltpu.make_async_copy(total.at[me.b], pin.at[me.b], ls.at[0])
        own.start()
        o_ref[...] = reduce_end(me, mine, passed, sends, land)
        for c in across:
            c.wait_send()
        for c in out:
            c.wait()
        own.wait()

    sh = jax.ShapeDtypeStruct
    return pl.pallas_call(
        kernel,
        out_shape=(sh((rows, cols), f32), sh((nb, shard, width), bf16)),
        in_specs=[VMEM, VMEM, VMEM],
        out_specs=(VMEM, ANY),
        scratch_shapes=[pltpu.VMEM((nz, nb, shard, width), bf16), pltpu.VMEM((nb, shard, width), bf16)]
        + [DMA((nz,))] * 2
        + [DMA((nb,))] * 2
        + [DMA((1,))]
        + reduce_scratch(nb, rows, cols),
        compiler_params=pltpu.CompilerParams(
            collective_id=cid, has_side_effects=True, vmem_limit_bytes=56 * MIB
        ),
        cost_estimate=cost(37),
        name="reduce_last",
    )(lhs, rhs, pieces)


def turn(a, c, s1, s2):
    return a * c + pltpu.roll(a, LANES - HW // 2, 1) * s1 + pltpu.roll(a, HW // 2, 1) * s2


def turn_back(a, c, s1, s2):
    return a * c - pltpu.roll(a, LANES - HW // 2, 1) * s1 - pltpu.roll(a, HW // 2, 1) * s2


def swap(a):
    return pltpu.roll(a, HW, 1)


def low_half():
    return lax.broadcasted_iota(jnp.int32, (1, LANES), 1) < HW


def row_block(step, width):
    return pl.BlockSpec((step, width), lambda i: (i, 0))


def whole_block(a):
    zeros = (0,) * a.ndim
    return pl.BlockSpec(a.shape, lambda i: zeros)


def project(x, gain, packed, c, s1, s2):
    R = x.shape[0]
    step = 256

    def kernel(x_ref, g_ref, w_ref, c_ref, a_ref, b_ref, q_ref, kv_ref, h_ref):
        v = x_ref[...].astype(f32)
        inv = lax.rsqrt(jnp.mean(v * v, axis=1, keepdims=True) + EPS)
        h = (v * inv * g_ref[...]).astype(bf16)
        h_ref[...] = h
        out = jnp.dot(h, w_ref[...], preferred_element_type=f32)
        tables = (c_ref[...], a_ref[...], b_ref[...])
        low = low_half()
        t0 = turn(out[:, :LANES], *tables)
        t1 = turn(out[:, LANES:2 * LANES], *tables)
        scale = lambda a: (jnp.where(low, a, 0.0) * (1.0 / math.sqrt(HW))).astype(bf16)
        q_ref[0] = scale(t0)
        q_ref[1] = scale(swap(t0))
        q_ref[2] = scale(t1)
        kv_ref[...] = jnp.where(low, swap(t1), swap(out[:, 2 * LANES:])).astype(bf16)

    sh = jax.ShapeDtypeStruct
    return pl.pallas_call(
        kernel,
        grid=(R // step,),
        out_shape=(sh((GROUP, R, LANES), bf16), sh((R, LANES), bf16), sh((R, D), bf16)),
        in_specs=[row_block(step, D), whole_block(gain), whole_block(packed)] + [row_block(step, LANES)] * 3,
        out_specs=(
            pl.BlockSpec((GROUP, step, LANES), lambda i: (0, i, 0)),
            row_block(step, LANES),
            row_block(step, D),
        ),
        compiler_params=pltpu.CompilerParams(vmem_limit_bytes=32 * MIB),
        cost_estimate=cost(4),
        name="project",
    )(x, gain, packed, c, s1, s2)


BQ = 256
BK = 512
NT = (((1,), (1,)), ((), ()))
NN = (((1,), (0,)), ((), ()))
TN = (((0,), (0,)), ((), ()))


def mm(a, b, dims=NN):
    return lax.dot_general(a, b, dims, preferred_element_type=f32)


def seen(meta, st, i, kb, nq):
    qpos = meta[nq] + i * BQ + lax.broadcasted_iota(jnp.int32, (BQ, 1), 0)
    kpos = kb * BK + lax.broadcasted_iota(jnp.int32, (1, BK), 1)
    return ((kpos <= qpos) & (kpos >= st))[None]


def attend(q, kv, starts, meta):
    _, Rq, _ = q.shape
    nq = Rq // BQ
    M = GROUP * BQ

    def kernel(meta, q_ref, kv_ref, st_ref, o_ref, l_ref):
        i = pl.program_id(0)
        qv = q_ref[...].reshape(M, LANES)
        st = st_ref[...]
        last = (meta[nq] + i * BQ + BQ - 1) // BK + 1

        def step(kb, carry):
            m, l, acc = carry
            keys = kv_ref[pl.ds(pl.multiple_of(kb * BK, BK), BK), :]
            s = mm(qv, keys, NT).reshape(GROUP, BQ, BK)
            s = jnp.where(seen(meta, st, i, kb, nq), s, NEG)
            m2 = jnp.maximum(m, jnp.max(s, axis=2, keepdims=True))
            w = jnp.exp(s - m2)
            f = jnp.exp(m - m2)
            l = l * f + jnp.sum(w, axis=2, keepdims=True)
            pv = mm(w.astype(bf16).reshape(M, BK), keys)
            return m2, l, acc * f + pv.reshape(GROUP, BQ, LANES)

        init = (
            jnp.full((GROUP, BQ, 1), NEG, f32),
            jnp.zeros((GROUP, BQ, 1), f32),
            jnp.zeros((GROUP, BQ, LANES), f32),
        )
        m, l, acc = lax.fori_loop(meta[i], last, step, init)
        o = acc / l
        o_ref[:, :LANES] = jnp.where(low_half(), swap(o[0]), o[1]).astype(bf16)
        o_ref[:, LANES:] = swap(o[2])[:, :HW].astype(bf16)
        l_ref[...] = m + jnp.log(l)

    sh = jax.ShapeDtypeStruct
    blk = lambda w: pl.BlockSpec((GROUP, BQ, w), lambda i, m: (0, i, 0))
    return pl.pallas_call(
        kernel,
        grid_spec=pltpu.PrefetchScalarGridSpec(
            num_scalar_prefetch=1,
            grid=(nq,),
            in_specs=[
                blk(LANES),
                pl.BlockSpec(kv.shape, lambda i, m: (0, 0)),
                pl.BlockSpec((BQ, 1), lambda i, m: (i, 0)),
            ],
            out_specs=(pl.BlockSpec((BQ, QCOLS), lambda i, m: (i, 0)), blk(1)),
        ),
        out_shape=(sh((Rq, QCOLS), bf16), sh((GROUP, Rq, 1), f32)),
        compiler_params=pltpu.CompilerParams(vmem_limit_bytes=48 * MIB),
        cost_estimate=cost(17),
        name="attend",
    )(meta, q, kv, starts)


def attend_back(q, kv, starts, meta, lse, mixed, dattn, wo):
    _, Rq, _ = q.shape
    nq = Rq // BQ
    M = GROUP * BQ
    K = kv.shape[0]

    def kernel(meta, q_ref, kv_ref, st_ref, l_ref, o_ref, g_ref, w_ref, dq_ref, dkv_ref, dw_ref):
        i = pl.program_id(0)

        @pl.when(i == 0)
        def _():
            dkv_ref[...] = jnp.zeros_like(dkv_ref)
            dw_ref[...] = jnp.zeros_like(dw_ref)

        g = g_ref[...]
        mixed = o_ref[...]
        dm = mm(g, w_ref[...], NT).astype(bf16).astype(f32)
        dw_ref[...] += mm(mixed, g, TN)
        low = low_half()
        d0 = dm[:, :LANES]
        d1 = jnp.concatenate([dm[:, LANES:], jnp.zeros((BQ, LANES - HW), f32)], axis=1)
        m0 = mixed[:, :LANES].astype(f32)
        m1 = jnp.concatenate([mixed[:, LANES:].astype(f32), jnp.zeros((BQ, LANES - HW), f32)], axis=1)
        total = lambda a: jnp.sum(a, axis=1, keepdims=True)
        e0, e1 = d0 * m0, d1 * m1
        first = total(jnp.where(low, e0, 0.0))
        delta = jnp.stack([first, total(jnp.where(low, 0.0, e0)), total(e1)])
        high = lambda a: jnp.where(low, 0.0, a).astype(bf16)
        do = jnp.concatenate([high(swap(d0)), high(d0), high(swap(d1))], axis=0)
        qv = q_ref[...].reshape(M, LANES)
        lse = l_ref[...]
        st = st_ref[...]
        last = (meta[nq] + i * BQ + BQ - 1) // BK + 1

        def step(kb, dq):
            at = pl.ds(pl.multiple_of(kb * BK, BK), BK)
            keys = kv_ref[at, :]
            s = mm(qv, keys, NT).reshape(GROUP, BQ, BK)
            p = jnp.where(seen(meta, st, i, kb, nq), jnp.exp(s - lse), 0.0)
            dp = mm(do, keys, NT).reshape(GROUP, BQ, BK)
            ds = (p * (dp - delta)).astype(bf16).reshape(M, BK)
            pb = p.astype(bf16).reshape(M, BK)
            dkv_ref[at, :] += mm(ds, qv, TN) + mm(pb, do, TN)
            return dq + mm(ds, keys)

        dq = lax.fori_loop(meta[i], last, step, jnp.zeros((M, LANES), f32))
        dq_ref[...] = (dq * (1.0 / math.sqrt(HW))).astype(bf16).reshape(GROUP, BQ, LANES)

    sh = jax.ShapeDtypeStruct
    blk = lambda w: pl.BlockSpec((GROUP, BQ, w), lambda i, m: (0, i, 0))
    rows = lambda w: pl.BlockSpec((BQ, w), lambda i, m: (i, 0))
    full = lambda *shape: pl.BlockSpec(shape, lambda i, m: (0, 0))
    return pl.pallas_call(
        kernel,
        grid_spec=pltpu.PrefetchScalarGridSpec(
            num_scalar_prefetch=1,
            grid=(nq,),
            in_specs=[
                blk(LANES), full(*kv.shape), rows(1), blk(1), rows(QCOLS), rows(D), full(QCOLS, D),
            ],
            out_specs=(blk(LANES), full(K, LANES), full(QCOLS, D)),
        ),
        out_shape=(sh((GROUP, Rq, LANES), bf16), sh((K, LANES), f32), sh((QCOLS, D), f32)),
        compiler_params=pltpu.CompilerParams(vmem_limit_bytes=48 * MIB),
        cost_estimate=cost(27),
        name="attend_back",
    )(meta, q, kv, starts, lse, mixed, dattn, wo)


def weight_grads(dq, dkv, kin, ok, tables, h1, packed, tail):
    _, Rq, _ = dq.shape
    step = 256
    arrivals = kin.shape[0]

    def kernel(ok_ref, dq_ref, dkv_ref, kin_ref, c_ref, a_ref, b_ref, h_ref, w_ref, t_ref, o_ref, p_ref, acc):
        i = pl.program_id(0)

        @pl.when(i == 0)
        def _():
            acc[...] = jnp.zeros_like(acc)

        kv = dkv_ref[...]
        for k in range(arrivals):
            kv = kv + jnp.where(ok_ref[k] > 0, kin_ref[k].astype(f32), 0.0)
        kv = kv.astype(bf16).astype(f32)
        low = low_half()
        tables = (c_ref[...], a_ref[...], b_ref[...])
        q = [dq_ref[h].astype(f32) for h in range(GROUP)]
        kv = swap(kv)
        t0 = turn_back(jnp.where(low, q[0], swap(q[1])), *tables)
        t1 = turn_back(jnp.where(low, q[2], kv), *tables)
        out = jnp.concatenate([t0, t1, jnp.where(low, kv, 0.0)], axis=1).astype(bf16)
        o_ref[...] = out
        acc[...] += mm(h_ref[...], out, TN)

        @pl.when(i == Rq // step - 1)
        def _():
            w = w_ref[...].astype(f32)
            dw = acc[...]
            t = t_ref[...]
            lane = lax.broadcasted_iota(jnp.int32, (1, LANES), 1)
            gain = jnp.sum(jnp.where(lane == ok_ref[arrivals], w[:, 2 * LANES:], 0.0), axis=1, keepdims=True)
            d_gain = jnp.sum(w * dw, axis=1, keepdims=True) / gain
            t = t + jnp.where(lane == ok_ref[arrivals] + 1, d_gain, 0.0)
            p_ref[:, :2 * LANES] = dw[:, :2 * LANES].astype(bf16)
            p_ref[:, 2 * LANES:] = jnp.where(low, dw[:, 2 * LANES:], t).astype(bf16)

    sh = jax.ShapeDtypeStruct
    heads = lambda n: pl.BlockSpec((n, step, LANES), lambda i: (0, i, 0))
    return pl.pallas_call(
        kernel,
        grid=(Rq // step,),
        out_shape=(sh((Rq, AUX), bf16), sh((D, AUX), bf16)),
        in_specs=[pl.BlockSpec(memory_space=pltpu.SMEM), heads(GROUP), row_block(step, LANES), heads(arrivals)]
        + [row_block(step, LANES)] * 3
        + [row_block(step, D), whole_block(packed), whole_block(tail)],
        out_specs=(row_block(step, AUX), pl.BlockSpec((D, AUX), lambda i: (0, 0))),
        scratch_shapes=[pltpu.VMEM((D, AUX), f32)],
        compiler_params=pltpu.CompilerParams(vmem_limit_bytes=48 * MIB),
        cost_estimate=cost(7),
        name="weight_grads",
    )(ok, dq, dkv, kin, *tables, h1, packed, tail)


def experts(h2, g_own, g_oth, router, hot, inner, outer, nz):
    rows2 = h2.shape[0]
    step = 256
    steps = rows2 // step
    half = steps // 2
    dz = D // nz
    nw = len(outer)
    dw = D // nw
    C = D + LANES

    def kernel(h_ref, g0_ref, g1_ref, r_ref, e_ref, *rest):
        win, wout = rest[:nz], rest[nz:nz + nw]
        y_ref, d_ref = rest[nz + nw:nz + nw + 2]
        outs = rest[nz + nw + 2:]
        din, dout = outs[:nz], outs[nz:nz + nw]
        wi, wo, ai, ao, sem = outs[nz + nw:]
        i = pl.program_id(0)
        z = lax.axis_index("ulysses")

        @pl.when(i == 0)
        def _():
            cps = [
                pltpu.make_async_copy(win[d], wi.at[pl.ds(pl.multiple_of((z ^ d) * dz, dz), dz)], sem.at[d])
                for d in range(nz)
            ] + [
                pltpu.make_async_copy(wout[d], wo.at[z ^ d if nw > 1 else 0], sem.at[nz + d])
                for d in range(nw)
            ]
            for c in cps:
                c.start()
            ai[...] = jnp.zeros_like(ai)
            ao[...] = jnp.zeros_like(ao)
            for c in cps:
                c.wait()

        h = h_ref[...]
        gm = jnp.where(i < half, g0_ref[...], g1_ref[...])
        g = gm[:, :D]
        hot = e_ref[...]
        mask = gm[:, D:].astype(f32) > 0
        logits = mm(h, r_ref[...])
        top = jnp.max(jnp.where(mask, logits, NEG), axis=1, keepdims=True)
        w = jnp.where(mask, jnp.exp(jnp.where(mask, logits - top, 0.0)), 0.0)
        gate = jnp.sum(w * hot, axis=1, keepdims=True) / jnp.sum(w, axis=1, keepdims=True)

        gu = mm(h, wi[...])
        a, up = gu[:, :FF], gu[:, FF:]
        sg = jax.nn.sigmoid(a)
        silu = a * sg
        act = (silu * up).astype(bf16)
        raw = 0.0
        dy = (gate * g.astype(f32)).astype(bf16)
        for k in range(nw):
            cols = slice(k * dw, (k + 1) * dw)
            y_ref[:, cols] = (gate * mm(act, wo[k])).astype(bf16)
            raw = raw + mm(g[:, cols], wo[k], NT)
            ao[k] += mm(act, dy[:, cols], TN)
        dgate = jnp.sum(act.astype(f32) * raw, axis=1, keepdims=True)
        dact = gate * raw
        dgu = jnp.concatenate(
            [dact * up * (sg * (1.0 + a * (1.0 - sg))), dact * silu], axis=1).astype(bf16)
        ai[...] += mm(h, dgu, TN)
        d_ref[:, :D] = mm(dgu, wi[...], NT).astype(bf16)
        hi = dgate.astype(bf16).astype(f32)
        d_ref[:, D:] = (hi * hot + swap((dgate - hi) * hot)).astype(bf16)

        @pl.when(i == steps - 1)
        def _():
            for d in range(nz):
                din[d][...] = ai[pl.ds(pl.multiple_of((z ^ d) * dz, dz), dz), :].astype(bf16)
            for d in range(nw):
                dout[d][...] = ao[z ^ d if nw > 1 else 0].astype(bf16)

    sh = jax.ShapeDtypeStruct
    full = lambda *shape: pl.BlockSpec(shape, lambda i: (0, 0))
    return pl.pallas_call(
        kernel,
        grid=(steps,),
        out_shape=(sh((rows2, D), bf16), sh((rows2, C), bf16))
        + (sh((dz, 2 * FF), bf16),) * nz
        + (sh((FF, dw), bf16),) * nw,
        in_specs=[
            row_block(step, D),
            pl.BlockSpec((step, C), lambda i: (jnp.minimum(i, half - 1), 0)),
            pl.BlockSpec((step, C), lambda i: (jnp.maximum(i - half, 0), 0)),
            whole_block(router),
            whole_block(hot),
        ]
        + [ANY] * (nz + nw),
        out_specs=(row_block(step, D), row_block(step, C)) + (full(dz, 2 * FF),) * nz + (full(FF, dw),) * nw,
        scratch_shapes=[
            pltpu.VMEM((D, 2 * FF), bf16), pltpu.VMEM((nw, FF, dw), bf16),
            pltpu.VMEM((D, 2 * FF), f32), pltpu.VMEM((nw, FF, dw), f32), DMA((nz + nw,)),
        ],
        compiler_params=pltpu.CompilerParams(vmem_limit_bytes=58 * MIB),
        cost_estimate=cost(45),
        name="experts",
    )(h2, g_own, g_oth, router, hot, *inner, *outer)


def finish(dh1, x, gain, dresid, pin, win, resid, ysum):
    T = x.shape[0]
    groups, rp, S, _ = pin.shape
    senders = win.shape[0]

    def kernel(d_ref, x_ref, g_ref, r_ref, p_ref, w_ref, s_ref, y_ref, t_ref, q_ref, k_ref, v_ref, m_ref, o_ref, out_ref):
        v = x_ref[...].astype(f32)
        inv = lax.rsqrt(jnp.mean(v * v, axis=1, keepdims=True) + EPS)
        n = v * inv
        w = d_ref[...] * g_ref[...]
        t_ref[...] = r_ref[...] + inv * (w - n * jnp.mean(w * n, axis=1, keepdims=True))
        out_ref[...] = s_ref[...] + y_ref[...]
        o_ref[...] = functools.reduce(lambda a, b: a + b, [w_ref[k].astype(f32) for k in range(senders)])
        small = 0.0
        for h in range(groups):
            row = 0.0
            for p in range(rp):
                row = row + p_ref[h, p].astype(f32)
            q_ref[:, h * QCOLS:(h + 1) * QCOLS] = row[:, :QCOLS]
            k_ref[:, h * HW:(h + 1) * HW] = row[:, QCOLS:QCOLS + HW]
            v_ref[:, h * HW:(h + 1) * HW] = row[:, QCOLS + HW:ROUTER_AT]
            small = small + row[:, 2 * LANES:]
        m_ref[...] = small

    sh = lambda *shape: jax.ShapeDtypeStruct(shape, f32)
    return pl.pallas_call(
        kernel,
        out_shape=(sh(T, D), sh(S, HEADS * HW), sh(S, KV * HW), sh(S, KV * HW), sh(S, LANES), sh(S, D), sh(T, D)),
        in_specs=[VMEM] * 8,
        out_specs=(VMEM,) * 7,
        compiler_params=pltpu.CompilerParams(vmem_limit_bytes=32 * MIB),
        cost_estimate=cost(2),
        name="finish",
    )(dh1, x, gain, dresid, pin, win, resid, ysum)


def locate(rows, lengths):
    passed = rows[:, None] >= jnp.cumsum(lengths)
    return jnp.sum(jnp.where(passed, lengths, 0), axis=-1)


def norm_rows(v, gain):
    inverse = lax.rsqrt(jnp.mean(v * v, axis=-1, keepdims=True) + EPS)
    normed = v * inverse
    return normed, inverse, normed * gain


def norm_back(upstream, normed, inverse, gain):
    d_normed = upstream * gain
    d_gain = jnp.sum(upstream * normed, axis=0)
    d_values = inverse * (d_normed - normed * jnp.mean(d_normed * normed, axis=-1, keepdims=True))
    return d_values, d_gain


def rows_of(a, start, count):
    return a if a.shape[0] == count else lax.dynamic_slice_in_dim(a, start, count, 0)


def widen(a, start, count):
    if a.shape[0] == count:
        return a
    return lax.dynamic_update_slice_in_dim(jnp.zeros((count,) + a.shape[1:], a.dtype), a, start, 0)


def on_device(tokens, lengths, routes, gain_attn, w_query, w_key, w_value, w_output, gain_moe,
              w_router, w_inner, w_outer, cotangent):
    nz = lax.axis_size("ulysses")
    nb = lax.axis_size("blk")
    z = lax.axis_index("ulysses")
    b = lax.axis_index("blk")
    T = tokens.shape[0]
    R = nb * T
    rp = nb // KV
    Rq = R // rp
    part = b % rp
    at = part * Rq
    n = nz * nb
    S = D // n
    E = w_router.shape[1]
    longest = min(LENMAX, n * T // 2)
    back = min(nz - 1, (longest - 1 + R - 1) // R)
    n_o = QCOLS // S
    odd = z % 2

    tail = jnp.concatenate(
        [w_router, gain_attn[:, None], gain_moe[:, None],
         jnp.zeros((S, AUX - ROUTER_AT - E - 2), bf16)], axis=1)
    pieces = jnp.stack([
        jnp.concatenate([
            w_query[:, h * QCOLS:(h + 1) * QCOLS], w_key[:, h * HW:(h + 1) * HW],
            w_value[:, h * HW:(h + 1) * HW], tail], axis=1)
        for h in range(KV)])
    lanes = jnp.arange(LANES, dtype=jnp.int32)
    named = jnp.any(routes[:, :, None] + HW == lanes[None, None, :], axis=1)
    cot_mask = jnp.concatenate([cotangent, named.astype(bf16)], axis=1)
    take = lambda *items: Swaps([(w, d) for w, d in items if d < nz])
    inner, outer = {}, {}
    xg, g_own, g_far, packed, wo, inner[1], outer[1] = gather_inputs(
        tokens, cot_mask, pieces, w_output, nz, nb, 0, take((w_inner, 1), (w_outer, 1)))
    xg = xg.reshape(R, D)
    g_own = g_own.reshape(R, D + LANES)
    packed = packed.reshape(D, AUX)
    wo = wo.reshape(QCOLS, D)
    router = packed[:, 2 * LANES:]
    gains = packed[:, ROUTER_AT + E:ROUTER_AT + E + 2].astype(f32).T
    gain1, gain2 = gains[0:1], gains[1:2]

    rows = z * R + jnp.arange(R, dtype=jnp.int32)
    opening = locate(rows, lengths)
    pair = lanes % HW
    frequency = THETA ** (-((pair % (HW // 2)).astype(f32) * 2.0 / HW))
    angles = (rows - opening).astype(f32)[:, None] * frequency[None, :]
    cos, sin = jnp.cos(angles), jnp.sin(angles)
    tables = (cos, jnp.where(pair < HW // 2, -sin, 0.0), jnp.where(pair < HW // 2, 0.0, sin))

    q, kv, h1 = project(xg, gain1, packed, *tables)
    if rp > 1:
        q = lax.dynamic_slice_in_dim(q, at, Rq, 1)
    far, g_oth, *got = halo_forward(kv, g_far, nz, nb, back, 1, take((w_outer, 3)))
    outer.update(zip([3], got))
    g_oth = g_oth.reshape(R, D + LANES)
    flip = lambda d: [(k, k ^ d) for k in range(nz)]
    pick = lambda w, d: lax.dynamic_index_in_dim(w, odd ^ (d % 2), 0, keepdims=False)
    late, g_oth = lax.optimization_barrier((w_inner, g_oth))
    later, g_oth = lax.optimization_barrier((w_outer, g_oth))
    for d in range(2, nz):
        if d != 3:
            inner[d] = lax.ppermute(pick(late, d), "ulysses", flip(d))
        if d > 3:
            outer[d] = lax.ppermute(pick(later, d), "ulysses", flip(d))

    kv_all = jnp.concatenate([far[d - 1] for d in range(back, 0, -1)] + [kv], axis=0)
    base = (z - back) * R
    starts = rows_of(opening, at, Rq) - base
    meta = jnp.concatenate([starts[::BQ] // BK, (back * R + at)[None]]).astype(jnp.int32)
    starts = starts[:, None]
    mixed, lse = attend(q, kv_all, starts, meta)
    attn, *got = reduce_product(widen(mixed, at, R), wo, nb, 2, take((w_outer, 2)))
    outer.update(zip([2], got))

    resid = tokens.astype(f32) + attn
    n2, inv2, scaled2 = norm_rows(resid, gain2)
    h2_own = scaled2.astype(bf16)
    h2_own, inner[2] = lax.optimization_barrier((h2_own, inner[2]))
    h2, *got = gather_pair(h2_own, nb, 3, take((w_inner, 3)))
    inner.update(zip([3], got))
    h2 = h2.reshape(2 * R, D)
    inner[0], outer[0] = pick(w_inner, 0), pick(w_outer, 0)
    inner, outer = ([w[d] for d in range(nz)] for w in (inner, outer))
    aligned = (D // nz) % LANES == 0
    if not aligned:
        outer = lax.optimization_barrier(outer)
        by_owner = jnp.take(jnp.stack(outer), z ^ jnp.arange(nz), axis=0)
        outer = [jnp.transpose(by_owner, (1, 0, 2)).reshape(FF, D)]
    hot = (lanes == HW + b * EXP_DEV + odd).astype(f32)[None, :]
    y, back_rows, *grads = experts(h2, g_own, g_oth, router, hot, inner, outer, nz)
    d_inner, d_outer = grads[:nz], grads[nz:]
    if not aligned:
        by_owner = jnp.transpose(d_outer[0].reshape(FF, nz, D // nz), (1, 0, 2))
        by_owner = jnp.take(by_owner, z ^ jnp.arange(nz), axis=0)
        d_outer = [by_owner[d] for d in range(nz)]
    summed, d_inner[1], d_inner[2], d_outer[1], d_outer[2] = reduce_pair(
        back_rows.reshape(2, nb, T, D + LANES), nb, 4,
        take((d_inner[1], 1), (d_inner[2], 2), (d_outer[1], 1), (d_outer[2], 2)))

    upstream = cotangent.astype(f32)
    dgates = summed[:, D:] + jnp.roll(summed[:, D:], HW, 1)
    logits = mm(h2_own, router)
    top = jnp.max(jnp.where(named, logits, NEG), axis=1, keepdims=True)
    w = jnp.where(named, jnp.exp(jnp.where(named, logits - top, 0.0)), 0.0)
    gates = w / jnp.sum(w, axis=1, keepdims=True)
    dlogits = gates * (dgates - jnp.sum(gates * dgates, axis=1, keepdims=True))
    dlogits = dlogits.astype(bf16)
    dh2 = summed[:, :D] + mm(dlogits, router, NT)
    d_norm2, d_gain2 = norm_back(dh2, n2, inv2, gain2)
    dresid = upstream + d_norm2
    dattn, d_outer[3] = gather_layer(dresid.astype(bf16), nb, 5, take((d_outer[3], 3)))
    dattn, *rest = lax.optimization_barrier((dattn, *d_inner[3:], *d_outer[4:]))
    rest = [lax.ppermute(r, "ulysses", flip(d)) for r, d in zip(rest, [*range(3, nz), *range(4, nz)])]
    d_inner[3:], d_outer[4:] = rest[:nz - 3], rest[nz - 3:]
    dattn = dattn.reshape(R, D)
    tail = mm(h2_own, dlogits, TN) + jnp.where(lanes == HW + E, d_gain2[:, None], 0.0)

    dq, dkv, dwo = attend_back(q, kv_all, starts, meta, lse, mixed, rows_of(dattn, at, Rq), wo)
    dkv, d_inner, d_outer = lax.optimization_barrier((dkv, d_inner, d_outer))
    dkv = dkv.reshape(back + 1, R, LANES)
    dkv_out = jnp.stack([dkv[back - d] for d in range(back + 1)]).astype(bf16)
    y = y.reshape(2, nb, T, D)
    kin, ysum, win = halo_back(dkv_out, y, dwo.astype(bf16).reshape(n_o, S, D), nz, nb, rp, back, 6)
    ok = [(z + d < nz) if d else (part != p) for d in range(back + 1) for p in range(rp)]
    ok = jnp.stack([jnp.asarray(o).astype(jnp.int32) for o in ok] + [jnp.int32(HW + E)])
    if rp > 1:
        kin = lax.dynamic_slice_in_dim(kin, at, Rq, 1)
    turned, dw = weight_grads(
        dq, rows_of(dkv[back], at, Rq), kin, ok, [rows_of(t, at, Rq) for t in tables],
        rows_of(h1, at, Rq), packed, tail)
    dh1, pin = reduce_last(widen(turned, at, R), packed, dw.reshape(nz, nb, S, AUX), nz, nb, 7)
    d_tokens, d_query, d_key, d_value, small, d_output, out = finish(
        dh1, tokens, gain1, dresid, pin.reshape(KV, rp, S, AUX), win, resid, ysum)

    def settle(parts):
        same = sum(p.astype(f32) for p in parts[0::2])
        other = sum(p.astype(f32) for p in parts[1::2])
        return jnp.where(odd == 0, jnp.stack([same, other]), jnp.stack([other, same]))

    return (
        out, d_tokens, small[:, HW + E + 1], d_query, d_key, d_value, d_output,
        small[:, HW + E], small[:, HW:HW + E], settle(d_inner), settle(d_outer),
    )


def solution(mesh):
    both = ("ulysses", "blk")
    rows = P(both, None)
    weights = (P(both), rows, rows, rows, rows, P(both), rows, P("blk", "ulysses", None), P("blk", None, "ulysses"))
    return jax.shard_map(
        on_device,
        mesh=mesh,
        in_specs=(rows, P(), rows) + weights + (rows,),
        out_specs=(rows, rows) + weights,
        check_vma=False,
    )
```

time: 642 us -> 549 us (0.86)
  matrix products: 89.3 us -> 1.16 us
  Pallas kernels: 395 us -> 478 us
  local copies, waits for them, and re-layouts: 87.9 us -> 33.1 us
  other arithmetic: 44.3 us -> 16.8 us
  between operations: 16 us -> 1.45 us
  starting transfers between devices: 0.96 us -> 13.5 us
    pallas_call x6 -> x9, Pallas kernels: 193 us -> 283 us  [the longest x1 66.9 us: reduce_pair(): pl.pallas_call(kernel, out_shape=(jax.ShapeDtypeStruct((rows, cols), f32)...]
    dot_general x19 -> x3, matrix products: 89.3 us -> 1.16 us  [mm(): return lax.dot_general(a, b, dims, preferred_element_type=f32)]
    pallas_call x1, Pallas kernels: 109 us -> 88.4 us  [halo_back(): pl.pallas_call(kernel, out_shape=(sh(((back + 1) * rp, R, LANES), bf16),...]
    slice x16 -> x6, local copies, waits for them, and re-layouts: 22.5 us -> 2.67 us  [the longest x1 1.06 us: on_device(): dgates = summed[:, D:] + jnp.roll(summed[:, D:], HW, 1)]
    ppermute x0 -> x2, starting transfers between devices: none -> 13.5 us  [the longest x1 11.9 us: on_device(): inner[d] = lax.ppermute(pick(late, d), 'ulysses', flip(d))]
    concatenate x7 -> x0, local copies, waits for them, and re-layouts: 12.9 us -> none  [the longest x2 6.53 us: on_device(): jnp.concatenate([dw[:, h * LANES:h * LANES + HW] for h in range(GROUP)] +...]
    unnamed x212 -> x128, local copies, waits for them, and re-layouts: 32.3 us -> 19.7 us
    pallas_call x1, Pallas kernels: 68.8 us -> 78 us  [gather_inputs(): pl.pallas_call(kernel, out_shape=(sh((nb,) + x.shape, x.dtype), sh((nb,)...]
  transfers between devices with their start and end apart: 8 -> 2, of which waited for: 0 -> 1; matrix products, arithmetic and copies ran while one was open for 30% -> 2% of each run, Pallas kernels for 62% -> 11%
where the time goes in v2:
time: 549 us; the launch traced here: 544 us
  Pallas kernels  478 us (87%)
  local copies, waits for them, and re-layouts  33.1 us (6%)
  other arithmetic  16.8 us (3%)
  starting transfers between devices  13.5 us (2%)
    pallas_call x1, Pallas kernels, halo_back(): pl.pallas_call(kernel, out_shape=(sh(((back + 1) * rp, R, LANES), bf16),...  88.4 us
    pallas_call x1, Pallas kernels, gather_inputs(): pl.pallas_call(kernel, out_shape=(sh((nb,) + x.shape, x.dtype), sh((nb,)...  78 us
    pallas_call x1, Pallas kernels, reduce_pair(): pl.pallas_call(kernel, out_shape=(jax.ShapeDtypeStruct((rows, cols), f32)...  66.9 us
    pallas_call x1, Pallas kernels, experts(): pl.pallas_call(kernel, grid=(steps,), out_shape=(sh((rows2, D), bf16), sh...  45.5 us
    pallas_call x1, Pallas kernels, gather_pair(): pl.pallas_call(kernel, out_shape=(jax.ShapeDtypeStruct((2, nb) + x.shape,...  41.3 us
    pallas_call x1, Pallas kernels, reduce_product(): pl.pallas_call(kernel, out_shape=(jax.ShapeDtypeStruct((rows, cols), f32)...  36.6 us
    pallas_call x1, Pallas kernels, reduce_last(): pl.pallas_call(kernel, out_shape=(sh((rows, cols), f32), sh((nb, shard, w...  32.4 us
    pallas_call x1, Pallas kernels, halo_forward(): pl.pallas_call(kernel, out_shape=(sh((back,) + kv.shape, kv.dtype), sh((n...  28 us
  transfers between devices with their start and end apart: 2, of which 1 were waited for; matrix products, arithmetic and copies ran while one was open for 2% of the time, Pallas kernels for 11%

profile of v2, /device:TPU:1, one launch (start us, length us, event | category | flops | bytes accessed | tf_op | source)
XLA Modules:
  0.0 544.2 jit_solution(1009598055141334456)
XLA Ops:
  0.7 0.9 reduce-window.8
  2.7 1.1 fusion.16
  3.8 0.8 copy.89
  4.5 0.8 copy.90
  6.1 1.0 fusion.17
  7.2 0.8 pad_maximum_fusion.2.g_ref
  9.6 78.0 %gather_inputs.1 = (bf16[8,128,1536]{2,1,0:T(8,128)(2,1)}, bf16[8,128,1664]{2,1,0:T(8,128)(2,1)}, bf16[128,1664]{1,0:T(8,128)(2,1)}, bf16[4,8,48,384]{3,2,1,0:T(...) custom-call(bf16[128,1536]{1,0:T(8,128)(2,1)} %x_ref.3, ...), custom_call_target="tpu_custom_call" | custom-call | flops 49999998976 | tf_op jit(solution)/shard_map/gather_inputs/pallas_call | solution.py:309
  87.7 1.3 slice_convert_fusion
  89.3 1.9 fusion
  91.3 2.4 copy-done.19
  93.8 4.1 project.1
  98.6 1.7 copy-done.28
  100.3 28.0 %halo_forward.1 = (bf16[2,1024,128]{2,1,0:T(8,128)(2,1)}, bf16[8,128,1664]{2,1,0:T(8,128)(2,1)}, bf16[512,384]{1,0:T(8,128)(2,1)}) custom-call(bf16[1024,128]{1,0:T(8,128)(2,1)} %copy-done.14, bf16[128,1664]{1,0:T(8,128)(2,1)} %get-tuple-element.84.g_ref, bf16[2,512,384]{2,1,0:T(8,128)(2,1)} %rest_0_.6), custom_call_target="tpu_custom_call" | custom-call | flops 20000000000 | tf_op jit(solution)/shard_map/halo_forward/pallas_call | solution.py:368
  128.3 2.1 dynamic-slice_bitcast_fusion.1
  130.3 11.9 %collective-permute-start = (bf16[384,1024]{1,0:T(8,128)(2,1)}, bf16[384,1024]{1,0:T(8,128)(2,1)}, u32[]{:S(2)}, u32[]{:S(2)}) collective-permute-start(bf16[384,1024]{1,0:T(8,128)(2,1)} %dynamic-slice_bitcast_fusion.1), channel_id=1, source_target_pairs={{0,16},{8,24},{16,0},{24,8},{1,17},{9,25},{17,1},{25,9},{2,18},{10... | collective-permute-start | bytes 2359304 | tf_op jit(solution)/shard_map/ppermute | solution.py:1164
  142.3 0.8 slice.187.r_ref
  143.1 2.1 dynamic-slice_bitcast_fusion.rest_0_
  145.2 0.8 dynamic-slice_bitcast_fusion.2.rest_4_
  147.8 8.6 %attend.1 = (bf16[1024,192]{1,0:T(8,128)(2,1)S(1)}, f32[3,1024,1]{2,1,0:T(8,128)S(1)}) custom-call(s32[5]{0:T(128)S(1)} %pad_add_fusion.1.meta, bf16[3,1024,128]{2,1,0:T(8,128)(2,1)S(1)} %get-tuple-element.82.q_ref, bf16[3072,128]{1,0:T(8,128)(2,1)S(1)} %pad_maximum_fusion.kv_ref, s32[1024,1]{1,0:T(8,128)S(1)} %copy.117.st_ref), custom_call_target="tpu_custom_call" | custom-call | flops 16999999488 | tf_op jit(solution)/shard_map/attend/pallas_call | solution.py:794
  156.5 1.1 copy-done.33
  157.6 36.6 %reduce_product2.1 = (f32[128,1536]{1,0:T(8,128)S(1)}, bf16[512,384]{1,0:T(8,128)(2,1)S(1)}) custom-call(bf16[1024,192]{1,0:T(8,128)(2,1)S(1)} %get-tuple-element.87.l_ref.o_ref, bf16[192,1536]{1,0:T(8,128)(2,1)S(1)} %bitcast.72, bf16[2,512,384]{2,1,0:T(8,128)(2,1)S(1)} %copy-done.16), custom_call_target="tpu_custom_call" | custom-call | flops 23000000512 | tf_op jit(solution)/shard_map/reduce_product2/pallas_call | solution.py:474
  195.7 0.9 multiply_convert_fusion.x_ref
  196.6 41.3 %gather_pair3.1 = (bf16[2,8,128,1536]{3,2,1,0:T(8,128)(2,1)}, bf16[384,1024]{1,0:T(8,128)(2,1)}) custom-call(bf16[128,1536]{1,0:T(8,128)(2,1)} %multiply_convert_fusion.x_ref, bf16[2,384,1024]{2,1,0:T(8,128)(2,1)} %rest_0_.7), custom_call_target="tpu_custom_call" | custom-call | flops 38000001024 | tf_op jit(solution)/shard_map/gather_pair3/pallas_call | solution.py:206
  237.9 45.5 %experts.1 = (bf16[2048,1536]{1,0:T(8,128)(2,1)}, bf16[2048,1664]{1,0:T(8,128)(2,1)}, bf16[384,1024]{1,0:T(8,128)(2,1)}, bf16[384,1024]{1,0:T(8,128)(2,1)}, bf16...) custom-call(bf16[2048,1536]{1,0:T(8,128)(2,1)} %bitcast.84, ...), custom_call_target="tpu_custom_call" | custom-call | flops 44999999488 | tf_op jit(solution)/shard_map/experts/pallas_call | solution.py:1012
  283.5 66.9 %reduce_pair4.1 = (f32[128,1664]{1,0:T(8,128)}, bf16[384,1024]{1,0:T(8,128)(2,1)}, bf16[384,1024]{1,0:T(8,128)(2,1)}, bf16[512,384]{1,0:T(8,128)(2,1)}, bf16[512,384]{1,0:T(8,128)(2,1)}) custom-call(bf16[2,8,128,1664]{3,2,1,0:T(8,128)(2,1)} %bitcast.82, bf16[384,1024]{1,0:T(8,128)(2,1)} %get-tuple-element.104.rest_0_, ...), custom_call_target="tpu_custom_call" | custom-call | flops 48000000000 | tf_op jit(solution)/shard_map/reduce_pair4/pallas_call | solution.py:502
  350.4 1.1 fusion.15
  352.1 1.0 multiply_reduce_fusion.3
  354.2 1.1 fusion.14
  355.2 23.6 %gather_layer5.1 = (bf16[8,128,1536]{2,1,0:T(8,128)(2,1)}, bf16[512,384]{1,0:T(8,128)(2,1)}) custom-call(bf16[128,1536]{1,0:T(8,128)(2,1)} %get-tuple-element.186.x_ref, bf16[512,384]{1,0:T(8,128)(2,1)} %get-tuple-element.109.rest_0_), custom_call_target="tpu_custom_call" | custom-call | flops 22000001024 | tf_op jit(solution)/shard_map/gather_layer5/pallas_call | solution.py:168
  378.9 1.6 collective-permute-start.1
  380.5 1.1 copy-done.30
  381.6 1.0 copy-done.35
  382.6 15.6 %attend_back.1 = (bf16[3,1024,128]{2,1,0:T(8,128)(2,1)S(1)}, f32[3072,128]{1,0:T(8,128)}, f32[192,1536]{1,0:T(8,128)S(1)}) custom-call(s32[5]{0:T(128)S(1)} %copy-done.24, bf16[3,1024,128]{2,1,0:T(8,128)(2,1)S(1)} %copy-done.30, bf16[3072,128]{1,0:T(8,128)(2,1)S(1)} %copy-done.3, s32[1024,1]{1,0:T(8,128)S(1)} %copy-done.5, f32[3,1024,1]{2,1,0:T(8,128)} %copy-done.33, ...), custom_call_target="tpu_custom_call" | custom-call | flops 27000000512 | tf_op jit(solution)/shard_map/attend_back/pallas_call | solution.py:865
  398.2 0.9 convert_element_type.83
  400.1 0.8 copy-done.46
  401.0 1.0 pad_maximum_fusion.1.d_ref
  401.9 88.4 %halo_back.1 = (bf16[3,1024,128]{2,1,0:T(8,128)(2,1)}, f32[128,1536]{1,0:T(8,128)}, bf16[4,48,1536]{2,1,0:T(8,128)(2,1)}) custom-call(bf16[3,1024,128]{2,1,0:T(8,128)(2,1)} %pad_maximum_fusion.1.d_ref, bf16[2,8,128,1536]{3,2,1,0:T(8,128)(2,1)} %bitcast.83, bf16[4,48,1536]{2,1,0:T(8,128)(2,1)} %bitcast.75), custom_call_target="tpu_custom_call" | custom-call | flops 44999999488 | tf_op jit(solution)/shard_map/halo_back/pallas_call | solution.py:586
  490.4 1.1 copy-done.31
  491.5 6.9 %weight_grads.1 = (bf16[1024,384]{1,0:T(8,128)(2,1)S(1)}, bf16[1536,384]{1,0:T(8,128)(2,1)}) custom-call(s32[4]{0:T(128)S(1)} %get-tuple-element.231.ok_ref, bf16[3,1024,128]{2,1,0:T(8,128)(2,1)S(1)} %get-tuple-element.113.dq_ref, f32[1024,128]{1,0:T(8,128)S(1)} %slice.175.dkv_ref, bf16[3,1024,128]{2,1,0:T(8,128)(2,1)S(1)} %copy-done.31, ...), custom_call_target="tpu_custom_call" | custom-call | flops 7000000000 | tf_op jit(solution)/shard_map/weight_grads/pallas_call | solution.py:922
  498.4 0.9 copy-done.32
  499.3 32.4 %reduce_last.1 = (f32[128,1536]{1,0:T(8,128)}, bf16[8,48,384]{2,1,0:T(8,128)(2,1)}) custom-call(bf16[1024,384]{1,0:T(8,128)(2,1)} %copy-done.32, bf16[1536,384]{1,0:T(8,128)(2,1)} %bitcast.66, bf16[4,8,48,384]{3,2,1,0:T(8,128)(2,1)} %bitcast.88), custom_call_target="tpu_custom_call" | custom-call | flops 36999999488 | tf_op jit(solution)/shard_map/reduce_last/pallas_call | solution.py:661
  531.8 1.0 copy-done.22
  532.7 1.1 copy-done.26
  533.9 1.7 finish.1
  537.3 0.8 copy-done.43
  539.6 0.9 copy-done.51
  540.7 2.2 maximum_select_fusion
  542.9 1.2 maximum_select_fusion.1
  (166 shorter events, 14.0 us)
Async XLA Ops:
  0.6 6.5 %copy-start.40 = (bf16[128,1536]{1,0:T(8,128)(2,1)S(1)}, bf16[128,1536]{1,0:T(8,128)(2,1)}, u32[]{:S(2)}) copy-start(bf16[128,1536]{1,0:T(8,128)(2,1)} %param.25) | copy-start | bytes 1179652
  2.6 143.4 %copy-start.48 = (pred[128,128]{1,0:T(8,128)(4,1)}, pred[128,128]{1,0:T(8,128)(4,1)S(1)}, u32[]{:S(2)}) copy-start(pred[128,128]{1,0:T(8,128)(4,1)S(1)} %fusion.3) | copy-start | bytes 49156
  87.6 1.6 copy-start.58
  87.6 3.7 copy-start
  89.2 8.6 %copy-start.17 = (f32[1,1536]{1,0:T(1,128)}, f32[1,1536]{1,0:T(1,128)S(1)}, u32[]{:S(2)}) copy-start(f32[1,1536]{1,0:T(1,128)S(1)} %get-tuple-element.221.g_ref) | copy-start | bytes 18436
  91.3 6.6 %copy-start.6 = (f32[1024,128]{1,0:T(8,128)}, f32[1024,128]{1,0:T(8,128)S(1)}, u32[]{:S(2)}) copy-start(f32[1024,128]{1,0:T(8,128)S(1)} %get-tuple-element.222.b_ref) | copy-start | bytes 1572868
  91.3 6.6 %copy-start.8 = (f32[1024,128]{1,0:T(8,128)}, f32[1024,128]{1,0:T(8,128)S(1)}, u32[]{:S(2)}) copy-start(f32[1024,128]{1,0:T(8,128)S(1)} %get-tuple-element.223.a_ref) | copy-start | bytes 1572868
  91.3 6.6 %copy-start.10 = (f32[1024,128]{1,0:T(8,128)}, f32[1024,128]{1,0:T(8,128)S(1)}, u32[]{:S(2)}) copy-start(f32[1024,128]{1,0:T(8,128)S(1)} %get-tuple-element.224.c_ref) | copy-start | bytes 1572868
  91.3 2.4 copy-start.19
  98.6 1.7 copy-start.28
  100.3 47.5 %copy-start.29 = (bf16[3,1024,128]{2,1,0:T(8,128)(2,1)}, bf16[3,1024,128]{2,1,0:T(8,128)(2,1)S(1)}, u32[]{:S(2)}) copy-start(bf16[3,1024,128]{2,1,0:T(8,128)(2,1)S(1)} %get-tuple-element.82.q_ref) | copy-start | bytes 2359300
  130.3 14.8 %copy-start.16 = (bf16[2,512,384]{2,1,0:T(8,128)(2,1)S(1)}, bf16[2,512,384]{2,1,0:T(8,128)(2,1)}, u32[]{:S(2)}) copy-start(bf16[2,512,384]{2,1,0:T(8,128)(2,1)} %rest_0_.6) | copy-start | bytes 2359300
  130.3 66.2 %collective-permute-start = (bf16[384,1024]{1,0:T(8,128)(2,1)}, bf16[384,1024]{1,0:T(8,128)(2,1)}, u32[]{:S(2)}, u32[]{:S(2)}) collective-permute-start(bf16[384,1024]{1,0:T(8,128)(2,1)} %dynamic-slice_bitcast_fusion.1), channel_id=1, source_target_pairs={{0,16},{8,24},{16,0},{24,8},{1,17},{9,25},{17,1},{25,9},{2,18},{10... | collective-permute-start | bytes 2359304 | tf_op jit(solution)/shard_map/ppermute | solution.py:1164
  142.3 5.0 copy-start.50
  145.2 2.6 copy-start.15
  147.6 8.9 %copy-start.4 = (s32[1024,1]{1,0:T(8,128)}, s32[1024,1]{1,0:T(8,128)S(1)}, u32[]{:S(2)}) copy-start(s32[1024,1]{1,0:T(8,128)S(1)} %copy.117.st_ref) | copy-start | bytes 12292
  147.7 8.7 %copy-start.23 = (s32[5]{0:T(128)}, s32[5]{0:T(128)S(1)}, u32[]{:S(2)}) copy-start(s32[5]{0:T(128)S(1)} %pad_add_fusion.1.meta) | copy-start | bytes 64
  147.8 8.6 %copy-start.2 = (bf16[3072,128]{1,0:T(8,128)(2,1)}, bf16[3072,128]{1,0:T(8,128)(2,1)S(1)}, u32[]{:S(2)}) copy-start(bf16[3072,128]{1,0:T(8,128)(2,1)S(1)} %pad_maximum_fusion.kv_ref) | copy-start | bytes 2359300
  147.8 9.8 %copy-start.20 = (bf16[4,48,1536]{2,1,0:T(8,128)(2,1)S(1)}, bf16[4,48,1536]{2,1,0:T(8,128)(2,1)}, u32[]{:S(2)}) copy-start(bf16[4,48,1536]{2,1,0:T(8,128)(2,1)} %get-tuple-element.88) | copy-start | bytes 1769476
  156.5 1.1 copy-start.33
  157.6 36.6 %copy-start.34 = (bf16[1024,192]{1,0:T(8,128)(2,1)}, bf16[1024,192]{1,0:T(8,128)(2,1)S(1)}, u32[]{:S(2)}) copy-start(bf16[1024,192]{1,0:T(8,128)(2,1)S(1)} %get-tuple-element.87.l_ref.o_ref) | copy-start | bytes 1179652
  157.6 37.4 %copy-start.12 = (bf16[128,1536]{1,0:T(8,128)(2,1)S(1)}, bf16[128,1536]{1,0:T(8,128)(2,1)}, u32[]{:S(2)}) copy-start(bf16[128,1536]{1,0:T(8,128)(2,1)} %x_ref.3) | copy-start | bytes 1179652
  283.4 68.1 %copy-start.1 = (bf16[4,8,48,384]{3,2,1,0:T(8,128)(2,1)S(1)}, bf16[4,8,48,384]{3,2,1,0:T(8,128)(2,1)}, u32[]{:S(2)}) copy-start(bf16[4,8,48,384]{3,2,1,0:T(8,128)(2,1)} %get-tuple-element.81) | copy-start | bytes 3538948
  283.4 68.1 %copy-start.38 = (bf16[128,1536]{1,0:T(8,128)(2,1)S(1)}, bf16[128,1536]{1,0:T(8,128)(2,1)}, u32[]{:S(2)}) copy-start(bf16[128,1536]{1,0:T(8,128)(2,1)} %multiply_convert_fusion.x_ref) | copy-start | bytes 1179652
  283.4 68.1 %copy-start.55 = (pred[128,128]{0,1:T(32,128)(4,1)S(1)}, pred[128,128]{0,1:T(32,128)(4,1)}, u32[]{:S(2)}) copy-start(pred[128,128]{0,1:T(32,128)(4,1)} %copy.115) | copy-start | bytes 49156
  283.4 68.5 %copy-start.49 = (pred[128,128]{1,0:T(8,128)(4,1)S(1)}, pred[128,128]{1,0:T(8,128)(4,1)}, u32[]{:S(2)}) copy-start(pred[128,128]{1,0:T(8,128)(4,1)} %copy-done.48) | copy-start | bytes 49156
  350.4 2.8 copy-start.42
  355.2 25.2 %copy-start.3 = (bf16[3072,128]{1,0:T(8,128)(2,1)S(1)}, bf16[3072,128]{1,0:T(8,128)(2,1)}, u32[]{:S(2)}) copy-start(bf16[3072,128]{1,0:T(8,128)(2,1)} %copy-done.2) | copy-start | bytes 2359300
  355.2 25.2 %copy-start.5 = (s32[1024,1]{1,0:T(8,128)S(1)}, s32[1024,1]{1,0:T(8,128)}, u32[]{:S(2)}) copy-start(s32[1024,1]{1,0:T(8,128)} %copy-done.4) | copy-start | bytes 12292
  355.2 25.2 %copy-start.21 = (bf16[4,48,1536]{2,1,0:T(8,128)(2,1)S(1)}, bf16[4,48,1536]{2,1,0:T(8,128)(2,1)}, u32[]{:S(2)}) copy-start(bf16[4,48,1536]{2,1,0:T(8,128)(2,1)} %get-tuple-element.88) | copy-start | bytes 1769476
  355.2 25.2 %copy-start.24 = (s32[5]{0:T(128)S(1)}, s32[5]{0:T(128)}, u32[]{:S(2)}) copy-start(s32[5]{0:T(128)} %copy-done.23) | copy-start | bytes 64
  378.9 21.1 %collective-permute-start.1 = (bf16[384,1024]{1,0:T(8,128)(2,1)}, bf16[384,1024]{1,0:T(8,128)(2,1)S(1)}, u32[]{:S(2)}, u32[]{:S(2)}) collective-permute-start(bf16[384,1024]{1,0:T(8,128)(2,1)} %get-tuple-element.118), channel_id=1, source_target_pairs={{0,24},{8,16},{16,8},{24,0},{1,25},{9,17},{17,9},{25,1},{2,26},{10... | collective-permute-start | bytes 2359304 | tf_op jit(solution)/shard_map/ppermute | solution.py:1215
  380.4 1.1 copy-start.30
  382.6 16.4 %copy-start.39 = (bf16[128,1536]{1,0:T(8,128)(2,1)S(1)}, bf16[128,1536]{1,0:T(8,128)(2,1)}, u32[]{:S(2)}) copy-start(bf16[128,1536]{1,0:T(8,128)(2,1)} %multiply_convert_fusion.x_ref) | copy-start | bytes 1179652
  398.2 1.8 copy-start.37
  401.9 88.4 %copy-start.7 = (f32[1024,128]{1,0:T(8,128)S(1)}, f32[1024,128]{1,0:T(8,128)}, u32[]{:S(2)}) copy-start(f32[1024,128]{1,0:T(8,128)} %copy-done.6) | copy-start | bytes 1572868
  401.9 88.4 %copy-start.9 = (f32[1024,128]{1,0:T(8,128)S(1)}, f32[1024,128]{1,0:T(8,128)}, u32[]{:S(2)}) copy-start(f32[1024,128]{1,0:T(8,128)} %copy-done.8) | copy-start | bytes 1572868
  401.9 88.5 %copy-start.11 = (f32[1024,128]{1,0:T(8,128)S(1)}, f32[1024,128]{1,0:T(8,128)}, u32[]{:S(2)}) copy-start(f32[1024,128]{1,0:T(8,128)} %copy-done.10) | copy-start | bytes 1572868
  490.4 1.1 copy-start.31
  499.3 32.4 %copy-start.13 = (bf16[128,1536]{1,0:T(8,128)(2,1)S(1)}, bf16[128,1536]{1,0:T(8,128)(2,1)}, u32[]{:S(2)}) copy-start(bf16[128,1536]{1,0:T(8,128)(2,1)} %x_ref.3) | copy-start | bytes 1179652
  499.3 32.4 %copy-start.18 = (f32[1,1536]{1,0:T(1,128)S(1)}, f32[1,1536]{1,0:T(1,128)}, u32[]{:S(2)}) copy-start(f32[1,1536]{1,0:T(1,128)} %copy-done.17) | copy-start | bytes 18436
  499.3 32.5 %copy-start.25 = (f32[128,1536]{1,0:T(8,128)S(1)}, f32[128,1536]{1,0:T(8,128)}, u32[]{:S(2)}) copy-start(f32[128,1536]{1,0:T(8,128)} %get-tuple-element.133.y_ref) | copy-start | bytes 2359300
  499.3 32.5 %copy-start.27 = (bf16[4,48,1536]{2,1,0:T(8,128)(2,1)S(1)}, bf16[4,48,1536]{2,1,0:T(8,128)(2,1)}, u32[]{:S(2)}) copy-start(bf16[4,48,1536]{2,1,0:T(8,128)(2,1)} %get-tuple-element.132.w_ref) | copy-start | bytes 1769476
  532.7 1.1 copy-start.26
  533.9 3.1 copy-start.45
  533.9 3.1 copy-start.47
  537.0 1.1 copy-start.43
  537.0 1.4 copy-start.44
  (13 other events, 12.0 us)

commit v3 on v2

v3 whole, which is shorter than its diff:
```python
import functools
import math

import jax
import jax.numpy as jnp
from jax import lax
from jax.experimental import pallas as pl
from jax.experimental.pallas import tpu as pltpu
from jax.sharding import PartitionSpec as P

D = 1536
HEADS = 24
KV = 8
HW = 64
GROUP = HEADS // KV
FF = 512
TOPK = 8
EXP_DEV = 2
LENMAX = 4096
EPS = 1e-05
THETA = 10000.0
NEG = -1e30
LANES = 128
AUX = 384
ROUTER_AT = 320
QCOLS = GROUP * HW

f32 = jnp.float32
bf16 = jnp.bfloat16
MESH = pl.DeviceIdType.MESH
ANY = pl.BlockSpec(memory_space=pl.ANY)
VMEM = pl.BlockSpec(memory_space=pltpu.VMEM)
DMA = pltpu.SemaphoreType.DMA
MIB = 1 << 20


def dev(u, b):
    return {"ulysses": u, "blk": b}


def remote(src, dst, ss, rs, u, b):
    return pltpu.make_async_remote_copy(
        src_ref=src, dst_ref=dst, send_sem=ss, recv_sem=rs,
        device_id=dev(u, b), device_id_type=MESH,
    )


def cost(us):
    return pl.CostEstimate(flops=us * 1_000_000_000, bytes_accessed=0, transcendentals=0)


def signal(sem, u, b):
    pl.semaphore_signal(sem, inc=1, device_id=dev(u, b), device_id_type=MESH)


class Layer:
    def __init__(self, nb):
        self.u = lax.axis_index("ulysses")
        self.b = lax.axis_index("blk")
        self.nb = nb
        self.nc = nb // 2
        self.chip = self.b // 2
        self.core = lax.rem(self.b, 2)
        self.sib = self.chip * 2 + 1 - self.core

    def peer(self, i):
        return lax.rem(self.chip + i, self.nc) * 2 + self.core

    def unit(self, j):
        if self.nc != 4:
            return lax.rem(self.chip + self.nc - j, self.nc)
        x, y = lax.rem(self.chip, 2), self.chip // 2
        jx, jy = j % 2, j // 2
        return x + jx - 2 * x * jx + 2 * (y + jy - 2 * y * jy)

    def far(self, j):
        return self.unit(j) * 2 + self.core

    def across(self, d):
        at = self.u
        for k in range(d.bit_length()):
            if (d >> k) & 1:
                at = at + (1 << k) - (2 << k) * lax.rem(self.u // (1 << k), 2)
        return at

    def enter(self, flips=()):
        bar = pltpu.get_barrier_semaphore()
        for i in range(1, self.nc):
            signal(bar, self.u, self.peer(i))
        signal(bar, self.u, self.sib)
        for d in flips:
            signal(bar, self.across(d), self.b)
        pl.semaphore_wait(bar, self.nc + len(flips))


class Gather:
    def __init__(self, me, src, dst, sems):
        self.me, self.src, self.dst, self.sems = me, src, dst, sems
        self.quad = me.nc == 4
        half = dst.shape[1] // 2
        self.a, self.b = pl.ds(0, half), pl.ds(half, half)

    @staticmethod
    def scratch(nb, *lead):
        return DMA(lead + (2, 10 if nb == 8 else nb))

    def copy(self, k):
        me, src, dst = self.me, self.src, self.dst
        send = lambda s, d, to: remote(s, d, self.sems.at[0, k], self.sems.at[1, k], me.u, to)
        same = lambda at, to: send(dst.at[at], dst.at[at], to)
        part = lambda at, rows, to: send(dst.at[at, rows], dst.at[at, rows], to)
        if self.quad:
            if k < 4:
                rows = self.b if k % 2 else self.a
                return send(src.at[rows], dst.at[me.b, rows], me.far(1 + k // 2))
            if k < 6:
                return part(me.far(k - 3), self.b if k == 5 else self.a, me.far(6 - k))
            if k == 6:
                return send(src, dst.at[me.b], me.sib)
            return same(me.far(k - 6), me.sib)
        if k < me.nc:
            return send(src, dst.at[me.b], me.peer(k))
        if k == me.nc:
            return send(src, dst.at[me.b], me.sib)
        return same(me.far(k - me.nc), me.sib)

    def start(self):
        if self.quad:
            for k in (0, 3, 1, 2, 6):
                self.copy(k).start()
        else:
            for k in range(1, self.me.nc + 1):
                self.copy(k).start()

    def relay1(self):
        if self.quad:
            self.copy(0).wait_recv()
            self.copy(4).start()
            self.copy(3).wait_recv()
            self.copy(5).start()

    def relay2(self):
        if self.quad:
            self.copy(1).wait_recv()
            self.copy(7).start()
            self.copy(2).wait_recv()
            self.copy(8).start()
        else:
            for k in range(1, self.me.nc):
                self.copy(k).wait_recv()
                self.copy(self.me.nc + k).start()

    def relay3(self):
        if self.quad:
            self.copy(4).wait_recv()
            self.copy(5).wait_recv()
            self.copy(9).start()

    def passed(self, j):
        self.copy((6 if self.quad else self.me.nc) + j).wait_recv()

    def sent(self):
        for k in range(10) if self.quad else range(1, 2 * self.me.nc):
            self.copy(k).wait_send()

    def rest(self):
        self.relay1()
        self.relay2()
        self.relay3()

    def finish(self):
        for j in range(self.me.nc):
            self.passed(j)
        self.sent()


class Reduce:
    def __init__(self, me, get, source, sib_in, snd, land, sems):
        self.me, self.get, self.source = me, get, source
        self.sib_in, self.snd, self.land, self.sems = sib_in, snd, land, sems
        self.quad = me.nc == 4
        self.rows = sib_in.shape[1]
        half = self.rows // 2
        self.a, self.b = pl.ds(0, half), pl.ds(half, half)
        self.order = (3, 1, 2, 0) if self.quad else (*range(1, me.nc), 0)

    @staticmethod
    def scratch(nb, rows, cols, *lead):
        nc = nb // 2
        shape = lead + ((6, rows // 2, cols) if nc == 4 else (nc, rows, cols))
        return [
            pltpu.VMEM(lead + (nc, rows, cols), bf16), pltpu.VMEM(shape, bf16), pltpu.VMEM(shape, bf16),
            DMA(lead + (2, 10 if nc == 4 else 2 * nc)),
        ]

    def copy(self, k):
        me = self.me
        ss, rs = self.sems.at[0, k], self.sems.at[1, k]
        if k < me.nc:
            return remote(self.source(k), self.sib_in.at[k], ss, rs, me.u, me.sib)
        k = k - me.nc
        to = me.far((1, 1, 2, 2, 2, 1)[k] if self.quad else k)
        return remote(self.snd.at[k], self.land.at[k], ss, rs, me.u, to)

    def start(self, j):
        self.copy(j).start()

    def part(self, j, rows):
        return self.get(j, rows) + self.sib_in[j, rows].astype(f32)

    def send(self, k, value):
        self.snd[k] = value.astype(bf16)
        self.copy(self.me.nc + k).start()

    def phase1(self, j):
        self.copy(j).wait_recv()
        if not self.quad:
            self.send(j, self.part(j, pl.ds(0, self.rows)))
            return
        if j != 2:
            self.send(0 if j == 1 else 1, self.part(j, self.a))
        if j != 1:
            self.send(2 if j == 2 else 3, self.part(j, self.b))

    def landed(self, k):
        self.copy(self.me.nc + k).wait_recv()
        return self.land[k].astype(f32)

    def phase2(self):
        if self.quad:
            self.send(4, self.part(2, self.a) + self.landed(1))
            self.send(5, self.part(1, self.b) + self.landed(3))

    def end(self, write):
        self.copy(0).wait_recv()
        if self.quad:
            write(self.a, self.part(0, self.a) + self.landed(0) + self.landed(4))
            write(self.b, self.part(0, self.b) + self.landed(2) + self.landed(5))
        else:
            total = self.part(0, pl.ds(0, self.rows))
            for j in range(1, self.me.nc):
                total = total + self.landed(j)
            write(pl.ds(0, self.rows), total)

    def sent(self):
        for k in range(10) if self.quad else (*range(self.me.nc + 1), *range(self.me.nc + 1, 2 * self.me.nc)):
            if self.quad or k != self.me.nc:
                self.copy(k).wait_send()


def made(me, block, mine, sib_out, sib_in, snd, land, sems):
    red = Reduce(me, lambda j, rows: mine[j, rows], lambda j: sib_out.at[j], sib_in, snd, land, sems)
    for j in red.order:
        sib_out[j] = block(me.unit(j) * 2 + 1 - me.core).astype(bf16)
        red.start(j)
    for j in red.order:
        mine[j] = block(me.far(j))
        if j:
            red.phase1(j)
    return red


def made_scratch(nb, rows, cols):
    nc = nb // 2
    return [pltpu.VMEM((nc, rows, cols), f32), pltpu.VMEM((nc, rows, cols), bf16)] + Reduce.scratch(nb, rows, cols)


def keep(me, src, dst, sem):
    c = pltpu.make_async_copy(src, dst.at[me.b], sem)
    c.start()
    return c


def gather_inputs(x, pieces, nz, nb, cid):
    groups, shard, _ = pieces.shape
    rp = nb // groups

    def kernel(x_ref, p_ref, xo, po, gs, ps, pr, zs, ls):
        me = Layer(nb)
        bar = pltpu.get_barrier_semaphore()
        for i in range(1, nb):
            signal(bar, me.u, lax.rem(me.b + i, nb))
        for i in range(1, nz):
            signal(bar, lax.rem(me.u + i, nz), me.b)
        pl.semaphore_wait(bar, nb + nz - 2)

        def piece(i):
            tb = lax.rem(me.b + i, nb)
            return remote(p_ref.at[tb // rp], po.at[me.u, me.b], ps.at[i], pr.at[i], me.u, tb)

        for i in range(1, nb):
            piece(i).start()
        own = pltpu.make_async_copy(p_ref.at[me.b // rp], po.at[me.u, me.b], ls.at[0])
        own.start()
        g = Gather(me, x_ref, xo, gs)
        g.start()
        for i in range(1, nb):
            piece(i).wait()
        own.wait()
        slabs = []
        for zo in range(1, nz):
            c = remote(po.at[me.u], po.at[me.u], zs.at[0, zo], zs.at[1, zo], lax.rem(me.u + zo, nz), me.b)
            c.start()
            slabs.append(c)
        xk = keep(me, x_ref, xo, ls.at[1])
        g.rest()
        g.finish()
        for c in slabs:
            c.wait()
        xk.wait()

    sh = jax.ShapeDtypeStruct
    return pl.pallas_call(
        kernel,
        out_shape=(sh((nb,) + x.shape, x.dtype), sh((nz, nb, shard, AUX), bf16)),
        in_specs=[ANY] * 2,
        out_specs=(ANY,) * 2,
        scratch_shapes=[Gather.scratch(nb)] + [DMA((nb,))] * 2 + [DMA((2, nz)), DMA((2,))],
        compiler_params=pltpu.CompilerParams(collective_id=cid, has_side_effects=True),
        cost_estimate=cost(30),
        name="gather_inputs",
    )(x, pieces)


def halo_forward(kv, gm, wo, nz, nb, rp, back, cid):
    shard = wo.shape[0]
    n_o = QCOLS // shard
    n = nz * nb

    def kernel(x_ref, g_ref, w_ref, o_ref, go, gx, wo_out, ks, kr, gs, ws, wr, ls):
        me = Layer(nb)
        lin = me.u * nb + me.b
        u, b = me.u, me.b
        bar = pltpu.get_barrier_semaphore()

        @pl.loop(1, n)
        def _(i):
            t = lax.rem(lin + i, n)
            signal(bar, t // nb, lax.rem(t, nb))

        pl.semaphore_wait(bar, n - 1)

        def copy(d):
            return remote(x_ref, o_ref.at[d - 1], ks.at[d - 1], kr.at[d - 1], u + d, b)

        for d in range(1, back + 1):
            pl.when(u + d < nz)(lambda d=d: copy(d).start())
        hg = lin // n_o
        slot = lax.rem(lin, n_o)

        def weight(zo, p):
            tz, tb = lax.rem(me.u + zo, nz), hg * rp + p
            return tb, remote(w_ref, wo_out.at[slot], ws.at[zo * rp + p], wr.at[slot], tz, tb)

        stay = pltpu.make_async_copy(w_ref, wo_out.at[slot], ls.at[1])
        for zo in range(nz):
            for p in range(rp):
                tb, c = weight(zo, p)
                if zo:
                    c.start()
                else:
                    pl.when(tb != b)(c.start)
                    pl.when(tb == b)(stay.start)
        mate = remote(g_ref, gx, ls.at[2], ls.at[3], me.across(1), b)
        mate.start()
        g = Gather(me, g_ref, go, gs)
        g.start()
        own = keep(me, g_ref, go, ls.at[0])
        g.rest()
        g.finish()
        own.wait()
        for d in range(1, back + 1):
            pl.when(u + d < nz)(lambda d=d: copy(d).wait_send())
            pl.when(u >= d)(lambda d=d: copy(d).wait_recv())
        for zo in range(nz):
            for p in range(rp):
                tb, c = weight(zo, p)
                if zo:
                    c.wait_send()
                else:
                    pl.when(tb != b)(c.wait_send)
                    pl.when(tb == b)(stay.wait)
        for j in range(n_o):
            src = (b // rp) * n_o + j
            c = remote(w_ref, wo_out.at[j], ws.at[0], wr.at[j], u, me.sib)
            pl.when(src != lin)(c.wait_recv)
        mate.wait()

    sh = jax.ShapeDtypeStruct
    return pl.pallas_call(
        kernel,
        out_shape=(
            sh((back,) + kv.shape, kv.dtype), sh((nb,) + gm.shape, gm.dtype), sh(gm.shape, gm.dtype),
            sh((n_o, shard, D), bf16),
        ),
        in_specs=[ANY] * 3,
        out_specs=(ANY,) * 4,
        scratch_shapes=[DMA((back,))] * 2 + [Gather.scratch(nb), DMA((nz * rp,)), DMA((n_o,)), DMA((4,))],
        compiler_params=pltpu.CompilerParams(collective_id=cid, has_side_effects=True),
        cost_estimate=cost(30),
        name="halo_forward",
    )(kv, gm, wo)


def pair_of(me, p_ref, sib_in, snd, land, sems):
    def one(h):
        return Reduce(
            me, lambda j, rows: p_ref[h, me.far(j), rows].astype(f32),
            lambda j: p_ref.at[h, me.unit(j) * 2 + 1 - me.core],
            sib_in.at[h], snd.at[h], land.at[h], sems.at[h])
    return one(0), one(1)


def write_to(ref, *lead):
    def write(rows, value):
        ref[(*lead, rows)] = value.astype(ref.dtype)
    return write


def add_to(ref, other, at):
    def write(rows, value):
        ref[rows] = value + other[at, rows].astype(f32)
    return write


def reduce_product(lhs, rhs, gx, nb, cid):
    rows = lhs.shape[0] // nb
    cols = rhs.shape[1]

    def kernel(l_ref, r_ref, g_ref, o_ref, go, gs, ls, *scratch):
        me = Layer(nb)
        me.enter()

        def block(t):
            part = l_ref[pl.ds(pl.multiple_of(t * rows, rows), rows), :]
            return jnp.dot(part, r_ref[...], preferred_element_type=f32)

        red = made(me, block, *scratch)
        g = Gather(me, g_ref, go, gs)
        g.start()
        own = keep(me, g_ref, go, ls)
        red.phase2()
        g.rest()
        red.end(write_to(o_ref))
        red.sent()
        g.finish()
        own.wait()

    sh = jax.ShapeDtypeStruct
    return pl.pallas_call(
        kernel,
        out_shape=(sh((rows, cols), f32), sh((nb,) + gx.shape, gx.dtype)),
        in_specs=[VMEM, VMEM, ANY],
        out_specs=(VMEM, ANY),
        scratch_shapes=[Gather.scratch(nb), DMA] + made_scratch(nb, rows, cols),
        compiler_params=pltpu.CompilerParams(
            collective_id=cid, has_side_effects=True, vmem_limit_bytes=48 * MIB
        ),
        cost_estimate=cost(30),
        name="reduce_product",
    )(lhs, rhs, gx)


def middle(x, ypart, grads, nz, nb, cid):
    _, _, rows, cols = ypart.shape
    m = len(grads)

    def kernel(x_ref, y_ref, *rest):
        srcs, xo, o_ref, dsts = rest[:m], rest[m], rest[m + 1], rest[m + 2:2 * m + 2]
        gs, ls, ws, zs, zbuf, *pair = rest[2 * m + 2:]
        me = Layer(nb)
        me.enter(range(1, m + 1))
        g = Gather(me, x_ref, xo, gs)
        g.start()
        r0, r1 = pair_of(me, y_ref, *pair)
        for r in (r1, r0):
            for j in r.order:
                r.start(j)
        moved = [
            remote(srcs[k], dsts[k], ws.at[0, k], ws.at[1, k], me.across(k + 1), me.b) for k in range(m)
        ]
        for c in reversed(moved):
            c.start()
        own = keep(me, x_ref, xo, ls)
        g.rest()
        for r in (r1, r0):
            for j in r.order[:-1]:
                r.phase1(j)
        r1.phase2()
        r0.phase2()
        r1.end(write_to(zbuf, 0))
        mate = remote(zbuf.at[0], zbuf.at[1], zs.at[0], zs.at[1], me.across(1), me.b)
        mate.start()
        mate.wait_recv()
        r0.end(add_to(o_ref, zbuf, 1))
        mate.wait_send()
        r0.sent()
        r1.sent()
        g.finish()
        own.wait()
        for c in moved:
            c.wait()

    sh = jax.ShapeDtypeStruct
    return pl.pallas_call(
        kernel,
        out_shape=(sh((nb,) + x.shape, x.dtype), sh((rows, cols), f32))
        + tuple(sh(a.shape, a.dtype) for a in grads),
        in_specs=[ANY, VMEM] + [ANY] * m,
        out_specs=(ANY, VMEM) + (ANY,) * m,
        scratch_shapes=[Gather.scratch(nb), DMA, DMA((2, m)), DMA((2,)), pltpu.VMEM((2, rows, cols), bf16)]
        + Reduce.scratch(nb, rows, cols, 2),
        compiler_params=pltpu.CompilerParams(
            collective_id=cid, has_side_effects=True, vmem_limit_bytes=56 * MIB
        ),
        cost_estimate=cost(50),
        name="middle",
    )(x, ypart, *grads)


def halo_back(dkv, nz, nb, rp, back, cid):
    R = dkv.shape[1]

    def kernel(d_ref, kin, ks, kr):
        me = Layer(nb)
        first = (me.b // rp) * rp
        part = lax.rem(me.b, rp)
        bar = pltpu.get_barrier_semaphore()
        others = [(zo, p) for zo in range(nz) for p in range(rp) if zo or p]
        for zo, p in others:
            signal(bar, lax.rem(me.u + zo, nz), first + lax.rem(part + p, rp))
        pl.semaphore_wait(bar, len(others))

        def copy(d, p):
            k = d * rp + p
            return remote(d_ref.at[d], kin.at[d * rp + part], ks.at[k], kr.at[d * rp + part], me.u - d, first + p)

        def arrival(d, p):
            k = d * rp + p
            return remote(d_ref.at[d], kin.at[k], ks.at[k], kr.at[k], me.u, me.sib)

        for d in range(back + 1):
            for p in range(rp):
                if d:
                    pl.when(me.u >= d)(lambda d=d, p=p: copy(d, p).start())
                elif rp > 1:
                    pl.when(part != p)(lambda d=d, p=p: copy(d, p).start())
        for d in range(back + 1):
            for p in range(rp):
                if d:
                    pl.when(me.u >= d)(lambda d=d, p=p: copy(d, p).wait_send())
                    pl.when(me.u + d < nz)(lambda d=d, p=p: arrival(d, p).wait_recv())
                elif rp > 1:
                    pl.when(part != p)(lambda d=d, p=p: copy(d, p).wait_send())
                    pl.when(part != p)(lambda d=d, p=p: arrival(d, p).wait_recv())

    return pl.pallas_call(
        kernel,
        out_shape=jax.ShapeDtypeStruct(((back + 1) * rp, R, LANES), bf16),
        in_specs=[ANY],
        out_specs=ANY,
        scratch_shapes=[DMA(((back + 1) * rp,))] * 2,
        compiler_params=pltpu.CompilerParams(collective_id=cid, has_side_effects=True),
        cost_estimate=cost(25),
        name="halo_back",
    )(dkv)


def reduce_last(lhs, rhs, pieces, dwo, nz, nb, rp, cid):
    rows = lhs.shape[0] // nb
    cols = rhs.shape[0]
    _, _, shard, width = pieces.shape
    n_o = nz * rp
    n = nz * nb

    def kernel(l_ref, r_ref, p_ref, w_ref, o_ref, pin, win, slab, total, wslab, wtotal, zs, zr, ps, pr, ws, wr,
               ls, *scratch):
        me = Layer(nb)
        lin = me.u * nb + me.b
        part = lax.rem(me.b, rp)
        bar = pltpu.get_barrier_semaphore()

        @pl.loop(1, n)
        def _(i):
            t = lax.rem(lin + i, n)
            signal(bar, t // nb, lax.rem(t, nb))

        pl.semaphore_wait(bar, n - 1)

        def weight(p):
            t = (me.b // rp) * n_o + me.u * rp + p
            return t, remote(wtotal.at[p], win.at[part], ws.at[0, p], wr.at[0, part], t // nb, lax.rem(t, nb))

        across = []
        for i in range(1, nz):
            to = lax.rem(me.u + i, nz)
            c = remote(p_ref.at[to], slab.at[i], zs.at[i], zr.at[i], to, me.b)
            c.start()
            across.append(c)

        def block(t):
            part = l_ref[pl.ds(pl.multiple_of(t * rows, rows), rows), :]
            return lax.dot_general(part, r_ref[...], NT, preferred_element_type=f32)

        parts = []
        for i in range(1, nz):
            to = lax.rem(me.u + i, nz)
            c = remote(w_ref.at[to], wslab.at[i], ws.at[1, i], wr.at[1, i], to, me.b)
            c.start()
            parts.append(c)
        red = made(me, block, *scratch)
        red.phase2()
        for c in across:
            c.wait_recv()
        out = []
        for t in range(nb):
            tile = p_ref[me.u, t].astype(f32)
            for i in range(1, nz):
                tile = tile + slab[i, t].astype(f32)
            total[t] = tile.astype(bf16)
        for i in range(1, nb):
            t = lax.rem(me.b + i, nb)
            c = remote(total.at[t], pin.at[me.b], ps.at[i], pr.at[i], me.u, t)
            c.start()
            out.append(c)
        own = pltpu.make_async_copy(total.at[me.b], pin.at[me.b], ls.at[0])
        own.start()
        for c in parts:
            c.wait_recv()
        stay = lambda p: pltpu.make_async_copy(wtotal.at[p], win.at[part], ls.at[1])
        for p in range(rp):
            tile = w_ref[me.u, p].astype(f32)
            for i in range(1, nz):
                tile = tile + wslab[i, p].astype(f32)
            wtotal[p] = tile.astype(bf16)
            t, c = weight(p)
            pl.when(t != lin)(c.start)
            pl.when(t == lin)(stay(p).start)
        red.end(write_to(o_ref))
        red.sent()
        for c in across:
            c.wait_send()
        for c in out:
            c.wait()
        own.wait()
        for c in parts:
            c.wait_send()
        for p in range(rp):
            t, c = weight(p)
            pl.when(t != lin)(c.wait_send)
            pl.when(t == lin)(stay(p).wait)
        hg = lin // n_o
        layer = lax.rem(lin, n_o) // rp
        for p in range(rp):
            c = remote(wtotal.at[0], win.at[p], ws.at[0, 0], wr.at[0, p], me.u, me.sib)
            pl.when(layer * nb + hg * rp + p != lin)(c.wait_recv)

    sh = jax.ShapeDtypeStruct
    return pl.pallas_call(
        kernel,
        out_shape=(
            sh((rows, cols), f32), sh((nb, shard, width), bf16), sh((rp, shard, D), bf16),
        ),
        in_specs=[VMEM, VMEM, VMEM, VMEM],
        out_specs=(VMEM, ANY, ANY),
        scratch_shapes=[pltpu.VMEM((nz, nb, shard, width), bf16), pltpu.VMEM((nb, shard, width), bf16)]
        + [pltpu.VMEM((nz, rp, shard, D), bf16), pltpu.VMEM((rp, shard, D), bf16)]
        + [DMA((nz,))] * 2
        + [DMA((nb,))] * 2
        + [DMA((2, max(nz, rp)))] * 2
        + [DMA((2,))]
        + made_scratch(nb, rows, cols),
        compiler_params=pltpu.CompilerParams(
            collective_id=cid, has_side_effects=True, vmem_limit_bytes=56 * MIB
        ),
        cost_estimate=cost(2),
        name="reduce_last",
    )(lhs, rhs, pieces, dwo)


def turn(a, c, s1, s2):
    return a * c + pltpu.roll(a, LANES - HW // 2, 1) * s1 + pltpu.roll(a, HW // 2, 1) * s2


def turn_back(a, c, s1, s2):
    return a * c - pltpu.roll(a, LANES - HW // 2, 1) * s1 - pltpu.roll(a, HW // 2, 1) * s2


def swap(a):
    return pltpu.roll(a, HW, 1)


def low_half():
    return lax.broadcasted_iota(jnp.int32, (1, LANES), 1) < HW


def row_block(step, width):
    return pl.BlockSpec((step, width), lambda i: (i, 0))


def whole_block(a):
    zeros = (0,) * a.ndim
    return pl.BlockSpec(a.shape, lambda i: zeros)


def project(x, gain, packed, c, s1, s2):
    R = x.shape[0]
    step = 256

    def kernel(x_ref, g_ref, w_ref, c_ref, a_ref, b_ref, q_ref, kv_ref, h_ref):
        v = x_ref[...].astype(f32)
        inv = lax.rsqrt(jnp.mean(v * v, axis=1, keepdims=True) + EPS)
        h = (v * inv * g_ref[...]).astype(bf16)
        h_ref[...] = h
        out = jnp.dot(h, w_ref[...], preferred_element_type=f32)
        tables = (c_ref[...], a_ref[...], b_ref[...])
        low = low_half()
        t0 = turn(out[:, :LANES], *tables)
        t1 = turn(out[:, LANES:2 * LANES], *tables)
        scale = lambda a: (jnp.where(low, a, 0.0) * (1.0 / math.sqrt(HW))).astype(bf16)
        q_ref[0] = scale(t0)
        q_ref[1] = scale(swap(t0))
        q_ref[2] = scale(t1)
        kv_ref[...] = jnp.where(low, swap(t1), swap(out[:, 2 * LANES:])).astype(bf16)

    sh = jax.ShapeDtypeStruct
    return pl.pallas_call(
        kernel,
        grid=(R // step,),
        out_shape=(sh((GROUP, R, LANES), bf16), sh((R, LANES), bf16), sh((R, D), bf16)),
        in_specs=[row_block(step, D), whole_block(gain), whole_block(packed)] + [row_block(step, LANES)] * 3,
        out_specs=(
            pl.BlockSpec((GROUP, step, LANES), lambda i: (0, i, 0)),
            row_block(step, LANES),
            row_block(step, D),
        ),
        compiler_params=pltpu.CompilerParams(vmem_limit_bytes=32 * MIB),
        cost_estimate=cost(4),
        name="project",
    )(x, gain, packed, c, s1, s2)


BQ = 256
BK = 512
NT = (((1,), (1,)), ((), ()))
NN = (((1,), (0,)), ((), ()))
TN = (((0,), (0,)), ((), ()))


def mm(a, b, dims=NN):
    return lax.dot_general(a, b, dims, preferred_element_type=f32)


def seen(meta, st, i, kb, nq):
    qpos = meta[nq] + i * BQ + lax.broadcasted_iota(jnp.int32, (BQ, 1), 0)
    kpos = kb * BK + lax.broadcasted_iota(jnp.int32, (1, BK), 1)
    return ((kpos <= qpos) & (kpos >= st))[None]


def attend(q, kv, starts, meta):
    _, Rq, _ = q.shape
    nq = Rq // BQ
    M = GROUP * BQ

    def kernel(meta, q_ref, kv_ref, st_ref, o_ref, l_ref):
        i = pl.program_id(0)
        qv = q_ref[...].reshape(M, LANES)
        st = st_ref[...]
        last = (meta[nq] + i * BQ + BQ - 1) // BK + 1

        def step(kb, carry):
            m, l, acc = carry
            keys = kv_ref[pl.ds(pl.multiple_of(kb * BK, BK), BK), :]
            s = mm(qv, keys, NT).reshape(GROUP, BQ, BK)
            s = jnp.where(seen(meta, st, i, kb, nq), s, NEG)
            m2 = jnp.maximum(m, jnp.max(s, axis=2, keepdims=True))
            w = jnp.exp(s - m2)
            f = jnp.exp(m - m2)
            l = l * f + jnp.sum(w, axis=2, keepdims=True)
            pv = mm(w.astype(bf16).reshape(M, BK), keys)
            return m2, l, acc * f + pv.reshape(GROUP, BQ, LANES)

        init = (
            jnp.full((GROUP, BQ, 1), NEG, f32),
            jnp.zeros((GROUP, BQ, 1), f32),
            jnp.zeros((GROUP, BQ, LANES), f32),
        )
        m, l, acc = lax.fori_loop(meta[i], last, step, init)
        o = acc / l
        o_ref[:, :LANES] = jnp.where(low_half(), swap(o[0]), o[1]).astype(bf16)
        o_ref[:, LANES:] = swap(o[2])[:, :HW].astype(bf16)
        l_ref[...] = m + jnp.log(l)

    sh = jax.ShapeDtypeStruct
    blk = lambda w: pl.BlockSpec((GROUP, BQ, w), lambda i, m: (0, i, 0))
    return pl.pallas_call(
        kernel,
        grid_spec=pltpu.PrefetchScalarGridSpec(
            num_scalar_prefetch=1,
            grid=(nq,),
            in_specs=[
                blk(LANES),
                pl.BlockSpec(kv.shape, lambda i, m: (0, 0)),
                pl.BlockSpec((BQ, 1), lambda i, m: (i, 0)),
            ],
            out_specs=(pl.BlockSpec((BQ, QCOLS), lambda i, m: (i, 0)), blk(1)),
        ),
        out_shape=(sh((Rq, QCOLS), bf16), sh((GROUP, Rq, 1), f32)),
        compiler_params=pltpu.CompilerParams(vmem_limit_bytes=48 * MIB),
        cost_estimate=cost(17),
        name="attend",
    )(meta, q, kv, starts)


def attend_back(q, kv, starts, meta, lse, mixed, dattn, wo):
    _, Rq, _ = q.shape
    nq = Rq // BQ
    M = GROUP * BQ
    K = kv.shape[0]

    def kernel(meta, q_ref, kv_ref, st_ref, l_ref, o_ref, g_ref, w_ref, dq_ref, dkv_ref, dw_ref):
        i = pl.program_id(0)

        @pl.when(i == 0)
        def _():
            dkv_ref[...] = jnp.zeros_like(dkv_ref)
            dw_ref[...] = jnp.zeros_like(dw_ref)

        g = g_ref[...]
        mixed = o_ref[...]
        dm = mm(g, w_ref[...], NT).astype(bf16).astype(f32)
        dw_ref[...] += mm(mixed, g, TN)
        low = low_half()
        d0 = dm[:, :LANES]
        d1 = jnp.concatenate([dm[:, LANES:], jnp.zeros((BQ, LANES - HW), f32)], axis=1)
        m0 = mixed[:, :LANES].astype(f32)
        m1 = jnp.concatenate([mixed[:, LANES:].astype(f32), jnp.zeros((BQ, LANES - HW), f32)], axis=1)
        total = lambda a: jnp.sum(a, axis=1, keepdims=True)
        e0, e1 = d0 * m0, d1 * m1
        first = total(jnp.where(low, e0, 0.0))
        delta = jnp.stack([first, total(jnp.where(low, 0.0, e0)), total(e1)])
        high = lambda a: jnp.where(low, 0.0, a).astype(bf16)
        do = jnp.concatenate([high(swap(d0)), high(d0), high(swap(d1))], axis=0)
        qv = q_ref[...].reshape(M, LANES)
        lse = l_ref[...]
        st = st_ref[...]
        last = (meta[nq] + i * BQ + BQ - 1) // BK + 1

        def step(kb, dq):
            at = pl.ds(pl.multiple_of(kb * BK, BK), BK)
            keys = kv_ref[at, :]
            s = mm(qv, keys, NT).reshape(GROUP, BQ, BK)
            p = jnp.where(seen(meta, st, i, kb, nq), jnp.exp(s - lse), 0.0)
            dp = mm(do, keys, NT).reshape(GROUP, BQ, BK)
            ds = (p * (dp - delta)).astype(bf16).reshape(M, BK)
            pb = p.astype(bf16).reshape(M, BK)
            dkv_ref[at, :] += mm(ds, qv, TN) + mm(pb, do, TN)
            return dq + mm(ds, keys)

        dq = lax.fori_loop(meta[i], last, step, jnp.zeros((M, LANES), f32))
        dq_ref[...] = (dq * (1.0 / math.sqrt(HW))).astype(bf16).reshape(GROUP, BQ, LANES)

    sh = jax.ShapeDtypeStruct
    blk = lambda w: pl.BlockSpec((GROUP, BQ, w), lambda i, m: (0, i, 0))
    rows = lambda w: pl.BlockSpec((BQ, w), lambda i, m: (i, 0))
    full = lambda *shape: pl.BlockSpec(shape, lambda i, m: (0, 0))
    return pl.pallas_call(
        kernel,
        grid_spec=pltpu.PrefetchScalarGridSpec(
            num_scalar_prefetch=1,
            grid=(nq,),
            in_specs=[
                blk(LANES), full(*kv.shape), rows(1), blk(1), rows(QCOLS), rows(D), full(QCOLS, D),
            ],
            out_specs=(blk(LANES), full(K, LANES), full(QCOLS, D)),
        ),
        out_shape=(sh((GROUP, Rq, LANES), bf16), sh((K, LANES), f32), sh((QCOLS, D), f32)),
        compiler_params=pltpu.CompilerParams(vmem_limit_bytes=48 * MIB),
        cost_estimate=cost(2),
        name="attend_back",
    )(meta, q, kv, starts, lse, mixed, dattn, wo)


def weight_grads(dq, dkv, kin, ok, tables, h1, packed, tail):
    _, Rq, _ = dq.shape
    step = 256
    arrivals = kin.shape[0]

    def kernel(ok_ref, dq_ref, dkv_ref, kin_ref, c_ref, a_ref, b_ref, h_ref, w_ref, t_ref, o_ref, p_ref, acc):
        i = pl.program_id(0)

        @pl.when(i == 0)
        def _():
            acc[...] = jnp.zeros_like(acc)

        kv = dkv_ref[...]
        for k in range(arrivals):
            kv = kv + jnp.where(ok_ref[k] > 0, kin_ref[k].astype(f32), 0.0)
        kv = kv.astype(bf16).astype(f32)
        low = low_half()
        tables = (c_ref[...], a_ref[...], b_ref[...])
        q = [dq_ref[h].astype(f32) for h in range(GROUP)]
        kv = swap(kv)
        t0 = turn_back(jnp.where(low, q[0], swap(q[1])), *tables)
        t1 = turn_back(jnp.where(low, q[2], kv), *tables)
        out = jnp.concatenate([t0, t1, jnp.where(low, kv, 0.0)], axis=1).astype(bf16)
        o_ref[...] = out
        acc[...] += mm(h_ref[...], out, TN)

        @pl.when(i == Rq // step - 1)
        def _():
            w = w_ref[...].astype(f32)
            dw = acc[...]
            t = t_ref[...]
            lane = lax.broadcasted_iota(jnp.int32, (1, LANES), 1)
            gain = jnp.sum(jnp.where(lane == ok_ref[arrivals], w[:, 2 * LANES:], 0.0), axis=1, keepdims=True)
            d_gain = jnp.sum(w * dw, axis=1, keepdims=True) / gain
            t = t + jnp.where(lane == ok_ref[arrivals] + 1, d_gain, 0.0)
            p_ref[:, :2 * LANES] = dw[:, :2 * LANES].astype(bf16)
            p_ref[:, 2 * LANES:] = jnp.where(low, dw[:, 2 * LANES:], t).astype(bf16)

    sh = jax.ShapeDtypeStruct
    heads = lambda n: pl.BlockSpec((n, step, LANES), lambda i: (0, i, 0))
    return pl.pallas_call(
        kernel,
        grid=(Rq // step,),
        out_shape=(sh((Rq, AUX), bf16), sh((D, AUX), bf16)),
        in_specs=[pl.BlockSpec(memory_space=pltpu.SMEM), heads(GROUP), row_block(step, LANES), heads(arrivals)]
        + [row_block(step, LANES)] * 3
        + [row_block(step, D), whole_block(packed), whole_block(tail)],
        out_specs=(row_block(step, AUX), pl.BlockSpec((D, AUX), lambda i: (0, 0))),
        scratch_shapes=[pltpu.VMEM((D, AUX), f32)],
        compiler_params=pltpu.CompilerParams(vmem_limit_bytes=48 * MIB),
        cost_estimate=cost(2),
        name="weight_grads",
    )(ok, dq, dkv, kin, *tables, h1, packed, tail)


def experts(h2_own, g_own, g_oth, router, hot, weights, nz, nb, cid):
    T = h2_own.shape[0]
    nc = nb // 2
    step = 2 * T
    units = 2 * nc
    dz = D // nz
    C = D + LANES
    W = 3 * FF
    nw = len(weights)
    resident = nb <= 8

    def kernel(x_ref, g0_ref, g1_ref, r_ref, e_ref, *rest):
        win = rest[:nw]
        y_ref, s_ref = rest[nw:nw + 2]
        rest = rest[nw + 2:]
        din = rest[:nz]
        h_all, hbuf, part, gbuf, ybuf, wc, acc, zbuf, gs, zs, sem, gsem, ysem, *pair = rest[nz:]
        me = Layer(nb)
        me.enter((1,))
        own, oth = h_all.at[0], h_all.at[1]
        mate = remote(x_ref, oth.at[me.b], zs.at[0], zs.at[1], me.across(1), me.b)
        mate.start()
        ga = Gather(me, x_ref, own, gs.at[0])
        gb = Gather(me, oth.at[me.b], oth, gs.at[1])
        ga.start()
        mine = pltpu.make_async_copy(x_ref, own.at[me.b], zs.at[2])
        mine.start()
        rows_at = lambda d: pl.ds(pl.multiple_of(me.across(d) * dz, dz), dz)
        loads = [
            pltpu.make_async_copy(win[k], wc.at[rows_at(d), pl.ds(c, a.shape[1])], sem.at[k])
            for k, (a, d, c) in enumerate(weights)
        ]
        for c in loads:
            c.start()

        def place(u):
            other = (u >= 2) & (u < nc + 2)
            j = jnp.where(u < 2, u, jnp.where(other, u - 2, 2 * nc + 1 - u))
            return jnp.where(other, 1, 0), j

        def cot(u, h):
            _, j = place(u)
            rows = pl.ds(pl.multiple_of(me.unit(j) * step, step), step)
            slot = lax.rem(u, 2)
            return pltpu.make_async_copy((g1_ref if h else g0_ref).at[rows], gbuf.at[slot], gsem.at[slot])

        def cot_start(u):
            h, _ = place(u)
            pl.when(h == 0)(lambda: cot(u, 0).start())
            pl.when(h == 1)(lambda: cot(u, 1).start())

        def result(u):
            h, j = place(u)
            slot = lax.rem(u, 2)
            return pltpu.make_async_copy(
                ybuf.at[slot], y_ref.at[h, pl.ds(pl.multiple_of(me.unit(j) * 2, 2), 2)], ysem.at[slot])

        cot_start(jnp.int32(0))
        acc[...] = jnp.zeros_like(acc)
        ra, rb = pair_of(me, part, *pair)
        ga.relay1()
        for c in loads:
            c.wait()
        mine.wait()

        def at(k, f):
            def run(u):
                pl.when(u == k)(f)
            return run

        def arrive(u):
            def first():
                ga.relay2()
                mate.wait_recv()
                gb.start()

            def second():
                ga.relay3()
                gb.relay1()

            at(1, first)(u)
            at(2, second)(u)
            at(3, gb.relay2)(u)
            at(4, gb.relay3)(u)
            for k in range(units):
                h = 1 if 2 <= k < nc + 2 else 0
                j = k if k < 2 else (k - 2 if h else 2 * nc + 1 - k)
                at(k, lambda h=h, j=j: (gb if h else ga).passed(j))(u)

        def depart(u):
            for k in range(units):
                h = 1 if 2 <= k < nc + 2 else 0
                j = k if k < 2 else (k - 2 if h else 2 * nc + 1 - k)
                at(k, lambda h=h, j=j: (rb if h else ra).start(j))(u)

            def mates():
                for j in rb.order[:-1]:
                    rb.phase1(j)

            at(nc + 1, mates)(u)

            def ours():
                ra.phase1(3)
                ra.phase1(1)

            if nc == 4:
                at(nc + 2, ours)(u)

        @pl.loop(0, units)
        def _(u):
            h, j = place(u)
            slot = lax.rem(u, 2)
            pl.when(u + 1 < units)(lambda: cot_start(u + 1))
            arrive(u)
            cot(u, 0).wait()
            pl.when(u >= 2)(lambda: result(u - 2).wait())
            two = pl.ds(pl.multiple_of(me.unit(j) * 2, 2), 2)
            if resident:
                x = h_all[h, two].reshape(step, D)
            else:
                c = pltpu.make_async_copy(h_all.at[h, two], hbuf, zs.at[5])
                c.start()
                c.wait()
                x = hbuf[...].reshape(step, D)
            hot = e_ref[...]
            mask = gbuf[slot, :, D:].astype(f32) > 0
            logits = mm(x, r_ref[...])
            top = jnp.max(jnp.where(mask, logits, NEG), axis=1, keepdims=True)
            w = jnp.where(mask, jnp.exp(jnp.where(mask, logits - top, 0.0)), 0.0)
            gate = jnp.sum(w * hot, axis=1, keepdims=True) / jnp.sum(w, axis=1, keepdims=True)
            gu = mm(x, wc[:, :2 * FF])
            a, up = gu[:, :FF], gu[:, FF:]
            sg = jax.nn.sigmoid(a)
            silu = a * sg
            act = (silu * up).astype(bf16)
            g = gbuf[slot, :, :D]
            ybuf[slot] = (gate * mm(act, wc[:, 2 * FF:], NT)).astype(bf16).reshape(2, T, D)
            result(u).start()
            raw = mm(g, wc[:, 2 * FF:])
            acc[:, 2 * FF:] += mm((gate * g.astype(f32)).astype(bf16), act, TN)
            dgate = jnp.sum(act.astype(f32) * raw, axis=1, keepdims=True)
            dact = gate * raw
            dgu = jnp.concatenate(
                [dact * up * (sg * (1.0 + a * (1.0 - sg))), dact * silu], axis=1).astype(bf16)
            acc[:, :2 * FF] += mm(x, dgu, TN)
            part[h, two, :, :D] = mm(dgu, wc[:, :2 * FF], NT).astype(bf16).reshape(2, T, D)
            hi = dgate.astype(bf16).astype(f32)
            part[h, two, :, D:] = (hi * hot + swap((dgate - hi) * hot)).astype(bf16).reshape(2, T, LANES)
            depart(u)

        rb.phase2()
        for j in (2,) if nc == 4 else ra.order[:-1]:
            ra.phase1(j)
        wc[...] = acc[...].astype(bf16)
        saves = [pltpu.make_async_copy(wc.at[rows_at(d)], din[d], sem.at[d]) for d in range(nz)]
        for c in saves:
            c.start()
        rb.end(write_to(zbuf, 0))
        back = remote(zbuf.at[0], zbuf.at[1], zs.at[3], zs.at[4], me.across(1), me.b)
        back.start()
        ra.phase2()
        back.wait_recv()
        ra.end(add_to(s_ref, zbuf, 1))
        back.wait_send()
        mate.wait_send()
        for r in (ga, gb, ra, rb):
            r.sent()
        for c in saves:
            c.wait()
        result(jnp.int32(units - 2)).wait()
        result(jnp.int32(units - 1)).wait()

    sh = jax.ShapeDtypeStruct
    v = lambda shape, kind=bf16: pltpu.VMEM(shape, kind)
    return pl.pallas_call(
        kernel,
        out_shape=(sh((2, nb, T, D), bf16), sh((T, C), f32))
        + (sh((dz, W), bf16),) * nz
        + (() if resident else (sh((2, nb, T, D), bf16),)),
        in_specs=[ANY] * 3 + [VMEM] * 2 + [ANY] * nw,
        out_specs=(ANY, VMEM) + (ANY,) * (nz + int(not resident)),
        scratch_shapes=([v((2, nb, T, D))] if resident else [])
        + [
            v((2, T, D)), v((2, nb, T, C)), v((2, step, C)), v((2, 2, T, D)),
            v((D, W)), v((D, W), f32), v((2, T, C)),
            Gather.scratch(nb, 2), DMA((6,)), DMA((nw,)), DMA((2,)), DMA((2,)),
        ]
        + Reduce.scratch(nb, T, C, 2),
        compiler_params=pltpu.CompilerParams(
            collective_id=cid, has_side_effects=True, vmem_limit_bytes=60 * MIB
        ),
        cost_estimate=cost(70),
        name="experts",
    )(h2_own, g_own, g_oth, router, hot, *[a for a, _, _ in weights])


def finish(dh1, x, gain, dresid, pin, win, resid, ysum, grads):
    T = x.shape[0]
    groups, rp, S, _ = pin.shape
    senders = win.shape[0]
    m = len(grads)
    dz = grads[0].shape[0]

    def kernel(d_ref, x_ref, g_ref, r_ref, p_ref, w_ref, s_ref, y_ref, *rest):
        srcs = rest[:m]
        t_ref, q_ref, k_ref, v_ref, m_ref, o_ref, out_ref, in_ref, ex_ref = rest[m:]
        odd = lax.rem(lax.axis_index("ulysses"), 2)
        for e in range(2):
            total = functools.reduce(lambda a, b: a + b, [r[...].astype(f32) for r in srcs[e::2]])
            at = odd if e == 0 else 1 - odd
            in_ref[at] = total[:, :2 * FF]
            ex_ref[at] = total[:, 2 * FF:].T
        v = x_ref[...].astype(f32)
        inv = lax.rsqrt(jnp.mean(v * v, axis=1, keepdims=True) + EPS)
        n = v * inv
        w = d_ref[...] * g_ref[...]
        t_ref[...] = r_ref[...] + inv * (w - n * jnp.mean(w * n, axis=1, keepdims=True))
        out_ref[...] = s_ref[...] + y_ref[...]
        o_ref[...] = functools.reduce(lambda a, b: a + b, [w_ref[k].astype(f32) for k in range(senders)])
        small = 0.0
        for h in range(groups):
            row = 0.0
            for p in range(rp):
                row = row + p_ref[h, p].astype(f32)
            q_ref[:, h * QCOLS:(h + 1) * QCOLS] = row[:, :QCOLS]
            k_ref[:, h * HW:(h + 1) * HW] = row[:, QCOLS:QCOLS + HW]
            v_ref[:, h * HW:(h + 1) * HW] = row[:, QCOLS + HW:ROUTER_AT]
            small = small + row[:, 2 * LANES:]
        m_ref[...] = small

    sh = lambda *shape: jax.ShapeDtypeStruct(shape, f32)
    return pl.pallas_call(
        kernel,
        out_shape=(sh(T, D), sh(S, HEADS * HW), sh(S, KV * HW), sh(S, KV * HW), sh(S, LANES), sh(S, D), sh(T, D),
                   sh(2, dz, 2 * FF), sh(2, FF, dz)),
        in_specs=[VMEM] * (8 + m),
        out_specs=(VMEM,) * 9,
        compiler_params=pltpu.CompilerParams(vmem_limit_bytes=60 * MIB),
        cost_estimate=cost(2),
        name="finish",
    )(dh1, x, gain, dresid, pin, win, resid, ysum, *grads)


def locate(rows, lengths):
    passed = rows[:, None] >= jnp.cumsum(lengths)
    return jnp.sum(jnp.where(passed, lengths, 0), axis=-1)


def norm_rows(v, gain):
    inverse = lax.rsqrt(jnp.mean(v * v, axis=-1, keepdims=True) + EPS)
    normed = v * inverse
    return normed, inverse, normed * gain


def norm_back(upstream, normed, inverse, gain):
    d_normed = upstream * gain
    d_gain = jnp.sum(upstream * normed, axis=0)
    d_values = inverse * (d_normed - normed * jnp.mean(d_normed * normed, axis=-1, keepdims=True))
    return d_values, d_gain


def rows_of(a, start, count):
    return a if a.shape[0] == count else lax.dynamic_slice_in_dim(a, start, count, 0)


def widen(a, start, count):
    if a.shape[0] == count:
        return a
    return lax.dynamic_update_slice_in_dim(jnp.zeros((count,) + a.shape[1:], a.dtype), a, start, 0)


def on_device(tokens, lengths, routes, gain_attn, w_query, w_key, w_value, w_output, gain_moe,
              w_router, w_inner, w_outer, cotangent):
    nz = lax.axis_size("ulysses")
    nb = lax.axis_size("blk")
    z = lax.axis_index("ulysses")
    b = lax.axis_index("blk")
    T = tokens.shape[0]
    R = nb * T
    rp = nb // KV
    Rq = R // rp
    part = b % rp
    at = part * Rq
    n = nz * nb
    S = D // n
    E = w_router.shape[1]
    longest = min(LENMAX, n * T // 2)
    back = min(nz - 1, (longest - 1 + R - 1) // R)
    n_o = QCOLS // S
    odd = z % 2

    tail = jnp.concatenate(
        [w_router, gain_attn[:, None], gain_moe[:, None],
         jnp.zeros((S, AUX - ROUTER_AT - E - 2), bf16)], axis=1)
    pieces = jnp.stack([
        jnp.concatenate([
            w_query[:, h * QCOLS:(h + 1) * QCOLS], w_key[:, h * HW:(h + 1) * HW],
            w_value[:, h * HW:(h + 1) * HW], tail], axis=1)
        for h in range(KV)])
    lanes = jnp.arange(LANES, dtype=jnp.int32)
    named = jnp.any(routes[:, :, None] + HW == lanes[None, None, :], axis=1)
    cot_mask = jnp.concatenate([cotangent, named.astype(bf16)], axis=1)
    xg, packed = gather_inputs(tokens, pieces, nz, nb, 0)
    xg = xg.reshape(R, D)
    packed = packed.reshape(D, AUX)
    router = packed[:, 2 * LANES:]
    gains = packed[:, ROUTER_AT + E:ROUTER_AT + E + 2].astype(f32).T
    gain1, gain2 = gains[0:1], gains[1:2]

    experts_of = jnp.concatenate([w_inner, jnp.swapaxes(w_outer, 1, 2)], axis=2)
    flip = lambda d: [(k, k ^ d) for k in range(nz)]
    give = lambda w, d, lo, hi: lax.ppermute(
        lax.dynamic_index_in_dim(w, odd ^ (d % 2), 0, keepdims=False)[:, lo:hi], "ulysses", flip(d))
    W = 3 * FF
    experts_of, packed = lax.optimization_barrier((experts_of, packed))
    early = min(2, nz - 1)
    weights = [(lax.dynamic_index_in_dim(experts_of, odd, 0, keepdims=False), 0, 0),
               (give(experts_of, early, 0, W // 2), early, 0)]

    rows = z * R + jnp.arange(R, dtype=jnp.int32)
    opening = locate(rows, lengths)
    pair = lanes % HW
    frequency = THETA ** (-((pair % (HW // 2)).astype(f32) * 2.0 / HW))
    angles = (rows - opening).astype(f32)[:, None] * frequency[None, :]
    cos, sin = jnp.cos(angles), jnp.sin(angles)
    tables = (cos, jnp.where(pair < HW // 2, -sin, 0.0), jnp.where(pair < HW // 2, 0.0, sin))

    q, kv, h1 = project(xg, gain1, packed, *tables)
    if rp > 1:
        q = lax.dynamic_slice_in_dim(q, at, Rq, 1)
    array, *place = weights[1]
    kv, array = lax.optimization_barrier((kv, array))
    weights[1] = (array, *place)
    far, g_own, g_far, wo = halo_forward(kv, cot_mask, w_output, nz, nb, rp, back, 1)
    wo = wo.reshape(QCOLS, D)
    later, far = lax.optimization_barrier((experts_of, far))
    weights.append((give(later, early, W // 2, W), early, W // 2))
    weights += [(give(later, d, 0, W), d, 0) for d in range(1, nz) if d != early]
    kv_all = jnp.concatenate([far[d - 1] for d in range(back, 0, -1)] + [kv], axis=0)
    base = (z - back) * R
    starts = rows_of(opening, at, Rq) - base
    meta = jnp.concatenate([starts[::BQ] // BK, (back * R + at)[None]]).astype(jnp.int32)
    starts = starts[:, None]
    mixed, lse = attend(q, kv_all, starts, meta)
    attn, g_oth = reduce_product(widen(mixed, at, R), wo, g_far, nb, 2)
    g_own, g_oth = g_own.reshape(R, D + LANES), g_oth.reshape(R, D + LANES)

    resid = tokens.astype(f32) + attn
    n2, inv2, scaled2 = norm_rows(resid, gain2)
    h2_own = scaled2.astype(bf16)
    hot = (lanes == HW + b * EXP_DEV + odd).astype(f32)[None, :]
    y, summed, *grads = experts(h2_own, g_own, g_oth, router, hot, weights, nz, nb, 3)
    grads = grads[:nz]

    upstream = cotangent.astype(f32)
    dgates = summed[:, D:] + jnp.roll(summed[:, D:], HW, 1)
    logits = mm(h2_own, router)
    top = jnp.max(jnp.where(named, logits, NEG), axis=1, keepdims=True)
    w = jnp.where(named, jnp.exp(jnp.where(named, logits - top, 0.0)), 0.0)
    gates = w / jnp.sum(w, axis=1, keepdims=True)
    dlogits = gates * (dgates - jnp.sum(gates * dgates, axis=1, keepdims=True))
    dlogits = dlogits.astype(bf16)
    dh2 = summed[:, :D] + mm(dlogits, router, NT)
    d_norm2, d_gain2 = norm_back(dh2, n2, inv2, gain2)
    dresid = upstream + d_norm2
    split = min(3, nz)
    dattn, ysum, *grads[1:split] = middle(dresid.astype(bf16), y, grads[1:split], nz, nb, 5)
    dattn, *late = lax.optimization_barrier((dattn, *grads[split:]))
    grads[split:] = [lax.ppermute(a, "ulysses", flip(d)) for d, a in enumerate(late, split)]
    dattn = dattn.reshape(R, D)
    tail = mm(h2_own, dlogits, TN) + jnp.where(lanes == HW + E, d_gain2[:, None], 0.0)

    dq, dkv, dwo = attend_back(q, kv_all, starts, meta, lse, mixed, rows_of(dattn, at, Rq), wo)
    dkv, *late = lax.optimization_barrier((dkv, *grads[split:]))
    grads[split:] = late
    dkv = dkv.reshape(back + 1, R, LANES)
    dkv_out = jnp.stack([dkv[back - d] for d in range(back + 1)]).astype(bf16)
    kin = halo_back(dkv_out, nz, nb, rp, back, 6)
    ok = [(z + d < nz) if d else (part != p) for d in range(back + 1) for p in range(rp)]
    ok = jnp.stack([jnp.asarray(o).astype(jnp.int32) for o in ok] + [jnp.int32(HW + E)])
    if rp > 1:
        kin = lax.dynamic_slice_in_dim(kin, at, Rq, 1)
    turned, dw = weight_grads(
        dq, rows_of(dkv[back], at, Rq), kin, ok, [rows_of(t, at, Rq) for t in tables],
        rows_of(h1, at, Rq), packed, tail)
    dh1, pin, win = reduce_last(
        widen(turned, at, R), packed, dw.reshape(nz, nb, S, AUX),
        dwo.astype(bf16).reshape(nz, rp, S, D), nz, nb, rp, 7)
    d_tokens, d_query, d_key, d_value, small, d_output, out, d_inner, d_outer = finish(
        dh1, tokens, gain1, dresid, pin.reshape(KV, rp, S, AUX), win, resid, ysum, grads)
    return (
        out, d_tokens, small[:, HW + E + 1], d_query, d_key, d_value, d_output,
        small[:, HW + E], small[:, HW:HW + E], d_inner, d_outer,
    )


def solution(mesh):
    both = ("ulysses", "blk")
    rows = P(both, None)
    weights = (P(both), rows, rows, rows, rows, P(both), rows, P("blk", "ulysses", None), P("blk", None, "ulysses"))
    return jax.shard_map(
        on_device,
        mesh=mesh,
        in_specs=(rows, P(), rows) + weights + (rows,),
        out_specs=(rows, rows) + weights,
        check_vma=False,
    )
```

time: 549 us -> 498 us (0.907)
  Pallas kernels: 478 us -> 392 us
  waiting for transfers between devices: 0.53 us -> 46.6 us
    pallas_call x7 -> x5, Pallas kernels: 380 us -> 254 us  [the longest x1 76.5 us: experts(): pl.pallas_call(kernel, out_shape=(sh((2, nb, T, D), bf16), sh((T, C), f32...]
    ppermute x2 -> x5, waiting for transfers between devices: 0.53 us -> 46.6 us  [the longest x4 36.1 us: on_device(): lax.ppermute(lax.dynamic_index_in_dim(w, odd ^ d % 2, 0, keepdims=False)[...]
    pallas_call x1, Pallas kernels: 32.4 us -> 59.5 us  [reduce_last(): pl.pallas_call(kernel, out_shape=(sh((rows, cols), f32), sh((nb, shard, w...]
    pallas_call x1, Pallas kernels: 28 us -> 36 us  [halo_forward(): pl.pallas_call(kernel, out_shape=(sh((back,) + kv.shape, kv.dtype), sh((n...]
    pallas_call x1, Pallas kernels: 1.67 us -> 7.29 us  [finish(): pl.pallas_call(kernel, out_shape=(sh(T, D), sh(S, HEADS * HW), sh(S, KV *...]
    unnamed x128 -> x100, local copies, waits for them, and re-layouts: 19.7 us -> 15.5 us
    ppermute x2 -> x5, starting transfers between devices: 13.5 us -> 10.8 us  [the longest x4 8.9 us: on_device(): lax.ppermute(lax.dynamic_index_in_dim(w, odd ^ d % 2, 0, keepdims=False)[...]
  transfers between devices with their start and end apart: 2 -> 5, of which waited for: 1 -> 3; matrix products, arithmetic and copies ran while one was open for 2% -> 2% of each run, Pallas kernels for 11% -> 13%
where the time goes in v3:
time: 498 us; the launch traced here: 497 us
  Pallas kernels  392 us (79%)
  waiting for transfers between devices  46.6 us (9%)
  local copies, waits for them, and re-layouts  30.6 us (6%)
  other arithmetic  12.3 us (2%)
  starting transfers between devices  10.8 us (2%)
    pallas_call x1, Pallas kernels, experts(): pl.pallas_call(kernel, out_shape=(sh((2, nb, T, D), bf16), sh((T, C), f32...  76.5 us
    pallas_call x1, Pallas kernels, middle(): pl.pallas_call(kernel, out_shape=(sh((nb,) + x.shape, x.dtype), sh((rows,...  70 us
    pallas_call x1, Pallas kernels, reduce_last(): pl.pallas_call(kernel, out_shape=(sh((rows, cols), f32), sh((nb, shard, w...  59.5 us
    pallas_call x1, Pallas kernels, halo_back(): pl.pallas_call(kernel, out_shape=jax.ShapeDtypeStruct(((back + 1) * rp, R...  38.3 us
    pallas_call x1, Pallas kernels, reduce_product(): pl.pallas_call(kernel, out_shape=(sh((rows, cols), f32), sh((nb,) + gx.sh...  37 us
    ppermute x4, waiting for transfers between devices, on_device(): lax.ppermute(lax.dynamic_index_in_dim(w, odd ^ d % 2, 0, keepdims=False)[...  36.1 us
    pallas_call x1, Pallas kernels, halo_forward(): pl.pallas_call(kernel, out_shape=(sh((back,) + kv.shape, kv.dtype), sh((n...  36 us
    pallas_call x1, Pallas kernels, gather_inputs(): pl.pallas_call(kernel, out_shape=(sh((nb,) + x.shape, x.dtype), sh((nz, n...  32.2 us
  transfers between devices with their start and end apart: 5, of which 3 were waited for; matrix products, arithmetic and copies ran while one was open for 2% of the time, Pallas kernels for 13%

profile of v3, /device:TPU:1, one launch (start us, length us, event | category | flops | bytes accessed | tf_op | source)
XLA Modules:
  0.0 497.0 jit_solution(18371365399940633492)
XLA Ops:
  0.7 1.0 fusion.19
  4.0 1.0 fusion.20
  7.0 32.2 %gather_inputs.1 = (bf16[8,128,1536]{2,1,0:T(8,128)(2,1)}, bf16[4,8,48,384]{3,2,1,0:T(8,128)(2,1)}) custom-call(bf16[128,1536]{1,0:T(8,128)(2,1)} %x_ref.3, bf16[8,48,384]{2,1,0:T(8,128)(2,1)} %copy-done.42), custom_call_target="tpu_custom_call" | custom-call | flops 30000001024 | tf_op jit(solution)/shard_map/gather_inputs/pallas_call | solution.py:313
  39.2 1.6 pad_maximum_fusion
  40.9 1.0 copy-done.30
  41.9 0.9 slice.194
  42.8 5.7 %collective-permute-start = (bf16[384,768]{1,0:T(8,128)(2,1)}, bf16[384,768]{1,0:T(8,128)(2,1)}, u32[]{:S(2)}, u32[]{:S(2)}) collective-permute-start(bf16[384,768]{1,0:T(8,128)(2,1)} %slice.194), channel_id=1, source_target_pairs={{0,16},{8,24},{16,0},{24,8},{1,17},{9,25},{17,1},{25,9},{2,18},{10... | collective-permute-start | bytes 1769480 | tf_op jit(solution)/shard_map/ppermute | solution.py:1250
  51.5 0.8 pad_maximum_fusion.3.g_ref
  52.3 1.9 fusion
  54.3 2.4 copy-done.22
  56.7 4.0 project.1
  60.8 1.7 copy-done.1
  63.1 11.9 %collective-permute-done.rest_1_ = bf16[384,768]{1,0:T(8,128)(2,1)} collective-permute-done((bf16[384,768]{1,0:T(8,128)(2,1)}, bf16[384,768]{1,0:T(8,128)(2,1)}, u32[]{:S(2)}, u32[]{:S(2)}) %collective-permute-start) | collective-permute-done | bytes 589856 | tf_op jit(solution)/shard_map/ppermute | solution.py:1250
  75.0 36.0 %halo_forward.1 = (bf16[2,1024,128]{2,1,0:T(8,128)(2,1)}, bf16[8,128,1664]{2,1,0:T(8,128)(2,1)}, bf16[128,1664]{1,0:T(8,128)(2,1)}, bf16[4,48,1536]{2,1,0:T(8,128)(2,1)}) custom-call(bf16[1024,128]{1,0:T(8,128)(2,1)} %copy-done.17, bf16[128,1664]{1,0:T(8,128)(2,1)} %pad_maximum_fusion.3.g_ref, bf16[48,1536]{1,0:T(8,128)(2,1)} %w_ref.1), custom_call_target="tpu_custom_call" | custom-call | flops 30000001024 | tf_op jit(solution)/shard_map/halo_forward/pallas_call | solution.py:390
  111.1 2.9 dynamic-slice_bitcast_fusion
  114.0 2.2 collective-permute-start.2
  116.3 8.6 %attend.1 = (bf16[1024,192]{1,0:T(8,128)(2,1)S(1)}, f32[3,1024,1]{2,1,0:T(8,128)S(1)}) custom-call(s32[5]{0:T(128)S(1)} %pad_add_fusion.1.meta, bf16[3,1024,128]{2,1,0:T(8,128)(2,1)S(1)} %get-tuple-element.64.q_ref, bf16[3072,128]{1,0:T(8,128)(2,1)S(1)} %pad_maximum_fusion.1.kv_ref, s32[1024,1]{1,0:T(8,128)S(1)} %copy.120.st_ref), custom_call_target="tpu_custom_call" | custom-call | flops 16999999488 | tf_op jit(solution)/shard_map/attend/pallas_call | solution.py:796
  124.9 1.1 copy-done.10
  126.1 37.0 %reduce_product.1 = (f32[128,1536]{1,0:T(8,128)S(1)}, bf16[8,128,1664]{2,1,0:T(8,128)(2,1)S(1)}) custom-call(bf16[1024,192]{1,0:T(8,128)(2,1)S(1)} %get-tuple-element.71.l_ref.o_ref, bf16[192,1536]{1,0:T(8,128)(2,1)S(1)} %bitcast.61, bf16[128,1664]{1,0:T(8,128)(2,1)S(1)} %copy-done.23), custom_call_target="tpu_custom_call" | custom-call | flops 30000001024 | tf_op jit(solution)/shard_map/reduce_product/pallas_call | solution.py:450
  163.1 1.8 copy-done.21
  165.1 0.9 slice.197
  166.0 1.0 collective-permute-start.1
  167.2 1.5 select_reduce_fusion
  168.7 0.9 copy.119
  169.6 0.9 fusion.5
  170.5 24.2 %collective-permute-done.1.rest_2_ = bf16[384,768]{1,0:T(8,128)(2,1)} collective-permute-done((bf16[384,768]{1,0:T(8,128)(2,1)}, bf16[384,768]{1,0:T(8,128)(2,1)}, u32[]{:S(2)}, u32[]{:S(2)}) %collective-permute-start.1) | collective-permute-done | bytes 589856 | tf_op jit(solution)/shard_map/ppermute | solution.py:1250
  194.7 76.5 %experts.1 = (bf16[2,8,128,1536]{3,2,1,0:T(8,128)(2,1)}, f32[128,1664]{1,0:T(8,128)}, bf16[384,1536]{1,0:T(8,128)(2,1)}, bf16[384,1536]{1,0:T(8,128)(2,1)}, bf16...) custom-call(bf16[128,1536]{1,0:T(8,128)(2,1)} %copy-done.28, bf16[1024,1664]{1,0:T(8,128)(2,1)} %bitcast.76, ...), custom_call_target="tpu_custom_call" | custom-call | flops 70000001024 | tf_op jit(solution)/shard_map/experts/pallas_call | solution.py:1113
  271.2 1.0 fusion.18
  272.2 1.0 multiply_reduce_fusion.3
  273.3 1.1 multiply_convert_fusion.1
  274.4 1.8 multiply_reduce_fusion
  276.2 1.3 fusion.17
  277.5 70.0 %middle.1 = (bf16[8,128,1536]{2,1,0:T(8,128)(2,1)}, f32[128,1536]{1,0:T(8,128)}, bf16[384,1536]{1,0:T(8,128)(2,1)}, bf16[384,1536]{1,0:T(8,128)(2,1)}) custom-call(bf16[128,1536]{1,0:T(8,128)(2,1)} %get-tuple-element.148.x_ref, bf16[2,8,128,1536]{3,2,1,0:T(8,128)(2,1)} %get-tuple-element.80.y_ref, bf16[384,1536]{1,0:T(8,128)(2,1)} %get-tuple-element.81.rest_0_, ...), custom_call_target="tpu_custom_call" | custom-call | flops 49999998976 | tf_op jit(solution)/shard_map/middle/pallas_call | solution.py:505
  347.5 1.9 collective-permute-start.4
  349.4 15.5 %attend_back.1 = (bf16[3,1024,128]{2,1,0:T(8,128)(2,1)S(1)}, f32[3072,128]{1,0:T(8,128)}, f32[192,1536]{1,0:T(8,128)S(1)}) custom-call(s32[5]{0:T(128)S(1)} %pad_add_fusion.1.meta, bf16[3,1024,128]{2,1,0:T(8,128)(2,1)S(1)} %get-tuple-element.64.q_ref, bf16[3072,128]{1,0:T(8,128)(2,1)S(1)} %copy-done.3, s32[1024,1]{1,0:T(8,128)S(1)} %copy.120.st_ref, ...), custom_call_target="tpu_custom_call" | custom-call | flops 2000000000 | tf_op jit(solution)/shard_map/attend_back/pallas_call | solution.py:867
  364.9 0.9 convert_element_type.59
  366.2 10.5 %collective-permute-done.4.rest_3_ = bf16[384,1536]{1,0:T(8,128)(2,1)S(1)} collective-permute-done((bf16[384,1536]{1,0:T(8,128)(2,1)}, bf16[384,1536]{1,0:T(8,128)(2,1)S(1)}, u32[]{:S(2)}, u32[]{:S(2)}) %collective-permute-start.4) | collective-permute-done | bytes 1179680 | tf_op jit(solution)/shard_map/ppermute | solution.py:1307
  376.8 0.9 copy-done.34
  377.8 1.0 pad_maximum_fusion.2.d_ref
  378.8 38.3 %halo_back.1.kin_ref = bf16[3,1024,128]{2,1,0:T(8,128)(2,1)} custom-call(bf16[3,1024,128]{2,1,0:T(8,128)(2,1)} %pad_maximum_fusion.2.d_ref), custom_call_target="tpu_custom_call" | custom-call | flops 24999999488 | tf_op jit(solution)/shard_map/halo_back/pallas_call | solution.py:557
  417.1 1.1 copy-done.12
  418.3 1.1 copy-done.13
  419.4 6.9 %weight_grads.1 = (bf16[1024,384]{1,0:T(8,128)(2,1)S(1)}, bf16[1536,384]{1,0:T(8,128)(2,1)}) custom-call(s32[4]{0:T(128)S(1)} %get-tuple-element.195.ok_ref, bf16[3,1024,128]{2,1,0:T(8,128)(2,1)S(1)} %copy-done.12, f32[1024,128]{1,0:T(8,128)S(1)} %slice.183.dkv_ref, bf16[3,1024,128]{2,1,0:T(8,128)(2,1)S(1)} %copy-done.13, f32[1024,128]{1,0:T(8,128)S(1)} %copy-done.9, ...), custom_call_target="tpu_custom_call" | custom-call | flops 2000000000 | tf_op jit(solution)/shard_map/weight_grads/pallas_call | solution.py:924
  426.3 0.9 copy-done.20
  427.2 59.5 %reduce_last.1 = (f32[128,1536]{1,0:T(8,128)}, bf16[8,48,384]{2,1,0:T(8,128)(2,1)}, bf16[1,48,1536]{2,1,0:T(8,128)(2,1)}) custom-call(bf16[1024,384]{1,0:T(8,128)(2,1)} %copy-done.20, bf16[1536,384]{1,0:T(8,128)(2,1)} %bitcast.55, bf16[4,8,48,384]{3,2,1,0:T(8,128)(2,1)} %bitcast.75, bf16[4,1,48,1536]{3,2,1,0:T(8,128)(2,1)} %bitcast.67), custom_call_target="tpu_custom_call" | custom-call | flops 2000000000 | tf_op jit(solution)/shard_map/reduce_last/pallas_call | solution.py:659
  486.7 7.3 %finish.1 = (f32[128,1536]{1,0:T(8,128)}, f32[48,1536]{1,0:T(8,128)}, f32[48,512]{1,0:T(8,128)}, f32[48,512]{1,0:T(8,128)}, f32[48,128]{1,0:T(8,128)}, /*index=5...) custom-call(f32[128,1536]{1,0:T(8,128)} %get-tuple-element.94.d_ref, ...), custom_call_target="tpu_custom_call" | custom-call | flops 2000000000 | tf_op jit(solution)/shard_map/finish/pallas_call | solution.py:1170
  494.0 1.5 slice_reduce_fusion
  495.5 0.8 slice.191
  (139 shorter events, 9.9 us)
Async XLA Ops:
  0.6 4.5 copy-start.35
  40.8 2.0 copy-start.26
  40.8 7.7 %copy-start = (bf16[4,8,48,384]{3,2,1,0:T(8,128)(2,1)S(1)}, bf16[4,8,48,384]{3,2,1,0:T(8,128)(2,1)}, u32[]{:S(2)}) copy-start(bf16[4,8,48,384]{3,2,1,0:T(8,128)(2,1)} %get-tuple-element.62) | copy-start | bytes 3538948
  40.9 1.0 copy-start.30
  41.9 7.5 %copy-start.43 = (s32[128,8]{0,1:T(8,128)S(1)}, s32[128,8]{0,1:T(8,128)}, u32[]{:S(2)}) copy-start(s32[128,8]{0,1:T(8,128)} %param.15) | copy-start | bytes 12292
  41.9 8.0 %copy-start.44 = (s32[3]{0:T(128)S(1)}, s32[3]{0:T(128)}, u32[]{:S(2)}) copy-start(s32[3]{0:T(128)} %param.14) | copy-start | bytes 40
  42.8 32.2 %collective-permute-start = (bf16[384,768]{1,0:T(8,128)(2,1)}, bf16[384,768]{1,0:T(8,128)(2,1)}, u32[]{:S(2)}, u32[]{:S(2)}) collective-permute-start(bf16[384,768]{1,0:T(8,128)(2,1)} %slice.194), channel_id=1, source_target_pairs={{0,16},{8,24},{16,0},{24,8},{1,17},{9,25},{17,1},{25,9},{2,18},{10... | collective-permute-start | bytes 1769480 | tf_op jit(solution)/shard_map/ppermute | solution.py:1250
  48.5 3.1 copy-start.32
  49.8 0.8 copy-start.36
  54.3 6.5 %copy-start.4 = (f32[1024,128]{1,0:T(8,128)}, f32[1024,128]{1,0:T(8,128)S(1)}, u32[]{:S(2)}) copy-start(f32[1024,128]{1,0:T(8,128)S(1)} %get-tuple-element.186.b_ref) | copy-start | bytes 1572868
  54.3 6.5 %copy-start.6 = (f32[1024,128]{1,0:T(8,128)}, f32[1024,128]{1,0:T(8,128)S(1)}, u32[]{:S(2)}) copy-start(f32[1024,128]{1,0:T(8,128)S(1)} %get-tuple-element.187.a_ref) | copy-start | bytes 1572868
  54.3 6.5 %copy-start.8 = (f32[1024,128]{1,0:T(8,128)}, f32[1024,128]{1,0:T(8,128)S(1)}, u32[]{:S(2)}) copy-start(f32[1024,128]{1,0:T(8,128)S(1)} %get-tuple-element.188.c_ref) | copy-start | bytes 1572868
  54.3 6.4 %copy-start.19 = (f32[1,1536]{1,0:T(1,128)}, f32[1,1536]{1,0:T(1,128)S(1)}, u32[]{:S(2)}) copy-start(f32[1,1536]{1,0:T(1,128)S(1)} %get-tuple-element.185.g_ref) | copy-start | bytes 18436
  54.3 2.4 copy-start.22
  60.8 1.7 copy-start.1
  111.1 5.1 %copy-start.38 = (bf16[2,1024,128]{2,1,0:T(8,128)(2,1)S(1)}, bf16[2,1024,128]{2,1,0:T(8,128)(2,1)}, u32[]{:S(2)}) copy-start(bf16[2,1024,128]{2,1,0:T(8,128)(2,1)} %get-tuple-element.69) | copy-start | bytes 1572868
  111.1 5.2 %copy-start.18 = (bf16[1024,128]{1,0:T(8,128)(2,1)S(1)}, bf16[1024,128]{1,0:T(8,128)(2,1)}, u32[]{:S(2)}) copy-start(bf16[1024,128]{1,0:T(8,128)(2,1)} %copy-done.17) | copy-start | bytes 786436
  114.0 80.7 %collective-permute-start.2 = (bf16[384,1536]{1,0:T(8,128)(2,1)}, bf16[384,1536]{1,0:T(8,128)(2,1)}, u32[]{:S(2)}, u32[]{:S(2)}) collective-permute-start(bf16[384,1536]{1,0:T(8,128)(2,1)} %get-tuple-element.152), channel_id=1, source_target_pairs={{0,8},{8,0},{16,24},{24,16},{1,9},{9,1},{17,25},{25,17},{2,10},{10... | collective-permute-start | bytes 3538952 | tf_op jit(solution)/shard_map/ppermute | solution.py:1250
  116.2 78.5 %collective-permute-start.3 = (bf16[384,1536]{1,0:T(8,128)(2,1)}, bf16[384,1536]{1,0:T(8,128)(2,1)}, u32[]{:S(2)}, u32[]{:S(2)}) collective-permute-start(bf16[384,1536]{1,0:T(8,128)(2,1)} %get-tuple-element.152), channel_id=1, source_target_pairs={{0,24},{8,16},{16,8},{24,0},{1,25},{9,17},{17,9},{25,1},{2,26},{10... | collective-permute-start | bytes 3538952 | tf_op jit(solution)/shard_map/ppermute | solution.py:1250
  116.3 8.6 %copy-start.2 = (bf16[3072,128]{1,0:T(8,128)(2,1)}, bf16[3072,128]{1,0:T(8,128)(2,1)S(1)}, u32[]{:S(2)}) copy-start(bf16[3072,128]{1,0:T(8,128)(2,1)S(1)} %pad_maximum_fusion.1.kv_ref) | copy-start | bytes 2359300
  116.3 9.8 %copy-start.14 = (bf16[4,48,1536]{2,1,0:T(8,128)(2,1)S(1)}, bf16[4,48,1536]{2,1,0:T(8,128)(2,1)}, u32[]{:S(2)}) copy-start(bf16[4,48,1536]{2,1,0:T(8,128)(2,1)} %get-tuple-element.72) | copy-start | bytes 1769476
  116.3 9.8 %copy-start.23 = (bf16[128,1664]{1,0:T(8,128)(2,1)S(1)}, bf16[128,1664]{1,0:T(8,128)(2,1)}, u32[]{:S(2)}) copy-start(bf16[128,1664]{1,0:T(8,128)(2,1)} %get-tuple-element.73.g_ref) | copy-start | bytes 1277956
  124.9 1.1 copy-start.10
  126.1 37.0 %copy-start.15 = (bf16[1024,192]{1,0:T(8,128)(2,1)}, bf16[1024,192]{1,0:T(8,128)(2,1)S(1)}, u32[]{:S(2)}) copy-start(bf16[1024,192]{1,0:T(8,128)(2,1)S(1)} %get-tuple-element.71.l_ref.o_ref) | copy-start | bytes 1179652
  126.1 38.9 %copy-start.31 = (bf16[128,1536]{1,0:T(8,128)(2,1)S(1)}, bf16[128,1536]{1,0:T(8,128)(2,1)}, u32[]{:S(2)}) copy-start(bf16[128,1536]{1,0:T(8,128)(2,1)} %x_ref.3) | copy-start | bytes 1179652
  163.1 1.8 copy-start.21
  165.1 3.6 copy-start.24
  166.0 28.6 %collective-permute-start.1 = (bf16[384,768]{1,0:T(8,128)(2,1)}, bf16[384,768]{1,0:T(8,128)(2,1)}, u32[]{:S(2)}, u32[]{:S(2)}) collective-permute-start(bf16[384,768]{1,0:T(8,128)(2,1)} %slice.197), channel_id=1, source_target_pairs={{0,16},{8,24},{16,0},{24,8},{1,17},{9,25},{17,1},{25,9},{2,18},{10... | collective-permute-start | bytes 1769480 | tf_op jit(solution)/shard_map/ppermute | solution.py:1250
  167.1 1.6 copy-start.40
  167.2 27.5 %copy-start.28 = (bf16[128,1536]{1,0:T(8,128)(2,1)}, bf16[128,1536]{1,0:T(8,128)(2,1)S(1)}, u32[]{:S(2)}) copy-start(bf16[128,1536]{1,0:T(8,128)(2,1)S(1)} %multiply_convert_fusion.x_ref) | copy-start | bytes 1179652
  194.7 77.5 %copy-start.37 = (pred[128,128]{1,0:T(8,128)(4,1)S(1)}, pred[128,128]{1,0:T(8,128)(4,1)}, u32[]{:S(2)}) copy-start(pred[128,128]{1,0:T(8,128)(4,1)} %copy-done.36) | copy-start | bytes 49156
  194.7 77.5 %copy-start.39 = (f32[128]{0:T(128)S(1)}, f32[128]{0:T(128)}, u32[]{:S(2)}) copy-start(f32[128]{0:T(128)} %get-tuple-element.191) | copy-start | bytes 1540
  194.7 79.7 %copy-start.41 = (f32[128]{0:T(128)S(1)}, f32[128]{0:T(128)}, u32[]{:S(2)}) copy-start(f32[128]{0:T(128)} %copy-done.40) | copy-start | bytes 1540
  273.3 2.9 copy-start.25
  273.3 2.9 copy-start.33
  277.5 71.8 %copy-start.3 = (bf16[3072,128]{1,0:T(8,128)(2,1)S(1)}, bf16[3072,128]{1,0:T(8,128)(2,1)}, u32[]{:S(2)}) copy-start(bf16[3072,128]{1,0:T(8,128)(2,1)} %copy-done.2) | copy-start | bytes 2359300
  277.5 71.8 %copy-start.16 = (bf16[1024,192]{1,0:T(8,128)(2,1)S(1)}, bf16[1024,192]{1,0:T(8,128)(2,1)}, u32[]{:S(2)}) copy-start(bf16[1024,192]{1,0:T(8,128)(2,1)} %copy-done.15) | copy-start | bytes 1179652
  347.5 29.2 %collective-permute-start.4 = (bf16[384,1536]{1,0:T(8,128)(2,1)}, bf16[384,1536]{1,0:T(8,128)(2,1)S(1)}, u32[]{:S(2)}, u32[]{:S(2)}) collective-permute-start(bf16[384,1536]{1,0:T(8,128)(2,1)} %get-tuple-element.88), channel_id=1, source_target_pairs={{0,24},{8,16},{16,8},{24,0},{1,25},{9,17},{17,9},{25,1},{2,26},{10... | collective-permute-start | bytes 3538952 | tf_op jit(solution)/shard_map/ppermute | solution.py:1307
  349.4 16.4 %copy-start.29 = (bf16[128,1536]{1,0:T(8,128)(2,1)S(1)}, bf16[128,1536]{1,0:T(8,128)(2,1)}, u32[]{:S(2)}) copy-start(bf16[128,1536]{1,0:T(8,128)(2,1)} %copy-done.28) | copy-start | bytes 1179652
  364.9 11.8 %copy-start.11 = (bf16[3,1024,128]{2,1,0:T(8,128)(2,1)}, bf16[3,1024,128]{2,1,0:T(8,128)(2,1)S(1)}, u32[]{:S(2)}) copy-start(bf16[3,1024,128]{2,1,0:T(8,128)(2,1)S(1)} %get-tuple-element.86.dq_ref) | copy-start | bytes 2359300
  364.9 11.8 %copy-start.27 = (f32[3072,128]{1,0:T(8,128)S(1)}, f32[3072,128]{1,0:T(8,128)}, u32[]{:S(2)}) copy-start(f32[3072,128]{1,0:T(8,128)} %get-tuple-element.89) | copy-start | bytes 4718596
  376.7 1.1 copy-start.34
  378.8 38.3 %copy-start.5 = (f32[1024,128]{1,0:T(8,128)S(1)}, f32[1024,128]{1,0:T(8,128)}, u32[]{:S(2)}) copy-start(f32[1024,128]{1,0:T(8,128)} %copy-done.4) | copy-start | bytes 1572868
  378.8 38.3 %copy-start.7 = (f32[1024,128]{1,0:T(8,128)S(1)}, f32[1024,128]{1,0:T(8,128)}, u32[]{:S(2)}) copy-start(f32[1024,128]{1,0:T(8,128)} %copy-done.6) | copy-start | bytes 1572868
  378.8 38.3 %copy-start.9 = (f32[1024,128]{1,0:T(8,128)S(1)}, f32[1024,128]{1,0:T(8,128)}, u32[]{:S(2)}) copy-start(f32[1024,128]{1,0:T(8,128)} %copy-done.8) | copy-start | bytes 1572868
  417.1 1.1 copy-start.12
  418.3 1.1 copy-start.13
  426.3 0.9 copy-start.20
  (2 other events, 1.4 us)

commit v4 on v3

--- a/solution.py
+++ b/solution.py
@@ -32,6 +32,7 @@
 VMEM = pl.BlockSpec(memory_space=pltpu.VMEM)
 DMA = pltpu.SemaphoreType.DMA
 MIB = 1 << 20
+NO_COST = pl.CostEstimate(flops=0, bytes_accessed=0, transcendentals=0)
 
 
 def dev(u, b):
@@ -43,10 +44,6 @@
         src_ref=src, dst_ref=dst, send_sem=ss, recv_sem=rs,
         device_id=dev(u, b), device_id_type=MESH,
     )
-
-
-def cost(us):
-    return pl.CostEstimate(flops=us * 1_000_000_000, bytes_accessed=0, transcendentals=0)
 
 
 def signal(sem, u, b):
@@ -248,14 +245,14 @@
                 self.copy(k).wait_send()
 
 
-def made(me, block, mine, sib_out, sib_in, snd, land, sems):
+def made(me, block, mine, sib_out, sib_in, snd, land, sems, waits=True):
     red = Reduce(me, lambda j, rows: mine[j, rows], lambda j: sib_out.at[j], sib_in, snd, land, sems)
     for j in red.order:
         sib_out[j] = block(me.unit(j) * 2 + 1 - me.core).astype(bf16)
         red.start(j)
     for j in red.order:
         mine[j] = block(me.far(j))
-        if j:
+        if j and waits:
             red.phase1(j)
     return red
 
@@ -271,63 +268,13 @@
     return c
 
 
-def gather_inputs(x, pieces, nz, nb, cid):
+def gather_inputs(x, pieces, wo, gm, expert, swap_d, nz, nb, cid):
     groups, shard, _ = pieces.shape
     rp = nb // groups
-
-    def kernel(x_ref, p_ref, xo, po, gs, ps, pr, zs, ls):
-        me = Layer(nb)
-        bar = pltpu.get_barrier_semaphore()
-        for i in range(1, nb):
-            signal(bar, me.u, lax.rem(me.b + i, nb))
-        for i in range(1, nz):
-            signal(bar, lax.rem(me.u + i, nz), me.b)
-        pl.semaphore_wait(bar, nb + nz - 2)
-
-        def piece(i):
-            tb = lax.rem(me.b + i, nb)
-            return remote(p_ref.at[tb // rp], po.at[me.u, me.b], ps.at[i], pr.at[i], me.u, tb)
-
-        for i in range(1, nb):
-            piece(i).start()
-        own = pltpu.make_async_copy(p_ref.at[me.b // rp], po.at[me.u, me.b], ls.at[0])
-        own.start()
-        g = Gather(me, x_ref, xo, gs)
-        g.start()
-        for i in range(1, nb):
-            piece(i).wait()
-        own.wait()
-        slabs = []
-        for zo in range(1, nz):
-            c = remote(po.at[me.u], po.at[me.u], zs.at[0, zo], zs.at[1, zo], lax.rem(me.u + zo, nz), me.b)
-            c.start()
-            slabs.append(c)
-        xk = keep(me, x_ref, xo, ls.at[1])
-        g.rest()
-        g.finish()
-        for c in slabs:
-            c.wait()
-        xk.wait()
-
-    sh = jax.ShapeDtypeStruct
-    return pl.pallas_call(
-        kernel,
-        out_shape=(sh((nb,) + x.shape, x.dtype), sh((nz, nb, shard, AUX), bf16)),
-        in_specs=[ANY] * 2,
-        out_specs=(ANY,) * 2,
-        scratch_shapes=[Gather.scratch(nb)] + [DMA((nb,))] * 2 + [DMA((2, nz)), DMA((2,))],
-        compiler_params=pltpu.CompilerParams(collective_id=cid, has_side_effects=True),
-        cost_estimate=cost(30),
-        name="gather_inputs",
-    )(x, pieces)
-
-
-def halo_forward(kv, gm, wo, nz, nb, rp, back, cid):
-    shard = wo.shape[0]
     n_o = QCOLS // shard
     n = nz * nb
 
-    def kernel(x_ref, g_ref, w_ref, o_ref, go, gx, wo_out, ks, kr, gs, ws, wr, ls):
+    def kernel(x_ref, p_ref, w_ref, g_ref, e_ref, xo, po, wo_out, go, gx, eo, gs, ps, pr, zs, zr, ws, wr, ls):
         me = Layer(nb)
         lin = me.u * nb + me.b
         u, b = me.u, me.b
@@ -340,18 +287,53 @@
 
         pl.semaphore_wait(bar, n - 1)
 
-        def copy(d):
-            return remote(x_ref, o_ref.at[d - 1], ks.at[d - 1], kr.at[d - 1], u + d, b)
-
-        for d in range(1, back + 1):
-            pl.when(u + d < nz)(lambda d=d: copy(d).start())
+        def piece(i):
+            tb = lax.rem(b + i, nb)
+            return remote(p_ref.at[tb // rp], po.at[u, b], ps.at[i], pr.at[i], u, tb)
+
+        for i in range(1, nb):
+            piece(i).start()
+        own = pltpu.make_async_copy(p_ref.at[b // rp], po.at[u, b], ls.at[0])
+        own.start()
+        g = Gather(me, x_ref, xo, gs.at[0])
+        g.start()
+        cot = Gather(me, g_ref, go, gs.at[1])
+        for i in range(1, nb):
+            piece(i).wait()
+        own.wait()
+
+        def up(k):
+            o = u - k + 1
+            return remote(po.at[o], po.at[o], zs.at[0, k], zr.at[0, k], u + 1, b)
+
+        def down(k):
+            o = u + k - 1
+            return remote(po.at[o], po.at[o], zs.at[1, k], zr.at[1, k], u - 1, b)
+
+        def here(way, k):
+            remote(po.at[u], po.at[u], zs.at[way, k], zr.at[way, k], u, me.sib).wait_recv()
+
+        def relay(k):
+            if k > 1:
+                pl.when(u >= k - 1)(lambda: here(0, k - 1))
+                pl.when(u + k - 1 < nz)(lambda: here(1, k - 1))
+            pl.when((u >= k - 1) & (u + 1 < nz))(lambda: up(k).start())
+            pl.when((u + k - 1 < nz) & (u > 0))(lambda: down(k).start())
+
+        relay(1)
         hg = lin // n_o
         slot = lax.rem(lin, n_o)
 
         def weight(zo, p):
-            tz, tb = lax.rem(me.u + zo, nz), hg * rp + p
+            tz, tb = lax.rem(u + zo, nz), hg * rp + p
             return tb, remote(w_ref, wo_out.at[slot], ws.at[zo * rp + p], wr.at[slot], tz, tb)
 
+        g.relay1()
+        for k in range(2, nz):
+            relay(k)
+            if k == 2:
+                g.relay2()
+                cot.start()
         stay = pltpu.make_async_copy(w_ref, wo_out.at[slot], ls.at[1])
         for zo in range(nz):
             for p in range(rp):
@@ -361,17 +343,21 @@
                 else:
                     pl.when(tb != b)(c.start)
                     pl.when(tb == b)(stay.start)
-        mate = remote(g_ref, gx, ls.at[2], ls.at[3], me.across(1), b)
+        mate = remote(g_ref, gx, ls.at[4], ls.at[5], me.across(1), b)
         mate.start()
-        g = Gather(me, g_ref, go, gs)
-        g.start()
-        own = keep(me, g_ref, go, ls.at[0])
-        g.rest()
+        half = remote(e_ref, eo, ls.at[6], ls.at[7], me.across(swap_d), b)
+        half.start()
+        xk = keep(me, x_ref, xo, ls.at[2])
+        gk = keep(me, g_ref, go, ls.at[3])
+        g.relay3()
+        cot.rest()
         g.finish()
-        own.wait()
-        for d in range(1, back + 1):
-            pl.when(u + d < nz)(lambda d=d: copy(d).wait_send())
-            pl.when(u >= d)(lambda d=d: copy(d).wait_recv())
+        cot.finish()
+        pl.when(u >= nz - 1)(lambda: here(0, nz - 1))
+        pl.when(u + nz - 1 < nz)(lambda: here(1, nz - 1))
+        for k in range(1, nz):
+            pl.when((u >= k - 1) & (u + 1 < nz))(lambda k=k: up(k).wait_send())
+            pl.when((u + k - 1 < nz) & (u > 0))(lambda k=k: down(k).wait_send())
         for zo in range(nz):
             for p in range(rp):
                 tb, c = weight(zo, p)
@@ -384,22 +370,73 @@
             src = (b // rp) * n_o + j
             c = remote(w_ref, wo_out.at[j], ws.at[0], wr.at[j], u, me.sib)
             pl.when(src != lin)(c.wait_recv)
-        mate.wait()
+        for c in (mate, half, xk, gk):
+            c.wait()
 
     sh = jax.ShapeDtypeStruct
     return pl.pallas_call(
         kernel,
         out_shape=(
-            sh((back,) + kv.shape, kv.dtype), sh((nb,) + gm.shape, gm.dtype), sh(gm.shape, gm.dtype),
-            sh((n_o, shard, D), bf16),
+            sh((nb,) + x.shape, x.dtype), sh((nz, nb, shard, AUX), bf16), sh((n_o, shard, D), bf16),
+            sh((nb,) + gm.shape, gm.dtype), sh(gm.shape, gm.dtype), sh(expert.shape, bf16),
         ),
-        in_specs=[ANY] * 3,
-        out_specs=(ANY,) * 4,
-        scratch_shapes=[DMA((back,))] * 2 + [Gather.scratch(nb), DMA((nz * rp,)), DMA((n_o,)), DMA((4,))],
+        in_specs=[ANY] * 5,
+        out_specs=(ANY,) * 6,
+        scratch_shapes=[Gather.scratch(nb, 2)]
+        + [DMA((nb,))] * 2
+        + [DMA((2, nz))] * 2
+        + [DMA((nz * rp,)), DMA((n_o,)), DMA((8,))],
         compiler_params=pltpu.CompilerParams(collective_id=cid, has_side_effects=True),
-        cost_estimate=cost(30),
+        cost_estimate=NO_COST,
+        name="gather_inputs",
+    )(x, pieces, wo, gm, expert)
+
+
+def halo_forward(kv, gx, nz, nb, back, cid):
+    def kernel(x_ref, g_ref, o_ref, go, ks, kr, gs, ls):
+        me = Layer(nb)
+        u, b = me.u, me.b
+        bar = pltpu.get_barrier_semaphore()
+        for d in range(1, nz):
+            signal(bar, lax.rem(u + d, nz), b)
+        for i in range(1, me.nc):
+            signal(bar, u, me.peer(i))
+        signal(bar, u, me.sib)
+        pl.semaphore_wait(bar, nz - 1 + me.nc)
+
+        def copy(d):
+            src = x_ref if d == 1 else o_ref.at[d - 2]
+            return remote(src, o_ref.at[d - 1], ks.at[d - 1], kr.at[d - 1], u + 1, b)
+
+        def relay(d):
+            if d > 1:
+                pl.when(u >= d - 1)(lambda: copy(d - 1).wait_recv())
+            pl.when((u >= d - 1) & (u + 1 < nz))(lambda: copy(d).start())
+
+        relay(1)
+        g = Gather(me, g_ref, go, gs)
+        g.start()
+        own = keep(me, g_ref, go, ls)
+        for d in range(2, back + 1):
+            relay(d)
+        g.rest()
+        g.finish()
+        own.wait()
+        pl.when(u >= back)(lambda: copy(back).wait_recv())
+        for d in range(1, back + 1):
+            pl.when((u >= d - 1) & (u + 1 < nz))(lambda d=d: copy(d).wait_send())
+
+    sh = jax.ShapeDtypeStruct
+    return pl.pallas_call(
+        kernel,
+        out_shape=(sh((back,) + kv.shape, kv.dtype), sh((nb,) + gx.shape, gx.dtype)),
+        in_specs=[ANY] * 2,
+        out_specs=(ANY,) * 2,
+        scratch_shapes=[DMA((back,))] * 2 + [Gather.scratch(nb), DMA],
+        compiler_params=pltpu.CompilerParams(collective_id=cid, has_side_effects=True),
+        cost_estimate=NO_COST,
         name="halo_forward",
-    )(kv, gm, wo)
+    )(kv, gx)
 
 
 def pair_of(me, p_ref, sib_in, snd, land, sems):
@@ -423,11 +460,11 @@
     return write
 
 
-def reduce_product(lhs, rhs, gx, nb, cid):
+def reduce_product(lhs, rhs, nb, cid):
     rows = lhs.shape[0] // nb
     cols = rhs.shape[1]
 
-    def kernel(l_ref, r_ref, g_ref, o_ref, go, gs, ls, *scratch):
+    def kernel(l_ref, r_ref, o_ref, *scratch):
         me = Layer(nb)
         me.enter()
 
@@ -436,92 +473,71 @@
             return jnp.dot(part, r_ref[...], preferred_element_type=f32)
 
         red = made(me, block, *scratch)
-        g = Gather(me, g_ref, go, gs)
-        g.start()
-        own = keep(me, g_ref, go, ls)
         red.phase2()
-        g.rest()
         red.end(write_to(o_ref))
         red.sent()
-        g.finish()
-        own.wait()
-
-    sh = jax.ShapeDtypeStruct
+
     return pl.pallas_call(
         kernel,
-        out_shape=(sh((rows, cols), f32), sh((nb,) + gx.shape, gx.dtype)),
-        in_specs=[VMEM, VMEM, ANY],
-        out_specs=(VMEM, ANY),
-        scratch_shapes=[Gather.scratch(nb), DMA] + made_scratch(nb, rows, cols),
+        out_shape=jax.ShapeDtypeStruct((rows, cols), f32),
+        in_specs=[VMEM, VMEM],
+        out_specs=VMEM,
+        scratch_shapes=made_scratch(nb, rows, cols),
         compiler_params=pltpu.CompilerParams(
             collective_id=cid, has_side_effects=True, vmem_limit_bytes=48 * MIB
         ),
-        cost_estimate=cost(30),
+        cost_estimate=NO_COST,
         name="reduce_product",
-    )(lhs, rhs, gx)
-
-
-def middle(x, ypart, grads, nz, nb, cid):
+    )(lhs, rhs)
+
+
+def middle(x, ypart, nb, cid):
     _, _, rows, cols = ypart.shape
-    m = len(grads)
-
-    def kernel(x_ref, y_ref, *rest):
-        srcs, xo, o_ref, dsts = rest[:m], rest[m], rest[m + 1], rest[m + 2:2 * m + 2]
-        gs, ls, ws, zs, zbuf, *pair = rest[2 * m + 2:]
+
+    def kernel(x_ref, y_ref, xo, o_ref, z_ref, gs, ls, *pair):
         me = Layer(nb)
-        me.enter(range(1, m + 1))
+        me.enter()
         g = Gather(me, x_ref, xo, gs)
         g.start()
         r0, r1 = pair_of(me, y_ref, *pair)
         for r in (r1, r0):
             for j in r.order:
                 r.start(j)
-        moved = [
-            remote(srcs[k], dsts[k], ws.at[0, k], ws.at[1, k], me.across(k + 1), me.b) for k in range(m)
-        ]
-        for c in reversed(moved):
-            c.start()
         own = keep(me, x_ref, xo, ls)
+        for j in r1.order[:-1]:
+            r1.phase1(j)
         g.rest()
-        for r in (r1, r0):
-            for j in r.order[:-1]:
-                r.phase1(j)
         r1.phase2()
+        for j in r0.order[:-1]:
+            r0.phase1(j)
         r0.phase2()
-        r1.end(write_to(zbuf, 0))
-        mate = remote(zbuf.at[0], zbuf.at[1], zs.at[0], zs.at[1], me.across(1), me.b)
-        mate.start()
-        mate.wait_recv()
-        r0.end(add_to(o_ref, zbuf, 1))
-        mate.wait_send()
+        r1.end(write_to(z_ref))
+        g.finish()
+        r0.end(write_to(o_ref))
         r0.sent()
         r1.sent()
-        g.finish()
         own.wait()
-        for c in moved:
-            c.wait()
 
     sh = jax.ShapeDtypeStruct
     return pl.pallas_call(
         kernel,
-        out_shape=(sh((nb,) + x.shape, x.dtype), sh((rows, cols), f32))
-        + tuple(sh(a.shape, a.dtype) for a in grads),
-        in_specs=[ANY, VMEM] + [ANY] * m,
-        out_specs=(ANY, VMEM) + (ANY,) * m,
-        scratch_shapes=[Gather.scratch(nb), DMA, DMA((2, m)), DMA((2,)), pltpu.VMEM((2, rows, cols), bf16)]
+        out_shape=(sh((nb,) + x.shape, x.dtype), sh((rows, cols), f32), sh((rows, cols), bf16)),
+        in_specs=[ANY, VMEM],
+        out_specs=(ANY, VMEM, VMEM),
+        scratch_shapes=[Gather.scratch(nb), DMA]
         + Reduce.scratch(nb, rows, cols, 2),
         compiler_params=pltpu.CompilerParams(
             collective_id=cid, has_side_effects=True, vmem_limit_bytes=56 * MIB
         ),
-        cost_estimate=cost(50),
+        cost_estimate=NO_COST,
         name="middle",
-    )(x, ypart, *grads)
-
-
-def halo_back(dkv, nz, nb, rp, back, cid):
+    )(x, ypart)
+
+
+def halo_back(dkv, yfar, nz, nb, rp, back, cid):
     R = dkv.shape[1]
 
-    def kernel(d_ref, kin, ks, kr):
+    def kernel(d_ref, y_ref, kin, yo, ks, kr, ys):
         me = Layer(nb)
         first = (me.b // rp) * rp
         part = lax.rem(me.b, rp)
@@ -545,6 +561,8 @@
                     pl.when(me.u >= d)(lambda d=d, p=p: copy(d, p).start())
                 elif rp > 1:
                     pl.when(part != p)(lambda d=d, p=p: copy(d, p).start())
+        mate = remote(y_ref, yo, ys.at[0], ys.at[1], me.across(1), me.b)
+        mate.start()
         for d in range(back + 1):
             for p in range(rp):
                 if d:
@@ -553,30 +571,34 @@
                 elif rp > 1:
                     pl.when(part != p)(lambda d=d, p=p: copy(d, p).wait_send())
                     pl.when(part != p)(lambda d=d, p=p: arrival(d, p).wait_recv())
+        mate.wait()
 
     return pl.pallas_call(
         kernel,
-        out_shape=jax.ShapeDtypeStruct(((back + 1) * rp, R, LANES), bf16),
-        in_specs=[ANY],
-        out_specs=ANY,
-        scratch_shapes=[DMA(((back + 1) * rp,))] * 2,
+        out_shape=(
+            jax.ShapeDtypeStruct(((back + 1) * rp, R, LANES), bf16), jax.ShapeDtypeStruct(yfar.shape, bf16),
+        ),
+        in_specs=[ANY] * 2,
+        out_specs=(ANY,) * 2,
+        scratch_shapes=[DMA(((back + 1) * rp,))] * 2 + [DMA((2,))],
         compiler_params=pltpu.CompilerParams(collective_id=cid, has_side_effects=True),
-        cost_estimate=cost(25),
+        cost_estimate=NO_COST,
         name="halo_back",
-    )(dkv)
-
-
-def reduce_last(lhs, rhs, pieces, dwo, nz, nb, rp, cid):
+    )(dkv, yfar)
+
+
+def reduce_last(lhs, rhs, pieces, nz, nb, rp, cid):
     rows = lhs.shape[0] // nb
     cols = rhs.shape[0]
-    _, _, shard, width = pieces.shape
+    _, count, shard, width = pieces.shape
     n_o = nz * rp
+    wide = (count - nb) // rp
     n = nz * nb
 
-    def kernel(l_ref, r_ref, p_ref, w_ref, o_ref, pin, win, slab, total, wslab, wtotal, zs, zr, ps, pr, ws, wr,
-               ls, *scratch):
+    def kernel(l_ref, r_ref, p_ref, o_ref, pin, win, land, tmp, total, zs, zr, ps, pr, ws, wr, ls, *scratch):
         me = Layer(nb)
-        lin = me.u * nb + me.b
+        u = me.u
+        lin = u * nb + me.b
         part = lax.rem(me.b, rp)
         bar = pltpu.get_barrier_semaphore()
 
@@ -587,64 +609,97 @@
 
         pl.semaphore_wait(bar, n - 1)
 
-        def weight(p):
-            t = (me.b // rp) * n_o + me.u * rp + p
-            return t, remote(wtotal.at[p], win.at[part], ws.at[0, p], wr.at[0, part], t // nb, lax.rem(t, nb))
-
-        across = []
-        for i in range(1, nz):
-            to = lax.rem(me.u + i, nz)
-            c = remote(p_ref.at[to], slab.at[i], zs.at[i], zr.at[i], to, me.b)
-            c.start()
-            across.append(c)
+        def hop(way, o):
+            to = u - 1 if way == 0 else u + 1
+            return remote(tmp.at[way, o], land.at[way, o], zs.at[way, o], zr.at[way, o], to, me.b)
+
+        def add(way, o):
+            @pl.loop(0, count)
+            def _(t):
+                tmp[way, o, t] = (p_ref[o, t].astype(f32) + land[way, o, t].astype(f32)).astype(bf16)
+
+        def ends(way, o):
+            def run():
+                tmp[way, o] = p_ref[o]
+                hop(way, o).start()
+            return run
+
+        def passes(way, o):
+            def run():
+                hop(way, o).wait_recv()
+                add(way, o)
+                hop(way, o).start()
+            return run
+
+        def down(o):
+            return u > o
+
+        def up(o):
+            return u < o
+
+        ways = [(0, o) for o in range(nz - 1)], [(1, o) for o in range(nz - 1, 0, -1)]
+        for pair in zip(*ways):
+            for way, o in pair:
+                pl.when(u == (0 if way else nz - 1))(ends(way, o))
+
+        def relay(way, o):
+            inner = (u > 0) & (u < nz - 1) & (up(o) if way else down(o))
+            pl.when(inner)(passes(way, o))
 
         def block(t):
-            part = l_ref[pl.ds(pl.multiple_of(t * rows, rows), rows), :]
-            return lax.dot_general(part, r_ref[...], NT, preferred_element_type=f32)
-
-        parts = []
-        for i in range(1, nz):
-            to = lax.rem(me.u + i, nz)
-            c = remote(w_ref.at[to], wslab.at[i], ws.at[1, i], wr.at[1, i], to, me.b)
-            c.start()
-            parts.append(c)
-        red = made(me, block, *scratch)
-        red.phase2()
-        for c in across:
-            c.wait_recv()
+            rows_t = l_ref[pl.ds(pl.multiple_of(t * rows, rows), rows), :]
+            return lax.dot_general(rows_t, r_ref[...], NT, preferred_element_type=f32)
+
+        red = made(me, block, *scratch, waits=False)
+        pairs = list(zip(*ways))
+        for k, pair in enumerate(pairs):
+            for way, o in pair:
+                relay(way, o)
+            if k == 0:
+                for j in red.order[:-1]:
+                    red.phase1(j)
+            if k == len(pairs) - 2:
+                red.phase2()
+
+        def here(way):
+            pl.when((u > 0) if way else (u < nz - 1))(
+                lambda: remote(tmp.at[way, u], land.at[way, u], zs.at[way, u], zr.at[way, u], u, me.sib).wait_recv())
+
+        here(0)
+        here(1)
+
+        @pl.loop(0, count)
+        def _(t):
+            tile = p_ref[u, t].astype(f32)
+            tile = tile + jnp.where(u < nz - 1, land[0, u, t].astype(f32), 0.0)
+            total[t] = (tile + jnp.where(u > 0, land[1, u, t].astype(f32), 0.0)).astype(bf16)
+
         out = []
-        for t in range(nb):
-            tile = p_ref[me.u, t].astype(f32)
-            for i in range(1, nz):
-                tile = tile + slab[i, t].astype(f32)
-            total[t] = tile.astype(bf16)
         for i in range(1, nb):
             t = lax.rem(me.b + i, nb)
-            c = remote(total.at[t], pin.at[me.b], ps.at[i], pr.at[i], me.u, t)
+            c = remote(total.at[t], pin.at[me.b], ps.at[i], pr.at[i], u, t)
             c.start()
             out.append(c)
         own = pltpu.make_async_copy(total.at[me.b], pin.at[me.b], ls.at[0])
         own.start()
-        for c in parts:
-            c.wait_recv()
-        stay = lambda p: pltpu.make_async_copy(wtotal.at[p], win.at[part], ls.at[1])
+
+        def weight(p):
+            t = (me.b // rp) * n_o + u * rp + p
+            src = total.at[pl.ds(nb + p * wide, wide)]
+            return t, remote(src, win.at[part], ws.at[p], wr.at[part], t // nb, lax.rem(t, nb))
+
+        stay = lambda p: pltpu.make_async_copy(total.at[pl.ds(nb + p * wide, wide)], win.at[part], ls.at[1])
         for p in range(rp):
-            tile = w_ref[me.u, p].astype(f32)
-            for i in range(1, nz):
-                tile = tile + wslab[i, p].astype(f32)
-            wtotal[p] = tile.astype(bf16)
             t, c = weight(p)
             pl.when(t != lin)(c.start)
             pl.when(t == lin)(stay(p).start)
         red.end(write_to(o_ref))
         red.sent()
-        for c in across:
-            c.wait_send()
+        for way, o in ways[0] + ways[1]:
+            pl.when(up(o) if way else down(o))(lambda way=way, o=o: hop(way, o).wait_send())
         for c in out:
             c.wait()
         own.wait()
-        for c in parts:
-            c.wait_send()
         for p in range(rp):
             t, c = weight(p)
             pl.when(t != lin)(c.wait_send)
@@ -652,30 +707,30 @@
         hg = lin // n_o
         layer = lax.rem(lin, n_o) // rp
         for p in range(rp):
-            c = remote(wtotal.at[0], win.at[p], ws.at[0, 0], wr.at[0, p], me.u, me.sib)
+            c = remote(total.at[pl.ds(nb, wide)], win.at[p], ws.at[0], wr.at[p], u, me.sib)
             pl.when(layer * nb + hg * rp + p != lin)(c.wait_recv)
 
     sh = jax.ShapeDtypeStruct
     return pl.pallas_call(
         kernel,
         out_shape=(
-            sh((rows, cols), f32), sh((nb, shard, width), bf16), sh((rp, shard, D), bf16),
+            sh((rows, cols), f32), sh((nb, shard, width), bf16), sh((rp, wide, shard, width), bf16),
         ),
-        in_specs=[VMEM, VMEM, VMEM, VMEM],
+        in_specs=[VMEM, VMEM, VMEM],
         out_specs=(VMEM, ANY, ANY),
-        scratch_shapes=[pltpu.VMEM((nz, nb, shard, width), bf16), pltpu.VMEM((nb, shard, width), bf16)]
-        + [pltpu.VMEM((nz, rp, shard, D), bf16), pltpu.VMEM((rp, shard, D), bf16)]
-        + [DMA((nz,))] * 2
+        scratch_shapes=[pltpu.VMEM((2, nz, count, shard, width), bf16)] * 2
+        + [pltpu.VMEM((count, shard, width), bf16)]
+        + [DMA((2, nz))] * 2
         + [DMA((nb,))] * 2
-        + [DMA((2, max(nz, rp)))] * 2
+        + [DMA((rp,))] * 2
         + [DMA((2,))]
         + made_scratch(nb, rows, cols),
         compiler_params=pltpu.CompilerParams(
             collective_id=cid, has_side_effects=True, vmem_limit_bytes=56 * MIB
         ),
-        cost_estimate=cost(2),
+        cost_estimate=NO_COST,
         name="reduce_last",
-    )(lhs, rhs, pieces, dwo)
+    )(lhs, rhs, pieces)
 
 
 def turn(a, c, s1, s2):
@@ -701,6 +756,58 @@
 def whole_block(a):
     zeros = (0,) * a.ndim
     return pl.BlockSpec(a.shape, lambda i: zeros)
+
+
+def prepare(w_query, w_key, w_value, extra, gains, w_inner, w_outer, cotangent, routes):
+    S = w_query.shape[0]
+    T = routes.shape[0]
+    dz = w_inner.shape[1]
+    W = 3 * FF
+    half = W // 2
+
+    def kernel(q_ref, k_ref, v_ref, x_ref, n_ref, i_ref, o_ref, c_ref, r_ref, p_ref, g_ref, a_ref, b_ref, f_ref):
+        low = low_half()
+        lane = lax.broadcasted_iota(jnp.int32, (1, LANES), 1)
+
+        def low64(ref, at):
+            a = ref[:, at // LANES * LANES:at // LANES * LANES + LANES].astype(f32)
+            return swap(a) if at % LANES else a
+
+        spread = lax.broadcasted_iota(jnp.int32, (S, S), 0) == lax.broadcasted_iota(jnp.int32, (S, S), 1)
+        tail = x_ref[...].astype(f32)
+        for i in range(2):
+            column = jnp.sum(jnp.where(spread, n_ref[i:i + 1, :], 0.0), axis=1, keepdims=True)
+            tail = jnp.where(lane == r_first + i, column, tail)
+        for h in range(KV):
+            at = h * QCOLS
+            two = lambda a, b: jnp.where(low, a, swap(b)).astype(bf16)
+            p_ref[h, :, :LANES] = two(low64(q_ref, at), low64(q_ref, at + HW))
+            p_ref[h, :, LANES:2 * LANES] = two(low64(q_ref, at + 2 * HW), low64(k_ref, h * HW))
+            p_ref[h, :, 2 * LANES:] = jnp.where(low, low64(v_ref, h * HW), tail).astype(bf16)
+        g_ref[:, :D] = c_ref[...]
+        named = r_ref[:, 0:1] + HW == lane
+        for j in range(1, TOPK):
+            named = named | (r_ref[:, j:j + 1] + HW == lane)
+        g_ref[:, D:] = jnp.where(named, 1.0, 0.0).astype(bf16)
+        odd = lax.rem(lax.axis_index("ulysses"), 2)
+        same, outer = i_ref[odd], o_ref[odd].astype(f32).T.astype(bf16)
+        a_ref[...] = same[:, :half]
+        b_ref[:, :2 * FF - half] = same[:, half:]
+        b_ref[:, 2 * FF - half:] = outer
+        f_ref[:, :2 * FF] = i_ref[1 - odd]
+        f_ref[:, 2 * FF:] = o_ref[1 - odd].astype(f32).T.astype(bf16)
+
+    r_first = extra[1]
+    sh = lambda *shape: jax.ShapeDtypeStruct(shape, bf16)
+    return pl.pallas_call(
+        kernel,
+        out_shape=(sh(KV, S, AUX), sh(T, D + LANES), sh(dz, half), sh(dz, half), sh(dz, W)),
+        in_specs=[VMEM] * 9,
+        out_specs=(VMEM,) * 5,
+        compiler_params=pltpu.CompilerParams(vmem_limit_bytes=48 * MIB),
+        cost_estimate=NO_COST,
+        name="prepare",
+    )(w_query, w_key, w_value, extra[0], gains, w_inner, w_outer, cotangent, routes)
 
 
 def project(x, gain, packed, c, s1, s2):
@@ -735,7 +842,7 @@
             row_block(step, D),
         ),
         compiler_params=pltpu.CompilerParams(vmem_limit_bytes=32 * MIB),
-        cost_estimate=cost(4),
+        cost_estimate=NO_COST,
         name="project",
     )(x, gain, packed, c, s1, s2)
 
@@ -807,7 +914,7 @@
         ),
         out_shape=(sh((Rq, QCOLS), bf16), sh((GROUP, Rq, 1), f32)),
         compiler_params=pltpu.CompilerParams(vmem_limit_bytes=48 * MIB),
-        cost_estimate=cost(17),
+        cost_estimate=NO_COST,
         name="attend",
     )(meta, q, kv, starts)
 
@@ -876,7 +983,7 @@
         ),
         out_shape=(sh((GROUP, Rq, LANES), bf16), sh((K, LANES), f32), sh((QCOLS, D), f32)),
         compiler_params=pltpu.CompilerParams(vmem_limit_bytes=48 * MIB),
-        cost_estimate=cost(2),
+        cost_estimate=NO_COST,
         name="attend_back",
     )(meta, q, kv, starts, lse, mixed, dattn, wo)
 
@@ -931,12 +1038,12 @@
         out_specs=(row_block(step, AUX), pl.BlockSpec((D, AUX), lambda i: (0, 0))),
         scratch_shapes=[pltpu.VMEM((D, AUX), f32)],
         compiler_params=pltpu.CompilerParams(vmem_limit_bytes=48 * MIB),
-        cost_estimate=cost(2),
+        cost_estimate=NO_COST,
         name="weight_grads",
     )(ok, dq, dkv, kin, *tables, h1, packed, tail)
 
 
-def experts(h2_own, g_own, g_oth, router, hot, weights, nz, nb, cid):
+def experts(h2_own, g_own, g_oth, router, hot, weights, sent, leave, nz, nb, cid):
     T = h2_own.shape[0]
     nc = nb // 2
     step = 2 * T
@@ -945,16 +1052,18 @@
     C = D + LANES
     W = 3 * FF
     nw = len(weights)
+    ng = len(leave)
     resident = nb <= 8
 
     def kernel(x_ref, g0_ref, g1_ref, r_ref, e_ref, *rest):
         win = rest[:nw]
         y_ref, s_ref = rest[nw:nw + 2]
         rest = rest[nw + 2:]
-        din = rest[:nz]
-        h_all, hbuf, part, gbuf, ybuf, wc, acc, zbuf, gs, zs, sem, gsem, ysem, *pair = rest[nz:]
+        din, gin = rest[:ng], rest[ng]
+        rest = rest[ng + 1:]
+        h_all, hbuf, part, gbuf, ybuf, wc, acc, zbuf, gs, zs, sem, gsem, ysem, *pair = rest
         me = Layer(nb)
-        me.enter((1,))
+        me.enter(sorted({1, sent[0]}))
         own, oth = h_all.at[0], h_all.at[1]
         mate = remote(x_ref, oth.at[me.b], zs.at[0], zs.at[1], me.across(1), me.b)
         mate.start()
@@ -996,6 +1105,7 @@
         cot_start(jnp.int32(0))
         acc[...] = jnp.zeros_like(acc)
         ra, rb = pair_of(me, part, *pair)
+        back = remote(zbuf.at[0], zbuf.at[1], zs.at[3], zs.at[4], me.across(1), me.b)
         ga.relay1()
         for c in loads:
             c.wait()
@@ -1038,11 +1148,18 @@
             at(nc + 1, mates)(u)
 
             def ours():
+                rb.phase2()
                 ra.phase1(3)
                 ra.phase1(1)
 
             if nc == 4:
                 at(nc + 2, ours)(u)
+
+            def across():
+                rb.end(write_to(zbuf, 0))
+                back.start()
+
+            at(units - 1, across)(u)
 
         @pl.loop(0, units)
         def _(u):
@@ -1086,16 +1203,15 @@
             part[h, two, :, D:] = (hi * hot + swap((dgate - hi) * hot)).astype(bf16).reshape(2, T, LANES)
             depart(u)
 
-        rb.phase2()
         for j in (2,) if nc == 4 else ra.order[:-1]:
             ra.phase1(j)
         wc[...] = acc[...].astype(bf16)
-        saves = [pltpu.make_async_copy(wc.at[rows_at(d)], din[d], sem.at[d]) for d in range(nz)]
+        grad = lambda d, c, width: wc.at[rows_at(d), pl.ds(c, width)]
+        going = remote(grad(*sent), gin, zs.at[6], zs.at[7], me.across(sent[0]), me.b)
+        going.start()
+        saves = [pltpu.make_async_copy(grad(*p), din[k], sem.at[k]) for k, p in enumerate(leave)]
         for c in saves:
             c.start()
-        rb.end(write_to(zbuf, 0))
-        back = remote(zbuf.at[0], zbuf.at[1], zs.at[3], zs.at[4], me.across(1), me.b)
-        back.start()
         ra.phase2()
         back.wait_recv()
         ra.end(add_to(s_ref, zbuf, 1))
@@ -1105,6 +1221,7 @@
             r.sent()
         for c in saves:
             c.wait()
+        going.wait()
         result(jnp.int32(units - 2)).wait()
         result(jnp.int32(units - 1)).wait()
 
@@ -1113,48 +1230,57 @@
     return pl.pallas_call(
         kernel,
         out_shape=(sh((2, nb, T, D), bf16), sh((T, C), f32))
-        + (sh((dz, W), bf16),) * nz
+        + tuple(sh((dz, width), bf16) for _, _, width in leave)
+        + (sh((dz, sent[2]), bf16),)
         + (() if resident else (sh((2, nb, T, D), bf16),)),
         in_specs=[ANY] * 3 + [VMEM] * 2 + [ANY] * nw,
-        out_specs=(ANY, VMEM) + (ANY,) * (nz + int(not resident)),
+        out_specs=(ANY, VMEM) + (ANY,) * (ng + 1 + int(not resident)),
         scratch_shapes=([v((2, nb, T, D))] if resident else [])
         + [
             v((2, T, D)), v((2, nb, T, C)), v((2, step, C)), v((2, 2, T, D)),
             v((D, W)), v((D, W), f32), v((2, T, C)),
-            Gather.scratch(nb, 2), DMA((6,)), DMA((nw,)), DMA((2,)), DMA((2,)),
+            Gather.scratch(nb, 2), DMA((8,)), DMA((max(nw, ng),)), DMA((2,)), DMA((2,)),
         ]
         + Reduce.scratch(nb, T, C, 2),
         compiler_params=pltpu.CompilerParams(
             collective_id=cid, has_side_effects=True, vmem_limit_bytes=60 * MIB
         ),
-        cost_estimate=cost(70),
+        cost_estimate=NO_COST,
         name="experts",
     )(h2_own, g_own, g_oth, router, hot, *[a for a, _, _ in weights])
 
 
-def finish(dh1, x, gain, dresid, pin, win, resid, ysum, grads):
+def finish(dh1, x, gain, dresid, pin, win, resid, ysum, yfar, grads, places):
     T = x.shape[0]
     groups, rp, S, _ = pin.shape
     senders = win.shape[0]
     m = len(grads)
     dz = grads[0].shape[0]
 
-    def kernel(d_ref, x_ref, g_ref, r_ref, p_ref, w_ref, s_ref, y_ref, *rest):
+    def kernel(d_ref, x_ref, g_ref, r_ref, p_ref, w_ref, s_ref, y_ref, f_ref, *rest):
         srcs = rest[:m]
         t_ref, q_ref, k_ref, v_ref, m_ref, o_ref, out_ref, in_ref, ex_ref = rest[m:]
         odd = lax.rem(lax.axis_index("ulysses"), 2)
         for e in range(2):
-            total = functools.reduce(lambda a, b: a + b, [r[...].astype(f32) for r in srcs[e::2]])
             at = odd if e == 0 else 1 - odd
-            in_ref[at] = total[:, :2 * FF]
-            ex_ref[at] = total[:, 2 * FF:].T
+            for c in range(0, 3 * FF, FF // 2):
+                total = 0.0
+                for r, (d, lo, width) in zip(srcs, places):
+                    if d % 2 == e and lo <= c < lo + width:
+                        total = total + r[:, c - lo:c - lo + FF // 2].astype(f32)
+                if c < 2 * FF:
+                    in_ref[at, :, c:c + FF // 2] = total
+                else:
+                    ex_ref[at, c - 2 * FF:c - 2 * FF + FF // 2, :] = total.T
         v = x_ref[...].astype(f32)
         inv = lax.rsqrt(jnp.mean(v * v, axis=1, keepdims=True) + EPS)
         n = v * inv
         w = d_ref[...] * g_ref[...]
         t_ref[...] = r_ref[...] + inv * (w - n * jnp.mean(w * n, axis=1, keepdims=True))
-        out_ref[...] = s_ref[...] + y_ref[...]
-        o_ref[...] = functools.reduce(lambda a, b: a + b, [w_ref[k].astype(f32) for k in range(senders)])
+        out_ref[...] = s_ref[...] + y_ref[...] + f_ref[...].astype(f32)
+        for k in range(D // AUX):
+            parts = [w_ref[p, k].astype(f32) for p in range(senders)]
+            o_ref[:, k * AUX:(k + 1) * AUX] = functools.reduce(lambda a, b: a + b, parts)
         small = 0.0
         for h in range(groups):
             row = 0.0
@@ -1171,12 +1297,12 @@
         kernel,
         out_shape=(sh(T, D), sh(S, HEADS * HW), sh(S, KV * HW), sh(S, KV * HW), sh(S, LANES), sh(S, D), sh(T, D),
                    sh(2, dz, 2 * FF), sh(2, FF, dz)),
-        in_specs=[VMEM] * (8 + m),
+        in_specs=[VMEM] * (9 + m),
         out_specs=(VMEM,) * 9,
         compiler_params=pltpu.CompilerParams(vmem_limit_bytes=60 * MIB),
-        cost_estimate=cost(2),
+        cost_estimate=NO_COST,
         name="finish",
-    )(dh1, x, gain, dresid, pin, win, resid, ysum, *grads)
+    )(dh1, x, gain, dresid, pin, win, resid, ysum, yfar, *grads)
 
 
 def locate(rows, lengths):
@@ -1227,33 +1353,28 @@
     n_o = QCOLS // S
     odd = z % 2
 
-    tail = jnp.concatenate(
-        [w_router, gain_attn[:, None], gain_moe[:, None],
-         jnp.zeros((S, AUX - ROUTER_AT - E - 2), bf16)], axis=1)
-    pieces = jnp.stack([
-        jnp.concatenate([
-            w_query[:, h * QCOLS:(h + 1) * QCOLS], w_key[:, h * HW:(h + 1) * HW],
-            w_value[:, h * HW:(h + 1) * HW], tail], axis=1)
-        for h in range(KV)])
     lanes = jnp.arange(LANES, dtype=jnp.int32)
-    named = jnp.any(routes[:, :, None] + HW == lanes[None, None, :], axis=1)
-    cot_mask = jnp.concatenate([cotangent, named.astype(bf16)], axis=1)
-    xg, packed = gather_inputs(tokens, pieces, nz, nb, 0)
+    extra = (jnp.pad(w_router, ((0, 0), (HW, LANES - HW - E))), HW + E)
+    gains = jnp.stack([gain_attn, gain_moe]).astype(f32)
+    pieces, cot_mask, same_a, same_b, other = prepare(
+        w_query, w_key, w_value, extra, gains, w_inner, w_outer, cotangent, routes)
+    W = 3 * FF
+    half = W // 2
+    early = min(2, nz - 1)
+    xg, packed, wo, g_own, g_far, first = gather_inputs(
+        tokens, pieces, w_output, cot_mask, same_a if early % 2 == 0 else other[:, :half], early, nz, nb, 0)
     xg = xg.reshape(R, D)
     packed = packed.reshape(D, AUX)
     router = packed[:, 2 * LANES:]
     gains = packed[:, ROUTER_AT + E:ROUTER_AT + E + 2].astype(f32).T
     gain1, gain2 = gains[0:1], gains[1:2]
 
-    experts_of = jnp.concatenate([w_inner, jnp.swapaxes(w_outer, 1, 2)], axis=2)
     flip = lambda d: [(k, k ^ d) for k in range(nz)]
-    give = lambda w, d, lo, hi: lax.ppermute(
-        lax.dynamic_index_in_dim(w, odd ^ (d % 2), 0, keepdims=False)[:, lo:hi], "ulysses", flip(d))
-    W = 3 * FF
-    experts_of, packed = lax.optimization_barrier((experts_of, packed))
-    early = min(2, nz - 1)
-    weights = [(lax.dynamic_index_in_dim(experts_of, odd, 0, keepdims=False), 0, 0),
-               (give(experts_of, early, 0, W // 2), early, 0)]
+    give = lambda w, d: lax.ppermute(w, "ulysses", flip(d))
+    named = jnp.any(routes[:, :, None] + HW == lanes[None, None, :], axis=1)
+    second, packed = lax.optimization_barrier((same_b if early % 2 == 0 else other[:, half:], packed))
+    second = give(second, early)
+    weights = [(same_a, 0, 0), (same_b, 0, half), (first, early, 0)]
 
     rows = z * R + jnp.arange(R, dtype=jnp.int32)
     opening = locate(rows, lengths)
@@ -1266,29 +1387,34 @@
     q, kv, h1 = project(xg, gain1, packed, *tables)
     if rp > 1:
         q = lax.dynamic_slice_in_dim(q, at, Rq, 1)
-    array, *place = weights[1]
-    kv, array = lax.optimization_barrier((kv, array))
-    weights[1] = (array, *place)
-    far, g_own, g_far, wo = halo_forward(kv, cot_mask, w_output, nz, nb, rp, back, 1)
+    kv, second = lax.optimization_barrier((kv, second))
+    weights.append((second, early, half))
+    far, g_oth = halo_forward(kv, g_far, nz, nb, back, 1)
+    g_own, g_oth = g_own.reshape(R, D + LANES), g_oth.reshape(R, D + LANES)
     wo = wo.reshape(QCOLS, D)
-    later, far = lax.optimization_barrier((experts_of, far))
-    weights.append((give(later, early, W // 2, W), early, W // 2))
-    weights += [(give(later, d, 0, W), d, 0) for d in range(1, nz) if d != early]
+    same_a, same_b, other, far = lax.optimization_barrier((same_a, same_b, other, far))
+    for d in range(1, nz):
+        if d % 2 and d != early:
+            weights.append((give(other, d), d, 0))
+        elif d != early:
+            weights += [(give(same_a, d), d, 0), (give(same_b, d), d, half)]
     kv_all = jnp.concatenate([far[d - 1] for d in range(back, 0, -1)] + [kv], axis=0)
     base = (z - back) * R
     starts = rows_of(opening, at, Rq) - base
     meta = jnp.concatenate([starts[::BQ] // BK, (back * R + at)[None]]).astype(jnp.int32)
     starts = starts[:, None]
     mixed, lse = attend(q, kv_all, starts, meta)
-    attn, g_oth = reduce_product(widen(mixed, at, R), wo, g_far, nb, 2)
-    g_own, g_oth = g_own.reshape(R, D + LANES), g_oth.reshape(R, D + LANES)
+    attn = reduce_product(widen(mixed, at, R), wo, nb, 2)
 
     resid = tokens.astype(f32) + attn
     n2, inv2, scaled2 = norm_rows(resid, gain2)
     h2_own = scaled2.astype(bf16)
     hot = (lanes == HW + b * EXP_DEV + odd).astype(f32)[None, :]
-    y, summed, *grads = experts(h2_own, g_own, g_oth, router, hot, weights, nz, nb, 3)
-    grads = grads[:nz]
+    sent = (early, 0, half)
+    leave = [(0, 0, W), (early, half, half), (nz - 1, 0, half), (nz - 1, half, half)]
+    leave += [(d, 0, W) for d in range(1, nz - 1) if d != early]
+    y, summed, *grads = experts(h2_own, g_own, g_oth, router, hot, weights, sent, leave, nz, nb, 3)
+    grads, got = grads[:len(leave)], grads[len(leave)]
 
     upstream = cotangent.astype(f32)
     dgates = summed[:, D:] + jnp.roll(summed[:, D:], HW, 1)
@@ -1301,19 +1427,16 @@
     dh2 = summed[:, :D] + mm(dlogits, router, NT)
     d_norm2, d_gain2 = norm_back(dh2, n2, inv2, gain2)
     dresid = upstream + d_norm2
-    split = min(3, nz)
-    dattn, ysum, *grads[1:split] = middle(dresid.astype(bf16), y, grads[1:split], nz, nb, 5)
-    dattn, *late = lax.optimization_barrier((dattn, *grads[split:]))
-    grads[split:] = [lax.ppermute(a, "ulysses", flip(d)) for d, a in enumerate(late, split)]
+    grads = [grads[0]] + [give(a, d) for a, (d, _, _) in zip(grads[1:], leave[1:])]
+    dattn, ysum, yfar = middle(dresid.astype(bf16), y, nb, 5)
     dattn = dattn.reshape(R, D)
     tail = mm(h2_own, dlogits, TN) + jnp.where(lanes == HW + E, d_gain2[:, None], 0.0)
 
     dq, dkv, dwo = attend_back(q, kv_all, starts, meta, lse, mixed, rows_of(dattn, at, Rq), wo)
-    dkv, *late = lax.optimization_barrier((dkv, *grads[split:]))
-    grads[split:] = late
+    dkv, *grads = lax.optimization_barrier((dkv, *grads))
     dkv = dkv.reshape(back + 1, R, LANES)
     dkv_out = jnp.stack([dkv[back - d] for d in range(back + 1)]).astype(bf16)
-    kin = halo_back(dkv_out, nz, nb, rp, back, 6)
+    kin, yfar = halo_back(dkv_out, yfar, nz, nb, rp, back, 6)
     ok = [(z + d < nz) if d else (part != p) for d in range(back + 1) for p in range(rp)]
     ok = jnp.stack([jnp.asarray(o).astype(jnp.int32) for o in ok] + [jnp.int32(HW + E)])
     if rp > 1:
@@ -1321,11 +1444,14 @@
     turned, dw = weight_grads(
         dq, rows_of(dkv[back], at, Rq), kin, ok, [rows_of(t, at, Rq) for t in tables],
         rows_of(h1, at, Rq), packed, tail)
-    dh1, pin, win = reduce_last(
-        widen(turned, at, R), packed, dw.reshape(nz, nb, S, AUX),
-        dwo.astype(bf16).reshape(nz, rp, S, D), nz, nb, rp, 7)
+    wide = D // AUX
+    dwo = dwo.astype(bf16).reshape(nz, rp, S, wide, AUX)
+    dwo = jnp.transpose(dwo, (0, 1, 3, 2, 4)).reshape(nz, rp * wide, S, AUX)
+    last = jnp.concatenate([dw.reshape(nz, nb, S, AUX), dwo], axis=1)
+    dh1, pin, win = reduce_last(widen(turned, at, R), packed, last, nz, nb, rp, 7)
     d_tokens, d_query, d_key, d_value, small, d_output, out, d_inner, d_outer = finish(
-        dh1, tokens, gain1, dresid, pin.reshape(KV, rp, S, AUX), win, resid, ysum, grads)
+        dh1, tokens, gain1, dresid, pin.reshape(KV, rp, S, AUX), win, resid, ysum, yfar,
+        grads + [got], leave + [sent])
     return (
         out, d_tokens, small[:, HW + E + 1], d_query, d_key, d_value, d_output,
         small[:, HW + E], small[:, HW:HW + E], d_inner, d_outer,

time: 498 us -> 468 us (0.940)
  waiting for transfers between devices: 46.6 us -> 25.5 us
  Pallas kernels: 392 us -> 380 us
    pallas_call x1, Pallas kernels: 32.2 us -> 72.1 us  [gather_inputs(): pl.pallas_call(kernel, out_shape=(sh((nb,) + x.shape, x.dtype), sh((nz, n...]
    pallas_call x2 -> x3, Pallas kernels: 75.3 us -> 48.9 us  [the longest x1 28.7 us: halo_back(): pl.pallas_call(kernel, out_shape=(jax.ShapeDtypeStruct(((back + 1) * rp,...]
    pallas_call x1, Pallas kernels: 70 us -> 48.2 us  [middle(): pl.pallas_call(kernel, out_shape=(sh((nb,) + x.shape, x.dtype), sh((rows,...]
    ppermute x5 -> x7, waiting for transfers between devices: 46.6 us -> 25.5 us  [on_device(): give = lambda w, d: lax.ppermute(w, 'ulysses', flip(d))]
    pallas_call x1, Pallas kernels: 36 us -> 20.8 us  [halo_forward(): pl.pallas_call(kernel, out_shape=(sh((back,) + kv.shape, kv.dtype), sh((n...]
    pallas_call x1, Pallas kernels: 76.5 us -> 84 us  [experts(): pl.pallas_call(kernel, out_shape=(sh((2, nb, T, D), bf16), sh((T, C), f32...]
    unnamed x100 -> x104, local copies, waits for them, and re-layouts: 15.5 us -> 22.2 us
    ppermute x5 -> x7, starting transfers between devices: 10.8 us -> 7.01 us  [on_device(): give = lambda w, d: lax.ppermute(w, 'ulysses', flip(d))]
  transfers between devices with their start and end apart: 5 -> 7, of which waited for: 3 -> 2; matrix products, arithmetic and copies ran while one was open for 2% -> 4% of each run, Pallas kernels for 13% -> 20%
where the time goes in v4:
time: 468 us; the launch traced here: 464 us
  Pallas kernels  380 us (81%)
  local copies, waits for them, and re-layouts  31.3 us (7%)
  waiting for transfers between devices  25.5 us (5%)
  other arithmetic  15.4 us (3%)
  starting transfers between devices  7.01 us (1%)
    pallas_call x1, Pallas kernels, experts(): pl.pallas_call(kernel, out_shape=(sh((2, nb, T, D), bf16), sh((T, C), f32...  84 us
    pallas_call x1, Pallas kernels, gather_inputs(): pl.pallas_call(kernel, out_shape=(sh((nb,) + x.shape, x.dtype), sh((nz, n...  72.1 us
    pallas_call x1, Pallas kernels, reduce_last(): pl.pallas_call(kernel, out_shape=(sh((rows, cols), f32), sh((nb, shard, w...  63.2 us
    pallas_call x1, Pallas kernels, middle(): pl.pallas_call(kernel, out_shape=(sh((nb,) + x.shape, x.dtype), sh((rows,...  48.2 us
    pallas_call x1, Pallas kernels, halo_back(): pl.pallas_call(kernel, out_shape=(jax.ShapeDtypeStruct(((back + 1) * rp,...  28.7 us
    ppermute x7, waiting for transfers between devices, on_device(): give = lambda w, d: lax.ppermute(w, 'ulysses', flip(d))  25.5 us
    unnamed x104, local copies, waits for them, and re-layouts  22.2 us
    pallas_call x1, Pallas kernels, halo_forward(): pl.pallas_call(kernel, out_shape=(sh((back,) + kv.shape, kv.dtype), sh((n...  20.8 us
  transfers between devices with their start and end apart: 7, of which 2 were waited for; matrix products, arithmetic and copies ran while one was open for 4% of the time, Pallas kernels for 20%

profile of v4, /device:TPU:1, one launch (start us, length us, event | category | flops | bytes accessed | tf_op | source)
XLA Modules:
  0.0 464.5 jit_solution(16365221881467055349)
XLA Ops:
  3.0 1.4 copy-done.13
  4.4 1.0 copy-done.15
  5.4 1.1 copy-done.22
  6.5 0.9 copy-done.25
  9.0 1.8 prepare.1
  10.8 0.8 copy-done.8
  13.1 1.0 copy-done.29
  14.1 72.1 %gather_inputs.1 = (bf16[8,128,1536]{2,1,0:T(8,128)(2,1)}, bf16[4,8,48,384]{3,2,1,0:T(8,128)(2,1)}, bf16[4,48,1536]{2,1,0:T(8,128)(2,1)}, bf16[8,128,1664]{2,1,0...) custom-call(bf16[128,1536]{1,0:T(8,128)(2,1)} %x_ref.3, bf16[8,48,384]{2,1,0:T(8,128)(2,1)} %copy-done.24, ...), custom_call_target="tpu_custom_call" | custom-call | tf_op jit(solution)/shard_map/gather_inputs/pallas_call | solution.py:377
  86.3 1.2 slice_convert_fusion
  88.6 1.9 fusion
  92.9 1.9 copy-done.4
  94.8 4.0 project.1
  98.8 1.7 copy-done.3
  100.5 0.9 copy-done.5
  102.7 9.1 %collective-permute-done.rest_3_ = bf16[384,768]{1,0:T(8,128)(2,1)} collective-permute-done((bf16[384,768]{1,0:T(8,128)(2,1)}, bf16[384,768]{1,0:T(8,128)(2,1)}, u32[]{:S(2)}, u32[]{:S(2)}) %collective-permute-start) | collective-permute-done | bytes 589856 | tf_op jit(solution)/shard_map/ppermute | solution.py:1373
  111.8 20.8 %halo_forward.1 = (bf16[2,1024,128]{2,1,0:T(8,128)(2,1)}, bf16[8,128,1664]{2,1,0:T(8,128)(2,1)}) custom-call(bf16[1024,128]{1,0:T(8,128)(2,1)} %copy-done.17, bf16[128,1664]{1,0:T(8,128)(2,1)} %get-tuple-element.83.g_ref), custom_call_target="tpu_custom_call" | custom-call | tf_op jit(solution)/shard_map/halo_forward/pallas_call | solution.py:430
  133.0 2.0 collective-permute-start.2
  135.0 1.1 slice_bitcast_fusion.3
  136.1 1.1 pad_maximum_fusion.1.kv_ref
  137.1 8.6 %attend.1 = (bf16[1024,192]{1,0:T(8,128)(2,1)S(1)}, f32[3,1024,1]{2,1,0:T(8,128)S(1)}) custom-call(s32[5]{0:T(128)S(1)} %pad_add_fusion.1.meta, bf16[3,1024,128]{2,1,0:T(8,128)(2,1)S(1)} %copy-done.6, bf16[3072,128]{1,0:T(8,128)(2,1)S(1)} %pad_maximum_fusion.1.kv_ref, s32[1024,1]{1,0:T(8,128)S(1)} %copy.52.st_ref), custom_call_target="tpu_custom_call" | custom-call | tf_op jit(solution)/shard_map/attend/pallas_call | solution.py:903
  145.8 18.4 %reduce_product.1 = f32[128,1536]{1,0:T(8,128)S(1)} custom-call(bf16[1024,192]{1,0:T(8,128)(2,1)S(1)} %get-tuple-element.87.l_ref.o_ref, bf16[192,1536]{1,0:T(8,128)(2,1)S(1)} %bitcast.43), custom_call_target="tpu_custom_call" | custom-call | tf_op jit(solution)/shard_map/reduce_product/pallas_call | solution.py:480
  164.4 0.8 copy-done.30
  166.2 1.4 select_reduce_fusion
  167.7 1.6 copy.51
  169.2 1.0 fusion.5
  170.3 16.3 %collective-permute-done.2.rest_5_ = bf16[384,1536]{1,0:T(8,128)(2,1)} collective-permute-done((bf16[384,1536]{1,0:T(8,128)(2,1)}, bf16[384,1536]{1,0:T(8,128)(2,1)}, u32[]{:S(2)}, u32[]{:S(2)}) %collective-permute-start.2) | collective-permute-done | bytes 1179680 | tf_op jit(solution)/shard_map/ppermute | solution.py:1373
  186.6 84.0 %experts.1 = (bf16[2,8,128,1536]{3,2,1,0:T(8,128)(2,1)}, f32[128,1664]{1,0:T(8,128)}, bf16[384,1536]{1,0:T(8,128)(2,1)}, bf16[384,768]{1,0:T(8,128)(2,1)}, bf16[...) custom-call(bf16[128,1536]{1,0:T(8,128)(2,1)} %copy-done.32, ...), custom_call_target="tpu_custom_call" | custom-call | tf_op jit(solution)/shard_map/experts/pallas_call | solution.py:1230
  270.6 1.0 fusion.18
  271.6 1.0 multiply_reduce_fusion.3
  272.7 1.1 multiply_convert_fusion.1
  273.9 2.4 multiply_reduce_fusion
  276.3 1.3 collective-permute-start.3
  277.6 2.2 collective-permute-start.4
  279.8 1.0 collective-permute-start.5
  280.8 1.3 fusion.17
  282.1 48.2 %middle.1 = (bf16[8,128,1536]{2,1,0:T(8,128)(2,1)}, f32[128,1536]{1,0:T(8,128)}, bf16[128,1536]{1,0:T(8,128)(2,1)}) custom-call(bf16[128,1536]{1,0:T(8,128)(2,1)} %get-tuple-element.168.x_ref, bf16[2,8,128,1536]{3,2,1,0:T(8,128)(2,1)} %get-tuple-element.95.y_ref), custom_call_target="tpu_custom_call" | custom-call | tf_op jit(solution)/shard_map/middle/pallas_call | solution.py:522
  330.4 15.6 %attend_back.1 = (bf16[3,1024,128]{2,1,0:T(8,128)(2,1)S(1)}, f32[3072,128]{1,0:T(8,128)}, f32[192,1536]{1,0:T(8,128)S(1)}) custom-call(s32[5]{0:T(128)S(1)} %pad_add_fusion.1.meta, bf16[3,1024,128]{2,1,0:T(8,128)(2,1)S(1)} %copy-done.7, bf16[3072,128]{1,0:T(8,128)(2,1)S(1)} %pad_maximum_fusion.1.kv_ref, s32[1024,1]{1,0:T(8,128)S(1)} %copy.52.st_ref, ...), custom_call_target="tpu_custom_call" | custom-call | tf_op jit(solution)/shard_map/attend_back/pallas_call | solution.py:974
  346.0 0.9 copy-done.18
  347.1 0.9 copy.58
  349.0 1.0 pad_maximum_fusion.2.d_ref
  349.9 28.7 %halo_back.1 = (bf16[3,1024,128]{2,1,0:T(8,128)(2,1)}, bf16[128,1536]{1,0:T(8,128)(2,1)}) custom-call(bf16[3,1024,128]{2,1,0:T(8,128)(2,1)} %pad_maximum_fusion.2.d_ref, bf16[128,1536]{1,0:T(8,128)(2,1)} %get-tuple-element.105.y_ref), custom_call_target="tpu_custom_call" | custom-call | tf_op jit(solution)/shard_map/halo_back/pallas_call | solution.py:576
  378.7 1.1 copy-done.19
  379.8 1.1 copy-done.21
  381.0 7.0 %weight_grads.1 = (bf16[1024,384]{1,0:T(8,128)(2,1)S(1)}, bf16[1536,384]{1,0:T(8,128)(2,1)}) custom-call(s32[4]{0:T(128)S(1)} %pad_add_fusion.ok_ref, bf16[3,1024,128]{2,1,0:T(8,128)(2,1)S(1)} %copy-done.19, f32[1024,128]{1,0:T(8,128)S(1)} %slice.79.dkv_ref, bf16[3,1024,128]{2,1,0:T(8,128)(2,1)S(1)} %copy-done.21, f32[1024,128]{1,0:T(8,128)S(1)} %copy-done.2, ...), custom_call_target="tpu_custom_call" | custom-call | tf_op jit(solution)/shard_map/weight_grads/pallas_call | solution.py:1031
  387.9 3.0 pad_maximum_fusion.p_ref
  390.9 63.2 %reduce_last.1 = (f32[128,1536]{1,0:T(8,128)}, bf16[8,48,384]{2,1,0:T(8,128)(2,1)}, bf16[1,4,48,384]{3,2,1,0:T(8,128)(2,1)}) custom-call(bf16[1024,384]{1,0:T(8,128)(2,1)} %copy-done.20, bf16[1536,384]{1,0:T(8,128)(2,1)} %bitcast.37, bf16[4,12,48,384]{3,2,1,0:T(8,128)(2,1)} %pad_maximum_fusion.p_ref), custom_call_target="tpu_custom_call" | custom-call | tf_op jit(solution)/shard_map/reduce_last/pallas_call | solution.py:714
  454.1 7.3 %finish.1 = (f32[128,1536]{1,0:T(8,128)}, f32[48,1536]{1,0:T(8,128)}, f32[48,512]{1,0:T(8,128)}, f32[48,512]{1,0:T(8,128)}, f32[48,128]{1,0:T(8,128)}, /*index=5...) custom-call(f32[128,1536]{1,0:T(8,128)} %get-tuple-element.111.d_ref, ...), custom_call_target="tpu_custom_call" | custom-call | tf_op jit(solution)/shard_map/finish/pallas_call | solution.py:1296
  461.5 1.5 slice_reduce_fusion
  (131 shorter events, 14.4 us)
Async XLA Ops:
  3.0 1.4 copy-start.13
  4.4 1.0 copy-start.15
  5.4 1.1 copy-start.22
  6.5 0.9 copy-start.25
  13.1 1.0 copy-start.29
  14.1 73.5 %copy-start.44 = (s32[128,8]{0,1:T(8,128)S(1)}, s32[128,8]{0,1:T(8,128)}, u32[]{:S(2)}) copy-start(s32[128,8]{0,1:T(8,128)} %param.15) | copy-start | bytes 12292
  14.1 74.2 %copy-start.49 = (s32[3]{0:T(128)S(1)}, s32[3]{0:T(128)}, u32[]{:S(2)}) copy-start(s32[3]{0:T(128)} %param.14) | copy-start | bytes 40
  86.3 25.6 %collective-permute-start = (bf16[384,768]{1,0:T(8,128)(2,1)}, bf16[384,768]{1,0:T(8,128)(2,1)}, u32[]{:S(2)}, u32[]{:S(2)}) collective-permute-start(bf16[384,768]{1,0:T(8,128)(2,1)} %get-tuple-element.81.rest_1_), channel_id=1, source_target_pairs={{0,16},{8,24},{16,0},{24,8},{1,17},{9,25},{17,1},{25,9},{2,18},{10... | collective-permute-start | bytes 1769480 | tf_op jit(solution)/shard_map/ppermute | solution.py:1373
  87.5 3.6 copy-start
  87.9 5.0 %copy-start.26 = (f32[1,1536]{1,0:T(1,128)}, f32[1,1536]{1,0:T(1,128)S(1)}, u32[]{:S(2)}) copy-start(f32[1,1536]{1,0:T(1,128)S(1)} %get-tuple-element.179.g_ref) | copy-start | bytes 18436
  88.3 10.5 %copy-start.38 = (pred[128,128]{1,0:T(8,128)(4,1)}, pred[128,128]{1,0:T(8,128)(4,1)S(1)}, u32[]{:S(2)}) copy-start(pred[128,128]{1,0:T(8,128)(4,1)S(1)} %fusion.3) | copy-start | bytes 49156
  90.5 8.3 %copy-start.1 = (f32[1024,128]{1,0:T(8,128)}, f32[1024,128]{1,0:T(8,128)S(1)}, u32[]{:S(2)}) copy-start(f32[1024,128]{1,0:T(8,128)S(1)} %get-tuple-element.182.c_ref) | copy-start | bytes 1572868
  92.9 1.9 copy-start.4
  98.8 1.7 copy-start.3
  132.7 4.5 copy-start.6
  132.7 37.6 %collective-permute-start.1 = (bf16[384,1536]{1,0:T(8,128)(2,1)}, bf16[384,1536]{1,0:T(8,128)(2,1)}, u32[]{:S(2)}, u32[]{:S(2)}) collective-permute-start(bf16[384,1536]{1,0:T(8,128)(2,1)} %copy-done.29), channel_id=1, source_target_pairs={{0,8},{8,0},{16,24},{24,16},{1,9},{9,1},{17,25},{25,17},{2,10},{10... | collective-permute-start | bytes 3538952 | tf_op jit(solution)/shard_map/ppermute | solution.py:1373
  133.0 53.6 %collective-permute-start.2 = (bf16[384,1536]{1,0:T(8,128)(2,1)}, bf16[384,1536]{1,0:T(8,128)(2,1)}, u32[]{:S(2)}, u32[]{:S(2)}) collective-permute-start(bf16[384,1536]{1,0:T(8,128)(2,1)} %copy-done.29), channel_id=1, source_target_pairs={{0,24},{8,16},{16,8},{24,0},{1,25},{9,17},{17,9},{25,1},{2,26},{10... | collective-permute-start | bytes 3538952 | tf_op jit(solution)/shard_map/ppermute | solution.py:1373
  136.0 9.7 %copy-start.9 = (bf16[4,48,1536]{2,1,0:T(8,128)(2,1)S(1)}, bf16[4,48,1536]{2,1,0:T(8,128)(2,1)}, u32[]{:S(2)}) copy-start(bf16[4,48,1536]{2,1,0:T(8,128)(2,1)} %get-tuple-element.88) | copy-start | bytes 1769476
  137.1 27.0 %copy-start.34 = (bf16[128,1536]{1,0:T(8,128)(2,1)S(1)}, bf16[128,1536]{1,0:T(8,128)(2,1)}, u32[]{:S(2)}) copy-start(bf16[128,1536]{1,0:T(8,128)(2,1)} %x_ref.3) | copy-start | bytes 1179652
  145.7 18.7 %copy-start.11 = (bf16[1024,192]{1,0:T(8,128)(2,1)}, bf16[1024,192]{1,0:T(8,128)(2,1)S(1)}, u32[]{:S(2)}) copy-start(bf16[1024,192]{1,0:T(8,128)(2,1)S(1)} %get-tuple-element.87.l_ref.o_ref) | copy-start | bytes 1179652
  145.7 18.6 %copy-start.14 = (f32[3,1024,1]{2,1,0:T(8,128)}, f32[3,1024,1]{2,1,0:T(8,128)S(1)}, u32[]{:S(2)}) copy-start(f32[3,1024,1]{2,1,0:T(8,128)S(1)} %get-tuple-element.86.l_ref) | copy-start | bytes 36868
  164.2 2.0 copy-start.42
  164.4 3.2 copy-start.46
  186.6 85.0 %copy-start.37 = (f32[128,128]{1,0:T(8,128)S(1)}, f32[128,128]{1,0:T(8,128)}, u32[]{:S(2)}) copy-start(f32[128,128]{1,0:T(8,128)} %copy.51) | copy-start | bytes 196612
  186.6 85.0 %copy-start.39 = (pred[128,128]{1,0:T(8,128)(4,1)S(1)}, pred[128,128]{1,0:T(8,128)(4,1)}, u32[]{:S(2)}) copy-start(pred[128,128]{1,0:T(8,128)(4,1)} %copy-done.38) | copy-start | bytes 49156
  186.6 85.0 %copy-start.45 = (f32[128]{0:T(128)S(1)}, f32[128]{0:T(128)}, u32[]{:S(2)}) copy-start(f32[128]{0:T(128)} %get-tuple-element.185) | copy-start | bytes 1540
  186.6 87.3 %copy-start.47 = (f32[128]{0:T(128)S(1)}, f32[128]{0:T(128)}, u32[]{:S(2)}) copy-start(f32[128]{0:T(128)} %copy-done.46) | copy-start | bytes 1540
  272.7 8.2 %copy-start.16 = (bf16[128,1536]{1,0:T(8,128)(2,1)S(1)}, bf16[128,1536]{1,0:T(8,128)(2,1)}, u32[]{:S(2)}) copy-start(bf16[128,1536]{1,0:T(8,128)(2,1)} %c_ref.1) | copy-start | bytes 1179652
  272.7 8.2 %copy-start.31 = (f32[128,1536]{1,0:T(8,128)S(1)}, f32[128,1536]{1,0:T(8,128)}, u32[]{:S(2)}) copy-start(f32[128,1536]{1,0:T(8,128)} %copy-done.30) | copy-start | bytes 2359300
  273.8 8.3 %copy-start.40 = (bf16[128,128]{1,0:T(8,128)(2,1)}, bf16[128,128]{1,0:T(8,128)(2,1)S(1)}, u32[]{:S(2)}) copy-start(bf16[128,128]{1,0:T(8,128)(2,1)S(1)} %multiply_convert_fusion.1) | copy-start | bytes 98308
  273.8 74.7 %collective-permute-start.6 = (bf16[384,1536]{1,0:T(8,128)(2,1)}, bf16[384,1536]{1,0:T(8,128)(2,1)}, u32[]{:S(2)}, u32[]{:S(2)}) collective-permute-start(bf16[384,1536]{1,0:T(8,128)(2,1)} %get-tuple-element.103), channel_id=1, source_target_pairs={{0,8},{8,0},{16,24},{24,16},{1,9},{9,1},{17,25},{25,17},{2,10},{10... | collective-permute-start | bytes 3538952 | tf_op jit(solution)/shard_map/ppermute | solution.py:1373
  276.3 72.1 %collective-permute-start.3 = (bf16[384,768]{1,0:T(8,128)(2,1)}, bf16[384,768]{1,0:T(8,128)(2,1)}, u32[]{:S(2)}, u32[]{:S(2)}) collective-permute-start(bf16[384,768]{1,0:T(8,128)(2,1)} %get-tuple-element.100), channel_id=1, source_target_pairs={{0,16},{8,24},{16,0},{24,8},{1,17},{9,25},{17,1},{25,9},{2,18},{10... | collective-permute-start | bytes 1769480 | tf_op jit(solution)/shard_map/ppermute | solution.py:1373
  277.6 70.9 %collective-permute-start.4 = (bf16[384,768]{1,0:T(8,128)(2,1)}, bf16[384,768]{1,0:T(8,128)(2,1)}, u32[]{:S(2)}, u32[]{:S(2)}) collective-permute-start(bf16[384,768]{1,0:T(8,128)(2,1)} %get-tuple-element.101), channel_id=1, source_target_pairs={{0,24},{8,16},{16,8},{24,0},{1,25},{9,17},{17,9},{25,1},{2,26},{10... | collective-permute-start | bytes 1769480 | tf_op jit(solution)/shard_map/ppermute | solution.py:1373
  279.8 68.6 %collective-permute-start.5 = (bf16[384,768]{1,0:T(8,128)(2,1)}, bf16[384,768]{1,0:T(8,128)(2,1)}, u32[]{:S(2)}, u32[]{:S(2)}) collective-permute-start(bf16[384,768]{1,0:T(8,128)(2,1)} %get-tuple-element.102), channel_id=1, source_target_pairs={{0,24},{8,16},{16,8},{24,0},{1,25},{9,17},{17,9},{25,1},{2,26},{10... | collective-permute-start | bytes 1769480 | tf_op jit(solution)/shard_map/ppermute | solution.py:1373
  282.1 48.3 %copy-start.7 = (bf16[3,1024,128]{2,1,0:T(8,128)(2,1)S(1)}, bf16[3,1024,128]{2,1,0:T(8,128)(2,1)}, u32[]{:S(2)}) copy-start(bf16[3,1024,128]{2,1,0:T(8,128)(2,1)} %copy-done.5) | copy-start | bytes 2359300
  282.1 48.3 %copy-start.10 = (bf16[4,48,1536]{2,1,0:T(8,128)(2,1)S(1)}, bf16[4,48,1536]{2,1,0:T(8,128)(2,1)}, u32[]{:S(2)}) copy-start(bf16[4,48,1536]{2,1,0:T(8,128)(2,1)} %get-tuple-element.88) | copy-start | bytes 1769476
  282.1 48.3 %copy-start.12 = (bf16[1024,192]{1,0:T(8,128)(2,1)S(1)}, bf16[1024,192]{1,0:T(8,128)(2,1)}, u32[]{:S(2)}) copy-start(bf16[1024,192]{1,0:T(8,128)(2,1)} %copy-done.11) | copy-start | bytes 1179652
  346.0 0.9 copy-start.18
  346.9 1.1 copy-start.33
  346.9 1.1 copy-start.41
  346.9 1.1 copy-start.43
  346.9 1.1 copy-start.48
  347.1 1.7 copy-start.35
  348.9 29.7 %copy-start.2 = (f32[1024,128]{1,0:T(8,128)S(1)}, f32[1024,128]{1,0:T(8,128)}, u32[]{:S(2)}) copy-start(f32[1024,128]{1,0:T(8,128)} %copy-done.1) | copy-start | bytes 1572868
  378.7 1.1 copy-start.19
  379.8 1.1 copy-start.21
  381.0 7.0 %copy-start.36 = (bf16[4,1,48,4,384]{4,2,3,0,1:T(8,128)(2,1)S(1)}, bf16[4,1,48,4,384]{4,2,3,0,1:T(8,128)(2,1)}, u32[]{:S(2)}) copy-start(bf16[4,1,48,4,384]{4,2,3,0,1:T(8,128)(2,1)} %copy.58) | copy-start | bytes 1769476
  387.9 3.0 copy-start.20
  (9 other events, 7.1 us)

commit v5 on v4

--- a/solution.py
+++ b/solution.py
@@ -609,26 +609,31 @@
 
         pl.semaphore_wait(bar, n - 1)
 
-        def hop(way, o):
+        chunk = count // 2
+        part_of = lambda c: pl.ds(c * chunk, chunk)
+
+        def hop(way, o, c):
             to = u - 1 if way == 0 else u + 1
-            return remote(tmp.at[way, o], land.at[way, o], zs.at[way, o], zr.at[way, o], to, me.b)
-
-        def add(way, o):
-            @pl.loop(0, count)
-            def _(t):
-                tmp[way, o, t] = (p_ref[o, t].astype(f32) + land[way, o, t].astype(f32)).astype(bf16)
+            return remote(tmp.at[way, o, part_of(c)], land.at[way, o, part_of(c)],
+                          zs.at[way, o, c], zr.at[way, o, c], to, me.b)
 
         def ends(way, o):
             def run():
-                tmp[way, o] = p_ref[o]
-                hop(way, o).start()
+                for c in range(2):
+                    tmp[way, o, part_of(c)] = p_ref[o, part_of(c)]
+                    hop(way, o, c).start()
             return run
 
         def passes(way, o):
             def run():
-                hop(way, o).wait_recv()
-                add(way, o)
-                hop(way, o).start()
+                for c in range(2):
+                    hop(way, o, c).wait_recv()
+
+                    @pl.loop(c * chunk, (c + 1) * chunk)
+                    def _(t):
+                        tmp[way, o, t] = (p_ref[o, t].astype(f32) + land[way, o, t].astype(f32)).astype(bf16)
+
+                    hop(way, o, c).start()
             return run
 
         def down(o):
@@ -638,32 +643,40 @@
             return u < o
 
         ways = [(0, o) for o in range(nz - 1)], [(1, o) for o in range(nz - 1, 0, -1)]
-        for pair in zip(*ways):
-            for way, o in pair:
-                pl.when(u == (0 if way else nz - 1))(ends(way, o))
+        for way, o in ways[0] + ways[1]:
+            pl.when(u == (0 if way else nz - 1))(ends(way, o))
 
         def relay(way, o):
             inner = (u > 0) & (u < nz - 1) & (up(o) if way else down(o))
-            pl.when(inner)(passes(way, o))
+            return inner, passes(way, o)
+
+        low = 2 * u < nz - 1
+
+        def relays(lo, hi, near):
+            for way in range(2):
+                mine = low if (way == 1) == near else jnp.logical_not(low)
+                for way_o in ways[way][lo:hi]:
+                    inner, run = relay(*way_o)
+                    pl.when(mine & inner)(run)
 
         def block(t):
             rows_t = l_ref[pl.ds(pl.multiple_of(t * rows, rows), rows), :]
             return lax.dot_general(rows_t, r_ref[...], NT, preferred_element_type=f32)
 
         red = made(me, block, *scratch, waits=False)
-        pairs = list(zip(*ways))
-        for k, pair in enumerate(pairs):
-            for way, o in pair:
-                relay(way, o)
-            if k == 0:
-                for j in red.order[:-1]:
-                    red.phase1(j)
-            if k == len(pairs) - 2:
-                red.phase2()
+        relays(0, 1, True)
+        for j in red.order[:-1]:
+            red.phase1(j)
+        relays(1, nz, True)
+        red.phase2()
+        relays(0, nz, False)
 
         def here(way):
-            pl.when((u > 0) if way else (u < nz - 1))(
-                lambda: remote(tmp.at[way, u], land.at[way, u], zs.at[way, u], zr.at[way, u], u, me.sib).wait_recv())
+            def run():
+                for c in range(2):
+                    at = tmp.at[way, u, part_of(c)]
+                    remote(at, at, zs.at[way, u, c], zr.at[way, u, c], u, me.sib).wait_recv()
+            pl.when((u > 0) if way else (u < nz - 1))(run)
 
         here(0)
         here(1)
@@ -696,7 +709,8 @@
         red.end(write_to(o_ref))
         red.sent()
         for way, o in ways[0] + ways[1]:
-            pl.when(up(o) if way else down(o))(lambda way=way, o=o: hop(way, o).wait_send())
+            for c in range(2):
+                pl.when(up(o) if way else down(o))(lambda way=way, o=o, c=c: hop(way, o, c).wait_send())
         for c in out:
             c.wait()
         own.wait()
@@ -720,7 +734,7 @@
         out_specs=(VMEM, ANY, ANY),
         scratch_shapes=[pltpu.VMEM((2, nz, count, shard, width), bf16)] * 2
         + [pltpu.VMEM((count, shard, width), bf16)]
-        + [DMA((2, nz))] * 2
+        + [DMA((2, nz, 2))] * 2
         + [DMA((nb,))] * 2
         + [DMA((rp,))] * 2
         + [DMA((2,))]
@@ -765,7 +779,19 @@
     W = 3 * FF
     half = W // 2
 
-    def kernel(q_ref, k_ref, v_ref, x_ref, n_ref, i_ref, o_ref, c_ref, r_ref, p_ref, g_ref, a_ref, b_ref, f_ref):
+    ins = (w_query, w_key, w_value, extra[0], gains, w_inner, w_outer, cotangent, routes)
+
+    def kernel(*refs):
+        n, m = len(ins), len(outs)
+        hbm, (isem, osem), vmem = refs[:n + m], refs[n + m:n + m + 2], refs[n + m + 2:]
+        loads = [pltpu.make_async_copy(hbm[k], vmem[k], isem.at[k]) for k in range(n)]
+        for c in loads:
+            c.start()
+        q_ref, k_ref, v_ref, x_ref, n_ref, i_ref, o_ref, c_ref, r_ref = vmem[:n]
+        p_ref, g_ref, a_ref, b_ref, f_ref = vmem[n:]
+        saves = [pltpu.make_async_copy(vmem[n + k], hbm[n + k], osem.at[k]) for k in range(m)]
+        for c in loads:
+            c.wait()
         low = low_half()
         lane = lax.broadcasted_iota(jnp.int32, (1, LANES), 1)
 
@@ -784,11 +810,13 @@
             p_ref[h, :, :LANES] = two(low64(q_ref, at), low64(q_ref, at + HW))
             p_ref[h, :, LANES:2 * LANES] = two(low64(q_ref, at + 2 * HW), low64(k_ref, h * HW))
             p_ref[h, :, 2 * LANES:] = jnp.where(low, low64(v_ref, h * HW), tail).astype(bf16)
+        saves[0].start()
         g_ref[:, :D] = c_ref[...]
         named = r_ref[:, 0:1] + HW == lane
         for j in range(1, TOPK):
             named = named | (r_ref[:, j:j + 1] + HW == lane)
         g_ref[:, D:] = jnp.where(named, 1.0, 0.0).astype(bf16)
+        saves[1].start()
         odd = lax.rem(lax.axis_index("ulysses"), 2)
         same, outer = i_ref[odd], o_ref[odd].astype(f32).T.astype(bf16)
         a_ref[...] = same[:, :half]
@@ -796,18 +824,25 @@
         b_ref[:, 2 * FF - half:] = outer
         f_ref[:, :2 * FF] = i_ref[1 - odd]
         f_ref[:, 2 * FF:] = o_ref[1 - odd].astype(f32).T.astype(bf16)
+        for c in saves[2:]:
+            c.start()
+        for c in saves:
+            c.wait()
 
     r_first = extra[1]
     sh = lambda *shape: jax.ShapeDtypeStruct(shape, bf16)
+    outs = (sh(KV, S, AUX), sh(T, D + LANES), sh(dz, half), sh(dz, half), sh(dz, W))
     return pl.pallas_call(
         kernel,
-        out_shape=(sh(KV, S, AUX), sh(T, D + LANES), sh(dz, half), sh(dz, half), sh(dz, W)),
-        in_specs=[VMEM] * 9,
-        out_specs=(VMEM,) * 5,
+        out_shape=outs,
+        in_specs=[ANY] * len(ins),
+        out_specs=(ANY,) * len(outs),
+        scratch_shapes=[DMA((len(ins),)), DMA((len(outs),))]
+        + [pltpu.VMEM(a.shape, a.dtype) for a in (*ins, *outs)],
         compiler_params=pltpu.CompilerParams(vmem_limit_bytes=48 * MIB),
         cost_estimate=NO_COST,
         name="prepare",
-    )(w_query, w_key, w_value, extra[0], gains, w_inner, w_outer, cotangent, routes)
+    )(*ins)
 
 
 def project(x, gain, packed, c, s1, s2):
@@ -1410,8 +1445,8 @@
     n2, inv2, scaled2 = norm_rows(resid, gain2)
     h2_own = scaled2.astype(bf16)
     hot = (lanes == HW + b * EXP_DEV + odd).astype(f32)[None, :]
-    sent = (early, 0, half)
-    leave = [(0, 0, W), (early, half, half), (nz - 1, 0, half), (nz - 1, half, half)]
+    sent = (early, 0, FF)
+    leave = [(0, 0, W), (early, FF, W - FF), (nz - 1, 0, half), (nz - 1, half, half)]
     leave += [(d, 0, W) for d in range(1, nz - 1) if d != early]
     y, summed, *grads = experts(h2_own, g_own, g_oth, router, hot, weights, sent, leave, nz, nb, 3)
     grads, got = grads[:len(leave)], grads[len(leave)]

time: 468 us -> 449 us (0.959)
  Pallas kernels: 380 us -> 361 us
    pallas_call x1, Pallas kernels: 63.2 us -> 51.1 us  [reduce_last(): pl.pallas_call(kernel, out_shape=(sh((rows, cols), f32), sh((nb, shard, w...]
    pallas_call x1, Pallas kernels: 84 us -> 74.9 us  [experts(): pl.pallas_call(kernel, out_shape=(sh((2, nb, T, D), bf16), sh((T, C), f32...]
  transfers between devices with their start and end apart: 7 -> 7, of which waited for: 2 -> 2; matrix products, arithmetic and copies ran while one was open for 4% -> 4% of each run, Pallas kernels for 20% -> 21%
where the time goes in v5:
time: 449 us; the launch traced here: 448 us
  Pallas kernels  361 us (80%)
  local copies, waits for them, and re-layouts  31.3 us (7%)
  waiting for transfers between devices  25.4 us (6%)
  other arithmetic  15.5 us (3%)
  starting transfers between devices  9.09 us (2%)
    pallas_call x1, Pallas kernels, experts(): pl.pallas_call(kernel, out_shape=(sh((2, nb, T, D), bf16), sh((T, C), f32...  74.9 us
    pallas_call x1, Pallas kernels, gather_inputs(): pl.pallas_call(kernel, out_shape=(sh((nb,) + x.shape, x.dtype), sh((nz, n...  72.1 us
    pallas_call x1, Pallas kernels, reduce_last(): pl.pallas_call(kernel, out_shape=(sh((rows, cols), f32), sh((nb, shard, w...  51.1 us
    pallas_call x1, Pallas kernels, middle(): pl.pallas_call(kernel, out_shape=(sh((nb,) + x.shape, x.dtype), sh((rows,...  46.8 us
    pallas_call x1, Pallas kernels, halo_back(): pl.pallas_call(kernel, out_shape=(jax.ShapeDtypeStruct(((back + 1) * rp,...  31.8 us
    ppermute x7, waiting for transfers between devices, on_device(): give = lambda w, d: lax.ppermute(w, 'ulysses', flip(d))  25.4 us
    unnamed x104, local copies, waits for them, and re-layouts  22.1 us
    pallas_call x1, Pallas kernels, halo_forward(): pl.pallas_call(kernel, out_shape=(sh((back,) + kv.shape, kv.dtype), sh((n...  20.8 us
  transfers between devices with their start and end apart: 7, of which 2 were waited for; matrix products, arithmetic and copies ran while one was open for 4% of the time, Pallas kernels for 21%

profile of v5, /device:TPU:1, one launch (start us, length us, event | category | flops | bytes accessed | tf_op | source)
XLA Modules:
  0.0 448.2 jit_solution(6699465943396237202)
XLA Ops:
  3.0 1.4 copy-done.13
  4.4 1.0 copy-done.15
  5.4 1.1 copy-done.22
  6.5 0.9 copy-done.25
  9.0 3.0 prepare.1
  12.1 0.8 copy-done.8
  14.4 1.0 copy-done.29
  15.4 72.1 %gather_inputs.1 = (bf16[8,128,1536]{2,1,0:T(8,128)(2,1)}, bf16[4,8,48,384]{3,2,1,0:T(8,128)(2,1)}, bf16[4,48,1536]{2,1,0:T(8,128)(2,1)}, bf16[8,128,1664]{2,1,0...) custom-call(bf16[128,1536]{1,0:T(8,128)(2,1)} %x_ref.3, bf16[8,48,384]{2,1,0:T(8,128)(2,1)} %copy-done.24, ...), custom_call_target="tpu_custom_call" | custom-call | tf_op jit(solution)/shard_map/gather_inputs/pallas_call | solution.py:377
  87.6 1.2 slice_convert_fusion
  89.8 1.9 fusion
  94.2 1.9 copy-done.4
  96.1 4.0 project.1
  100.1 1.7 copy-done.3
  101.8 0.9 copy-done.5
  104.1 9.1 %collective-permute-done.rest_3_ = bf16[384,768]{1,0:T(8,128)(2,1)} collective-permute-done((bf16[384,768]{1,0:T(8,128)(2,1)}, bf16[384,768]{1,0:T(8,128)(2,1)}, u32[]{:S(2)}, u32[]{:S(2)}) %collective-permute-start) | collective-permute-done | bytes 589856 | tf_op jit(solution)/shard_map/ppermute | solution.py:1408
  113.1 20.8 %halo_forward.1 = (bf16[2,1024,128]{2,1,0:T(8,128)(2,1)}, bf16[8,128,1664]{2,1,0:T(8,128)(2,1)}) custom-call(bf16[1024,128]{1,0:T(8,128)(2,1)} %copy-done.17, bf16[128,1664]{1,0:T(8,128)(2,1)} %get-tuple-element.83.g_ref), custom_call_target="tpu_custom_call" | custom-call | tf_op jit(solution)/shard_map/halo_forward/pallas_call | solution.py:430
  134.3 2.0 collective-permute-start.2
  136.3 1.1 slice_bitcast_fusion.3
  137.3 1.1 pad_maximum_fusion.1.kv_ref
  138.4 8.6 %attend.1 = (bf16[1024,192]{1,0:T(8,128)(2,1)S(1)}, f32[3,1024,1]{2,1,0:T(8,128)S(1)}) custom-call(s32[5]{0:T(128)S(1)} %pad_add_fusion.1.meta, bf16[3,1024,128]{2,1,0:T(8,128)(2,1)S(1)} %copy-done.6, bf16[3072,128]{1,0:T(8,128)(2,1)S(1)} %pad_maximum_fusion.1.kv_ref, s32[1024,1]{1,0:T(8,128)S(1)} %copy.52.st_ref), custom_call_target="tpu_custom_call" | custom-call | tf_op jit(solution)/shard_map/attend/pallas_call | solution.py:938
  147.1 18.4 %reduce_product.1 = f32[128,1536]{1,0:T(8,128)S(1)} custom-call(bf16[1024,192]{1,0:T(8,128)(2,1)S(1)} %get-tuple-element.87.l_ref.o_ref, bf16[192,1536]{1,0:T(8,128)(2,1)S(1)} %bitcast.43), custom_call_target="tpu_custom_call" | custom-call | tf_op jit(solution)/shard_map/reduce_product/pallas_call | solution.py:480
  165.7 0.8 copy-done.30
  167.5 1.5 select_reduce_fusion
  168.9 1.6 copy.51
  170.5 1.0 fusion.5
  171.5 16.3 %collective-permute-done.2.rest_5_ = bf16[384,1536]{1,0:T(8,128)(2,1)} collective-permute-done((bf16[384,1536]{1,0:T(8,128)(2,1)}, bf16[384,1536]{1,0:T(8,128)(2,1)}, u32[]{:S(2)}, u32[]{:S(2)}) %collective-permute-start.2) | collective-permute-done | bytes 1179680 | tf_op jit(solution)/shard_map/ppermute | solution.py:1408
  187.9 74.9 %experts.1 = (bf16[2,8,128,1536]{3,2,1,0:T(8,128)(2,1)}, f32[128,1664]{1,0:T(8,128)}, bf16[384,1536]{1,0:T(8,128)(2,1)}, bf16[384,1024]{1,0:T(8,128)(2,1)}, bf16...) custom-call(bf16[128,1536]{1,0:T(8,128)(2,1)} %copy-done.32, ...), custom_call_target="tpu_custom_call" | custom-call | tf_op jit(solution)/shard_map/experts/pallas_call | solution.py:1265
  262.8 1.0 fusion.18
  263.8 1.0 multiply_reduce_fusion.3
  264.9 1.1 multiply_convert_fusion.1
  266.1 2.4 multiply_reduce_fusion
  268.5 3.4 collective-permute-start.3
  272.0 3.1 collective-permute-start.5
  275.1 1.3 fusion.17
  276.4 46.8 %middle.1 = (bf16[8,128,1536]{2,1,0:T(8,128)(2,1)}, f32[128,1536]{1,0:T(8,128)}, bf16[128,1536]{1,0:T(8,128)(2,1)}) custom-call(bf16[128,1536]{1,0:T(8,128)(2,1)} %get-tuple-element.168.x_ref, bf16[2,8,128,1536]{3,2,1,0:T(8,128)(2,1)} %get-tuple-element.95.y_ref), custom_call_target="tpu_custom_call" | custom-call | tf_op jit(solution)/shard_map/middle/pallas_call | solution.py:522
  323.3 15.5 %attend_back.1 = (bf16[3,1024,128]{2,1,0:T(8,128)(2,1)S(1)}, f32[3072,128]{1,0:T(8,128)}, f32[192,1536]{1,0:T(8,128)S(1)}) custom-call(s32[5]{0:T(128)S(1)} %pad_add_fusion.1.meta, bf16[3,1024,128]{2,1,0:T(8,128)(2,1)S(1)} %copy-done.7, bf16[3072,128]{1,0:T(8,128)(2,1)S(1)} %pad_maximum_fusion.1.kv_ref, s32[1024,1]{1,0:T(8,128)S(1)} %copy.52.st_ref, ...), custom_call_target="tpu_custom_call" | custom-call | tf_op jit(solution)/shard_map/attend_back/pallas_call | solution.py:1009
  338.8 0.9 copy-done.18
  339.9 0.9 copy.58
  341.8 1.0 pad_maximum_fusion.2.d_ref
  342.8 31.8 %halo_back.1 = (bf16[3,1024,128]{2,1,0:T(8,128)(2,1)}, bf16[128,1536]{1,0:T(8,128)(2,1)}) custom-call(bf16[3,1024,128]{2,1,0:T(8,128)(2,1)} %pad_maximum_fusion.2.d_ref, bf16[128,1536]{1,0:T(8,128)(2,1)} %get-tuple-element.105.y_ref), custom_call_target="tpu_custom_call" | custom-call | tf_op jit(solution)/shard_map/halo_back/pallas_call | solution.py:576
  374.6 1.1 copy-done.19
  375.7 1.1 copy-done.21
  376.8 7.0 %weight_grads.1 = (bf16[1024,384]{1,0:T(8,128)(2,1)S(1)}, bf16[1536,384]{1,0:T(8,128)(2,1)}) custom-call(s32[4]{0:T(128)S(1)} %pad_add_fusion.ok_ref, bf16[3,1024,128]{2,1,0:T(8,128)(2,1)S(1)} %copy-done.19, f32[1024,128]{1,0:T(8,128)S(1)} %slice.79.dkv_ref, bf16[3,1024,128]{2,1,0:T(8,128)(2,1)S(1)} %copy-done.21, f32[1024,128]{1,0:T(8,128)S(1)} %copy-done.2, ...), custom_call_target="tpu_custom_call" | custom-call | tf_op jit(solution)/shard_map/weight_grads/pallas_call | solution.py:1066
  383.8 3.0 pad_maximum_fusion.p_ref
  386.8 51.1 %reduce_last.1 = (f32[128,1536]{1,0:T(8,128)}, bf16[8,48,384]{2,1,0:T(8,128)(2,1)}, bf16[1,4,48,384]{3,2,1,0:T(8,128)(2,1)}) custom-call(bf16[1024,384]{1,0:T(8,128)(2,1)} %copy-done.20, bf16[1536,384]{1,0:T(8,128)(2,1)} %bitcast.37, bf16[4,12,48,384]{3,2,1,0:T(8,128)(2,1)} %pad_maximum_fusion.p_ref), custom_call_target="tpu_custom_call" | custom-call | tf_op jit(solution)/shard_map/reduce_last/pallas_call | solution.py:728
  437.9 7.3 %finish.1 = (f32[128,1536]{1,0:T(8,128)}, f32[48,1536]{1,0:T(8,128)}, f32[48,512]{1,0:T(8,128)}, f32[48,512]{1,0:T(8,128)}, f32[48,128]{1,0:T(8,128)}, /*index=5...) custom-call(f32[128,1536]{1,0:T(8,128)} %get-tuple-element.111.d_ref, ...), custom_call_target="tpu_custom_call" | custom-call | tf_op jit(solution)/shard_map/finish/pallas_call | solution.py:1331
  445.2 1.5 slice_reduce_fusion
  446.7 0.8 slice.87
  (131 shorter events, 13.8 us)
Async XLA Ops:
  3.0 1.4 copy-start.13
  4.4 1.0 copy-start.15
  5.4 1.1 copy-start.22
  6.5 0.9 copy-start.25
  14.4 1.0 copy-start.29
  15.4 73.5 %copy-start.44 = (s32[128,8]{0,1:T(8,128)S(1)}, s32[128,8]{0,1:T(8,128)}, u32[]{:S(2)}) copy-start(s32[128,8]{0,1:T(8,128)} %param.15) | copy-start | bytes 12292
  15.4 74.2 %copy-start.49 = (s32[3]{0:T(128)S(1)}, s32[3]{0:T(128)}, u32[]{:S(2)}) copy-start(s32[3]{0:T(128)} %param.14) | copy-start | bytes 40
  87.5 25.6 %collective-permute-start = (bf16[384,768]{1,0:T(8,128)(2,1)}, bf16[384,768]{1,0:T(8,128)(2,1)}, u32[]{:S(2)}, u32[]{:S(2)}) collective-permute-start(bf16[384,768]{1,0:T(8,128)(2,1)} %get-tuple-element.81.rest_1_), channel_id=1, source_target_pairs={{0,16},{8,24},{16,0},{24,8},{1,17},{9,25},{17,1},{25,9},{2,18},{10... | collective-permute-start | bytes 1769480 | tf_op jit(solution)/shard_map/ppermute | solution.py:1408
  88.8 3.6 copy-start
  89.2 5.1 %copy-start.26 = (f32[1,1536]{1,0:T(1,128)}, f32[1,1536]{1,0:T(1,128)S(1)}, u32[]{:S(2)}) copy-start(f32[1,1536]{1,0:T(1,128)S(1)} %get-tuple-element.179.g_ref) | copy-start | bytes 18436
  89.5 10.6 %copy-start.38 = (pred[128,128]{1,0:T(8,128)(4,1)}, pred[128,128]{1,0:T(8,128)(4,1)S(1)}, u32[]{:S(2)}) copy-start(pred[128,128]{1,0:T(8,128)(4,1)S(1)} %fusion.3) | copy-start | bytes 49156
  91.8 8.3 %copy-start.1 = (f32[1024,128]{1,0:T(8,128)}, f32[1024,128]{1,0:T(8,128)S(1)}, u32[]{:S(2)}) copy-start(f32[1024,128]{1,0:T(8,128)S(1)} %get-tuple-element.182.c_ref) | copy-start | bytes 1572868
  94.2 1.9 copy-start.4
  100.1 1.7 copy-start.3
  101.8 0.9 copy-start.5
  133.9 4.5 copy-start.6
  133.9 37.6 %collective-permute-start.1 = (bf16[384,1536]{1,0:T(8,128)(2,1)}, bf16[384,1536]{1,0:T(8,128)(2,1)}, u32[]{:S(2)}, u32[]{:S(2)}) collective-permute-start(bf16[384,1536]{1,0:T(8,128)(2,1)} %copy-done.29), channel_id=1, source_target_pairs={{0,8},{8,0},{16,24},{24,16},{1,9},{9,1},{17,25},{25,17},{2,10},{10... | collective-permute-start | bytes 3538952 | tf_op jit(solution)/shard_map/ppermute | solution.py:1408
  134.3 53.6 %collective-permute-start.2 = (bf16[384,1536]{1,0:T(8,128)(2,1)}, bf16[384,1536]{1,0:T(8,128)(2,1)}, u32[]{:S(2)}, u32[]{:S(2)}) collective-permute-start(bf16[384,1536]{1,0:T(8,128)(2,1)} %copy-done.29), channel_id=1, source_target_pairs={{0,24},{8,16},{16,8},{24,0},{1,25},{9,17},{17,9},{25,1},{2,26},{10... | collective-permute-start | bytes 3538952 | tf_op jit(solution)/shard_map/ppermute | solution.py:1408
  137.3 9.7 %copy-start.9 = (bf16[4,48,1536]{2,1,0:T(8,128)(2,1)S(1)}, bf16[4,48,1536]{2,1,0:T(8,128)(2,1)}, u32[]{:S(2)}) copy-start(bf16[4,48,1536]{2,1,0:T(8,128)(2,1)} %get-tuple-element.88) | copy-start | bytes 1769476
  138.4 27.0 %copy-start.34 = (bf16[128,1536]{1,0:T(8,128)(2,1)S(1)}, bf16[128,1536]{1,0:T(8,128)(2,1)}, u32[]{:S(2)}) copy-start(bf16[128,1536]{1,0:T(8,128)(2,1)} %x_ref.3) | copy-start | bytes 1179652
  147.0 18.7 %copy-start.11 = (bf16[1024,192]{1,0:T(8,128)(2,1)}, bf16[1024,192]{1,0:T(8,128)(2,1)S(1)}, u32[]{:S(2)}) copy-start(bf16[1024,192]{1,0:T(8,128)(2,1)S(1)} %get-tuple-element.87.l_ref.o_ref) | copy-start | bytes 1179652
  147.0 18.6 %copy-start.14 = (f32[3,1024,1]{2,1,0:T(8,128)}, f32[3,1024,1]{2,1,0:T(8,128)S(1)}, u32[]{:S(2)}) copy-start(f32[3,1024,1]{2,1,0:T(8,128)S(1)} %get-tuple-element.86.l_ref) | copy-start | bytes 36868
  165.5 2.0 copy-start.42
  165.7 3.2 copy-start.46
  187.9 75.9 %copy-start.37 = (f32[128,128]{1,0:T(8,128)S(1)}, f32[128,128]{1,0:T(8,128)}, u32[]{:S(2)}) copy-start(f32[128,128]{1,0:T(8,128)} %copy.51) | copy-start | bytes 196612
  187.9 76.0 %copy-start.39 = (pred[128,128]{1,0:T(8,128)(4,1)S(1)}, pred[128,128]{1,0:T(8,128)(4,1)}, u32[]{:S(2)}) copy-start(pred[128,128]{1,0:T(8,128)(4,1)} %copy-done.38) | copy-start | bytes 49156
  187.9 76.0 %copy-start.45 = (f32[128]{0:T(128)S(1)}, f32[128]{0:T(128)}, u32[]{:S(2)}) copy-start(f32[128]{0:T(128)} %get-tuple-element.185) | copy-start | bytes 1540
  187.9 78.2 %copy-start.47 = (f32[128]{0:T(128)S(1)}, f32[128]{0:T(128)}, u32[]{:S(2)}) copy-start(f32[128]{0:T(128)} %copy-done.46) | copy-start | bytes 1540
  264.9 10.2 %copy-start.16 = (bf16[128,1536]{1,0:T(8,128)(2,1)S(1)}, bf16[128,1536]{1,0:T(8,128)(2,1)}, u32[]{:S(2)}) copy-start(bf16[128,1536]{1,0:T(8,128)(2,1)} %refs_7_.1) | copy-start | bytes 1179652
  264.9 10.2 %copy-start.31 = (f32[128,1536]{1,0:T(8,128)S(1)}, f32[128,1536]{1,0:T(8,128)}, u32[]{:S(2)}) copy-start(f32[128,1536]{1,0:T(8,128)} %copy-done.30) | copy-start | bytes 2359300
  266.0 10.4 %copy-start.40 = (bf16[128,128]{1,0:T(8,128)(2,1)}, bf16[128,128]{1,0:T(8,128)(2,1)S(1)}, u32[]{:S(2)}) copy-start(bf16[128,128]{1,0:T(8,128)(2,1)S(1)} %multiply_convert_fusion.1) | copy-start | bytes 98308
  266.0 75.3 %collective-permute-start.6 = (bf16[384,1536]{1,0:T(8,128)(2,1)}, bf16[384,1536]{1,0:T(8,128)(2,1)}, u32[]{:S(2)}, u32[]{:S(2)}) collective-permute-start(bf16[384,1536]{1,0:T(8,128)(2,1)} %get-tuple-element.103), channel_id=1, source_target_pairs={{0,8},{8,0},{16,24},{24,16},{1,9},{9,1},{17,25},{25,17},{2,10},{10... | collective-permute-start | bytes 3538952 | tf_op jit(solution)/shard_map/ppermute | solution.py:1408
  268.5 72.8 %collective-permute-start.3 = (bf16[384,1024]{1,0:T(8,128)(2,1)}, bf16[384,1024]{1,0:T(8,128)(2,1)}, u32[]{:S(2)}, u32[]{:S(2)}) collective-permute-start(bf16[384,1024]{1,0:T(8,128)(2,1)} %get-tuple-element.100), channel_id=1, source_target_pairs={{0,16},{8,24},{16,0},{24,8},{1,17},{9,25},{17,1},{25,9},{2,18},{10... | collective-permute-start | bytes 2359304 | tf_op jit(solution)/shard_map/ppermute | solution.py:1408
  271.9 69.4 %collective-permute-start.4 = (bf16[384,768]{1,0:T(8,128)(2,1)}, bf16[384,768]{1,0:T(8,128)(2,1)}, u32[]{:S(2)}, u32[]{:S(2)}) collective-permute-start(bf16[384,768]{1,0:T(8,128)(2,1)} %get-tuple-element.101), channel_id=1, source_target_pairs={{0,24},{8,16},{16,8},{24,0},{1,25},{9,17},{17,9},{25,1},{2,26},{10... | collective-permute-start | bytes 1769480 | tf_op jit(solution)/shard_map/ppermute | solution.py:1408
  272.0 69.3 %collective-permute-start.5 = (bf16[384,768]{1,0:T(8,128)(2,1)}, bf16[384,768]{1,0:T(8,128)(2,1)}, u32[]{:S(2)}, u32[]{:S(2)}) collective-permute-start(bf16[384,768]{1,0:T(8,128)(2,1)} %get-tuple-element.102), channel_id=1, source_target_pairs={{0,24},{8,16},{16,8},{24,0},{1,25},{9,17},{17,9},{25,1},{2,26},{10... | collective-permute-start | bytes 1769480 | tf_op jit(solution)/shard_map/ppermute | solution.py:1408
  276.4 46.8 %copy-start.7 = (bf16[3,1024,128]{2,1,0:T(8,128)(2,1)S(1)}, bf16[3,1024,128]{2,1,0:T(8,128)(2,1)}, u32[]{:S(2)}) copy-start(bf16[3,1024,128]{2,1,0:T(8,128)(2,1)} %copy-done.5) | copy-start | bytes 2359300
  276.4 46.8 %copy-start.10 = (bf16[4,48,1536]{2,1,0:T(8,128)(2,1)S(1)}, bf16[4,48,1536]{2,1,0:T(8,128)(2,1)}, u32[]{:S(2)}) copy-start(bf16[4,48,1536]{2,1,0:T(8,128)(2,1)} %get-tuple-element.88) | copy-start | bytes 1769476
  276.4 46.8 %copy-start.12 = (bf16[1024,192]{1,0:T(8,128)(2,1)S(1)}, bf16[1024,192]{1,0:T(8,128)(2,1)}, u32[]{:S(2)}) copy-start(bf16[1024,192]{1,0:T(8,128)(2,1)} %copy-done.11) | copy-start | bytes 1179652
  339.7 1.1 copy-start.33
  339.7 1.1 copy-start.41
  339.8 1.1 copy-start.43
  339.8 1.1 copy-start.48
  339.9 1.7 copy-start.35
  341.8 32.8 %copy-start.2 = (f32[1024,128]{1,0:T(8,128)S(1)}, f32[1024,128]{1,0:T(8,128)}, u32[]{:S(2)}) copy-start(f32[1024,128]{1,0:T(8,128)} %copy-done.1) | copy-start | bytes 1572868
  374.6 1.1 copy-start.19
  375.7 1.1 copy-start.21
  376.8 7.0 %copy-start.36 = (bf16[4,1,48,4,384]{4,2,3,0,1:T(8,128)(2,1)S(1)}, bf16[4,1,48,4,384]{4,2,3,0,1:T(8,128)(2,1)}, u32[]{:S(2)}) copy-start(bf16[4,1,48,4,384]{4,2,3,0,1:T(8,128)(2,1)} %copy.58) | copy-start | bytes 1769476
  383.8 3.0 copy-start.20
  (9 other events, 7.1 us)

commit v6 on v5

--- a/solution.py
+++ b/solution.py
@@ -408,9 +408,12 @@
             src = x_ref if d == 1 else o_ref.at[d - 2]
             return remote(src, o_ref.at[d - 1], ks.at[d - 1], kr.at[d - 1], u + 1, b)
 
+        def here(d):
+            remote(x_ref, o_ref.at[d - 1], ks.at[d - 1], kr.at[d - 1], u, me.sib).wait_recv()
+
         def relay(d):
             if d > 1:
-                pl.when(u >= d - 1)(lambda: copy(d - 1).wait_recv())
+                pl.when(u >= d - 1)(lambda: here(d - 1))
             pl.when((u >= d - 1) & (u + 1 < nz))(lambda: copy(d).start())
 
         relay(1)
@@ -422,7 +425,7 @@
         g.rest()
         g.finish()
         own.wait()
-        pl.when(u >= back)(lambda: copy(back).wait_recv())
+        pl.when(u >= back)(lambda: here(back))
         for d in range(1, back + 1):
             pl.when((u >= d - 1) & (u + 1 < nz))(lambda d=d: copy(d).wait_send())
 
@@ -1078,7 +1081,7 @@
     )(ok, dq, dkv, kin, *tables, h1, packed, tail)
 
 
-def experts(h2_own, g_own, g_oth, router, hot, weights, sent, leave, nz, nb, cid):
+def experts(h2_own, g_own, g_oth, router, hot, n2, inv2, gain2, cot, weights, sent, leave, nz, nb, cid):
     T = h2_own.shape[0]
     nc = nb // 2
     step = 2 * T
@@ -1090,13 +1093,13 @@
     ng = len(leave)
     resident = nb <= 8
 
-    def kernel(x_ref, g0_ref, g1_ref, r_ref, e_ref, *rest):
+    def kernel(x_ref, g0_ref, g1_ref, r_ref, e_ref, n_ref, v_ref, k_ref, c_ref, *rest):
         win = rest[:nw]
-        y_ref, s_ref = rest[nw:nw + 2]
-        rest = rest[nw + 2:]
+        y_ref, dr_ref, da_ref, dl_ref, dg_ref = rest[nw:nw + 5]
+        rest = rest[nw + 5:]
         din, gin = rest[:ng], rest[ng]
         rest = rest[ng + 1:]
-        h_all, hbuf, part, gbuf, ybuf, wc, acc, zbuf, gs, zs, sem, gsem, ysem, *pair = rest
+        h_all, hbuf, s_ref, part, gbuf, ybuf, wc, acc, zbuf, gs, zs, sem, gsem, ysem, *pair = rest
         me = Layer(nb)
         me.enter(sorted({1, sent[0]}))
         own, oth = h_all.at[0], h_all.at[1]
@@ -1250,6 +1253,26 @@
         ra.phase2()
         back.wait_recv()
         ra.end(add_to(s_ref, zbuf, 1))
+        again = pltpu.make_async_copy(x_ref, hbuf.at[0], zs.at[5])
+        again.start()
+        again.wait()
+        dgates = s_ref[:, D:] + swap(s_ref[:, D:])
+        mask = c_ref[:, D:].astype(f32) > 0
+        logits = mm(hbuf[0], r_ref[...])
+        top = jnp.max(jnp.where(mask, logits, NEG), axis=1, keepdims=True)
+        w = jnp.where(mask, jnp.exp(jnp.where(mask, logits - top, 0.0)), 0.0)
+        gates = w / jnp.sum(w, axis=1, keepdims=True)
+        dlogits = gates * (dgates - jnp.sum(gates * dgates, axis=1, keepdims=True))
+        dlogits = dlogits.astype(bf16)
+        dl_ref[...] = dlogits
+        n = n_ref[...]
+        dh2 = s_ref[:, :D] + mm(dlogits, r_ref[...], NT)
+        dg_ref[...] = jnp.sum(dh2 * n, axis=0, keepdims=True)
+        d_normed = dh2 * k_ref[...]
+        dv = v_ref[...] * (d_normed - n * jnp.mean(d_normed * n, axis=1, keepdims=True))
+        dresid = c_ref[:, :D].astype(f32) + dv
+        dr_ref[...] = dresid
+        da_ref[...] = dresid.astype(bf16)
         back.wait_send()
         mate.wait_send()
         for r in (ga, gb, ra, rb):
@@ -1264,15 +1287,17 @@
     v = lambda shape, kind=bf16: pltpu.VMEM(shape, kind)
     return pl.pallas_call(
         kernel,
-        out_shape=(sh((2, nb, T, D), bf16), sh((T, C), f32))
+        out_shape=(
+            sh((2, nb, T, D), bf16), sh((T, D), f32), sh((T, D), bf16), sh((T, LANES), bf16), sh((1, D), f32),
+        )
         + tuple(sh((dz, width), bf16) for _, _, width in leave)
         + (sh((dz, sent[2]), bf16),)
         + (() if resident else (sh((2, nb, T, D), bf16),)),
-        in_specs=[ANY] * 3 + [VMEM] * 2 + [ANY] * nw,
-        out_specs=(ANY, VMEM) + (ANY,) * (ng + 1 + int(not resident)),
+        in_specs=[ANY] * 3 + [VMEM] * 6 + [ANY] * nw,
+        out_specs=(ANY,) + (VMEM,) * 4 + (ANY,) * (ng + 1 + int(not resident)),
         scratch_shapes=([v((2, nb, T, D))] if resident else [])
         + [
-            v((2, T, D)), v((2, nb, T, C)), v((2, step, C)), v((2, 2, T, D)),
+            v((2, T, D)), v((T, C), f32), v((2, nb, T, C)), v((2, step, C)), v((2, 2, T, D)),
             v((D, W)), v((D, W), f32), v((2, T, C)),
             Gather.scratch(nb, 2), DMA((8,)), DMA((max(nw, ng),)), DMA((2,)), DMA((2,)),
         ]
@@ -1282,7 +1307,7 @@
         ),
         cost_estimate=NO_COST,
         name="experts",
-    )(h2_own, g_own, g_oth, router, hot, *[a for a, _, _ in weights])
+    )(h2_own, g_own, g_oth, router, hot, n2, inv2, gain2, cot, *[a for a, _, _ in weights])
 
 
 def finish(dh1, x, gain, dresid, pin, win, resid, ysum, yfar, grads, places):
@@ -1351,13 +1376,6 @@
     return normed, inverse, normed * gain
 
 
-def norm_back(upstream, normed, inverse, gain):
-    d_normed = upstream * gain
-    d_gain = jnp.sum(upstream * normed, axis=0)
-    d_values = inverse * (d_normed - normed * jnp.mean(d_normed * normed, axis=-1, keepdims=True))
-    return d_values, d_gain
-
-
 def rows_of(a, start, count):
     return a if a.shape[0] == count else lax.dynamic_slice_in_dim(a, start, count, 0)
 
@@ -1406,7 +1424,6 @@
 
     flip = lambda d: [(k, k ^ d) for k in range(nz)]
     give = lambda w, d: lax.ppermute(w, "ulysses", flip(d))
-    named = jnp.any(routes[:, :, None] + HW == lanes[None, None, :], axis=1)
     second, packed = lax.optimization_barrier((same_b if early % 2 == 0 else other[:, half:], packed))
     second = give(second, early)
     weights = [(same_a, 0, 0), (same_b, 0, half), (first, early, 0)]
@@ -1448,24 +1465,14 @@
     sent = (early, 0, FF)
     leave = [(0, 0, W), (early, FF, W - FF), (nz - 1, 0, half), (nz - 1, half, half)]
     leave += [(d, 0, W) for d in range(1, nz - 1) if d != early]
-    y, summed, *grads = experts(h2_own, g_own, g_oth, router, hot, weights, sent, leave, nz, nb, 3)
+    y, dresid, dattn, dlogits, d_gain2, *grads = experts(
+        h2_own, g_own, g_oth, router, hot, n2, inv2, gain2, cot_mask, weights, sent, leave, nz, nb, 3)
     grads, got = grads[:len(leave)], grads[len(leave)]
 
-    upstream = cotangent.astype(f32)
-    dgates = summed[:, D:] + jnp.roll(summed[:, D:], HW, 1)
-    logits = mm(h2_own, router)
-    top = jnp.max(jnp.where(named, logits, NEG), axis=1, keepdims=True)
-    w = jnp.where(named, jnp.exp(jnp.where(named, logits - top, 0.0)), 0.0)
-    gates = w / jnp.sum(w, axis=1, keepdims=True)
-    dlogits = gates * (dgates - jnp.sum(gates * dgates, axis=1, keepdims=True))
-    dlogits = dlogits.astype(bf16)
-    dh2 = summed[:, :D] + mm(dlogits, router, NT)
-    d_norm2, d_gain2 = norm_back(dh2, n2, inv2, gain2)
-    dresid = upstream + d_norm2
     grads = [grads[0]] + [give(a, d) for a, (d, _, _) in zip(grads[1:], leave[1:])]
-    dattn, ysum, yfar = middle(dresid.astype(bf16), y, nb, 5)
+    dattn, ysum, yfar = middle(dattn, y, nb, 5)
     dattn = dattn.reshape(R, D)
-    tail = mm(h2_own, dlogits, TN) + jnp.where(lanes == HW + E, d_gain2[:, None], 0.0)
+    tail = mm(h2_own, dlogits, TN) + jnp.where(lanes == HW + E, d_gain2[0][:, None], 0.0)
 
     dq, dkv, dwo = attend_back(q, kv_all, starts, meta, lse, mixed, rows_of(dattn, at, Rq), wo)
     dkv, *grads = lax.optimization_barrier((dkv, *grads))

time: 449 us -> 450 us (level)
    unnamed x104 -> x70, local copies, waits for them, and re-layouts: 22.1 us -> 20.3 us
  transfers between devices with their start and end apart: 7 -> 7, of which waited for: 2 -> 2; matrix products, arithmetic and copies ran while one was open for 4% -> 4% of each run, Pallas kernels for 21% -> 20%
where the time goes in v6:
time: 450 us; the launch traced here: 449 us
  Pallas kernels  365 us (81%)
  local copies, waits for them, and re-layouts  31.5 us (7%)
  waiting for transfers between devices  26.7 us (6%)
  other arithmetic  14.5 us (3%)
  starting transfers between devices  9.05 us (2%)
    pallas_call x1, Pallas kernels, experts(): pl.pallas_call(kernel, out_shape=(sh((2, nb, T, D), bf16), sh((T, D), f32...  77.4 us
    pallas_call x1, Pallas kernels, gather_inputs(): pl.pallas_call(kernel, out_shape=(sh((nb,) + x.shape, x.dtype), sh((nz, n...  72.1 us
    pallas_call x1, Pallas kernels, reduce_last(): pl.pallas_call(kernel, out_shape=(sh((rows, cols), f32), sh((nb, shard, w...  51.7 us
    pallas_call x1, Pallas kernels, middle(): pl.pallas_call(kernel, out_shape=(sh((nb,) + x.shape, x.dtype), sh((rows,...  45.1 us
    pallas_call x1, Pallas kernels, halo_back(): pl.pallas_call(kernel, out_shape=(jax.ShapeDtypeStruct(((back + 1) * rp,...  34.4 us
    ppermute x7, waiting for transfers between devices, on_device(): give = lambda w, d: lax.ppermute(w, 'ulysses', flip(d))  26.7 us
    pallas_call x1, Pallas kernels, halo_forward(): pl.pallas_call(kernel, out_shape=(sh((back,) + kv.shape, kv.dtype), sh((n...  20.8 us
    unnamed x70, local copies, waits for them, and re-layouts  20.3 us
  transfers between devices with their start and end apart: 7, of which 2 were waited for; matrix products, arithmetic and copies ran while one was open for 4% of the time, Pallas kernels for 20%

profile of v6, /device:TPU:1, one launch (start us, length us, event | category | flops | bytes accessed | tf_op | source)
XLA Modules:
  0.0 448.6 jit_solution(10659567684508857094)
XLA Ops:
  1.4 0.8 copy.42.refs_8_
  3.0 1.4 copy-done.12
  4.4 1.1 copy-done.20
  5.5 1.0 copy-done.21
  6.5 0.9 copy-done.23
  7.4 0.8 copy-done.25
  8.2 0.8 copy-done.26
  9.0 3.1 prepare.1
  12.1 0.8 copy-done.6
  14.4 72.1 %gather_inputs.1 = (bf16[8,128,1536]{2,1,0:T(8,128)(2,1)}, bf16[4,8,48,384]{3,2,1,0:T(8,128)(2,1)}, bf16[4,48,1536]{2,1,0:T(8,128)(2,1)}, bf16[8,128,1664]{2,1,0...) custom-call(bf16[128,1536]{1,0:T(8,128)(2,1)} %x_ref.3, bf16[8,48,384]{2,1,0:T(8,128)(2,1)} %copy-done.22, ...), custom_call_target="tpu_custom_call" | custom-call | tf_op jit(solution)/shard_map/gather_inputs/pallas_call | solution.py:377
  86.6 2.0 slice_convert_fusion
  88.7 1.8 slice.70.r_ref
  90.9 1.4 copy.50
  92.5 1.9 fusion
  95.1 1.9 copy-done.2
  97.0 4.0 project.1
  101.0 1.7 copy-done.1
  102.6 0.9 copy-done.3
  104.8 7.3 %collective-permute-done.rest_3_ = bf16[384,768]{1,0:T(8,128)(2,1)} collective-permute-done((bf16[384,768]{1,0:T(8,128)(2,1)}, bf16[384,768]{1,0:T(8,128)(2,1)}, u32[]{:S(2)}, u32[]{:S(2)}) %collective-permute-start) | collective-permute-done | bytes 589856 | tf_op jit(solution)/shard_map/ppermute | solution.py:1426
  112.1 20.8 %halo_forward.1 = (bf16[2,1024,128]{2,1,0:T(8,128)(2,1)}, bf16[8,128,1664]{2,1,0:T(8,128)(2,1)}) custom-call(bf16[1024,128]{1,0:T(8,128)(2,1)} %copy-done.14, bf16[128,1664]{1,0:T(8,128)(2,1)} %get-tuple-element.86.g_ref), custom_call_target="tpu_custom_call" | custom-call | tf_op jit(solution)/shard_map/halo_forward/pallas_call | solution.py:433
  133.3 2.0 collective-permute-start.2
  135.3 1.1 slice_bitcast_fusion.3
  136.4 8.6 %attend.1 = (bf16[1024,192]{1,0:T(8,128)(2,1)S(1)}, f32[3,1024,1]{2,1,0:T(8,128)S(1)}) custom-call(s32[5]{0:T(128)S(1)} %pad_add_fusion.1.meta, bf16[3,1024,128]{2,1,0:T(8,128)(2,1)S(1)} %copy-done.4, bf16[3072,128]{1,0:T(8,128)(2,1)S(1)} %pad_maximum_fusion.1.kv_ref, s32[1024,1]{1,0:T(8,128)S(1)} %copy.46.st_ref), custom_call_target="tpu_custom_call" | custom-call | tf_op jit(solution)/shard_map/attend/pallas_call | solution.py:941
  145.1 18.4 %reduce_product.1 = f32[128,1536]{1,0:T(8,128)S(1)} custom-call(bf16[1024,192]{1,0:T(8,128)(2,1)S(1)} %get-tuple-element.90.l_ref.o_ref, bf16[192,1536]{1,0:T(8,128)(2,1)S(1)} %bitcast.41), custom_call_target="tpu_custom_call" | custom-call | tf_op jit(solution)/shard_map/reduce_product/pallas_call | solution.py:483
  163.5 1.0 multiply_reduce_fusion
  165.2 2.3 multiply_convert_fusion
  167.5 19.3 %collective-permute-done.2.rest_5_ = bf16[384,1536]{1,0:T(8,128)(2,1)} collective-permute-done((bf16[384,1536]{1,0:T(8,128)(2,1)}, bf16[384,1536]{1,0:T(8,128)(2,1)}, u32[]{:S(2)}, u32[]{:S(2)}) %collective-permute-start.2) | collective-permute-done | bytes 1179680 | tf_op jit(solution)/shard_map/ppermute | solution.py:1426
  186.9 77.4 %experts.1 = (bf16[2,8,128,1536]{3,2,1,0:T(8,128)(2,1)}, f32[128,1536]{1,0:T(8,128)}, bf16[128,1536]{1,0:T(8,128)(2,1)}, bf16[128,128]{1,0:T(8,128)(2,1)}, f32[1...) custom-call(bf16[128,1536]{1,0:T(8,128)(2,1)} %get-tuple-element.172, ...), custom_call_target="tpu_custom_call" | custom-call | tf_op jit(solution)/shard_map/experts/pallas_call | solution.py:1288
  264.4 3.3 collective-permute-start.3
  267.9 3.1 collective-permute-start.5
  271.1 45.1 %middle.1 = (bf16[8,128,1536]{2,1,0:T(8,128)(2,1)}, f32[128,1536]{1,0:T(8,128)}, bf16[128,1536]{1,0:T(8,128)(2,1)}) custom-call(bf16[128,1536]{1,0:T(8,128)(2,1)} %get-tuple-element.97.x_ref, bf16[2,8,128,1536]{3,2,1,0:T(8,128)(2,1)} %get-tuple-element.98.y_ref), custom_call_target="tpu_custom_call" | custom-call | tf_op jit(solution)/shard_map/middle/pallas_call | solution.py:525
  316.2 15.6 %attend_back.1 = (bf16[3,1024,128]{2,1,0:T(8,128)(2,1)S(1)}, f32[3072,128]{1,0:T(8,128)}, f32[192,1536]{1,0:T(8,128)S(1)}) custom-call(s32[5]{0:T(128)S(1)} %pad_add_fusion.1.meta, bf16[3,1024,128]{2,1,0:T(8,128)(2,1)S(1)} %copy-done.5, bf16[3072,128]{1,0:T(8,128)(2,1)S(1)} %pad_maximum_fusion.1.kv_ref, s32[1024,1]{1,0:T(8,128)S(1)} %copy.46.st_ref, ...), custom_call_target="tpu_custom_call" | custom-call | tf_op jit(solution)/shard_map/attend_back/pallas_call | solution.py:1012
  331.8 0.9 copy-done.16
  332.8 0.9 reshape.168
  333.7 1.1 copy.52
  335.3 1.1 slice.58.dkv_ref
  336.4 1.5 convert.16
  337.9 1.1 slice_bitcast_fusion.1
  339.0 1.0 pad_maximum_fusion.2.d_ref
  340.0 34.4 %halo_back.1 = (bf16[3,1024,128]{2,1,0:T(8,128)(2,1)}, bf16[128,1536]{1,0:T(8,128)(2,1)}) custom-call(bf16[3,1024,128]{2,1,0:T(8,128)(2,1)} %pad_maximum_fusion.2.d_ref, bf16[128,1536]{1,0:T(8,128)(2,1)} %get-tuple-element.108.y_ref), custom_call_target="tpu_custom_call" | custom-call | tf_op jit(solution)/shard_map/halo_back/pallas_call | solution.py:579
  374.4 1.1 copy-done.17
  375.6 1.1 copy-done.19
  376.7 6.9 %weight_grads.1 = (bf16[1024,384]{1,0:T(8,128)(2,1)S(1)}, bf16[1536,384]{1,0:T(8,128)(2,1)}) custom-call(s32[4]{0:T(128)S(1)} %pad_add_fusion.ok_ref, bf16[3,1024,128]{2,1,0:T(8,128)(2,1)S(1)} %copy-done.17, f32[1024,128]{1,0:T(8,128)S(1)} %slice.58.dkv_ref, bf16[3,1024,128]{2,1,0:T(8,128)(2,1)S(1)} %copy-done.19, f32[1024,128]{1,0:T(8,128)S(1)} %get-tuple-element.185.c_ref, ...), custom_call_target="tpu_custom_call" | custom-call | tf_op jit(solution)/shard_map/weight_grads/pallas_call | solution.py:1069
  383.6 3.0 pad_maximum_fusion.p_ref
  386.6 51.7 %reduce_last.1 = (f32[128,1536]{1,0:T(8,128)}, bf16[8,48,384]{2,1,0:T(8,128)(2,1)}, bf16[1,4,48,384]{3,2,1,0:T(8,128)(2,1)}) custom-call(bf16[1024,384]{1,0:T(8,128)(2,1)} %copy-done.18, bf16[1536,384]{1,0:T(8,128)(2,1)} %bitcast.38, bf16[4,12,48,384]{3,2,1,0:T(8,128)(2,1)} %pad_maximum_fusion.p_ref), custom_call_target="tpu_custom_call" | custom-call | tf_op jit(solution)/shard_map/reduce_last/pallas_call | solution.py:731
  438.3 7.3 %finish.1 = (f32[128,1536]{1,0:T(8,128)}, f32[48,1536]{1,0:T(8,128)}, f32[48,512]{1,0:T(8,128)}, f32[48,512]{1,0:T(8,128)}, f32[48,128]{1,0:T(8,128)}, /*index=5...) custom-call(f32[128,1536]{1,0:T(8,128)} %get-tuple-element.116.d_ref, ...), custom_call_target="tpu_custom_call" | custom-call | tf_op jit(solution)/shard_map/finish/pallas_call | solution.py:1356
  445.6 1.5 slice_reduce_fusion
  447.1 0.8 slice.66
  (86 shorter events, 8.4 us)
Async XLA Ops:
  3.0 1.4 copy-start.12
  4.4 1.1 copy-start.20
  5.5 1.0 copy-start.21
  6.5 0.9 copy-start.23
  7.4 0.8 copy-start.25
  8.2 0.8 copy-start.26
  12.1 0.8 copy-start.6
  12.9 0.8 copy-start.11
  13.7 0.7 copy-start.22
  14.4 76.1 %copy-start.27 = (bf16[384,1536]{1,0:T(8,128)(2,1)}, bf16[384,1536]{1,0:T(8,128)(2,1)S(1)}, u32[]{:S(2)}) copy-start(bf16[384,1536]{1,0:T(8,128)(2,1)S(1)} %get-tuple-element.96) | copy-start | bytes 3538948
  14.4 76.1 %copy-start.32 = (s32[3]{0:T(128)S(1)}, s32[3]{0:T(128)}, u32[]{:S(2)}) copy-start(s32[3]{0:T(128)} %param.14) | copy-start | bytes 40
  86.5 25.6 %collective-permute-start = (bf16[384,768]{1,0:T(8,128)(2,1)}, bf16[384,768]{1,0:T(8,128)(2,1)}, u32[]{:S(2)}, u32[]{:S(2)}) collective-permute-start(bf16[384,768]{1,0:T(8,128)(2,1)} %get-tuple-element.84.rest_1_), channel_id=1, source_target_pairs={{0,16},{8,24},{16,0},{24,8},{1,17},{9,25},{17,1},{25,9},{2,18},{10... | collective-permute-start | bytes 1769480 | tf_op jit(solution)/shard_map/ppermute | solution.py:1426
  90.5 4.6 %copy-start = (bf16[4,8,48,384]{3,2,1,0:T(8,128)(2,1)S(1)}, bf16[4,8,48,384]{3,2,1,0:T(8,128)(2,1)}, u32[]{:S(2)}) copy-start(bf16[4,8,48,384]{3,2,1,0:T(8,128)(2,1)} %get-tuple-element.78) | copy-start | bytes 3538948
  95.1 5.9 %copy-start.24 = (f32[1,1536]{1,0:T(1,128)}, f32[1,1536]{1,0:T(1,128)S(1)}, u32[]{:S(2)}) copy-start(f32[1,1536]{1,0:T(1,128)S(1)} %get-tuple-element.182.g_ref) | copy-start | bytes 18436
  95.1 1.9 copy-start.2
  101.0 1.7 copy-start.1
  102.6 0.9 copy-start.3
  103.5 0.7 copy-start.14
  104.7 31.6 %copy-start.15 = (bf16[1024,128]{1,0:T(8,128)(2,1)S(1)}, bf16[1024,128]{1,0:T(8,128)(2,1)}, u32[]{:S(2)}) copy-start(bf16[1024,128]{1,0:T(8,128)(2,1)} %copy-done.14) | copy-start | bytes 786436
  132.9 3.5 copy-start.4
  133.0 34.6 %collective-permute-start.1 = (bf16[384,1536]{1,0:T(8,128)(2,1)}, bf16[384,1536]{1,0:T(8,128)(2,1)}, u32[]{:S(2)}, u32[]{:S(2)}) collective-permute-start(bf16[384,1536]{1,0:T(8,128)(2,1)} %copy-done.27), channel_id=1, source_target_pairs={{0,8},{8,0},{16,24},{24,16},{1,9},{9,1},{17,25},{25,17},{2,10},{10... | collective-permute-start | bytes 3538952 | tf_op jit(solution)/shard_map/ppermute | solution.py:1426
  133.3 53.6 %collective-permute-start.2 = (bf16[384,1536]{1,0:T(8,128)(2,1)}, bf16[384,1536]{1,0:T(8,128)(2,1)}, u32[]{:S(2)}, u32[]{:S(2)}) collective-permute-start(bf16[384,1536]{1,0:T(8,128)(2,1)} %copy-done.27), channel_id=1, source_target_pairs={{0,24},{8,16},{16,8},{24,0},{1,25},{9,17},{17,9},{25,1},{2,26},{10... | collective-permute-start | bytes 3538952 | tf_op jit(solution)/shard_map/ppermute | solution.py:1426
  136.3 8.7 %copy-start.7 = (bf16[4,48,1536]{2,1,0:T(8,128)(2,1)S(1)}, bf16[4,48,1536]{2,1,0:T(8,128)(2,1)}, u32[]{:S(2)}) copy-start(bf16[4,48,1536]{2,1,0:T(8,128)(2,1)} %get-tuple-element.91) | copy-start | bytes 1769476
  136.4 27.1 %copy-start.28 = (bf16[128,1536]{1,0:T(8,128)(2,1)S(1)}, bf16[128,1536]{1,0:T(8,128)(2,1)}, u32[]{:S(2)}) copy-start(bf16[128,1536]{1,0:T(8,128)(2,1)} %x_ref.3) | copy-start | bytes 1179652
  145.0 19.4 %copy-start.9 = (bf16[1024,192]{1,0:T(8,128)(2,1)}, bf16[1024,192]{1,0:T(8,128)(2,1)S(1)}, u32[]{:S(2)}) copy-start(bf16[1024,192]{1,0:T(8,128)(2,1)S(1)} %get-tuple-element.90.l_ref.o_ref) | copy-start | bytes 1179652
  145.0 19.4 %copy-start.13 = (f32[3,1024,1]{2,1,0:T(8,128)}, f32[3,1024,1]{2,1,0:T(8,128)S(1)}, u32[]{:S(2)}) copy-start(f32[3,1024,1]{2,1,0:T(8,128)S(1)} %get-tuple-element.89.l_ref) | copy-start | bytes 36868
  264.3 71.0 %collective-permute-start.6 = (bf16[384,1536]{1,0:T(8,128)(2,1)}, bf16[384,1536]{1,0:T(8,128)(2,1)}, u32[]{:S(2)}, u32[]{:S(2)}) collective-permute-start(bf16[384,1536]{1,0:T(8,128)(2,1)} %get-tuple-element.106), channel_id=1, source_target_pairs={{0,8},{8,0},{16,24},{24,16},{1,9},{9,1},{17,25},{25,17},{2,10},{10... | collective-permute-start | bytes 3538952 | tf_op jit(solution)/shard_map/ppermute | solution.py:1426
  264.4 70.9 %collective-permute-start.3 = (bf16[384,1024]{1,0:T(8,128)(2,1)}, bf16[384,1024]{1,0:T(8,128)(2,1)}, u32[]{:S(2)}, u32[]{:S(2)}) collective-permute-start(bf16[384,1024]{1,0:T(8,128)(2,1)} %get-tuple-element.103), channel_id=1, source_target_pairs={{0,16},{8,24},{16,0},{24,8},{1,17},{9,25},{17,1},{25,9},{2,18},{10... | collective-permute-start | bytes 2359304 | tf_op jit(solution)/shard_map/ppermute | solution.py:1426
  267.7 67.6 %collective-permute-start.4 = (bf16[384,768]{1,0:T(8,128)(2,1)}, bf16[384,768]{1,0:T(8,128)(2,1)}, u32[]{:S(2)}, u32[]{:S(2)}) collective-permute-start(bf16[384,768]{1,0:T(8,128)(2,1)} %get-tuple-element.104), channel_id=1, source_target_pairs={{0,24},{8,16},{16,8},{24,0},{1,25},{9,17},{17,9},{25,1},{2,26},{10... | collective-permute-start | bytes 1769480 | tf_op jit(solution)/shard_map/ppermute | solution.py:1426
  267.9 67.4 %collective-permute-start.5 = (bf16[384,768]{1,0:T(8,128)(2,1)}, bf16[384,768]{1,0:T(8,128)(2,1)}, u32[]{:S(2)}, u32[]{:S(2)}) collective-permute-start(bf16[384,768]{1,0:T(8,128)(2,1)} %get-tuple-element.105), channel_id=1, source_target_pairs={{0,24},{8,16},{16,8},{24,0},{1,25},{9,17},{17,9},{25,1},{2,26},{10... | collective-permute-start | bytes 1769480 | tf_op jit(solution)/shard_map/ppermute | solution.py:1426
  271.1 45.1 %copy-start.5 = (bf16[3,1024,128]{2,1,0:T(8,128)(2,1)S(1)}, bf16[3,1024,128]{2,1,0:T(8,128)(2,1)}, u32[]{:S(2)}) copy-start(bf16[3,1024,128]{2,1,0:T(8,128)(2,1)} %copy-done.3) | copy-start | bytes 2359300
  271.1 45.1 %copy-start.8 = (bf16[4,48,1536]{2,1,0:T(8,128)(2,1)S(1)}, bf16[4,48,1536]{2,1,0:T(8,128)(2,1)}, u32[]{:S(2)}) copy-start(bf16[4,48,1536]{2,1,0:T(8,128)(2,1)} %get-tuple-element.91) | copy-start | bytes 1769476
  271.1 45.1 %copy-start.10 = (bf16[1024,192]{1,0:T(8,128)(2,1)S(1)}, bf16[1024,192]{1,0:T(8,128)(2,1)}, u32[]{:S(2)}) copy-start(bf16[1024,192]{1,0:T(8,128)(2,1)} %copy-done.9) | copy-start | bytes 1179652
  331.8 0.9 copy-start.16
  332.7 2.1 copy-start.31
  332.7 2.2 copy-start.29
  332.8 2.2 copy-start.30
  374.4 1.1 copy-start.17
  375.6 1.1 copy-start.19
  383.6 3.0 copy-start.18
